TPU v7x, 32 devices: a whole 2x2x4 slice. The times are simulated.
32 devices in a mesh: ctx: 4 (over y, x), tp: 8 (over z, core).
Axes of the slice: x: 2, y: 2, z: 4, core: 2. Of those that a mesh axis runs over, the one named last changes fastest.
Arguments:
- token_ids: int32 [1536], P('ctx'), may hold values from 65 to 84, as said below
- embed_table: bfloat16 [512, 4096], replicated, may hold values from -6 to 6
- norm_gain: float32 [4096], replicated, may hold values from 0.5 to 1.5
- input_weight: bfloat16 [4096, 3, 4096], P(None, None, 'tp'), may hold values from -0.09375 to 0.09375
- short_weight: float32 [3, 3, 4096], P(None, None, 'tp'), may hold values from -3 to 3
- filters: float32 [256, 1536], P('tp', 'ctx'), may hold values from -1.1 to 1.1
- skip_gain: float32 [4096], P('tp'), may hold values from 0.1 to 1.9
- output_weight: bfloat16 [4096, 4096], P(None, 'tp'), may hold values from -0.09375 to 0.09375
- output_grad: bfloat16 [1536, 4096], P('ctx'), may hold values from -6 to 6
Outputs:
- block_output: bfloat16 [1536, 4096], P('ctx')
- output_weight_grad: float32 [4096, 4096], P('ctx', 'tp')
- projection_grad: bfloat16 [1536, 3, 4096], P('ctx', None, 'tp')
- normed_grad: float32 [1536, 4096], P(('ctx', 'tp'))
Inputs may be any that keep to these rules, and one draw needn't show every extreme that they name: `token_ids`: each id is the byte code of A, C, G, T or N.
All inputs are finite; a program needn't handle non-finite values.
Results may differ from a plain program's by a relative error of at most 0.0065.
Values may be sent and summed in bfloat16 or wider, within the bound.
No kernel may reach another device: no remote copies, remote signals or barrier semaphores. Data moves between devices by JAX's collectives and lax.ppermute only.
A program may use at most 256 MiB of HBM per device.

v0:
```python
import math

import jax
import jax.numpy as jnp
from jax import lax
from jax.sharding import PartitionSpec as P

precise = lax.Precision.HIGHEST


def from_partner(value, axis, distance):
    mask = 2**distance
    pairs = [(source, source ^ mask) for source in range(lax.axis_size(axis))]
    return lax.ppermute(value, axis, pairs)


def from_behind(value, axis, steps):
    count = lax.axis_size(axis)
    first, last = (max(0, -steps), min(count, count - steps))
    return lax.ppermute(value, axis, [(source, source + steps) for source in range(first, last)])


def cosine_sine(numerator, denominator):
    angles = 2.0 * math.pi / denominator * (numerator % denominator).astype(jnp.float32)
    return (jnp.cos(angles), jnp.sin(angles))


def bit_reverse(shard_index, depth_bits):
    result = jnp.zeros((), jnp.int32)
    for position in range(depth_bits):
        result = result + ((shard_index >> position & 1) << depth_bits - 1 - position)
    return result


def start_stack(signal, shard_index, shards):
    shift_cos, shift_sin = cosine_sine(shard_index, 2 * shards)
    real_part = jnp.stack([signal, signal * shift_cos])
    imag_part = jnp.stack([jnp.zeros_like(signal), -signal * shift_sin])
    return jnp.stack([real_part, imag_part], axis=1)


def forward_level(own_part, theirs, upper_half, angle_index, half_span):
    rotate_cos, rotate_sin = cosine_sine(angle_index, 2 * half_span)
    difference = theirs - own_part
    rotated = jnp.stack(
        [
            difference[:, 0] * rotate_cos + difference[:, 1] * rotate_sin,
            difference[:, 1] * rotate_cos - difference[:, 0] * rotate_sin,
        ],
        axis=1,
    )
    return jnp.where(upper_half, rotated, own_part + theirs)


def rotate_conj(spectrum_stack, rotate_cos, rotate_sin):
    return jnp.stack(
        [
            spectrum_stack[:, 0] * rotate_cos - spectrum_stack[:, 1] * rotate_sin,
            spectrum_stack[:, 1] * rotate_cos + spectrum_stack[:, 0] * rotate_sin,
        ],
        axis=1,
    )


def finish_spectrum(spectrum_stack, reversed_index, period, tables):
    local_rows = spectrum_stack.shape[2]
    positions = jnp.arange(local_rows, dtype=jnp.int32)
    frequency = 2 * reversed_index + jnp.arange(2, dtype=jnp.int32)
    twist_cos, twist_sin = cosine_sine(frequency[:, None] * positions[None, :], period)
    twist_cos = twist_cos[:, :, None]
    twist_sin = twist_sin[:, :, None]
    real_in = spectrum_stack[:, 0] * twist_cos + spectrum_stack[:, 1] * twist_sin
    imag_in = spectrum_stack[:, 1] * twist_cos - spectrum_stack[:, 0] * twist_sin
    table_cos, table_sin = tables
    real_out = jnp.einsum("br,erw->ebw", table_cos, real_in, precision=precise) + jnp.einsum(
        "br,erw->ebw", table_sin, imag_in, precision=precise
    )
    imag_out = jnp.einsum("br,erw->ebw", table_cos, imag_in, precision=precise) - jnp.einsum(
        "br,erw->ebw", table_sin, real_in, precision=precise
    )
    return jnp.stack([real_out, imag_out], axis=1)


def to_spectra(signals, tables):
    shards = lax.axis_size("ctx")
    shard_index = lax.axis_index("ctx")
    depth_bits = shards.bit_length() - 1
    stacks = tuple((start_stack(signal, shard_index, shards) for signal in signals))
    for section_index in range(depth_bits):
        which_bit = depth_bits - 1 - section_index
        half_span = 1 << which_bit
        if len(stacks) == 2:
            partners = from_partner((stacks[0], stacks[1]), "ctx", which_bit)
        else:
            partners = (from_partner(stacks[0], "ctx", which_bit),)
        upper_half = shard_index >> which_bit & 1 == 1
        stacks = tuple(
            (
                forward_level(own_part, theirs, upper_half, shard_index % half_span, half_span)
                for own_part, theirs in zip(stacks, partners)
            )
        )
    reversed_index = bit_reverse(shard_index, depth_bits)
    period = 2 * shards * signals[0].shape[0]
    return tuple(
        (
            finish_spectrum(spectrum_stack, reversed_index, period, tables)
            for spectrum_stack in stacks
        )
    )


def from_spectrum(spectrum, tables):
    shards = lax.axis_size("ctx")
    shard_index = lax.axis_index("ctx")
    depth_bits = shards.bit_length() - 1
    local_rows = spectrum.shape[2]
    period = 2 * shards * local_rows
    table_cos, table_sin = tables
    real_in = spectrum[:, 0]
    imag_in = spectrum[:, 1]
    real_mid = jnp.einsum("rb,ebw->erw", table_cos, real_in, precision=precise) - jnp.einsum(
        "rb,ebw->erw", table_sin, imag_in, precision=precise
    )
    imag_mid = jnp.einsum("rb,ebw->erw", table_cos, imag_in, precision=precise) + jnp.einsum(
        "rb,ebw->erw", table_sin, real_in, precision=precise
    )
    positions = jnp.arange(local_rows, dtype=jnp.int32)
    frequency = 2 * bit_reverse(shard_index, depth_bits) + jnp.arange(2, dtype=jnp.int32)
    twist_cos, twist_sin = cosine_sine(frequency[:, None] * positions[None, :], period)
    twist_cos = twist_cos[:, :, None]
    twist_sin = twist_sin[:, :, None]
    real_part = real_mid * twist_cos - imag_mid * twist_sin
    imag_part = imag_mid * twist_cos + real_mid * twist_sin
    current = jnp.stack([real_part, imag_part], axis=1)
    for which_bit in range(depth_bits):
        half_span = 1 << which_bit
        theirs = from_partner(current, "ctx", which_bit)
        upper_half = shard_index >> which_bit & 1 == 1
        rotate_cos, rotate_sin = cosine_sine(shard_index % half_span, 2 * half_span)
        current = jnp.where(
            upper_half,
            theirs - rotate_conj(current, rotate_cos, rotate_sin),
            current + rotate_conj(theirs, rotate_cos, rotate_sin),
        )
    shift_cos, shift_sin = cosine_sine(shard_index, 2 * shards)
    return (current[0, 0] + shift_cos * current[1, 0] - shift_sin * current[1, 1]) / period


def group_product(signal_spec, filter_spec, conjugate):
    spec_shape = signal_spec.shape
    groups = filter_spec.shape[3]
    signal_view = signal_spec.reshape(
        spec_shape[0], spec_shape[1], spec_shape[2], groups, spec_shape[3] // groups
    )
    filter_view = filter_spec[..., None]
    real_signal = signal_view[:, 0]
    imag_signal = signal_view[:, 1]
    real_filter = filter_view[:, 0]
    imag_filter = -filter_view[:, 1] if conjugate else filter_view[:, 1]
    real_out = real_filter * real_signal - imag_filter * imag_signal
    imag_out = real_filter * imag_signal + imag_filter * real_signal
    return jnp.stack([real_out, imag_out], axis=1).reshape(spec_shape)


def body(
    token_ids,
    embed_table,
    norm_gain,
    input_weight,
    short_weight,
    filters,
    skip_gain,
    output_weight,
    output_grad,
):
    local_rows = token_ids.shape[0]
    tokens = jnp.take(embed_table, token_ids, axis=0)
    token_values = tokens.astype(jnp.float32)
    inverse_rms = lax.rsqrt(jnp.mean(token_values * token_values, axis=-1, keepdims=True) + 1e-06)
    normed = (token_values * inverse_rms * norm_gain).astype(jnp.bfloat16)
    projected = jnp.einsum("td,djc->tjc", normed, input_weight, preferred_element_type=jnp.float32)
    short_taps = short_weight.shape[0]
    before = from_behind(projected[local_rows - (short_taps - 1) :], "ctx", 1)
    extended = jnp.concatenate([before, projected], axis=0)
    features = sum(
        (
            short_weight[tap_index]
            * extended[short_taps - 1 - tap_index : short_taps - 1 - tap_index + local_rows]
            for tap_index in range(short_taps)
        )
    )
    queries = features[:, 0]
    key_part = features[:, 1]
    value_part = features[:, 2]
    mixture = key_part * value_part
    filter_rows = filters.T
    positions = jnp.arange(local_rows, dtype=jnp.int32)
    tables = cosine_sine(positions[:, None] * positions[None, :], local_rows)
    mixture_spec, filter_spec = to_spectra((mixture, filter_rows), tables)
    long_part = from_spectrum(group_product(mixture_spec, filter_spec, False), tables)
    mixed_out = skip_gain * mixture + long_part
    hidden = (queries * mixed_out).astype(jnp.bfloat16)
    partial_sums = jnp.einsum(
        "tc,dc->td", hidden, output_weight, preferred_element_type=jnp.float32
    )
    total_sums = lax.psum(partial_sums, "tp")
    block_output = (token_values + total_sums).astype(jnp.bfloat16)
    hidden_grad = jnp.dot(output_grad, output_weight, preferred_element_type=jnp.float32)
    output_weight_grad = lax.psum_scatter(
        jnp.einsum("td,tc->dc", output_grad, hidden, preferred_element_type=jnp.float32),
        "ctx",
        scatter_dimension=0,
        tiled=True,
    )
    mixed_grad = hidden_grad * queries
    (grad_spec,) = to_spectra((mixed_grad,), tables)
    carried = from_spectrum(group_product(grad_spec, filter_spec, True), tables)
    mixture_grad = skip_gain * mixed_grad + carried
    feature_grad = jnp.stack(
        [hidden_grad * mixed_out, mixture_grad * value_part, mixture_grad * key_part], axis=1
    )
    following = from_behind(feature_grad[: short_taps - 1], "ctx", -1)
    extended_grads = jnp.concatenate([feature_grad, following], axis=0)
    projection_grad = sum(
        (
            short_weight[tap_index] * extended_grads[tap_index : tap_index + local_rows]
            for tap_index in range(short_taps)
        )
    ).astype(jnp.bfloat16)
    normed_grad = lax.psum_scatter(
        jnp.einsum(
            "tjc,djc->td", projection_grad, input_weight, preferred_element_type=jnp.float32
        ),
        "tp",
        scatter_dimension=0,
        tiled=True,
    )
    return (block_output, output_weight_grad, projection_grad, normed_grad)


def solution(mesh):
    in_specs = (
        P("ctx"),
        P(),
        P(),
        P(None, None, "tp"),
        P(None, None, "tp"),
        P("tp", "ctx"),
        P("tp"),
        P(None, "tp"),
        P("ctx", None),
    )
    out_specs = (P("ctx", None), P("ctx", "tp"), P("ctx", None, "tp"), P(("ctx", "tp"), None))
    return jax.shard_map(body, mesh=mesh, in_specs=in_specs, out_specs=out_specs, check_vma=False)
```

profile of v0, /device:TPU:0, one launch (start us, length us, event | category | flops | bytes accessed | tf_op | source)
XLA Modules:
  0.0 953.0 jit_solution(6518519907281478356)
XLA Ops:
  9.7 11.0 %gather_fusion = bf16[384,4096]{1,0:T(8,128)(2,1)} fusion(bf16[512,4096]{1,0:T(8,128)(2,1)} %param.10, s32[1024]{0:T(1024)S(1)} %pad_clamp_fusion), kind=kCustom, calls=%fused_computation | custom fusion | bytes 6292992 | tf_op jit(solution)/shard_map/jit(_take)/gather | solution.py:178
  20.6 3.0 fusion
  23.7 8.7 fusion.5
  32.4 1.4 copy-done.18
  33.8 5.4 collective-permute-start
  40.0 4.1 fusion.16
  46.0 2.2 pad_maximum_fusion
  48.7 3.2 collective-permute-start.3
  52.1 67.1 %collective-permute-done.3 = f32[2,2,384,512]{3,2,0,1:T(8,128)} collective-permute-done((f32[2,2,384,512]{3,2,0,1:T(8,128)}, f32[2,2,384,512]{3,2,0,1:T(8,128)}, u32[]{:S(2)}, u32[]{:S(2)}) %collective-permute-start.3) | collective-permute-done | bytes 3145760 | tf_op jit(solution)/shard_map/ppermute | solution.py:14
  119.2 3.6 fusion.234
  124.2 1.6 copy-done.5
  125.8 4.8 maximum_select_fusion
  132.1 1.5 collective-permute-start.1
  133.6 4.4 collective-permute-done.1
  138.0 1.3 collective-permute-start.2
  139.5 63.5 %collective-permute-done.2 = f32[2,2,384,32]{2,3,0,1:T(8,128)S(1)} collective-permute-done((f32[2,2,384,32]{2,3,0,1:T(8,128)S(1)}, f32[2,2,384,32]{2,3,0,1:T(8,128)S(1)}, u32[]{:S(2)}, u32[]{:S(2)}) %collective-permute-start.2) | collective-permute-done | bytes 196640 | tf_op jit(solution)/shard_map/ppermute | solution.py:14
  203.2 3.0 fusion.75
  206.2 3.0 fusion.31
  209.2 3.1 fusion.77
  212.3 3.0 fusion.32
  215.4 4.4 fusion.262
  220.2 4.1 maximum_select_fusion.1
  224.3 7.4 fusion.57
  231.7 7.8 fusion.59
  239.5 7.4 convolution_add_fusion.3
  246.9 7.7 fusion.21
  254.7 4.9 fusion.71
  259.6 5.3 fusion.69
  264.9 4.9 convolution_add_fusion.2
  269.8 5.4 fusion.30
  276.5 66.3 %collective-permute-done.5 = f32[2,2,384,512]{3,2,0,1:T(8,128)S(1)} collective-permute-done((f32[2,2,384,512]{3,2,0,1:T(8,128)S(1)}, f32[2,2,384,512]{3,2,0,1:T(8,128)S(1)}, u32[]{:S(2)}, u32[]{:S(2)}) %collective-permute-start.5) | collective-permute-done | bytes 3145760 | tf_op jit(solution)/shard_map/ppermute | solution.py:14
  343.4 1.6 fusion.7
  345.0 1.2 collective-permute-start.6
  346.7 64.7 %collective-permute-done.6 = f32[2,2,384,512]{3,2,0,1:T(8,128)S(1)} collective-permute-done((f32[2,2,384,512]{3,2,0,1:T(8,128)S(1)}, f32[2,2,384,512]{3,2,0,1:T(8,128)S(1)}, u32[]{:S(2)}, u32[]{:S(2)}) %collective-permute-start.6) | collective-permute-done | bytes 3145760 | tf_op jit(solution)/shard_map/ppermute | solution.py:14
  411.9 2.8 fusion.8
  414.7 5.3 multiply_bitcast_fusion.1
  421.6 64.5 %collective-permute-done.7 = f32[2,2,384,512]{3,2,0,1:T(8,128)S(1)} collective-permute-done((f32[2,2,384,512]{3,2,0,1:T(8,128)S(1)}, f32[2,2,384,512]{3,2,0,1:T(8,128)S(1)}, u32[]{:S(2)}, u32[]{:S(2)}) %collective-permute-start.7) | collective-permute-done | bytes 3145760 | tf_op jit(solution)/shard_map/ppermute | solution.py:14
  488.7 64.4 %collective-permute-done.8 = f32[2,2,384,512]{3,2,0,1:T(8,128)S(1)} collective-permute-done((f32[2,2,384,512]{3,2,0,1:T(8,128)S(1)}, f32[2,2,384,512]{3,2,0,1:T(8,128)S(1)}, u32[]{:S(2)}, u32[]{:S(2)}) %collective-permute-start.8) | collective-permute-done | bytes 3145760 | tf_op jit(solution)/shard_map/ppermute | solution.py:14
  553.1 1.7 fusion.260
  555.2 2.4 maximum_select_fusion.3
  557.6 7.4 fusion.51
  565.0 7.5 fusion.53
  572.5 7.4 convolution_add_fusion.1
  579.8 7.8 fusion.23
  587.6 4.9 fusion.65
  592.5 5.3 fusion.63
  597.8 4.9 convolution_add_fusion
  602.8 5.4 fusion.27
  609.2 62.9 %collective-permute-done.9 = f32[2,2,384,512]{3,2,0,1:T(8,128)S(1)} collective-permute-done((f32[2,2,384,512]{3,2,0,1:T(8,128)S(1)}, f32[2,2,384,512]{3,2,0,1:T(8,128)S(1)}, u32[]{:S(2)}, u32[]{:S(2)}) %collective-permute-start.9) | collective-permute-done | bytes 3145760 | tf_op jit(solution)/shard_map/ppermute | solution.py:14
  672.7 1.6 fusion.9
  674.9 62.0 %collective-permute-done.10 = f32[2,2,384,512]{3,2,0,1:T(8,128)S(1)} collective-permute-done((f32[2,2,384,512]{3,2,0,1:T(8,128)S(1)}, f32[2,2,384,512]{3,2,0,1:T(8,128)S(1)}, u32[]{:S(2)}, u32[]{:S(2)}) %collective-permute-start.10) | collective-permute-done | bytes 3145760 | tf_op jit(solution)/shard_map/ppermute | solution.py:14
  737.4 2.8 fusion.10
  740.2 1.4 fusion.44
  742.7 1.3 copy-done.17
  744.0 4.5 fusion.242
  748.6 5.8 convolution_bitcast_fusion
  754.5 2.0 pad_maximum_fusion.6
  756.5 1.4 collective-permute-start.11
  757.9 4.3 collective-permute-done.11
  764.3 11.1 %convolution_bitcast_fusion.1 = f32[384,4096]{1,0:T(8,128)} fusion(bf16[384,3,512]{2,0,1:T(8,128)(2,1)S(1)} %fusion.18, bf16[4096,3,512]{2,0,1:T(8,128)(2,1)} %param.12), kind=kOutput, calls=%fused_computation.9 | convolution fusion | flops 4831838208 | bytes 20054016 | tf_op jit(solution)/shard_map/tjc,djc->td/dot_general | solution.py:232
  775.4 136.8 %all-reduce.5.cloned.1.call-done = f32[384,4096]{1,0:T(8,128)} async-done(((f32[384,4096]{1,0:T(8,128)}), f32[384,4096]{1,0:T(8,128)}) %all-reduce.5.cloned.1.call-update) | async-done | bytes 6291472 | tf_op jit(solution)/shard_map/psum | solution.py:207
  912.2 6.7 fusion.3
  918.9 2.9 copy.29
  921.8 23.6 %reduce-scatter.5.cloned.1.call-done = f32[48,4096]{1,0:T(8,128)} async-done(((f32[384,4096]{1,0:T(8,128)}), f32[48,4096]{1,0:T(8,128)}) %reduce-scatter.5.cloned.1.call-update) | async-done | bytes 786448 | tf_op jit(solution)/shard_map/reduce_scatter | solution.py:231
  (121 shorter events, 21.7 us)
Async XLA Ops:
  8.0 406.7 %copy-start = (bf16[384,4096]{1,0:T(8,128)(2,1)S(1)}, bf16[384,4096]{1,0:T(8,128)(2,1)}, u32[]{:S(2)}) copy-start(bf16[384,4096]{1,0:T(8,128)(2,1)} %param.17) | copy-start | bytes 9437188
  8.0 904.2 %all-reduce.5.cloned.1.call-start = ((), (), s32[]{:S(2)}) async-start(), calls=%async_computation.2 | async-start | bytes 12582912 | tf_op jit(solution)/shard_map/psum | solution.py:207
  8.9 14.8 %copy-start.27 = (pred[384]{0:T(512)(128)(4,1)}, pred[384]{0:T(512)(128)(4,1)S(1)}, u32[]{:S(2)}) copy-start(pred[384]{0:T(512)(128)(4,1)S(1)} %compare_and_fusion) | copy-start | bytes 1156
  9.7 14.0 %copy-start.30 = (f32[4096]{0:T(1024)S(1)}, f32[4096]{0:T(1024)}, u32[]{:S(2)}) copy-start(f32[4096]{0:T(1024)} %param.11) | copy-start | bytes 49156
  20.6 3.0 copy-start.7
  23.7 15.5 %copy-start.26 = (f32[3,3,512]{2,1,0:T(4,128)S(1)}, f32[3,3,512]{2,1,0:T(4,128)}, u32[]{:S(2)}) copy-start(f32[3,3,512]{2,1,0:T(4,128)} %param.13) | copy-start | bytes 55300
  32.4 1.4 copy-start.18
  33.8 6.2 collective-permute-start
  39.2 4.9 copy-start.22
  39.2 4.9 copy-start.24
  44.1 1.4 copy-start.12
  46.0 2.2 copy-start.1
  46.0 2.7 copy-start.4
  46.0 6.1 copy-start.21
  48.7 70.5 %collective-permute-start.3 = (f32[2,2,384,512]{3,2,0,1:T(8,128)}, f32[2,2,384,512]{3,2,0,1:T(8,128)}, u32[]{:S(2)}, u32[]{:S(2)}) collective-permute-start(f32[2,2,384,512]{3,2,0,1:T(8,128)} %pad_maximum_fusion), channel_id=1, source_target_pairs={{0,16},{8,24},{16,0},{24,8},{1,17},{9,25},{17,1},{25,9},{2,18},{10... | collective-permute-start | bytes 9437192 | tf_op jit(solution)/shard_map/ppermute | solution.py:14
  122.7 1.4 copy-start.2
  122.8 3.0 copy-start.5
  123.2 7.3 copy-start.8
  123.2 7.3 copy-start.10
  130.5 84.8 %collective-permute-start.4 = (f32[2,2,384,512]{3,2,0,1:T(8,128)}, f32[2,2,384,512]{3,2,0,1:T(8,128)}, u32[]{:S(2)}, u32[]{:S(2)}) collective-permute-start(f32[2,2,384,512]{3,2,0,1:T(8,128)} %maximum_select_fusion), channel_id=1, source_target_pairs={{0,8},{8,0},{16,24},{24,16},{1,9},{9,1},{17,25},{25,17},{2,10},{10... | collective-permute-start | bytes 9437192 | tf_op jit(solution)/shard_map/ppermute | solution.py:14
  132.1 5.9 collective-permute-start.1
  138.0 65.0 %collective-permute-start.2 = (f32[2,2,384,32]{2,3,0,1:T(8,128)S(1)}, f32[2,2,384,32]{2,3,0,1:T(8,128)S(1)}, u32[]{:S(2)}, u32[]{:S(2)}) collective-permute-start(f32[2,2,384,32]{2,3,0,1:T(8,128)S(1)} %maximum_select_fusion.4), channel_id=1, source_target_pairs={{0,8},{8,0},{16,24},{24,16},{1,9},{9,1},{17,25},{25,17},{2,10},{10... | collective-permute-start | bytes 589832 | tf_op jit(solution)/shard_map/ppermute | solution.py:14
  203.2 12.2 %copy-start.11 = (f32[2,1,384,512]{3,2,0,1:T(8,128)S(1)}, f32[2,1,384,512]{3,2,0,1:T(8,128)}, u32[]{:S(2)}) copy-start(f32[2,1,384,512]{3,2,0,1:T(8,128)} %copy-done.10) | copy-start | bytes 4718596
  206.1 9.2 copy-start.9
  209.1 6.2 copy-start.6
  212.3 3.1 copy-start.3
  275.6 67.3 %collective-permute-start.5 = (f32[2,2,384,512]{3,2,0,1:T(8,128)S(1)}, f32[2,2,384,512]{3,2,0,1:T(8,128)S(1)}, u32[]{:S(2)}, u32[]{:S(2)}) collective-permute-start(f32[2,2,384,512]{3,2,0,1:T(8,128)S(1)} %pad_maximum_fusion.1), channel_id=1, source_target_pairs={{0,8},{8,0},{16,24},{24,16},{1,9},{9,1},{17,25},{25,17},{2,10},{10... | collective-permute-start | bytes 9437192 | tf_op jit(solution)/shard_map/ppermute | solution.py:14
  345.0 66.4 %collective-permute-start.6 = (f32[2,2,384,512]{3,2,0,1:T(8,128)S(1)}, f32[2,2,384,512]{3,2,0,1:T(8,128)S(1)}, u32[]{:S(2)}, u32[]{:S(2)}) collective-permute-start(f32[2,2,384,512]{3,2,0,1:T(8,128)S(1)} %fusion.7), channel_id=1, source_target_pairs={{0,16},{8,24},{16,0},{24,8},{1,17},{9,25},{17,1},{25,9},{2,18},{10... | collective-permute-start | bytes 9437192 | tf_op jit(solution)/shard_map/ppermute | solution.py:14
  411.9 2.8 copy-start.13
  411.9 2.8 copy-start.29
  420.7 65.5 %collective-permute-start.7 = (f32[2,2,384,512]{3,2,0,1:T(8,128)S(1)}, f32[2,2,384,512]{3,2,0,1:T(8,128)S(1)}, u32[]{:S(2)}, u32[]{:S(2)}) collective-permute-start(f32[2,2,384,512]{3,2,0,1:T(8,128)S(1)} %pad_maximum_fusion.2), channel_id=1, source_target_pairs={{0,16},{8,24},{16,0},{24,8},{1,17},{9,25},{17,1},{25,9},{2,18},{10... | collective-permute-start | bytes 9437192 | tf_op jit(solution)/shard_map/ppermute | solution.py:14
  488.6 64.5 %collective-permute-start.8 = (f32[2,2,384,512]{3,2,0,1:T(8,128)S(1)}, f32[2,2,384,512]{3,2,0,1:T(8,128)S(1)}, u32[]{:S(2)}, u32[]{:S(2)}) collective-permute-start(f32[2,2,384,512]{3,2,0,1:T(8,128)S(1)} %maximum_select_fusion.2), channel_id=1, source_target_pairs={{0,8},{8,0},{16,24},{24,16},{1,9},{9,1},{17,25},{25,17},{2,10},{10... | collective-permute-start | bytes 9437192 | tf_op jit(solution)/shard_map/ppermute | solution.py:14
  608.5 63.6 %collective-permute-start.9 = (f32[2,2,384,512]{3,2,0,1:T(8,128)S(1)}, f32[2,2,384,512]{3,2,0,1:T(8,128)S(1)}, u32[]{:S(2)}, u32[]{:S(2)}) collective-permute-start(f32[2,2,384,512]{3,2,0,1:T(8,128)S(1)} %pad_maximum_fusion.3), channel_id=1, source_target_pairs={{0,8},{8,0},{16,24},{24,16},{1,9},{9,1},{17,25},{25,17},{2,10},{10... | collective-permute-start | bytes 9437192 | tf_op jit(solution)/shard_map/ppermute | solution.py:14
  674.2 62.7 %collective-permute-start.10 = (f32[2,2,384,512]{3,2,0,1:T(8,128)S(1)}, f32[2,2,384,512]{3,2,0,1:T(8,128)S(1)}, u32[]{:S(2)}, u32[]{:S(2)}) collective-permute-start(f32[2,2,384,512]{3,2,0,1:T(8,128)S(1)} %fusion.9), channel_id=1, source_target_pairs={{0,16},{8,24},{16,0},{24,8},{1,17},{9,25},{17,1},{25,9},{2,18},{10... | collective-permute-start | bytes 9437192 | tf_op jit(solution)/shard_map/ppermute | solution.py:14
  740.2 1.4 copy-start.20
  741.5 2.5 copy-start.17
  748.5 170.4 %reduce-scatter.3.cloned.1.call-start = ((), (), s32[]{:S(2)}) async-start(), calls=%async_computation.3 | async-start | bytes 10485760 | tf_op jit(solution)/shard_map/reduce_scatter | solution.py:210
  754.4 191.0 %reduce-scatter.5.cloned.1.call-start = ((), (), s32[]{:S(2)}) async-start(), calls=%async_computation.4 | async-start | bytes 7077888 | tf_op jit(solution)/shard_map/reduce_scatter | solution.py:231
  754.4 7.8 copy-start.14
  754.4 7.8 copy-start.15
  754.4 7.7 copy-start.16
  756.4 6.1 copy-start.23
  756.4 6.1 copy-start.25
  756.5 5.7 collective-permute-start.11
  763.3 1.0 copy-start.19
  775.4 136.8 %copy-start.28 = (pred[384]{0:T(512)(128)(4,1)S(1)}, pred[384]{0:T(512)(128)(4,1)}, u32[]{:S(2)}) copy-start(pred[384]{0:T(512)(128)(4,1)} %copy-done.27) | copy-start | bytes 1156
Sparse Core Ops, SparseCore 0:
  748.7 163.5 all-reduce.4
Sparse Core Ops, SparseCore 1:
  754.4 85.8 reduce-scatter.2
  843.1 102.2 reduce-scatter.4
where the time goes:
time: 959 us; the launch traced here: 953 us
  waiting for transfers between devices  685 us (71%)
  matrix products  149 us (16%)
  other arithmetic  63 us (7%)
  local copies, waits for them, and re-layouts  22.2 us (2%)
  starting transfers between devices  17 us (2%)
  between operations  16.9 us (2%)
    ppermute x10, waiting for transfers between devices, from_partner(): return lax.ppermute(value, axis, pairs)  520 us
    psum x1, waiting for transfers between devices, body(): total_sums = lax.psum(partial_sums, 'tp')  137 us
    reduce_scatter x1, waiting for transfers between devices, body(): lax.psum_scatter(jnp.einsum('tjc,djc->td', projection_grad, input_weight,...  23.6 us
  transfers between devices with their start and end apart: 15, of which 13 were waited for; matrix products, arithmetic and copies ran while one was open for 5% of the time, Pallas kernels for 0%

commit v1 on v0

v1 whole, which is shorter than its diff:
```python
import functools

import jax
import jax.numpy as jnp
from jax import lax
from jax.experimental import pallas as pl
from jax.experimental.pallas import tpu as pltpu
from jax.sharding import PartitionSpec as P

LANES = 128
FIRST_ID = 64
IDS = 24
VMEM_BYTES = 60 * 1024 * 1024
f32 = jnp.float32
bf16 = jnp.bfloat16


def one_hot(ids, taps):
    length = ids.shape[1]
    lane = lax.broadcasted_iota(jnp.int32, (1, length), 1)
    code = lax.broadcasted_iota(jnp.int32, (IDS, length), 0) + FIRST_ID
    rows = []
    for tap in range(taps):
        moved = ids if tap == 0 else jnp.where(lane < tap, 0, pltpu.roll(ids, tap, axis=1))
        rows.append(jnp.where(code == moved, 1.0, 0.0))
    return jnp.concatenate(rows, axis=0)


def tap_weights(taps_ref, table_ref, part):
    table = table_ref[part]
    value = jnp.concatenate([taps_ref[i, part][None, :] * table for i in range(taps_ref.shape[0])], axis=0)
    high = value.astype(bf16).astype(f32)
    return jnp.concatenate([high, value - high], axis=0).astype(bf16)


def expand(weights, hot):
    return lax.dot_general(weights, hot, (((0,), (0,)), ((), ())), preferred_element_type=f32)


def toeplitz_tiles(row, blocks):
    sub = lax.broadcasted_iota(jnp.int32, (LANES, LANES), 0)
    lane = lax.broadcasted_iota(jnp.int32, (LANES, LANES), 1)
    keep = lane >= sub
    before = jnp.zeros((LANES, LANES), f32)
    tiles = []
    for q in range(blocks):
        part = jnp.broadcast_to(row[:, LANES * q : LANES * (q + 1)], (LANES, LANES))
        turned = pltpu.roll(part, 0, 1, stride=1, stride_axis=0)
        tiles.append(jnp.where(keep, turned, before).astype(bf16))
        before = turned
    return tiles


def lanes_at(block, count):
    return pl.ds(pl.multiple_of(block * LANES, LANES), count * LANES)


def gather_slots(me, slots, store):
    for step, slot in enumerate(slots):
        store(jnp.bitwise_xor(me, step), slot)


def forward_kernel(shards, me_ref, *refs):
    ids_slots, filter_slots = refs[:shards], refs[shards : 2 * shards]
    table_ref, taps_ref, columns_ref, hidden_ref, mixed_ref = refs[2 * shards : 2 * shards + 5]
    ids_all, hot, filters, signal, exact, long_part = refs[2 * shards + 5 :]
    me = me_ref[0]
    groups, local_rows = filter_slots[0].shape
    channels = table_ref.shape[2]
    width = channels // groups
    local_blocks = local_rows // LANES
    blocks = shards * local_blocks
    length = blocks * LANES
    window = local_blocks + 1

    for step in range(shards):
        place = lanes_at(jnp.bitwise_xor(me, step) * local_blocks, local_blocks)
        ids_all[:, place] = ids_slots[step][...]
        filters[:, place] = filter_slots[step][...]
    marks = one_hot(ids_all[...], taps_ref.shape[0])
    hot[:, :length] = jnp.concatenate([marks, marks], axis=0).astype(bf16)
    hot[:, length:] = jnp.zeros((hot.shape[0], LANES), bf16)

    signal[:, :length] = jnp.zeros((channels, length), bf16)
    signal[:, 2 * length :] = jnp.zeros((channels, LANES), bf16)
    exact[:, length:] = jnp.zeros((channels, LANES), f32)
    key_weights = tap_weights(taps_ref, table_ref, 1)
    value_weights = tap_weights(taps_ref, table_ref, 2)
    for start in range(0, channels, LANES):
        rows = slice(start, start + LANES)
        mixture = expand(key_weights[:, rows], hot[:, :length]) * expand(value_weights[:, rows], hot[:, :length])
        exact[rows, :length] = mixture
        signal[rows, length : 2 * length] = mixture.astype(bf16)

    first = me * local_blocks

    def one_group(group, carry):
        tiles = toeplitz_tiles(filters[pl.ds(group, 1), :], blocks)
        matrix = jnp.concatenate(tiles[::-1], axis=0)
        rows = pl.ds(pl.multiple_of(group * width, width), width)
        left = jnp.concatenate([signal[rows, lanes_at(first + i + 1, blocks)] for i in range(window)], axis=0)
        result = jnp.dot(left, matrix, preferred_element_type=f32)
        for i in range(window):
            long_part[rows, i * LANES : (i + 1) * LANES] = result[i * width : (i + 1) * width]
        return carry

    lax.fori_loop(0, groups, one_group, 0, unroll=2)
    own = lanes_at(first, window)
    mixed = columns_ref[:, 9:10] * exact[:, own] + long_part[...]
    mixed_ref[...] = mixed
    queries = expand(tap_weights(taps_ref, table_ref, 0), hot[:, lanes_at(first, local_blocks)])
    hidden_ref[...] = jnp.transpose(queries * mixed[:, :local_rows]).astype(bf16)


def backward_kernel(shards, me_ref, *refs):
    ids_slots, filter_slots, grad_slots = refs[:shards], refs[shards : 2 * shards], refs[2 * shards : 3 * shards]
    table_ref, taps_ref, columns_ref, mixed_ref, out_ref = refs[3 * shards : 3 * shards + 5]
    ids_all, hot, filters, grads, signal, exact, long_part = refs[3 * shards + 5 :]
    me = me_ref[0]
    groups, local_rows = filter_slots[0].shape
    channels = table_ref.shape[2]
    width = channels // groups
    local_blocks = local_rows // LANES
    blocks = shards * local_blocks
    length = blocks * LANES
    window = local_blocks + 1
    taps = taps_ref.shape[0]

    for step in range(shards):
        place = lanes_at(jnp.bitwise_xor(me, step) * local_blocks, local_blocks)
        ids_all[:, place] = ids_slots[step][...]
        filters[:, place] = filter_slots[step][...]
        grads[:, place] = grad_slots[step][...]
    grads[:, length:] = jnp.zeros((channels, LANES), bf16)
    marks = one_hot(ids_all[...], taps)
    hot[:, :length] = jnp.concatenate([marks, marks], axis=0).astype(bf16)
    hot[:, length:] = jnp.zeros((hot.shape[0], LANES), bf16)

    signal[:, length:] = jnp.zeros((channels, length + LANES), bf16)
    exact[:, length:] = jnp.zeros((channels, LANES), f32)
    query_weights = tap_weights(taps_ref, table_ref, 0)
    for start in range(0, channels, LANES):
        rows = slice(start, start + LANES)
        mixed_grad = expand(query_weights[:, rows], hot[:, :length]) * grads[rows, :length].astype(f32)
        exact[rows, :length] = mixed_grad
        signal[rows, :length] = mixed_grad.astype(bf16)

    first = me * local_blocks

    def one_group(group, carry):
        tiles = toeplitz_tiles(filters[pl.ds(group, 1), :], blocks)
        matrix = jnp.concatenate(tiles, axis=1)
        rows = pl.ds(pl.multiple_of(group * width, width), width)
        left = jnp.concatenate([signal[rows, lanes_at(first + i, blocks)] for i in range(window)], axis=0)
        result = lax.dot_general(left, matrix, (((1,), (1,)), ((), ())), preferred_element_type=f32)
        for i in range(window):
            long_part[rows, i * LANES : (i + 1) * LANES] = result[i * width : (i + 1) * width]
        return carry

    lax.fori_loop(0, groups, one_group, 0, unroll=2)
    own = lanes_at(first, window)
    mixture_grad = columns_ref[:, 9:10] * exact[:, own] + long_part[...]
    span = window * LANES
    for part in range(3):
        if part == 0:
            feature_grad = grads[:, own].astype(f32) * mixed_ref[...]
        else:
            other = expand(tap_weights(taps_ref, table_ref, 3 - part), hot[:, own])
            feature_grad = mixture_grad * other
        total = columns_ref[:, part : part + 1] * feature_grad
        for tap in range(1, taps):
            column = 3 * tap + part
            total = total + columns_ref[:, column : column + 1] * pltpu.roll(feature_grad, span - tap, axis=1)
        out_ref[part] = jnp.transpose(total[:, :local_rows]).astype(bf16)


def in_vmem(count):
    return [pl.BlockSpec(memory_space=pltpu.VMEM)] * count


def run_forward(me, ids, filters, table, taps, columns):
    shards = len(ids)
    groups, local_rows = filters[0].shape
    channels = table.shape[2]
    length = shards * local_rows
    span = local_rows + LANES
    rows = 2 * taps.shape[0] * IDS
    return pl.pallas_call(
        functools.partial(forward_kernel, shards),
        out_shape=(
            jax.ShapeDtypeStruct((local_rows, channels), bf16),
            jax.ShapeDtypeStruct((channels, span), f32),
        ),
        in_specs=[pl.BlockSpec(memory_space=pltpu.SMEM)] + in_vmem(2 * shards + 3),
        out_specs=tuple(in_vmem(2)),
        scratch_shapes=[
            pltpu.VMEM((1, length), jnp.int32),
            pltpu.VMEM((rows, length + LANES), bf16),
            pltpu.VMEM((groups, length), f32),
            pltpu.VMEM((channels, 2 * length + LANES), bf16),
            pltpu.VMEM((channels, length + LANES), f32),
            pltpu.VMEM((channels, span), f32),
        ],
        compiler_params=pltpu.CompilerParams(vmem_limit_bytes=VMEM_BYTES),
        cost_estimate=pl.CostEstimate(flops=20_000_000_000, bytes_accessed=4_000_000, transcendentals=0),
        name="forward_conv",
    )(me, *ids, *filters, table, taps, columns)


def run_backward(me, ids, filters, grads, table, taps, columns, mixed):
    shards = len(ids)
    groups, local_rows = filters[0].shape
    channels = table.shape[2]
    length = shards * local_rows
    span = local_rows + LANES
    rows = 2 * taps.shape[0] * IDS
    return pl.pallas_call(
        functools.partial(backward_kernel, shards),
        out_shape=jax.ShapeDtypeStruct((3, local_rows, channels), bf16),
        in_specs=[pl.BlockSpec(memory_space=pltpu.SMEM)] + in_vmem(3 * shards + 4),
        out_specs=pl.BlockSpec(memory_space=pltpu.VMEM),
        scratch_shapes=[
            pltpu.VMEM((1, length), jnp.int32),
            pltpu.VMEM((rows, length + LANES), bf16),
            pltpu.VMEM((groups, length), f32),
            pltpu.VMEM((channels, length + LANES), bf16),
            pltpu.VMEM((channels, 2 * length + LANES), bf16),
            pltpu.VMEM((channels, length + LANES), f32),
            pltpu.VMEM((channels, span), f32),
        ],
        compiler_params=pltpu.CompilerParams(vmem_limit_bytes=VMEM_BYTES),
        cost_estimate=pl.CostEstimate(flops=20_000_000_000, bytes_accessed=4_000_000, transcendentals=0),
        name="backward_conv",
    )(me, *ids, *filters, *grads, table, taps, columns, mixed)


def exchange(value, step):
    count = lax.axis_size("ctx")
    return lax.ppermute(value, "ctx", [(i, i ^ step) for i in range(count)])


def gather_ctx(value):
    return [value] + [exchange(value, step) for step in range(1, lax.axis_size("ctx"))]


def to_sibling(value):
    count = lax.axis_size("tp")
    return lax.ppermute(value, "tp", [(i, i ^ 1) for i in range(count)])


def along_chain(value, direction, senders):
    pairs = [(2 * chip + core, 2 * (chip + direction) + core) for chip in senders for core in range(2)]
    return lax.ppermute(value, "tp", pairs)


def chain_reduce_scatter(own):
    chips = own.shape[0]
    chip = lax.axis_index("tp") // 2
    right = left = None
    for step in range(1, chips):
        to_right = own[jnp.clip(chips + chip - step, 0, chips - 1)]
        to_left = own[jnp.clip(chip + step - chips, 0, chips - 1)]
        if right is not None:
            to_right = to_right + right.astype(f32)
            to_left = to_left + left.astype(f32)
        right = along_chain(to_right.astype(bf16), 1, range(0, step))
        left = along_chain(to_left.astype(bf16), -1, range(chips - step, chips))
    return own[chip] + right.astype(f32) + left.astype(f32)


def chain_all_gather(block, chips):
    chip = lax.axis_index("tp") // 2
    from_left, from_right = [], []
    right = left = block
    for step in range(1, chips):
        right = along_chain(right, 1, range(step - 1, chips - 1))
        left = along_chain(left, -1, range(1, chips - step + 1))
        from_left.append(right)
        from_right.append(left)
    line = jnp.concatenate(from_left[::-1] + [block] + from_right, axis=0)
    rows = block.shape[0]
    return lax.dynamic_slice_in_dim(line, (chips - 1 - chip) * rows, chips * rows, axis=0)


def body(
    token_ids,
    embed_table,
    norm_gain,
    input_weight,
    short_weight,
    filters,
    skip_gain,
    output_weight,
    output_grad,
):
    shards = lax.axis_size("ctx")
    chips = lax.axis_size("tp") // 2
    me = lax.axis_index("ctx")
    core = lax.axis_index("tp") % 2
    chip = lax.axis_index("tp") // 2
    local_rows = token_ids.shape[0]
    width, channels = output_weight.shape
    me_array = jnp.reshape(me, (1,)).astype(jnp.int32)

    ids = [jnp.reshape(slot, (1, local_rows)) for slot in gather_ctx(token_ids)]
    filter_slots = gather_ctx(filters)

    hidden_grad = lax.dot_general(
        output_weight, output_grad, (((0,), (1,)), ((), ())), preferred_element_type=f32
    ).astype(bf16)
    grad_slots = gather_ctx(hidden_grad)

    letters = lax.slice_in_dim(embed_table, FIRST_ID, FIRST_ID + IDS, axis=0)
    letter_values = letters.astype(f32)
    inverse_rms = lax.rsqrt(jnp.mean(letter_values * letter_values, axis=-1, keepdims=True) + 1e-06)
    normed = (letter_values * inverse_rms * norm_gain).astype(bf16)
    table = jnp.einsum("qd,djc->jqc", normed, input_weight, preferred_element_type=f32)

    taps = short_weight.shape[0]
    columns = jnp.transpose(
        jnp.concatenate([short_weight.reshape(3 * taps, channels), skip_gain[None, :]], axis=0)
    )
    hidden, mixed = run_forward(me_array, ids, filter_slots, table, short_weight, columns)

    half = width // 2
    theirs = lax.dynamic_slice_in_dim(output_weight, (1 - core) * half, half, axis=0)
    mine = lax.dynamic_slice_in_dim(output_weight, core * half, half, axis=0)
    contract = (((1,), (1,)), ((), ()))
    received = to_sibling(lax.dot_general(hidden, theirs, contract, preferred_element_type=f32).astype(bf16))
    partial_out = lax.dot_general(hidden, mine, contract, preferred_element_type=f32) + received.astype(f32)
    block_rows = local_rows // chips
    own_out = chain_reduce_scatter(partial_out.reshape(chips, block_rows, half))
    own_ids = lax.dynamic_slice_in_dim(token_ids, chip * block_rows, block_rows, axis=0)
    own_hot = (own_ids[:, None] == jnp.arange(FIRST_ID, FIRST_ID + IDS)[None, :]).astype(bf16)
    own_letters = lax.dynamic_slice_in_dim(letters, core * half, half, axis=1)
    own_tokens = jnp.dot(own_hot, own_letters, preferred_element_type=f32)
    final_block = (own_tokens + own_out).astype(bf16)

    projection_grad = run_backward(
        me_array, ids, filter_slots, grad_slots, table, short_weight, columns, mixed
    )
    split_rows = projection_grad.reshape(3, chips, 2, local_rows // (2 * chips), channels)

    def input_part(which):
        rows = lax.dynamic_index_in_dim(split_rows, which, axis=2, keepdims=False)
        rows = rows.reshape(3, local_rows // 2, channels)
        return jnp.einsum("jtc,djc->td", rows, input_weight, preferred_element_type=f32)

    received_grad = to_sibling(input_part(1 - core).astype(bf16))
    partial_grad = input_part(core) + received_grad.astype(f32)
    normed_grad = chain_reduce_scatter(partial_grad.reshape(chips, local_rows // (2 * chips), width))

    my_half = chain_all_gather(final_block, chips)
    other_half = to_sibling(my_half)
    block_output = jnp.where(
        core == 0,
        jnp.concatenate([my_half, other_half], axis=1),
        jnp.concatenate([other_half, my_half], axis=1),
    )

    share = width // shards
    late_grad, late_hidden = lax.optimization_barrier((output_grad, hidden))
    hidden_slots = gather_ctx(late_hidden)
    output_slots = []
    for step in range(shards):
        piece = lax.dynamic_slice_in_dim(late_grad, jnp.bitwise_xor(me, step) * share, share, axis=1)
        output_slots.append(piece if step == 0 else exchange(piece, step))
    output_weight_grad = lax.dot_general(
        jnp.concatenate(output_slots, axis=0),
        jnp.concatenate(hidden_slots, axis=0),
        (((0,), (0,)), ((), ())),
        preferred_element_type=f32,
    )
    return (block_output, output_weight_grad, jnp.transpose(projection_grad, (1, 0, 2)), normed_grad)


def solution(mesh):
    in_specs = (
        P("ctx"),
        P(),
        P(),
        P(None, None, "tp"),
        P(None, None, "tp"),
        P("tp", "ctx"),
        P("tp"),
        P(None, "tp"),
        P("ctx", None),
    )
    out_specs = (P("ctx", None), P("ctx", "tp"), P("ctx", None, "tp"), P(("ctx", "tp"), None))
    return jax.shard_map(body, mesh=mesh, in_specs=in_specs, out_specs=out_specs, check_vma=False)
```

time: 959 us -> 202 us (0.21)
  waiting for transfers between devices: 685 us -> 44.8 us
  matrix products: 149 us -> 41.2 us
  other arithmetic: 63 us -> 9.01 us
  starting transfers between devices: 17 us -> 65.4 us
  Pallas kernels: 0 us -> 26.7 us
  between operations: 16.9 us -> 1.23 us
  local copies, waits for them, and re-layouts: 22.2 us -> 12.1 us
    ppermute x12 -> x36, waiting for transfers between devices: 525 us -> 44.8 us  [the longest x18 34.3 us: along_chain(): return lax.ppermute(value, 'tp', pairs)]
    psum x1 -> x0, waiting for transfers between devices: 137 us -> none  [body(): total_sums = lax.psum(partial_sums, 'tp')]
    dot_general x25 -> x8, matrix products: 149 us -> 41.2 us  [the longest x2 19.2 us: input_part(): jnp.einsum('jtc,djc->td', rows, input_weight, preferred_element_type=f32)]
    ppermute x12 -> x36, starting transfers between devices: 16.9 us -> 65.4 us  [the longest x18 45 us: along_chain(): return lax.ppermute(value, 'tp', pairs)]
    pallas_call x0 -> x2, Pallas kernels: none -> 26.7 us  [the longest x1 15.1 us: run_backward(): pl.pallas_call(functools.partial(backward_kernel, shards), out_shape=jax....]
    reduce_scatter x2 -> x0, waiting for transfers between devices: 23.6 us -> none  [the longest x1 23.6 us: body(): lax.psum_scatter(jnp.einsum('tjc,djc->td', projection_grad, input_weight,...]
    select_n x11 -> x1, other arithmetic: 22 us -> 2.28 us  [body(): jnp.where(core == 0, jnp.concatenate([my_half, other_half], axis=1), jnp....]
    sub x12 -> x0, other arithmetic: 13.5 us -> none  [the longest x6 10.5 us: forward_level(): difference = theirs - own_part]
  transfers between devices with their start and end apart: 15 -> 36, of which waited for: 13 -> 10; matrix products, arithmetic and copies ran while one was open for 5% -> 27% of each run, Pallas kernels for 0% -> 13%
where the time goes in v1:
time: 202 us; the launch traced here: 200 us
  starting transfers between devices  65.4 us (32%)
  waiting for transfers between devices  44.8 us (22%)
  matrix products  41.2 us (20%)
  Pallas kernels  26.7 us (13%)
  local copies, waits for them, and re-layouts  12.1 us (6%)
  other arithmetic  9.01 us (4%)
    ppermute x18, starting transfers between devices, along_chain(): return lax.ppermute(value, 'tp', pairs)  45 us
    ppermute x18, waiting for transfers between devices, along_chain(): return lax.ppermute(value, 'tp', pairs)  34.3 us
    ppermute x15, starting transfers between devices, exchange(): return lax.ppermute(value, 'ctx', [(i, i ^ step) for i in range(count)])  20.1 us
    dot_general x2, matrix products, input_part(): jnp.einsum('jtc,djc->td', rows, input_weight, preferred_element_type=f32)  19.2 us
    pallas_call x1, Pallas kernels, run_backward(): pl.pallas_call(functools.partial(backward_kernel, shards), out_shape=jax....  15.1 us
    pallas_call x1, Pallas kernels, run_forward(): pl.pallas_call(functools.partial(forward_kernel, shards), out_shape=(jax....  11.5 us
    ppermute x15, waiting for transfers between devices, exchange(): return lax.ppermute(value, 'ctx', [(i, i ^ step) for i in range(count)])  10.5 us
    dot_general x1, matrix products, body(): jnp.einsum('qd,djc->jqc', normed, input_weight, preferred_element_type=f32)  7.19 us
  transfers between devices with their start and end apart: 36, of which 10 were waited for; matrix products, arithmetic and copies ran while one was open for 27% of the time, Pallas kernels for 13%

profile of v1, /device:TPU:0, one launch (start us, length us, event | category | flops | bytes accessed | tf_op | source)
XLA Modules:
  0.0 200.4 jit_solution(2119391335653335197)
XLA Ops:
  0.6 3.0 %collective-permute-start = (s32[384]{0:T(512)}, s32[384]{0:T(512)S(1)}, u32[]{:S(2)}, u32[]{:S(2)}) collective-permute-start(s32[384]{0:T(512)} %param.9), channel_id=1, source_target_pairs={{0,8},{8,0},{16,24},{24,16},{1,9},{9,1},{17,25},{25,17},{2,10},{10... | collective-permute-start | bytes 4616 | tf_op jit(solution)/shard_map/ppermute | solution.py:239
  3.6 1.5 collective-permute-start.1
  5.7 2.9 %collective-permute-start.5 = (f32[32,384]{1,0:T(8,128)}, f32[32,384]{1,0:T(8,128)S(1)}, u32[]{:S(2)}, u32[]{:S(2)}) collective-permute-start(f32[32,384]{1,0:T(8,128)} %refs_4_.3), channel_id=1, source_target_pairs={{0,24},{8,16},{16,8},{24,0},{1,25},{9,17},{17,9},{25,1},{2,26},{10... | collective-permute-start | bytes 147464 | tf_op jit(solution)/shard_map/ppermute | solution.py:239
  8.6 1.1 fusion.31
  9.7 0.8 reshape.66
  10.5 5.7 %convolution_convert_fusion.1.refs_8_ = bf16[512,384]{1,0:T(8,128)(2,1)S(1)} fusion(bf16[4096,512]{1,0:T(8,128)(2,1)} %param.16, bf16[384,4096]{1,0:T(8,128)(2,1)} %param.17), kind=kOutput, calls=%fused_computation.24 | convolution fusion | flops 1610809344 | bytes 7733248 | tf_op jit(solution)/shard_map/dot_general | solution.py:308
  16.2 7.2 %convolution_bitcast_fusion.2.refs_8_.refs_12_ = f32[3,24,512]{2,1,0:T(8,128)} fusion(bf16[4096,3,512]{2,0,1:T(8,128)(2,1)} %param.12, f32[4096]{0:T(1024)S(1)} %copy-done.6, f32[24]{0:T(128)S(1)} %add_rsqrt_fusion, bf16[512,4096]{1,0:T(8,128)(2,1)S(1)} %copy-done.3), kind=kOutput, calls=%fused_computation.25 | convolution fusion | flops 302383104 | bytes 12943872 | tf_op jit(solution)/shard_map/qd,djc->jqc/dot_general | solution.py:317
  24.1 0.8 copy.16
  25.5 1.9 collective-permute-start.26
  27.4 0.6 reshape.64.refs_2_
  28.0 0.6 collective-permute-done.2
  28.6 0.9 collective-permute-start.27
  30.1 1.2 collective-permute-start.28
  31.3 0.6 copy-done.14
  31.9 11.5 %forward_conv.1 = (bf16[384,512]{1,0:T(8,128)(2,1)}, f32[512,512]{1,0:T(8,128)}) custom-call(s32[1]{0:T(128)} %bitcast.me_ref, s32[1,384]{1,0:T(1,128)} %reshape.62.refs_0_, s32[1,384]{1,0:T(1,128)} %reshape.63.refs_1_, s32[1,384]{1,0:T(1,128)} %reshape.64.refs_2_, s32[1,384]{1,0:T(1,128)} %reshape.65.refs_3_, f32[32,384]{1,0:T(8,128)} %refs_4_.3, ...), custom_call_target="tpu_custom_call" | custom-call | flops 20000000000 | bytes 4000000 | tf_op jit(solution)/shard_map/forward_conv/pallas_call | solution.py:188
  43.4 2.7 %convolution_convert_fusion = bf16[384,2048]{1,0:T(8,128)(2,1)S(1)} fusion(bf16[384,512]{1,0:T(8,128)(2,1)} %get-tuple-element.10, bf16[4096,512]{1,0:T(8,128)(2,1)} %param.16, s32[]{:T(128)S(6)} %select_n.75), kind=kOutput, calls=%fused_computation.14 | convolution fusion | flops 806092800 | bytes 4063236 | tf_op jit(solution)/shard_map/dot_general | solution.py:329
  46.3 0.7 copy-done.10
  47.3 15.1 %backward_conv.1 = bf16[3,384,512]{2,1,0:T(8,128)(2,1)} custom-call(s32[1]{0:T(128)} %bitcast.me_ref, s32[1,384]{1,0:T(1,128)} %reshape.62.refs_0_, s32[1,384]{1,0:T(1,128)} %reshape.63.refs_1_, s32[1,384]{1,0:T(1,128)} %reshape.64.refs_2_, s32[1,384]{1,0:T(1,128)} %reshape.65.refs_3_, f32[32,384]{1,0:T(8,128)} %refs_4_.3, f32[32,384]{1,0:T(8,128)} %copy-done.13, ...), custom_call_target="tpu_custom_call" | custom-call | flops 20000000000 | bytes 4000000 | tf_op jit(solution)/shard_map/backward_conv/pallas_call | solution.py:217
  62.4 2.2 %constant_dynamic-slice_fusion = (bf16[3,4,1,48,512]{4,3,2,1,0:T(8,128)(2,1)S(1)}, bf16[3,4,1,48,512]{4,3,2,1,0:T(8,128)(2,1)}) fusion(bf16[3,4,2,48,512]{4,3,2,1,0:T(8,128)(2,1)} %bitcast.94, s32[]{:T(128)S(6)} %select_n.84, s32[]{:T(128)S(6)} %select_n.83), kind=kLoop, calls=%fused_computation.77 | loop fusion | bytes 2359304 | tf_op jit(solution)/shard_map/jit(dynamic_index_in_dim)/dynamic_slice | solution.py:345
  64.6 3.0 %convert_add_fusion = f32[384,2048]{1,0:T(8,128)S(1)} fusion(bf16[384,2048]{1,0:T(8,128)(2,1)} %collective-permute-done.6, bf16[384,512]{1,0:T(8,128)(2,1)S(1)} %copy-done.4, bf16[4096,512]{1,0:T(8,128)(2,1)} %param.16, s32[]{:T(128)S(6)} %select_n.74), kind=kOutput, calls=%fused_computation.13 | convolution fusion | flops 806879232 | bytes 7208964 | tf_op jit(solution)/shard_map/dot_general | solution.py:330
  67.6 1.0 fusion.34
  68.6 4.2 %collective-permute-start.7 = (bf16[96,2048]{1,0:T(8,128)(2,1)}, bf16[96,2048]{1,0:T(8,128)(2,1)}, u32[]{:S(2)}, u32[]{:S(2)}) collective-permute-start(bf16[96,2048]{1,0:T(8,128)(2,1)} %get-tuple-element.22), channel_id=1, source_target_pairs={{0,2},{1,3},{8,10},{9,11},{16,18},{17,19},{24,26},{25,27}} | collective-permute-start | bytes 1179656 | tf_op jit(solution)/shard_map/ppermute | solution.py:253
  72.9 10.0 %fusion.1 = bf16[192,4096]{1,0:T(8,128)(2,1)} fusion(bf16[3,192,512]{2,1,0:T(8,128)(2,1)S(1)} %bitcast.96, bf16[4096,3,512]{2,0,1:T(8,128)(2,1)} %param.12), kind=kOutput, calls=%fused_computation.3 | convolution fusion | flops 2416705536 | bytes 14745600 | tf_op jit(solution)/shard_map/jtc,djc->td/dot_general | solution.py:347
  83.1 1.4 collective-permute-start.10
  84.5 1.8 fusion.26
  86.3 2.1 %collective-permute-start.8 = (bf16[96,2048]{1,0:T(8,128)(2,1)}, bf16[96,2048]{1,0:T(8,128)(2,1)}, u32[]{:S(2)}, u32[]{:S(2)}) collective-permute-start(bf16[96,2048]{1,0:T(8,128)(2,1)} %fusion.26), channel_id=1, source_target_pairs={{0,2},{1,3},{2,4},{3,5},{8,10},{9,11},{10,12},{11,13},{16,18},{17,... | collective-permute-start | bytes 1179656 | tf_op jit(solution)/shard_map/ppermute | solution.py:253
  88.8 8.2 %collective-permute-done.8 = bf16[96,2048]{1,0:T(8,128)(2,1)} collective-permute-done((bf16[96,2048]{1,0:T(8,128)(2,1)}, bf16[96,2048]{1,0:T(8,128)(2,1)}, u32[]{:S(2)}, u32[]{:S(2)}) %collective-permute-start.8) | collective-permute-done | bytes 393248 | tf_op jit(solution)/shard_map/ppermute | solution.py:253
  97.0 1.3 fusion.27
  98.3 0.9 collective-permute-start.11
  99.2 9.2 %fusion = f32[192,4096]{1,0:T(8,128)S(1)} fusion(bf16[3,192,512]{2,1,0:T(8,128)(2,1)S(1)} %bitcast.93, bf16[4096,3,512]{2,0,1:T(8,128)(2,1)} %param.12, bf16[192,4096]{1,0:T(8,128)(2,1)} %collective-permute-done.29), kind=kOutput, calls=%fused_computation.2 | convolution fusion | flops 2417491968 | bytes 17891328 | tf_op jit(solution)/shard_map/jtc,djc->td/dot_general | solution.py:347
  108.4 5.0 %collective-permute-start.9 = (bf16[96,2048]{1,0:T(8,128)(2,1)S(1)}, bf16[96,2048]{1,0:T(8,128)(2,1)S(1)}, u32[]{:S(2)}, u32[]{:S(2)}) collective-permute-start(bf16[96,2048]{1,0:T(8,128)(2,1)S(1)} %get-tuple-element.20), channel_id=1, source_target_pairs={{0,2},{1,3},{2,4},{3,5},{4,6},{5,7},{8,10},{9,11},{10,12},{11,13},... | collective-permute-start | bytes 1179656 | tf_op jit(solution)/shard_map/ppermute | solution.py:253
  113.6 1.3 collective-permute-start.12
  114.9 0.8 fusion.36
  115.7 5.2 %collective-permute-start.30 = (bf16[48,4096]{1,0:T(8,128)(2,1)S(1)}, bf16[48,4096]{1,0:T(8,128)(2,1)S(1)}, u32[]{:S(2)}, u32[]{:S(2)}) collective-permute-start(bf16[48,4096]{1,0:T(8,128)(2,1)S(1)} %get-tuple-element.14), channel_id=1, source_target_pairs={{0,2},{1,3},{8,10},{9,11},{16,18},{17,19},{24,26},{25,27}} | collective-permute-start | bytes 1179656 | tf_op jit(solution)/shard_map/ppermute | solution.py:253
  120.9 1.4 collective-permute-start.33
  122.3 0.6 collective-permute-done.9
  123.0 3.6 %collective-permute-done.12 = bf16[96,2048]{1,0:T(8,128)(2,1)S(1)} collective-permute-done((bf16[96,2048]{1,0:T(8,128)(2,1)S(1)}, bf16[96,2048]{1,0:T(8,128)(2,1)S(1)}, u32[]{:S(2)}, u32[]{:S(2)}) %collective-permute-start.12) | collective-permute-done | bytes 393248 | tf_op jit(solution)/shard_map/ppermute | solution.py:253
  126.7 3.7 %collective-permute-start.13 = (bf16[96,2048]{1,0:T(8,128)(2,1)S(1)}, bf16[96,2048]{1,0:T(8,128)(2,1)S(1)}, u32[]{:S(2)}, u32[]{:S(2)}) collective-permute-start(bf16[96,2048]{1,0:T(8,128)(2,1)S(1)} %fusion.30), channel_id=1, source_target_pairs={{0,2},{1,3},{2,4},{3,5},{4,6},{5,7},{8,10},{9,11},{10,12},{11,13},... | collective-permute-start | bytes 1179656 | tf_op jit(solution)/shard_map/ppermute | solution.py:253
  130.4 1.0 collective-permute-done.30
  131.5 4.4 %collective-permute-start.31 = (bf16[48,4096]{1,0:T(8,128)(2,1)S(1)}, bf16[48,4096]{1,0:T(8,128)(2,1)S(1)}, u32[]{:S(2)}, u32[]{:S(2)}) collective-permute-start(bf16[48,4096]{1,0:T(8,128)(2,1)S(1)} %fusion.21), channel_id=1, source_target_pairs={{0,2},{1,3},{2,4},{3,5},{8,10},{9,11},{10,12},{11,13},{16,18},{17,... | collective-permute-start | bytes 1179656 | tf_op jit(solution)/shard_map/ppermute | solution.py:253
  135.9 1.3 collective-permute-start.16
  137.2 2.7 %collective-permute-done.13 = bf16[96,2048]{1,0:T(8,128)(2,1)S(1)} collective-permute-done((bf16[96,2048]{1,0:T(8,128)(2,1)S(1)}, bf16[96,2048]{1,0:T(8,128)(2,1)S(1)}, u32[]{:S(2)}, u32[]{:S(2)}) %collective-permute-start.13) | collective-permute-done | bytes 393248 | tf_op jit(solution)/shard_map/ppermute | solution.py:253
  139.9 0.7 collective-permute-start.14
  140.6 1.8 collective-permute-start.25
  142.5 2.2 %constant_dynamic-slice_fusion.5 = (bf16[384,1024]{1,0:T(8,128)(2,1)S(1)}, bf16[384,1024]{1,0:T(8,128)(2,1)S(1)}, bf16[384,1024]{1,0:T(8,128)(2,1)S(1)}, bf16[384,1024]{1,0:T(8,128)(2,1)S(1)}) fusion(bf16[384,4096]{1,0:T(8,128)(2,1)} %param.17, s32[]{:T(128)S(6)} %select_n.79, s32[]{:T(128)S(6)} %select_n.82, s32[]{:T(128)S(6)} %select_n.81, s32[]{:T(128)S(6)} %select_n.80), kind=kLoop, calls=%fused_computation.82 | loop fusion | bytes 6291472 | tf_op jit(solution)/shard_map/dynamic_slice | solution.py:366
  144.7 1.2 collective-permute-start.24
  145.9 1.0 collective-permute-done.31
  147.0 1.5 collective-permute-start.23
  148.5 1.3 collective-permute-start.17
  149.8 0.7 collective-permute-start.15
  150.5 1.1 fusion.22
  151.6 9.0 %collective-permute-done.17 = bf16[96,2048]{1,0:T(8,128)(2,1)S(1)} collective-permute-done((bf16[96,2048]{1,0:T(8,128)(2,1)S(1)}, bf16[96,2048]{1,0:T(8,128)(2,1)S(1)}, u32[]{:S(2)}, u32[]{:S(2)}) %collective-permute-start.17) | collective-permute-done | bytes 393248 | tf_op jit(solution)/shard_map/ppermute | solution.py:253
  160.6 1.4 collective-permute-start.22
  162.0 1.3 collective-permute-start.18
  163.5 8.2 %collective-permute-done.18 = bf16[96,2048]{1,0:T(8,128)(2,1)S(1)} collective-permute-done((bf16[96,2048]{1,0:T(8,128)(2,1)S(1)}, bf16[96,2048]{1,0:T(8,128)(2,1)S(1)}, u32[]{:S(2)}, u32[]{:S(2)}) %collective-permute-start.18) | collective-permute-done | bytes 393248 | tf_op jit(solution)/shard_map/ppermute | solution.py:253
  171.6 0.7 collective-permute-start.34
  172.5 1.3 collective-permute-start.21
  173.7 0.9 collective-permute-start.20
  174.7 8.1 %collective-permute-start.32 = (bf16[48,4096]{1,0:T(8,128)(2,1)S(1)}, bf16[48,4096]{1,0:T(8,128)(2,1)S(1)}, u32[]{:S(2)}, u32[]{:S(2)}) collective-permute-start(bf16[48,4096]{1,0:T(8,128)(2,1)S(1)} %get-tuple-element.12), channel_id=1, source_target_pairs={{0,2},{1,3},{2,4},{3,5},{4,6},{5,7},{8,10},{9,11},{10,12},{11,13},... | collective-permute-start | bytes 1179656 | tf_op jit(solution)/shard_map/ppermute | solution.py:253
  182.9 1.3 collective-permute-start.35
  184.2 9.8 %collective-permute-done.21 = bf16[384,1024]{1,0:T(8,128)(2,1)S(1)} collective-permute-done((bf16[384,1024]{1,0:T(8,128)(2,1)S(1)}, bf16[384,1024]{1,0:T(8,128)(2,1)S(1)}, u32[]{:S(2)}, u32[]{:S(2)}) %collective-permute-start.21) | collective-permute-done | bytes 786464 | tf_op jit(solution)/shard_map/ppermute | solution.py:239
  194.0 3.1 %fusion.2 = f32[1024,512]{1,0:T(8,128)} fusion(bf16[384,1024]{1,0:T(8,128)(2,1)S(1)} %collective-permute-done.22, bf16[384,1024]{1,0:T(8,128)(2,1)S(1)} %collective-permute-done.21, bf16[384,1024]{1,0:T(8,128)(2,1)S(1)} %collective-permute-done.20, bf16[384,1024]{1,0:T(8,128)(2,1)S(1)} %get-tuple-element.16, ...), kind=kOutput, calls=%fused_computation.5 | convolution fusion | flops 1629487104 | bytes 6815744 | tf_op jit(solution)/shard_map/dot_general | solution.py:368
  197.1 1.0 fusion.23
  198.1 2.3 %maximum_select_fusion = bf16[384,4096]{1,0:T(8,128)(2,1)} fusion(bf16[384,2048]{1,0:T(8,128)(2,1)S(1)} %collective-permute-done.19, bf16[384,2048]{1,0:T(8,128)(2,1)S(1)} %constant_dynamic-slice_fusion.6, pred[]{:T(512)S(6)} %eq.18), kind=kLoop, calls=%fused_computation.4 | loop fusion | flops 14155776 | bytes 6291457 | tf_op jit(solution)/shard_map/jit(_where)/select_n | solution.py:355
  (84 shorter events, 4.1 us)
Async XLA Ops:
  0.6 23.4 %collective-permute-start = (s32[384]{0:T(512)}, s32[384]{0:T(512)S(1)}, u32[]{:S(2)}, u32[]{:S(2)}) collective-permute-start(s32[384]{0:T(512)} %param.9), channel_id=1, source_target_pairs={{0,8},{8,0},{16,24},{24,16},{1,9},{9,1},{17,25},{25,17},{2,10},{10... | collective-permute-start | bytes 4616 | tf_op jit(solution)/shard_map/ppermute | solution.py:239
  3.6 21.8 %collective-permute-start.1 = (s32[384]{0:T(512)}, s32[384]{0:T(512)S(1)}, u32[]{:S(2)}, u32[]{:S(2)}) collective-permute-start(s32[384]{0:T(512)} %param.9), channel_id=1, source_target_pairs={{0,16},{8,24},{16,0},{24,8},{1,17},{9,25},{17,1},{25,9},{2,18},{10... | collective-permute-start | bytes 4616 | tf_op jit(solution)/shard_map/ppermute | solution.py:239
  5.2 24.9 %collective-permute-start.3 = (f32[32,384]{1,0:T(8,128)}, f32[32,384]{1,0:T(8,128)S(1)}, u32[]{:S(2)}, u32[]{:S(2)}) collective-permute-start(f32[32,384]{1,0:T(8,128)} %refs_4_.3), channel_id=1, source_target_pairs={{0,8},{8,0},{16,24},{24,16},{1,9},{9,1},{17,25},{25,17},{2,10},{10... | collective-permute-start | bytes 147464 | tf_op jit(solution)/shard_map/ppermute | solution.py:239
  5.7 25.6 %collective-permute-start.4 = (f32[32,384]{1,0:T(8,128)}, f32[32,384]{1,0:T(8,128)S(1)}, u32[]{:S(2)}, u32[]{:S(2)}) collective-permute-start(f32[32,384]{1,0:T(8,128)} %refs_4_.3), channel_id=1, source_target_pairs={{0,16},{8,24},{16,0},{24,8},{1,17},{9,25},{17,1},{25,9},{2,18},{10... | collective-permute-start | bytes 147464 | tf_op jit(solution)/shard_map/ppermute | solution.py:239
  5.7 25.5 %collective-permute-start.5 = (f32[32,384]{1,0:T(8,128)}, f32[32,384]{1,0:T(8,128)S(1)}, u32[]{:S(2)}, u32[]{:S(2)}) collective-permute-start(f32[32,384]{1,0:T(8,128)} %refs_4_.3), channel_id=1, source_target_pairs={{0,24},{8,16},{16,8},{24,0},{1,25},{9,17},{17,9},{25,1},{2,26},{10... | collective-permute-start | bytes 147464 | tf_op jit(solution)/shard_map/ppermute | solution.py:239
  10.5 5.7 %copy-start.3 = (bf16[512,4096]{1,0:T(8,128)(2,1)S(1)}, bf16[512,4096]{1,0:T(8,128)(2,1)}, u32[]{:S(2)}) copy-start(bf16[512,4096]{1,0:T(8,128)(2,1)} %param.10) | copy-start | bytes 12582916
  10.5 5.7 %copy-start.6 = (f32[4096]{0:T(1024)S(1)}, f32[4096]{0:T(1024)}, u32[]{:S(2)}) copy-start(f32[4096]{0:T(1024)} %param.11) | copy-start | bytes 49156
  16.2 13.9 %copy-start.9 = (bf16[512,384]{1,0:T(8,128)(2,1)}, bf16[512,384]{1,0:T(8,128)(2,1)S(1)}, u32[]{:S(2)}) copy-start(bf16[512,384]{1,0:T(8,128)(2,1)S(1)} %convolution_convert_fusion.1.refs_8_) | copy-start | bytes 1179652
  16.2 7.2 %copy-start.7 = (f32[512]{0:T(512)S(1)}, f32[512]{0:T(512)}, u32[]{:S(2)}) copy-start(f32[512]{0:T(512)} %param.15) | copy-start | bytes 6148
  16.2 7.2 %copy-start.8 = (s32[384]{0:T(512)S(1)}, s32[384]{0:T(512)}, u32[]{:S(2)}) copy-start(s32[384]{0:T(512)} %param.9) | copy-start | bytes 4612
  24.1 4.6 %collective-permute-start.2 = (s32[384]{0:T(512)S(1)}, s32[384]{0:T(512)S(1)}, u32[]{:S(2)}, u32[]{:S(2)}) collective-permute-start(s32[384]{0:T(512)S(1)} %copy-done.8), channel_id=1, source_target_pairs={{0,24},{8,16},{16,8},{24,0},{1,25},{9,17},{17,9},{25,1},{2,26},{10... | collective-permute-start | bytes 4616 | tf_op jit(solution)/shard_map/ppermute | solution.py:239
  25.5 20.8 %collective-permute-start.26 = (bf16[512,384]{1,0:T(8,128)(2,1)S(1)}, bf16[512,384]{1,0:T(8,128)(2,1)S(1)}, u32[]{:S(2)}, u32[]{:S(2)}) collective-permute-start(bf16[512,384]{1,0:T(8,128)(2,1)S(1)} %convolution_convert_fusion.1.refs_8_), channel_id=1, source_target_pairs={{0,8},{8,0},{16,24},{24,16},{1,9},{9,1},{17,25},{25,17},{2,10},{10... | collective-permute-start | bytes 1179656 | tf_op jit(solution)/shard_map/ppermute | solution.py:239
  28.6 17.6 %collective-permute-start.27 = (bf16[512,384]{1,0:T(8,128)(2,1)S(1)}, bf16[512,384]{1,0:T(8,128)(2,1)S(1)}, u32[]{:S(2)}, u32[]{:S(2)}) collective-permute-start(bf16[512,384]{1,0:T(8,128)(2,1)S(1)} %convolution_convert_fusion.1.refs_8_), channel_id=1, source_target_pairs={{0,16},{8,24},{16,0},{24,8},{1,17},{9,25},{17,1},{25,9},{2,18},{10... | collective-permute-start | bytes 1179656 | tf_op jit(solution)/shard_map/ppermute | solution.py:239
  30.1 1.2 copy-start.13
  30.1 16.2 %collective-permute-start.28 = (bf16[512,384]{1,0:T(8,128)(2,1)S(1)}, bf16[512,384]{1,0:T(8,128)(2,1)S(1)}, u32[]{:S(2)}, u32[]{:S(2)}) collective-permute-start(bf16[512,384]{1,0:T(8,128)(2,1)S(1)} %convolution_convert_fusion.1.refs_8_), channel_id=1, source_target_pairs={{0,24},{8,16},{16,8},{24,0},{1,25},{9,17},{17,9},{25,1},{2,26},{10... | collective-permute-start | bytes 1179656 | tf_op jit(solution)/shard_map/ppermute | solution.py:239
  31.3 0.6 copy-start.14
  31.3 0.6 copy-start.15
  46.2 18.4 %collective-permute-start.6 = (bf16[384,2048]{1,0:T(8,128)(2,1)S(1)}, bf16[384,2048]{1,0:T(8,128)(2,1)}, u32[]{:S(2)}, u32[]{:S(2)}) collective-permute-start(bf16[384,2048]{1,0:T(8,128)(2,1)S(1)} %convolution_convert_fusion), channel_id=1, source_target_pairs={{0,1},{1,0},{2,3},{3,2},{4,5},{5,4},{6,7},{7,6},{8,9},{9,8},{10,11... | collective-permute-start | bytes 4718600 | tf_op jit(solution)/shard_map/ppermute | solution.py:248
  46.3 0.7 copy-start.10
  46.3 0.9 copy-start.11
  46.3 1.0 copy-start.12
  47.3 17.3 %copy-start.4 = (bf16[384,512]{1,0:T(8,128)(2,1)S(1)}, bf16[384,512]{1,0:T(8,128)(2,1)}, u32[]{:S(2)}) copy-start(bf16[384,512]{1,0:T(8,128)(2,1)} %get-tuple-element.10) | copy-start | bytes 1179652
  68.6 15.8 %collective-permute-start.7 = (bf16[96,2048]{1,0:T(8,128)(2,1)}, bf16[96,2048]{1,0:T(8,128)(2,1)}, u32[]{:S(2)}, u32[]{:S(2)}) collective-permute-start(bf16[96,2048]{1,0:T(8,128)(2,1)} %get-tuple-element.22), channel_id=1, source_target_pairs={{0,2},{1,3},{8,10},{9,11},{16,18},{17,19},{24,26},{25,27}} | collective-permute-start | bytes 1179656 | tf_op jit(solution)/shard_map/ppermute | solution.py:253
  72.9 15.6 %slice-start = ((bf16[512,4096]{1,0:T(8,128)(2,1)}), bf16[24,4096]{1,0:T(8,128)(2,1)S(1)}, s32[]{:S(2)}) async-start(bf16[512,4096]{1,0:T(8,128)(2,1)} %param.10), calls=%async_computation | async-start | bytes 393216 | tf_op jit(solution)/shard_map/slice | solution.py:313
  82.8 16.4 %collective-permute-start.29 = (bf16[192,4096]{1,0:T(8,128)(2,1)}, bf16[192,4096]{1,0:T(8,128)(2,1)}, u32[]{:S(2)}, u32[]{:S(2)}) collective-permute-start(bf16[192,4096]{1,0:T(8,128)(2,1)} %fusion.1), channel_id=1, source_target_pairs={{0,1},{1,0},{2,3},{3,2},{4,5},{5,4},{6,7},{7,6},{8,9},{9,8},{10,11... | collective-permute-start | bytes 4718600 | tf_op jit(solution)/shard_map/ppermute | solution.py:248
  83.1 5.8 %collective-permute-start.10 = (bf16[96,2048]{1,0:T(8,128)(2,1)}, bf16[96,2048]{1,0:T(8,128)(2,1)}, u32[]{:S(2)}, u32[]{:S(2)}) collective-permute-start(bf16[96,2048]{1,0:T(8,128)(2,1)} %get-tuple-element.23), channel_id=1, source_target_pairs={{6,4},{7,5},{14,12},{15,13},{22,20},{23,21},{30,28},{31,29}} | collective-permute-start | bytes 1179656 | tf_op jit(solution)/shard_map/ppermute | solution.py:253
  86.3 10.7 %collective-permute-start.8 = (bf16[96,2048]{1,0:T(8,128)(2,1)}, bf16[96,2048]{1,0:T(8,128)(2,1)}, u32[]{:S(2)}, u32[]{:S(2)}) collective-permute-start(bf16[96,2048]{1,0:T(8,128)(2,1)} %fusion.26), channel_id=1, source_target_pairs={{0,2},{1,3},{2,4},{3,5},{8,10},{9,11},{10,12},{11,13},{16,18},{17,... | collective-permute-start | bytes 1179656 | tf_op jit(solution)/shard_map/ppermute | solution.py:253
  88.5 10.7 %copy-start.2 = (bf16[3,4,1,48,512]{4,3,2,1,0:T(8,128)(2,1)S(1)}, bf16[3,4,1,48,512]{4,3,2,1,0:T(8,128)(2,1)}, u32[]{:S(2)}) copy-start(bf16[3,4,1,48,512]{4,3,2,1,0:T(8,128)(2,1)} %get-tuple-element.25) | copy-start | bytes 1769476
  98.3 15.2 %collective-permute-start.11 = (bf16[96,2048]{1,0:T(8,128)(2,1)S(1)}, bf16[96,2048]{1,0:T(8,128)(2,1)S(1)}, u32[]{:S(2)}, u32[]{:S(2)}) collective-permute-start(bf16[96,2048]{1,0:T(8,128)(2,1)S(1)} %get-tuple-element.21), channel_id=1, source_target_pairs={{4,2},{5,3},{6,4},{7,5},{12,10},{13,11},{14,12},{15,13},{20,18},{2... | collective-permute-start | bytes 1179656 | tf_op jit(solution)/shard_map/ppermute | solution.py:253
  108.4 23.0 %copy-start = (f32[192,4096]{1,0:T(8,128)}, f32[192,4096]{1,0:T(8,128)S(1)}, u32[]{:S(2)}) copy-start(f32[192,4096]{1,0:T(8,128)S(1)} %fusion) | copy-start | bytes 9437188
  108.4 14.5 %collective-permute-start.9 = (bf16[96,2048]{1,0:T(8,128)(2,1)S(1)}, bf16[96,2048]{1,0:T(8,128)(2,1)S(1)}, u32[]{:S(2)}, u32[]{:S(2)}) collective-permute-start(bf16[96,2048]{1,0:T(8,128)(2,1)S(1)} %get-tuple-element.20), channel_id=1, source_target_pairs={{0,2},{1,3},{2,4},{3,5},{4,6},{5,7},{8,10},{9,11},{10,12},{11,13},... | collective-permute-start | bytes 1179656 | tf_op jit(solution)/shard_map/ppermute | solution.py:253
  113.6 13.0 %collective-permute-start.12 = (bf16[96,2048]{1,0:T(8,128)(2,1)S(1)}, bf16[96,2048]{1,0:T(8,128)(2,1)S(1)}, u32[]{:S(2)}, u32[]{:S(2)}) collective-permute-start(bf16[96,2048]{1,0:T(8,128)(2,1)S(1)} %fusion.25), channel_id=1, source_target_pairs={{2,0},{3,1},{4,2},{5,3},{6,4},{7,5},{10,8},{11,9},{12,10},{13,11},... | collective-permute-start | bytes 1179656 | tf_op jit(solution)/shard_map/ppermute | solution.py:253
  115.7 15.7 %collective-permute-start.30 = (bf16[48,4096]{1,0:T(8,128)(2,1)S(1)}, bf16[48,4096]{1,0:T(8,128)(2,1)S(1)}, u32[]{:S(2)}, u32[]{:S(2)}) collective-permute-start(bf16[48,4096]{1,0:T(8,128)(2,1)S(1)} %get-tuple-element.14), channel_id=1, source_target_pairs={{0,2},{1,3},{8,10},{9,11},{16,18},{17,19},{24,26},{25,27}} | collective-permute-start | bytes 1179656 | tf_op jit(solution)/shard_map/ppermute | solution.py:253
  120.9 23.8 %collective-permute-start.33 = (bf16[48,4096]{1,0:T(8,128)(2,1)}, bf16[48,4096]{1,0:T(8,128)(2,1)}, u32[]{:S(2)}, u32[]{:S(2)}) collective-permute-start(bf16[48,4096]{1,0:T(8,128)(2,1)} %get-tuple-element.15), channel_id=1, source_target_pairs={{6,4},{7,5},{14,12},{15,13},{22,20},{23,21},{30,28},{31,29}} | collective-permute-start | bytes 1179656 | tf_op jit(solution)/shard_map/ppermute | solution.py:253
  126.7 13.2 %collective-permute-start.13 = (bf16[96,2048]{1,0:T(8,128)(2,1)S(1)}, bf16[96,2048]{1,0:T(8,128)(2,1)S(1)}, u32[]{:S(2)}, u32[]{:S(2)}) collective-permute-start(bf16[96,2048]{1,0:T(8,128)(2,1)S(1)} %fusion.30), channel_id=1, source_target_pairs={{0,2},{1,3},{2,4},{3,5},{4,6},{5,7},{8,10},{9,11},{10,12},{11,13},... | collective-permute-start | bytes 1179656 | tf_op jit(solution)/shard_map/ppermute | solution.py:253
  131.5 15.5 %collective-permute-start.31 = (bf16[48,4096]{1,0:T(8,128)(2,1)S(1)}, bf16[48,4096]{1,0:T(8,128)(2,1)S(1)}, u32[]{:S(2)}, u32[]{:S(2)}) collective-permute-start(bf16[48,4096]{1,0:T(8,128)(2,1)S(1)} %fusion.21), channel_id=1, source_target_pairs={{0,2},{1,3},{2,4},{3,5},{8,10},{9,11},{10,12},{11,13},{16,18},{17,... | collective-permute-start | bytes 1179656 | tf_op jit(solution)/shard_map/ppermute | solution.py:253
  135.9 12.6 %collective-permute-start.16 = (bf16[96,2048]{1,0:T(8,128)(2,1)S(1)}, bf16[96,2048]{1,0:T(8,128)(2,1)S(1)}, u32[]{:S(2)}, u32[]{:S(2)}) collective-permute-start(bf16[96,2048]{1,0:T(8,128)(2,1)S(1)} %fusion.30), channel_id=1, source_target_pairs={{2,0},{3,1},{4,2},{5,3},{6,4},{7,5},{10,8},{11,9},{12,10},{13,11},... | collective-permute-start | bytes 1179656 | tf_op jit(solution)/shard_map/ppermute | solution.py:253
  139.9 9.8 %collective-permute-start.14 = (bf16[96,2048]{1,0:T(8,128)(2,1)S(1)}, bf16[96,2048]{1,0:T(8,128)(2,1)S(1)}, u32[]{:S(2)}, u32[]{:S(2)}) collective-permute-start(bf16[96,2048]{1,0:T(8,128)(2,1)S(1)} %collective-permute-done.13), channel_id=1, source_target_pairs={{2,4},{3,5},{4,6},{5,7},{10,12},{11,13},{12,14},{13,15},{18,20},{1... | collective-permute-start | bytes 1179656 | tf_op jit(solution)/shard_map/ppermute | solution.py:253
  140.6 4.1 %copy-start.5 = (bf16[384,512]{1,0:T(8,128)(2,1)S(1)}, bf16[384,512]{1,0:T(8,128)(2,1)}, u32[]{:S(2)}) copy-start(bf16[384,512]{1,0:T(8,128)(2,1)} %get-tuple-element.10) | copy-start | bytes 1179652
  140.6 9.8 %copy-start.1 = (f32[192,4096]{1,0:T(8,128)S(1)}, f32[192,4096]{1,0:T(8,128)}, u32[]{:S(2)}) copy-start(f32[192,4096]{1,0:T(8,128)} %copy-done) | copy-start | bytes 9437188
  140.6 31.8 %collective-permute-start.25 = (bf16[384,512]{1,0:T(8,128)(2,1)}, bf16[384,512]{1,0:T(8,128)(2,1)S(1)}, u32[]{:S(2)}, u32[]{:S(2)}) collective-permute-start(bf16[384,512]{1,0:T(8,128)(2,1)} %get-tuple-element.10), channel_id=1, source_target_pairs={{0,24},{8,16},{16,8},{24,0},{1,25},{9,17},{17,9},{25,1},{2,26},{10... | collective-permute-start | bytes 1179656 | tf_op jit(solution)/shard_map/ppermute | solution.py:239
  144.7 29.1 %collective-permute-start.24 = (bf16[384,512]{1,0:T(8,128)(2,1)S(1)}, bf16[384,512]{1,0:T(8,128)(2,1)S(1)}, u32[]{:S(2)}, u32[]{:S(2)}) collective-permute-start(bf16[384,512]{1,0:T(8,128)(2,1)S(1)} %copy-done.5), channel_id=1, source_target_pairs={{0,16},{8,24},{16,0},{24,8},{1,17},{9,25},{17,1},{25,9},{2,18},{10... | collective-permute-start | bytes 1179656 | tf_op jit(solution)/shard_map/ppermute | solution.py:239
  147.0 27.8 %collective-permute-start.23 = (bf16[384,512]{1,0:T(8,128)(2,1)S(1)}, bf16[384,512]{1,0:T(8,128)(2,1)S(1)}, u32[]{:S(2)}, u32[]{:S(2)}) collective-permute-start(bf16[384,512]{1,0:T(8,128)(2,1)S(1)} %copy-done.5), channel_id=1, source_target_pairs={{0,8},{8,0},{16,24},{24,16},{1,9},{9,1},{17,25},{25,17},{2,10},{10... | collective-permute-start | bytes 1179656 | tf_op jit(solution)/shard_map/ppermute | solution.py:239
  148.5 12.1 %collective-permute-start.17 = (bf16[96,2048]{1,0:T(8,128)(2,1)S(1)}, bf16[96,2048]{1,0:T(8,128)(2,1)S(1)}, u32[]{:S(2)}, u32[]{:S(2)}) collective-permute-start(bf16[96,2048]{1,0:T(8,128)(2,1)S(1)} %collective-permute-done.16), channel_id=1, source_target_pairs={{2,0},{3,1},{4,2},{5,3},{10,8},{11,9},{12,10},{13,11},{18,16},{19,... | collective-permute-start | bytes 1179656 | tf_op jit(solution)/shard_map/ppermute | solution.py:253
  149.8 12.2 %collective-permute-start.15 = (bf16[96,2048]{1,0:T(8,128)(2,1)S(1)}, bf16[96,2048]{1,0:T(8,128)(2,1)S(1)}, u32[]{:S(2)}, u32[]{:S(2)}) collective-permute-start(bf16[96,2048]{1,0:T(8,128)(2,1)S(1)} %collective-permute-done.14), channel_id=1, source_target_pairs={{4,6},{5,7},{12,14},{13,15},{20,22},{21,23},{28,30},{29,31}} | collective-permute-start | bytes 1179656 | tf_op jit(solution)/shard_map/ppermute | solution.py:253
  160.6 22.3 %collective-permute-start.22 = (bf16[384,1024]{1,0:T(8,128)(2,1)S(1)}, bf16[384,1024]{1,0:T(8,128)(2,1)S(1)}, u32[]{:S(2)}, u32[]{:S(2)}) collective-permute-start(bf16[384,1024]{1,0:T(8,128)(2,1)S(1)} %get-tuple-element.17), channel_id=1, source_target_pairs={{0,24},{8,16},{16,8},{24,0},{1,25},{9,17},{17,9},{25,1},{2,26},{10... | collective-permute-start | bytes 2359304 | tf_op jit(solution)/shard_map/ppermute | solution.py:239
  162.0 9.7 %collective-permute-start.18 = (bf16[96,2048]{1,0:T(8,128)(2,1)S(1)}, bf16[96,2048]{1,0:T(8,128)(2,1)S(1)}, u32[]{:S(2)}, u32[]{:S(2)}) collective-permute-start(bf16[96,2048]{1,0:T(8,128)(2,1)S(1)} %collective-permute-done.17), channel_id=1, source_target_pairs={{2,0},{3,1},{10,8},{11,9},{18,16},{19,17},{26,24},{27,25}} | collective-permute-start | bytes 1179656 | tf_op jit(solution)/shard_map/ppermute | solution.py:253
  171.6 3.0 %collective-permute-start.34 = (bf16[48,4096]{1,0:T(8,128)(2,1)S(1)}, bf16[48,4096]{1,0:T(8,128)(2,1)S(1)}, u32[]{:S(2)}, u32[]{:S(2)}) collective-permute-start(bf16[48,4096]{1,0:T(8,128)(2,1)S(1)} %get-tuple-element.13), channel_id=1, source_target_pairs={{4,2},{5,3},{6,4},{7,5},{12,10},{13,11},{14,12},{15,13},{20,18},{2... | collective-permute-start | bytes 1179656 | tf_op jit(solution)/shard_map/ppermute | solution.py:253
  172.5 21.5 %collective-permute-start.21 = (bf16[384,1024]{1,0:T(8,128)(2,1)S(1)}, bf16[384,1024]{1,0:T(8,128)(2,1)S(1)}, u32[]{:S(2)}, u32[]{:S(2)}) collective-permute-start(bf16[384,1024]{1,0:T(8,128)(2,1)S(1)} %get-tuple-element.18), channel_id=1, source_target_pairs={{0,16},{8,24},{16,0},{24,8},{1,17},{9,25},{17,1},{25,9},{2,18},{10... | collective-permute-start | bytes 2359304 | tf_op jit(solution)/shard_map/ppermute | solution.py:239
  173.7 20.2 %collective-permute-start.20 = (bf16[384,1024]{1,0:T(8,128)(2,1)S(1)}, bf16[384,1024]{1,0:T(8,128)(2,1)S(1)}, u32[]{:S(2)}, u32[]{:S(2)}) collective-permute-start(bf16[384,1024]{1,0:T(8,128)(2,1)S(1)} %get-tuple-element.19), channel_id=1, source_target_pairs={{0,8},{8,0},{16,24},{24,16},{1,9},{9,1},{17,25},{25,17},{2,10},{10... | collective-permute-start | bytes 2359304 | tf_op jit(solution)/shard_map/ppermute | solution.py:239
  174.6 23.5 %collective-permute-start.19 = (bf16[384,2048]{1,0:T(8,128)(2,1)S(1)}, bf16[384,2048]{1,0:T(8,128)(2,1)S(1)}, u32[]{:S(2)}, u32[]{:S(2)}) collective-permute-start(bf16[384,2048]{1,0:T(8,128)(2,1)S(1)} %constant_dynamic-slice_fusion.6), channel_id=1, source_target_pairs={{0,1},{1,0},{2,3},{3,2},{4,5},{5,4},{6,7},{7,6},{8,9},{9,8},{10,11... | collective-permute-start | bytes 4718600 | tf_op jit(solution)/shard_map/ppermute | solution.py:248
  174.7 22.4 %collective-permute-start.32 = (bf16[48,4096]{1,0:T(8,128)(2,1)S(1)}, bf16[48,4096]{1,0:T(8,128)(2,1)S(1)}, u32[]{:S(2)}, u32[]{:S(2)}) collective-permute-start(bf16[48,4096]{1,0:T(8,128)(2,1)S(1)} %get-tuple-element.12), channel_id=1, source_target_pairs={{0,2},{1,3},{2,4},{3,5},{4,6},{5,7},{8,10},{9,11},{10,12},{11,13},... | collective-permute-start | bytes 1179656 | tf_op jit(solution)/shard_map/ppermute | solution.py:253
  182.9 14.2 %collective-permute-start.35 = (bf16[48,4096]{1,0:T(8,128)(2,1)S(1)}, bf16[48,4096]{1,0:T(8,128)(2,1)S(1)}, u32[]{:S(2)}, u32[]{:S(2)}) collective-permute-start(bf16[48,4096]{1,0:T(8,128)(2,1)S(1)} %fusion.20), channel_id=1, source_target_pairs={{2,0},{3,1},{4,2},{5,3},{6,4},{7,5},{10,8},{11,9},{12,10},{13,11},... | collective-permute-start | bytes 1179656 | tf_op jit(solution)/shard_map/ppermute | solution.py:253

commit v2 on v1

v2 whole, which is shorter than its diff:
```python
import functools

import jax
import jax.numpy as jnp
from jax import lax
from jax.experimental import pallas as pl
from jax.experimental.pallas import tpu as pltpu
from jax.sharding import PartitionSpec as P

LANES = 128
FIRST_ID = 64
IDS = 32
VMEM_BYTES = 56 * 1024 * 1024
f32 = jnp.float32
bf16 = jnp.bfloat16
CONTRACT_LAST = (((1,), (1,)), ((), ()))


def one_hot(ids, taps):
    length = ids.shape[1]
    lane = lax.broadcasted_iota(jnp.int32, (1, length), 1)
    code = lax.broadcasted_iota(jnp.int32, (IDS, length), 0) + FIRST_ID
    rows = []
    for tap in range(taps):
        moved = ids if tap == 0 else jnp.where(lane < tap, 0, pltpu.roll(ids, tap, axis=1))
        rows.append(jnp.where(code == moved, 1.0, 0.0))
    return jnp.concatenate(rows, axis=0)


def tap_weights(taps_ref, table_ref, part):
    table = table_ref[part]
    value = jnp.concatenate([taps_ref[i, part][None, :] * table for i in range(taps_ref.shape[0])], axis=0)
    high = value.astype(bf16).astype(f32)
    return jnp.concatenate([high, value - high], axis=0).astype(bf16)


def expand(weights, hot):
    return lax.dot_general(weights, hot, (((0,), (0,)), ((), ())), preferred_element_type=f32)


def toeplitz_tiles(row, blocks, mirrored):
    sub = lax.broadcasted_iota(jnp.int32, (LANES, LANES), 0)
    lane = lax.broadcasted_iota(jnp.int32, (LANES, LANES), 1)
    keep = lane <= sub if mirrored else lane >= sub
    before = jnp.zeros((LANES, LANES), f32)
    tiles = []
    for q in range(blocks):
        part = jnp.broadcast_to(row[:, LANES * q : LANES * (q + 1)], (LANES, LANES))
        turned = pltpu.roll(part, 1 if mirrored else 0, 1, stride=1, stride_axis=0)
        tiles.append(jnp.where(keep, turned, before).astype(bf16))
        before = turned
    return tiles


def reverse_blocks(value):
    sub = lax.broadcasted_iota(jnp.int32, (LANES, LANES), 0)
    lane = lax.broadcasted_iota(jnp.int32, (LANES, LANES), 1)
    mirror = jnp.where(sub + lane == LANES - 1, 1.0, 0.0).astype(bf16)
    blocks = [value[:, start : start + LANES].astype(bf16) for start in range(0, value.shape[1], LANES)]
    return jnp.concatenate([jnp.dot(block, mirror, preferred_element_type=f32) for block in blocks], axis=1)


def lanes_at(block, count):
    return pl.ds(pl.multiple_of(block * LANES, LANES), count * LANES)


def channel_columns(taps_ref, skip_ref):
    taps = taps_ref.shape[0]
    rows = [taps_ref[i] for i in range(taps)] + [skip_ref[...][None, :]]
    channels = skip_ref.shape[0]
    rows.append(jnp.zeros((LANES - 3 * taps - 1, channels), f32))
    return jnp.transpose(jnp.concatenate(rows, axis=0))


def place_slots(me, local_blocks, slots, store):
    for step, slot in enumerate(slots):
        store(lanes_at(jnp.bitwise_xor(me, step) * local_blocks, local_blocks), slot)


def start_rows(source_ref, start, held, arrived):
    copies = []
    chunk = held.shape[0] // arrived.shape[0]
    for index in range(arrived.shape[0]):
        rows = pl.ds(pl.multiple_of(start + index * chunk, chunk), chunk)
        copies.append(
            pltpu.make_async_copy(source_ref.at[rows], held.at[index * chunk : (index + 1) * chunk], arrived.at[index])
        )
        copies[-1].start()
    return copies


def project(hidden, copies, weight, out_ref):
    chunk = weight.shape[0] // len(copies)
    for index, copy in enumerate(copies):
        rows = slice(index * chunk, (index + 1) * chunk)
        copy.wait()
        value = lax.dot_general(hidden, weight[rows], CONTRACT_LAST, preferred_element_type=f32)
        out_ref[:, rows] = value.astype(out_ref.dtype)


def own_part_kernel(core_ref, hidden_ref, last_ref, out_ref, last, arrived):
    copies = start_rows(last_ref, core_ref[0] * last.shape[0], last, arrived)
    project(hidden_ref[...], copies, last, out_ref)


def assemble_kernel(chip_ref, core_ref, *refs):
    out_ref = refs[-1]
    chips = (len(refs) - 1) // 2
    rows, columns = refs[0].shape
    for index in range(2 * chips):
        place = jnp.bitwise_xor(chip_ref[0], index % chips)
        side = core_ref[0] if index < chips else 1 - core_ref[0]
        at = (pl.ds(pl.multiple_of(place * rows, rows), rows), pl.ds(pl.multiple_of(side * columns, columns), columns))
        out_ref[at] = refs[index][...]


def forward_kernel(shards, me_ref, core_ref, *refs):
    slots = refs[:shards]
    letters_ref, gain_ref, weight_ref, taps_ref, skip_ref, last_ref = refs[shards : shards + 6]
    hidden_ref, mixed_ref, table_ref, theirs_ref = refs[shards + 6 : shards + 10]
    normed, hot, filters, matrices, signal, exact, long_part, weight, arrived, last, last_arrived = refs[shards + 10 :]
    groups = filters.shape[0]
    local_rows = slots[0].shape[1]
    channels = table_ref.shape[2]
    width = channels // groups
    local_blocks = local_rows // LANES
    blocks = shards * local_blocks
    length = blocks * LANES
    window = local_blocks + 1
    chunks = arrived.shape[0]
    chunk = weight.shape[1] // chunks
    taps = taps_ref.shape[0]
    me = me_ref[0]
    first = me * local_blocks

    copies = []
    for index in range(chunks):
        rows = slice(index * chunk, (index + 1) * chunk)
        copies.append(pltpu.make_async_copy(weight_ref.at[:, rows], weight.at[:, rows], arrived.at[index]))
        copies[-1].start()
    last_copies = start_rows(last_ref, (1 - core_ref[0]) * last.shape[0], last, last_arrived)
    for index, slot in enumerate(slots):
        place = lanes_at(jnp.bitwise_xor(me, index) * local_blocks, local_blocks)
        filters[:, place] = slot[:groups]
        exact[0:1, place] = slot[groups : groups + 1]
    marks = one_hot(exact[0:1, :length].astype(jnp.int32), taps)
    hot[:, :length] = jnp.concatenate([marks, marks], axis=0).astype(bf16)
    hot[:, length:] = jnp.zeros((hot.shape[0], LANES), bf16)
    signal[:, :length] = jnp.zeros((channels, length), bf16)
    signal[:, 2 * length :] = jnp.zeros((channels, LANES), bf16)
    exact[:, length:] = jnp.zeros((channels, LANES), f32)
    values = letters_ref[...].astype(f32)
    inverse = lax.rsqrt(jnp.mean(values * values, axis=-1, keepdims=True) + 1e-06)
    normed[...] = (values * inverse * gain_ref[...][None, :]).astype(bf16)

    def one_matrix(group, carry):
        tiles = toeplitz_tiles(filters[pl.ds(group, 1), :], blocks, False)
        for q in range(blocks):
            matrices[group, (blocks - 1 - q) * LANES : (blocks - q) * LANES] = tiles[q]
        return carry

    for index in range(chunks):
        lax.fori_loop(index * groups // chunks, (index + 1) * groups // chunks, one_matrix, 0)
        rows = slice(index * chunk, (index + 1) * chunk)
        copies[index].wait()
        for part in range(3):
            term = jnp.dot(normed[:, rows], weight[part, rows], preferred_element_type=f32)
            table_ref[part] = term if index == 0 else table_ref[part] + term

    key_weights = tap_weights(taps_ref, table_ref, 1)
    value_weights = tap_weights(taps_ref, table_ref, 2)
    for start in range(0, channels, LANES):
        rows = slice(start, start + LANES)
        mixture = expand(key_weights[:, rows], hot[:, :length]) * expand(value_weights[:, rows], hot[:, :length])
        exact[rows, :length] = mixture
        signal[rows, length : 2 * length] = mixture.astype(bf16)

    def one_group(group, carry):
        rows = pl.ds(pl.multiple_of(group * width, width), width)
        left = jnp.concatenate([signal[rows, lanes_at(first + i + 1, blocks)] for i in range(window)], axis=0)
        result = jnp.dot(left, matrices[group], preferred_element_type=f32)
        for i in range(window):
            long_part[rows, i * LANES : (i + 1) * LANES] = result[i * width : (i + 1) * width]
        return carry

    lax.fori_loop(0, groups, one_group, 0, unroll=4)
    columns = channel_columns(taps_ref, skip_ref)
    mixed = columns[:, 3 * taps : 3 * taps + 1] * exact[:, lanes_at(first, window)] + long_part[...]
    mixed_ref[...] = mixed
    queries = expand(tap_weights(taps_ref, table_ref, 0), hot[:, lanes_at(first, local_blocks)])
    hidden = jnp.transpose(queries * mixed[:, :local_rows]).astype(bf16)
    hidden_ref[...] = hidden
    project(hidden, last_copies, last, theirs_ref)


def backward_kernel(shards, me_ref, *refs):
    slots, grad_slots = refs[:shards], refs[shards : 2 * shards]
    table_ref, taps_ref, skip_ref, mixed_ref, out_ref = refs[2 * shards : 2 * shards + 5]
    hot, filters, grads, signal, exact, long_part = refs[2 * shards + 5 :]
    me = me_ref[0]
    groups = filters.shape[0]
    local_rows = slots[0].shape[1]
    channels = table_ref.shape[2]
    width = channels // groups
    local_blocks = local_rows // LANES
    blocks = shards * local_blocks
    length = blocks * LANES
    window = local_blocks + 1
    taps = taps_ref.shape[0]

    for step in range(shards):
        place = lanes_at(jnp.bitwise_xor(me, step) * local_blocks, local_blocks)
        exact[0:1, place] = slots[step][groups : groups + 1]
        filters[:, place] = reverse_blocks(slots[step][:groups])
        grads[:, place] = grad_slots[step][...]
    grads[:, length:] = jnp.zeros((channels, LANES), bf16)
    marks = one_hot(exact[0:1, :length].astype(jnp.int32), taps)
    hot[:, :length] = jnp.concatenate([marks, marks], axis=0).astype(bf16)
    hot[:, length:] = jnp.zeros((hot.shape[0], LANES), bf16)

    signal[:, length:] = jnp.zeros((channels, length + LANES), bf16)
    exact[:, length:] = jnp.zeros((channels, LANES), f32)
    query_weights = tap_weights(taps_ref, table_ref, 0)
    for start in range(0, channels, LANES):
        rows = slice(start, start + LANES)
        mixed_grad = expand(query_weights[:, rows], hot[:, :length]) * grads[rows, :length].astype(f32)
        exact[rows, :length] = mixed_grad
        signal[rows, :length] = mixed_grad.astype(bf16)

    first = me * local_blocks

    def one_group(group, carry):
        matrix = jnp.concatenate(toeplitz_tiles(filters[pl.ds(group, 1), :], blocks, True), axis=0)
        rows = pl.ds(pl.multiple_of(group * width, width), width)
        left = jnp.concatenate([signal[rows, lanes_at(first + i, blocks)] for i in range(window)], axis=0)
        result = jnp.dot(left, matrix, preferred_element_type=f32)
        for i in range(window):
            long_part[rows, i * LANES : (i + 1) * LANES] = result[i * width : (i + 1) * width]
        return carry

    lax.fori_loop(0, groups, one_group, 0, unroll=4)
    own = lanes_at(first, window)
    columns = channel_columns(taps_ref, skip_ref)
    mixture_grad = columns[:, 3 * taps : 3 * taps + 1] * exact[:, own] + long_part[...]
    span = window * LANES
    for part in range(3):
        if part == 0:
            feature_grad = grads[:, own].astype(f32) * mixed_ref[...]
        else:
            other = expand(tap_weights(taps_ref, table_ref, 3 - part), hot[:, own])
            feature_grad = mixture_grad * other
        total = columns[:, part : part + 1] * feature_grad
        for tap in range(1, taps):
            column = 3 * tap + part
            total = total + columns[:, column : column + 1] * pltpu.roll(feature_grad, span - tap, axis=1)
        out_ref[part] = jnp.transpose(total[:, :local_rows]).astype(bf16)


def hidden_grad_kernel(grad_ref, weight_ref, out_ref, grad, weight, total, arrived):
    chunks = arrived.shape[0] // 2
    chunk = weight.shape[0] // chunks
    copies = []
    for index in range(chunks):
        part = slice(index * chunk, (index + 1) * chunk)
        copies.append(pltpu.make_async_copy(grad_ref.at[:, part], grad.at[:, part], arrived.at[2 * index]))
        copies.append(pltpu.make_async_copy(weight_ref.at[part], weight.at[part], arrived.at[2 * index + 1]))
    for copy in copies:
        copy.start()
    for index in range(chunks):
        part = slice(index * chunk, (index + 1) * chunk)
        copies[2 * index].wait()
        copies[2 * index + 1].wait()
        term = jnp.dot(grad[:, part], weight[part], preferred_element_type=f32)
        total[...] = term if index == 0 else total[...] + term
    out_ref[...] = jnp.transpose(total[...]).astype(bf16)


def input_grad_kernel(chips, start, core_ref, *refs):
    grad_ref, weight_ref, theirs_ref, mine_ref, weight, total, arrived = refs
    chunks = arrived.shape[0]
    chunk = weight.shape[1] // chunks
    copies = []
    for index in range(chunks):
        rows = slice(index * chunk, (index + 1) * chunk)
        source = weight_ref.at[:, start + index * chunk : start + (index + 1) * chunk]
        copies.append(pltpu.make_async_copy(source, weight.at[:, rows], arrived.at[index]))
        copies[-1].start()
    core = core_ref[0]
    rows = total.shape[0] // (2 * chips)

    def half(which):
        starts = [pl.multiple_of((2 * chip + which) * rows, 8) for chip in range(chips)]
        return jnp.concatenate([total[pl.ds(start, rows), :] for start in starts], axis=0)

    for index in range(chunks):
        part_rows = slice(index * chunk, (index + 1) * chunk)
        copies[index].wait()
        value = None
        for part in range(3):
            term = lax.dot_general(
                grad_ref[part], weight[part, part_rows], CONTRACT_LAST, preferred_element_type=f32
            )
            value = term if value is None else value + term
        total[...] = value
        mine_ref[:, part_rows] = half(core)
        theirs_ref[:, part_rows] = half(1 - core).astype(bf16)


def in_vmem(count):
    return [pl.BlockSpec(memory_space=pltpu.VMEM)] * count


SMEM_SPEC = pl.BlockSpec(memory_space=pltpu.SMEM)
ANY_SPEC = pl.BlockSpec(memory_space=pl.ANY)
VMEM_SPEC = pl.BlockSpec(memory_space=pltpu.VMEM)
CHUNKS = 8


def params():
    return pltpu.CompilerParams(vmem_limit_bytes=VMEM_BYTES)


LARGE_COST = pl.CostEstimate(flops=20_000_000_000, bytes_accessed=10_000_000, transcendentals=0)
SMALL_COST = pl.CostEstimate(flops=1000, bytes_accessed=1000, transcendentals=0)


def run_own_part(core, hidden, output_weight):
    half = output_weight.shape[0] // 2
    return pl.pallas_call(
        own_part_kernel,
        out_shape=jax.ShapeDtypeStruct((hidden.shape[0], half), f32),
        in_specs=[SMEM_SPEC, VMEM_SPEC, ANY_SPEC],
        out_specs=VMEM_SPEC,
        scratch_shapes=[pltpu.VMEM((half, hidden.shape[1]), bf16), pltpu.SemaphoreType.DMA((4,))],
        compiler_params=params(),
        cost_estimate=SMALL_COST,
        name="own_part",
    )(core, hidden, output_weight)


def run_assemble(chip, core, own, theirs):
    chips = len(own)
    rows, columns = own[0].shape
    return pl.pallas_call(
        assemble_kernel,
        out_shape=jax.ShapeDtypeStruct((chips * rows, 2 * columns), bf16),
        in_specs=[SMEM_SPEC, SMEM_SPEC] + in_vmem(2 * len(own)),
        out_specs=VMEM_SPEC,
        compiler_params=params(),
        cost_estimate=SMALL_COST,
        name="assemble",
    )(chip, core, *own, *theirs)


def run_forward(me, core, slots, embed_table, norm_gain, weight, taps, skip_gain, output_weight):
    shards = len(slots)
    local_rows = slots[0].shape[1]
    _, width, channels = weight.shape
    groups = slots[0].shape[0] - 8
    length = shards * local_rows
    span = local_rows + LANES
    return pl.pallas_call(
        functools.partial(forward_kernel, shards),
        grid=(1,),
        out_shape=(
            jax.ShapeDtypeStruct((local_rows, channels), bf16),
            jax.ShapeDtypeStruct((channels, span), f32),
            jax.ShapeDtypeStruct((3, IDS, channels), f32),
            jax.ShapeDtypeStruct((local_rows, width // 2), bf16),
        ),
        in_specs=[SMEM_SPEC, SMEM_SPEC]
        + in_vmem(shards)
        + [pl.BlockSpec((IDS, width), lambda step: (FIRST_ID // IDS, 0)), VMEM_SPEC, ANY_SPEC, VMEM_SPEC, VMEM_SPEC]
        + [ANY_SPEC],
        out_specs=tuple(in_vmem(4)),
        scratch_shapes=[
            pltpu.VMEM((IDS, width), bf16),
            pltpu.VMEM((2 * taps.shape[0] * IDS, length + LANES), bf16),
            pltpu.VMEM((groups, length), f32),
            pltpu.VMEM((groups, length, LANES), bf16),
            pltpu.VMEM((channels, 2 * length + LANES), bf16),
            pltpu.VMEM((channels, length + LANES), f32),
            pltpu.VMEM((channels, span), f32),
            pltpu.VMEM(weight.shape, bf16),
            pltpu.SemaphoreType.DMA((CHUNKS,)),
            pltpu.VMEM((width // 2, channels), bf16),
            pltpu.SemaphoreType.DMA((4,)),
        ],
        compiler_params=params(),
        cost_estimate=LARGE_COST,
        name="forward_conv",
    )(me, core, *slots, embed_table, norm_gain, weight, taps, skip_gain, output_weight)


def run_backward(me, slots, grads, table, taps, skip_gain, mixed):
    shards = len(slots)
    local_rows = slots[0].shape[1]
    channels = table.shape[2]
    groups = slots[0].shape[0] - 8
    length = shards * local_rows
    span = local_rows + LANES
    return pl.pallas_call(
        functools.partial(backward_kernel, shards),
        out_shape=jax.ShapeDtypeStruct((3, local_rows, channels), bf16),
        in_specs=[SMEM_SPEC] + in_vmem(2 * shards + 4),
        out_specs=VMEM_SPEC,
        scratch_shapes=[
            pltpu.VMEM((2 * taps.shape[0] * IDS, length + LANES), bf16),
            pltpu.VMEM((groups, length), f32),
            pltpu.VMEM((channels, length + LANES), bf16),
            pltpu.VMEM((channels, 2 * length + LANES), bf16),
            pltpu.VMEM((channels, length + LANES), f32),
            pltpu.VMEM((channels, span), f32),
        ],
        compiler_params=params(),
        cost_estimate=LARGE_COST,
        name="backward_conv",
    )(me, *slots, *grads, table, taps, skip_gain, mixed)


def run_hidden_grad(output_grad, output_weight):
    rows, width = output_grad.shape
    channels = output_weight.shape[1]
    return pl.pallas_call(
        hidden_grad_kernel,
        out_shape=jax.ShapeDtypeStruct((channels, rows), bf16),
        in_specs=[ANY_SPEC, ANY_SPEC],
        out_specs=VMEM_SPEC,
        scratch_shapes=[
            pltpu.VMEM((rows, width), bf16),
            pltpu.VMEM((width, channels), bf16),
            pltpu.VMEM((rows, channels), f32),
            pltpu.SemaphoreType.DMA((2 * CHUNKS,)),
        ],
        compiler_params=params(),
        cost_estimate=SMALL_COST,
        name="hidden_grad",
    )(output_grad, output_weight)


def run_input_grad(side, core, chips, projection_grad, weight):
    _, rows, channels = projection_grad.shape
    width = weight.shape[1] // 2
    return pl.pallas_call(
        functools.partial(input_grad_kernel, chips, side * width),
        out_shape=(
            jax.ShapeDtypeStruct((rows // 2, width), bf16),
            jax.ShapeDtypeStruct((rows // 2, width), f32),
        ),
        in_specs=[SMEM_SPEC, VMEM_SPEC, ANY_SPEC],
        out_specs=(VMEM_SPEC, VMEM_SPEC),
        scratch_shapes=[
            pltpu.VMEM((3, width, channels), bf16),
            pltpu.VMEM((rows, width // 4), f32),
            pltpu.SemaphoreType.DMA((4,)),
        ],
        compiler_params=params(),
        cost_estimate=LARGE_COST,
        name="input_grad",
    )(core, projection_grad, weight)


def ctx_exchange(value, step):
    count = lax.axis_size("ctx")
    return lax.ppermute(value, "ctx", [(i, i ^ step) for i in range(count)])


def gather_ctx(value):
    return [value] + [ctx_exchange(value, step) for step in range(1, lax.axis_size("ctx"))]


def tp_exchange(value, mask):
    count = lax.axis_size("tp")
    return lax.ppermute(value, "tp", [(i, i ^ mask) for i in range(count)])


def together(*values):
    return lax.optimization_barrier(values)


def pick(value, index, axis=0):
    return lax.dynamic_index_in_dim(value, index, axis=axis, keepdims=False)


def scalar_array(value):
    return jnp.reshape(value, (1,)).astype(jnp.int32)


def body(
    token_ids,
    embed_table,
    norm_gain,
    input_weight,
    short_weight,
    filters,
    skip_gain,
    output_weight,
    output_grad,
):
    shards = lax.axis_size("ctx")
    chips = lax.axis_size("tp") // 2
    hops = chips - 1
    me = lax.axis_index("ctx")
    core = lax.axis_index("tp") % 2
    chip = lax.axis_index("tp") // 2
    local_rows = token_ids.shape[0]
    width, channels = output_weight.shape
    me_tie, core_tie, chip_tie = scalar_array(me), scalar_array(core), scalar_array(chip)
    weight = jnp.transpose(input_weight, (1, 0, 2))

    groups = filters.shape[0]
    row_number = lax.broadcasted_iota(jnp.int32, (groups + 8, local_rows), 0)
    packed = jnp.where(
        row_number < groups, jnp.pad(filters, ((0, 8), (0, 0))), token_ids.astype(f32)[None, :]
    )
    slots = gather_ctx(packed)
    hidden_grad = run_hidden_grad(output_grad, output_weight)
    arrived, hidden_grad, me_tie = together(slots[1:], hidden_grad, me_tie)
    slots = [packed] + arrived
    grad_slots = gather_ctx(hidden_grad)

    hidden, mixed, table, for_sibling = run_forward(
        me_tie, core_tie, slots, embed_table, norm_gain, weight, short_weight, skip_gain, output_weight
    )
    for_sibling, hidden, grad_slots = together(for_sibling, hidden, grad_slots)
    half = width // 2
    block_rows = local_rows // chips
    received = tp_exchange(for_sibling, 1)
    mine = run_own_part(core_tie, hidden, output_weight)
    received, mine, me_tie, late_hidden = together(received, mine, me_tie, hidden)
    mine = mine.reshape(chips, block_rows, half)
    received = received.reshape(chips, block_rows, half)

    def out_block(index):
        return pick(mine, index) + pick(received, index).astype(f32)

    order = list(range(2, chips)) + [1]
    first, second = order[: (chips - 1) // 2], order[(chips - 1) // 2 :]
    share = width // shards
    part = share // 2

    def out_sends(steps):
        return [out_block(jnp.bitwise_xor(chip, step)).astype(bf16) for step in steps]

    def ctx_pieces(steps):
        starts = [jnp.bitwise_xor(me, step) * share + core * part for step in steps]
        return [
            jnp.concatenate([lax.dynamic_slice_in_dim(output_grad, start, part, axis=1), late_hidden], axis=1)
            for start in starts
        ]

    ctx_first, ctx_second = range(1, shards // 2 + 1), range(shards // 2 + 1, shards)
    sends, pieces, me_tie = together(out_sends(first), ctx_pieces(ctx_first), me_tie)
    out_arrived = [tp_exchange(value, 2 * step) for step, value in zip(first, sends)]
    ctx_arrived = [ctx_exchange(value, step) for step, value in zip(ctx_first, pieces)]
    projection_grad = run_backward(
        me_tie, slots, grad_slots, table, short_weight, skip_gain, mixed
    )
    sends, pieces = out_sends(second), ctx_pieces(ctx_second)
    out_arrived, ctx_arrived, projection_grad, sends, pieces, core_tie = together(
        out_arrived, ctx_arrived, projection_grad, sends, pieces, core_tie
    )
    out_more = [tp_exchange(value, 2 * step) for step, value in zip(second, sends)]
    ctx_more = [ctx_exchange(value, step) for step, value in zip(ctx_second, pieces)]
    theirs_low, mine_low = run_input_grad(0, core_tie, chips, projection_grad, weight)
    theirs_low, mine_low, core_tie = together(theirs_low, mine_low, core_tie)
    received_low = tp_exchange(theirs_low, 1)
    theirs_high, mine_high = run_input_grad(1, core_tie, chips, projection_grad, weight)
    out_more, ctx_more, received_low, theirs_high, mine_high, core_tie = together(
        out_more, ctx_more, received_low, theirs_high, mine_high, core_tie
    )
    ctx_arrived = ctx_arrived + ctx_more

    received_high = tp_exchange(theirs_high, 1)
    own_ids = lax.dynamic_slice_in_dim(token_ids, chip * block_rows, block_rows, axis=0)
    own_hot = (own_ids[:, None] == jnp.arange(FIRST_ID, FIRST_ID + IDS)[None, :]).astype(bf16)
    own_letters = lax.dynamic_slice(embed_table, (FIRST_ID, core * half), (IDS, half))
    block = jnp.dot(own_hot, own_letters, preferred_element_type=f32) + out_block(chip)
    for value in out_arrived + out_more:
        block = block + value.astype(f32)
    block = block.astype(bf16)
    block, received_high = together(block, received_high)
    line = {step: tp_exchange(block, 2 * step) for step in order[:-1]}
    other_line = {0: tp_exchange(block, 1)}
    line[0] = block
    split = (chips, local_rows // (2 * chips), width)
    total = jnp.concatenate([mine_low, mine_high], axis=1).reshape(split)
    total = total + jnp.concatenate([received_low, received_high], axis=1).reshape(split).astype(f32)

    def halve(value, bit):
        pairs = value.reshape((value.shape[0] // 2, 2) + value.shape[1:])
        which = chip >> bit & 1
        return pick(pairs, which, 1), pick(pairs, 1 - which, 1).astype(bf16)

    levels = chips.bit_length() - 1
    ctx_parts = jnp.concatenate([value[:, :part] for value in ctx_arrived], axis=0)
    for bit in range(levels):
        kept, leaving = halve(total, bit)
        if bit == levels - 1:
            line[1] = tp_exchange(block, 2)
        arriving = tp_exchange(leaving, 2 << bit)
        if bit == 0:
            other_parts = tp_exchange(ctx_parts, 1)
            steps = order[:-1]
            values = [line[step] for step in steps]
            arriving, values, other_parts, line[0], block = together(
                arriving, values, other_parts, line[0], block
            )
            line.update(zip(steps, values))
            for step in steps:
                other_line[step] = tp_exchange(line[step], 1)
        total = kept + arriving.astype(f32)
    other_line[1] = tp_exchange(line[1], 1)

    own_piece = lax.dynamic_slice_in_dim(output_grad, me * share, share, axis=1)
    own_parts = own_piece.reshape(local_rows, 2, part)
    my_columns = jnp.concatenate([pick(own_parts, core, 1), ctx_parts], axis=0)
    other_columns = jnp.concatenate([pick(own_parts, 1 - core, 1), other_parts], axis=0)
    columns = jnp.where(
        core == 0,
        jnp.concatenate([my_columns, other_columns], axis=1),
        jnp.concatenate([other_columns, my_columns], axis=1),
    )
    all_hidden = jnp.concatenate([late_hidden] + [value[:, part:] for value in ctx_arrived], axis=0)
    output_weight_grad = lax.dot_general(
        columns, all_hidden, (((0,), (0,)), ((), ())), preferred_element_type=f32
    )
    block_output = run_assemble(
        chip_tie,
        core_tie,
        [line[step] for step in range(chips)],
        [other_line[step] for step in range(chips)],
    )
    normed_grad = total.reshape(local_rows // (2 * chips), width)
    return (block_output, output_weight_grad, jnp.transpose(projection_grad, (1, 0, 2)), normed_grad)


def solution(mesh):
    in_specs = (
        P("ctx"),
        P(),
        P(),
        P(None, None, "tp"),
        P(None, None, "tp"),
        P("tp", "ctx"),
        P("tp"),
        P(None, "tp"),
        P("ctx", None),
    )
    out_specs = (P("ctx", None), P("ctx", "tp"), P("ctx", None, "tp"), P(("ctx", "tp"), None))
    return jax.shard_map(body, mesh=mesh, in_specs=in_specs, out_specs=out_specs, check_vma=False)
```

time: 202 us -> 160 us (0.79)
  starting transfers between devices: 65.4 us -> 27.1 us
  matrix products: 41.2 us -> 6.07 us
  Pallas kernels: 26.7 us -> 59 us
  waiting for transfers between devices: 44.8 us -> 37.7 us
  local copies, waits for them, and re-layouts: 12.1 us -> 18.3 us
    ppermute x36 -> x25, starting transfers between devices: 65.4 us -> 27.1 us  [the longest x16 14.4 us: tp_exchange(): return lax.ppermute(value, 'tp', [(i, i ^ mask) for i in range(count)])]
    dot_general x8 -> x2, matrix products: 41.2 us -> 6.07 us  [the longest x1 4.86 us: body(): lax.dot_general(columns, all_hidden, (((0,), (0,)), ((), ())), preferred_...]
    pallas_call x1 -> x6, Pallas kernels: 11.5 us -> 46 us  [the longest x1 17.5 us: run_forward(): pl.pallas_call(functools.partial(forward_kernel, shards), grid=(1,), out_...]
    ppermute x36 -> x25, waiting for transfers between devices: 44.8 us -> 37.7 us  [the longest x16 33.8 us: tp_exchange(): return lax.ppermute(value, 'tp', [(i, i ^ mask) for i in range(count)])]
    dynamic_slice x3 -> x5, local copies, waits for them, and re-layouts: 4.45 us -> 9.27 us  [the longest x3 5.9 us: pick(): return lax.dynamic_index_in_dim(value, index, axis=axis, keepdims=False)]
    unnamed x38 -> x59, local copies, waits for them, and re-layouts: 1.81 us -> 5.41 us
    reshape x5 -> x0, local copies, waits for them, and re-layouts: 3 us -> none  [the longest x4 2.24 us: body(): ids = [jnp.reshape(slot, (1, local_rows)) for slot in gather_ctx(token_ids)]]
    concatenate x1 -> x2, other arithmetic: 0.01 us -> 2.72 us  [the longest x1 1.63 us: ctx_pieces(): jnp.concatenate([lax.dynamic_slice_in_dim(output_grad, start, part, axis=...]
  transfers between devices with their start and end apart: 36 -> 25, of which waited for: 10 -> 11; matrix products, arithmetic and copies ran while one was open for 27% -> 17% of each run, Pallas kernels for 13% -> 35%
where the time goes in v2:
time: 160 us; the launch traced here: 159 us
  Pallas kernels  59 us (37%)
  waiting for transfers between devices  37.7 us (24%)
  starting transfers between devices  27.1 us (17%)
  local copies, waits for them, and re-layouts  18.3 us (11%)
  other arithmetic  10.2 us (6%)
  matrix products  6.07 us (4%)
    ppermute x16, waiting for transfers between devices, tp_exchange(): return lax.ppermute(value, 'tp', [(i, i ^ mask) for i in range(count)])  33.8 us
    pallas_call x1, Pallas kernels, run_forward(): pl.pallas_call(functools.partial(forward_kernel, shards), grid=(1,), out_...  17.5 us
    pallas_call x2, Pallas kernels, run_input_grad(): pl.pallas_call(functools.partial(input_grad_kernel, chips, side * width),...  15 us
    ppermute x16, starting transfers between devices, tp_exchange(): return lax.ppermute(value, 'tp', [(i, i ^ mask) for i in range(count)])  14.4 us
    pallas_call x1, Pallas kernels, run_backward(): pl.pallas_call(functools.partial(backward_kernel, shards), out_shape=jax....  13 us
    ppermute x9, starting transfers between devices, ctx_exchange(): return lax.ppermute(value, 'ctx', [(i, i ^ step) for i in range(count)])  12.7 us
    dynamic_slice x3, local copies, waits for them, and re-layouts, pick(): return lax.dynamic_index_in_dim(value, index, axis=axis, keepdims=False)  5.9 us
    unnamed x59, local copies, waits for them, and re-layouts  5.41 us
  transfers between devices with their start and end apart: 25, of which 11 were waited for; matrix products, arithmetic and copies ran while one was open for 17% of the time, Pallas kernels for 35%

profile of v2, /device:TPU:0, one launch (start us, length us, event | category | flops | bytes accessed | tf_op | source)
XLA Modules:
  0.0 159.5 jit_solution(7731566073218465321)
XLA Ops:
  0.6 0.7 convert_element_type.74
  1.3 0.9 pad_select_fusion.refs_0_
  2.2 4.0 %collective-permute-start.2 = (f32[40,384]{1,0:T(8,128)S(1)}, f32[40,384]{1,0:T(8,128)S(1)}, u32[]{:S(2)}, u32[]{:S(2)}) collective-permute-start(f32[40,384]{1,0:T(8,128)S(1)} %pad_select_fusion.refs_0_), channel_id=1, source_target_pairs={{0,24},{8,16},{16,8},{24,0},{1,25},{9,17},{17,9},{25,1},{2,26},{10... | collective-permute-start | bytes 184328 | tf_op jit(solution)/shard_map/ppermute | solution.py:465
  6.2 0.5 collective-permute-start.1
  6.7 0.1 collective-permute-start
  6.8 4.4 %hidden_grad.1.refs_4_ = bf16[512,384]{1,0:T(8,128)(2,1)} custom-call(bf16[384,4096]{1,0:T(8,128)(2,1)} %grad_ref.1, bf16[4096,512]{1,0:T(8,128)(2,1)} %last_ref.1), custom_call_target="tpu_custom_call" | custom-call | flops 1000 | bytes 1000 | tf_op jit(solution)/shard_map/hidden_grad/pallas_call | solution.py:424
  11.3 2.9 %collective-permute-start.5 = (bf16[512,384]{1,0:T(8,128)(2,1)}, bf16[512,384]{1,0:T(8,128)(2,1)S(1)}, u32[]{:S(2)}, u32[]{:S(2)}) collective-permute-start(bf16[512,384]{1,0:T(8,128)(2,1)} %hidden_grad.1.refs_4_), channel_id=1, source_target_pairs={{0,24},{8,16},{16,8},{24,0},{1,25},{9,17},{17,9},{25,1},{2,26},{10... | collective-permute-start | bytes 1179656 | tf_op jit(solution)/shard_map/ppermute | solution.py:465
  14.2 0.5 collective-permute-start.4
  14.8 0.1 collective-permute-start.3
  14.9 17.5 %forward_conv.1 = (bf16[384,512]{1,0:T(8,128)(2,1)}, f32[512,512]{1,0:T(8,128)}, f32[3,32,512]{2,1,0:T(8,128)}, bf16[384,2048]{1,0:T(8,128)(2,1)}) custom-call(s32[1]{0:T(128)} %bitcast.1.me_ref, s32[1]{0:T(128)} %bitcast.2.core_ref, f32[40,384]{1,0:T(8,128)} %copy-done.21, f32[40,384]{1,0:T(8,128)} %copy-done.28, f32[40,384]{1,0:T(8,128)} %copy-done.27, ...), custom_call_target="tpu_custom_call" | custom-call | flops 20000000000 | bytes 10000000 | tf_op jit(solution)/shard_map/forward_conv/pallas_call | solution.py:362
  32.5 0.7 copy-done.23
  33.3 0.1 copy-done.25
  33.4 0.8 dynamic_slice.70
  34.2 1.3 constant_dynamic-slice_fusion.3
  35.5 5.4 %own_part.1 = f32[384,2048]{1,0:T(8,128)} custom-call(s32[1]{0:T(128)} %bitcast.2.core_ref, bf16[384,512]{1,0:T(8,128)(2,1)} %get-tuple-element.68.hidden_ref, bf16[4096,512]{1,0:T(8,128)(2,1)} %last_ref.1), custom_call_target="tpu_custom_call" | custom-call | flops 1000 | bytes 1000 | tf_op jit(solution)/shard_map/own_part/pallas_call | solution.py:329
  41.0 1.6 %pad_maximum_fusion.1 = (bf16[384,1024]{1,0:T(8,128)(2,1)}, bf16[384,1024]{1,0:T(8,128)(2,1)}, bf16[384,1024]{1,0:T(8,128)(2,1)}) fusion(bf16[384,512]{1,0:T(8,128)(2,1)S(1)} %copy-done.1, bf16[384,512]{1,0:T(8,128)(2,1)S(1)} %get-tuple-element.113, bf16[384,512]{1,0:T(8,128)(2,1)S(1)} %get-tuple-element.114, bf16[384,512]{1,0:T(8,128)(2,1)S(1)} %get-tuple-element.115), kind=kLoop, calls=%fused_computation.36 | loop fusion | flops 3932160 | bytes 3932160 | tf_op jit(solution)/shard_map/concatenate | solution.py:548
  42.6 1.1 copy-done
  43.7 1.2 fusion.33
  44.9 3.0 %collective-permute-start.7 = (bf16[96,2048]{1,0:T(8,128)(2,1)S(1)}, bf16[96,2048]{1,0:T(8,128)(2,1)S(1)}, u32[]{:S(2)}, u32[]{:S(2)}) collective-permute-start(bf16[96,2048]{1,0:T(8,128)(2,1)S(1)} %get-tuple-element.70), channel_id=1, source_target_pairs={{0,4},{1,5},{2,6},{3,7},{4,0},{5,1},{6,2},{7,3},{8,12},{9,13},{10,... | collective-permute-start | bytes 1179656 | tf_op jit(solution)/shard_map/ppermute | solution.py:474
  47.9 1.6 collective-permute-start.8
  49.5 1.5 collective-permute-start.9
  51.0 13.0 %backward_conv.1.refs_0_ = bf16[3,384,512]{2,1,0:T(8,128)(2,1)} custom-call(s32[1]{0:T(128)} %bitcast.1.me_ref, f32[40,384]{1,0:T(8,128)} %copy-done.21, f32[40,384]{1,0:T(8,128)} %copy-done.28, f32[40,384]{1,0:T(8,128)} %copy-done.27, f32[40,384]{1,0:T(8,128)} %copy-done.26, bf16[512,384]{1,0:T(8,128)(2,1)} %hidden_grad.1.refs_4_, ...), custom_call_target="tpu_custom_call" | custom-call | flops 20000000000 | bytes 10000000 | tf_op jit(solution)/shard_map/backward_conv/pallas_call | solution.py:402
  64.0 1.2 convolution_add_fusion
  65.2 0.9 collective-permute-done.7
  66.1 1.7 %collective-permute-done.8 = bf16[384,1024]{1,0:T(8,128)(2,1)S(1)} collective-permute-done((bf16[384,1024]{1,0:T(8,128)(2,1)}, bf16[384,1024]{1,0:T(8,128)(2,1)S(1)}, u32[]{:S(2)}, u32[]{:S(2)}) %collective-permute-start.8) | collective-permute-done | bytes 786464 | tf_op jit(solution)/shard_map/ppermute | solution.py:465
  67.8 1.3 collective-permute-done.9
  69.1 1.4 collective-permute-start.10
  70.4 0.2 collective-permute-start.11
  70.7 1.5 collective-permute-start.12
  72.2 7.5 %input_grad.2 = (bf16[192,2048]{1,0:T(8,128)(2,1)}, f32[192,2048]{1,0:T(8,128)}) custom-call(s32[1]{0:T(128)} %bitcast.2.core_ref, bf16[3,384,512]{2,1,0:T(8,128)(2,1)} %backward_conv.1.refs_0_, bf16[3,4096,512]{2,1,0:T(8,128)(2,1)} %bitcast.39), custom_call_target="tpu_custom_call" | custom-call | flops 20000000000 | bytes 10000000 | tf_op jit(solution)/shard_map/input_grad/pallas_call | solution.py:444
  79.7 7.5 %input_grad.3 = (bf16[192,2048]{1,0:T(8,128)(2,1)}, f32[192,2048]{1,0:T(8,128)}) custom-call(s32[1]{0:T(128)} %bitcast.2.core_ref, bf16[3,384,512]{2,1,0:T(8,128)(2,1)} %backward_conv.1.refs_0_, bf16[3,4096,512]{2,1,0:T(8,128)(2,1)} %bitcast.40), custom_call_target="tpu_custom_call" | custom-call | flops 20000000000 | bytes 10000000 | tf_op jit(solution)/shard_map/input_grad/pallas_call | solution.py:444
  87.3 1.0 fusion.40
  88.3 0.8 collective-permute-done.11
  89.1 0.9 collective-permute-done.12
  90.2 0.8 fusion.42
  91.0 1.1 pad_maximum_fusion
  92.1 0.6 collective-permute-start.18
  92.6 0.9 add_convert_fusion.refs_0_
  93.6 1.5 maximum_add_fusion
  95.2 1.0 fusion.30
  96.1 1.7 %collective-permute-start.15 = (bf16[2,48,4096]{2,1,0:T(8,128)(2,1)}, bf16[2,48,4096]{2,1,0:T(8,128)(2,1)}, u32[]{:S(2)}, u32[]{:S(2)}) collective-permute-start(bf16[2,48,4096]{2,1,0:T(8,128)(2,1)} %fusion.30), channel_id=1, source_target_pairs={{0,2},{1,3},{2,0},{3,1},{4,6},{5,7},{6,4},{7,5},{8,10},{9,11},{10,... | collective-permute-start | bytes 2359304 | tf_op jit(solution)/shard_map/ppermute | solution.py:474
  97.8 2.3 %collective-permute-start.17 = (bf16[96,2048]{1,0:T(8,128)(2,1)}, bf16[96,2048]{1,0:T(8,128)(2,1)}, u32[]{:S(2)}, u32[]{:S(2)}) collective-permute-start(bf16[96,2048]{1,0:T(8,128)(2,1)} %add_convert_fusion.refs_0_), channel_id=1, source_target_pairs={{0,6},{1,7},{2,4},{3,5},{4,2},{5,3},{6,0},{7,1},{8,14},{9,15},{10,... | collective-permute-start | bytes 1179656 | tf_op jit(solution)/shard_map/ppermute | solution.py:474
  100.1 2.1 %constant_dynamic-slice_fusion.2 = bf16[384,1024]{1,0:T(8,128)(2,1)} fusion(bf16[384,4096]{1,0:T(8,128)(2,1)} %grad_ref.1, s32[]{:T(128)S(6)} %select_n.94), kind=kLoop, calls=%fused_computation.56 | loop fusion | bytes 1572868 | tf_op jit(solution)/shard_map/dynamic_slice | solution.py:615
  102.2 2.3 %copy.19 = bf16[384,1024]{0,1:T(8,128)(2,1)} copy(bf16[384,1024]{1,0:T(8,128)(2,1)} %constant_dynamic-slice_fusion.2) | data formatting | bytes 1572864
  104.5 2.1 %constant_dynamic-slice_fusion.1 = (bf16[384,1,512]{0,2,1:T(8,128)(2,1)}, bf16[384,1,512]{0,2,1:T(8,128)(2,1)}) fusion(bf16[384,2,512]{0,2,1:T(8,128)(2,1)} %bitcast.33, s32[]{:T(128)S(6)} %select_n.95, s32[]{:T(128)S(6)} %select_n.96), kind=kLoop, calls=%fused_computation.55 | loop fusion | bytes 1572872 | tf_op jit(solution)/shard_map/jit(dynamic_index_in_dim)/dynamic_slice | solution.py:482
  106.5 1.9 %copy.16 = bf16[384,1,512]{2,0,1:T(8,128)(2,1)} copy(bf16[384,1,512]{0,2,1:T(8,128)(2,1)} %get-tuple-element.122) | data formatting | bytes 786432 | tf_op jit(solution)/shard_map/jit(dynamic_index_in_dim)/dynamic_slice | solution.py:482
  108.5 1.9 %copy.17 = bf16[384,1,512]{2,0,1:T(8,128)(2,1)} copy(bf16[384,1,512]{0,2,1:T(8,128)(2,1)} %get-tuple-element.123) | data formatting | bytes 786432 | tf_op jit(solution)/shard_map/jit(dynamic_index_in_dim)/dynamic_slice | solution.py:482
  110.5 16.7 %collective-permute-done.17.refs_3_ = bf16[96,2048]{1,0:T(8,128)(2,1)} collective-permute-done((bf16[96,2048]{1,0:T(8,128)(2,1)}, bf16[96,2048]{1,0:T(8,128)(2,1)}, u32[]{:S(2)}, u32[]{:S(2)}) %collective-permute-start.17) | collective-permute-done | bytes 393248 | tf_op jit(solution)/shard_map/ppermute | solution.py:474
  127.3 4.8 %collective-permute-done.16.refs_2_ = bf16[96,2048]{1,0:T(8,128)(2,1)} collective-permute-done((bf16[96,2048]{1,0:T(8,128)(2,1)}, bf16[96,2048]{1,0:T(8,128)(2,1)}, u32[]{:S(2)}, u32[]{:S(2)}) %collective-permute-start.16) | collective-permute-done | bytes 393248 | tf_op jit(solution)/shard_map/ppermute | solution.py:474
  132.0 0.7 collective-permute-done.15
  132.8 1.3 bitcast_add_fusion
  134.1 2.8 %collective-permute-start.24 = (bf16[1,48,4096]{2,1,0:T(8,128)(2,1)S(1)}, bf16[1,48,4096]{2,1,0:T(8,128)(2,1)S(1)}, u32[]{:S(2)}, u32[]{:S(2)}) collective-permute-start(bf16[1,48,4096]{2,1,0:T(8,128)(2,1)S(1)} %dynamic-slice_convert_fusion), channel_id=1, source_target_pairs={{0,4},{1,5},{2,6},{3,7},{4,0},{5,1},{6,2},{7,3},{8,12},{9,13},{10,... | collective-permute-start | bytes 1179656 | tf_op jit(solution)/shard_map/ppermute | solution.py:474
  136.9 1.7 %collective-permute-start.19 = (bf16[96,2048]{1,0:T(8,128)(2,1)}, bf16[96,2048]{1,0:T(8,128)(2,1)S(1)}, u32[]{:S(2)}, u32[]{:S(2)}) collective-permute-start(bf16[96,2048]{1,0:T(8,128)(2,1)} %add_convert_fusion.refs_0_), channel_id=1, source_target_pairs={{0,2},{1,3},{2,0},{3,1},{4,6},{5,7},{6,4},{7,5},{8,10},{9,11},{10,... | collective-permute-start | bytes 1179656 | tf_op jit(solution)/shard_map/ppermute | solution.py:474
  138.6 0.5 collective-permute-start.23
  139.2 4.9 %fusion = f32[1024,512]{1,0:T(8,128)} fusion(bf16[1152,512]{1,0:T(8,128)(2,1)} %collective-permute-done.18, bf16[384,512]{1,0:T(8,128)(2,1)S(1)} %bitcast.37, bf16[384,512]{1,0:T(8,128)(2,1)S(1)} %copy-done.7, bf16[384,512]{1,0:T(8,128)(2,1)S(1)} %copy-done.5, bf16[384,512]{1,0:T(8,128)(2,1)S(1)} %copy-done.3, bf16[384,512]{1,0:T(8,128)(2,1)S(1)} %bitcast.36, ...), kind=kOutput, calls=%fused_computation.2 | convolution fusion | flops 1656225792 | bytes 6815745 | tf_op jit(solution)/shard_map/dot_general | solution.py:625
  144.0 9.1 %collective-permute-done.19.refs_1_ = bf16[96,2048]{1,0:T(8,128)(2,1)S(1)} collective-permute-done((bf16[96,2048]{1,0:T(8,128)(2,1)}, bf16[96,2048]{1,0:T(8,128)(2,1)S(1)}, u32[]{:S(2)}, u32[]{:S(2)}) %collective-permute-start.19) | collective-permute-done | bytes 393248 | tf_op jit(solution)/shard_map/ppermute | solution.py:474
  153.1 0.6 collective-permute-done.24
  153.7 0.9 add_bitcast_fusion
  154.7 0.1 collective-permute-done.21.refs_5_
  154.8 0.6 copy-done.16
  155.4 0.1 copy-done.18
  155.5 0.1 copy-done.19
  155.7 0.1 copy-done.20
  155.8 3.7 %assemble.1 = bf16[384,4096]{1,0:T(8,128)(2,1)} custom-call(s32[1]{0:T(128)} %bitcast.chip_ref, s32[1]{0:T(128)} %bitcast.2.core_ref, bf16[96,2048]{1,0:T(8,128)(2,1)} %add_convert_fusion.refs_0_, bf16[96,2048]{1,0:T(8,128)(2,1)} %copy-done.17, bf16[96,2048]{1,0:T(8,128)(2,1)} %collective-permute-done.16.refs_2_, ...), custom_call_target="tpu_custom_call" | custom-call | flops 1000 | bytes 1000 | tf_op jit(solution)/shard_map/assemble/pallas_call | solution.py:344
  (75 shorter events, 0.5 us)
Async XLA Ops:
  2.2 9.0 %copy-start.21 = (f32[40,384]{1,0:T(8,128)}, f32[40,384]{1,0:T(8,128)S(1)}, u32[]{:S(2)}) copy-start(f32[40,384]{1,0:T(8,128)S(1)} %pad_select_fusion.refs_0_) | copy-start | bytes 184324
  2.2 9.1 %collective-permute-start.2 = (f32[40,384]{1,0:T(8,128)S(1)}, f32[40,384]{1,0:T(8,128)S(1)}, u32[]{:S(2)}, u32[]{:S(2)}) collective-permute-start(f32[40,384]{1,0:T(8,128)S(1)} %pad_select_fusion.refs_0_), channel_id=1, source_target_pairs={{0,24},{8,16},{16,8},{24,0},{1,25},{9,17},{17,9},{25,1},{2,26},{10... | collective-permute-start | bytes 184328 | tf_op jit(solution)/shard_map/ppermute | solution.py:465
  6.2 5.1 %collective-permute-start.1 = (f32[40,384]{1,0:T(8,128)S(1)}, f32[40,384]{1,0:T(8,128)S(1)}, u32[]{:S(2)}, u32[]{:S(2)}) collective-permute-start(f32[40,384]{1,0:T(8,128)S(1)} %pad_select_fusion.refs_0_), channel_id=1, source_target_pairs={{0,16},{8,24},{16,0},{24,8},{1,17},{9,25},{17,1},{25,9},{2,18},{10... | collective-permute-start | bytes 184328 | tf_op jit(solution)/shard_map/ppermute | solution.py:465
  6.7 4.6 %collective-permute-start = (f32[40,384]{1,0:T(8,128)S(1)}, f32[40,384]{1,0:T(8,128)S(1)}, u32[]{:S(2)}, u32[]{:S(2)}) collective-permute-start(f32[40,384]{1,0:T(8,128)S(1)} %pad_select_fusion.refs_0_), channel_id=1, source_target_pairs={{0,8},{8,0},{16,24},{24,16},{1,9},{9,1},{17,25},{25,17},{2,10},{10... | collective-permute-start | bytes 184328 | tf_op jit(solution)/shard_map/ppermute | solution.py:465
  11.3 3.6 %copy-start.26 = (f32[40,384]{1,0:T(8,128)}, f32[40,384]{1,0:T(8,128)S(1)}, u32[]{:S(2)}) copy-start(f32[40,384]{1,0:T(8,128)S(1)} %collective-permute-done.2.refs_3_) | copy-start | bytes 184324
  11.3 3.6 %copy-start.27 = (f32[40,384]{1,0:T(8,128)}, f32[40,384]{1,0:T(8,128)S(1)}, u32[]{:S(2)}) copy-start(f32[40,384]{1,0:T(8,128)S(1)} %collective-permute-done.1.refs_2_) | copy-start | bytes 184324
  11.3 3.6 %copy-start.28 = (f32[40,384]{1,0:T(8,128)}, f32[40,384]{1,0:T(8,128)S(1)}, u32[]{:S(2)}) copy-start(f32[40,384]{1,0:T(8,128)S(1)} %collective-permute-done.refs_1_) | copy-start | bytes 184324
  11.3 21.1 %collective-permute-start.5 = (bf16[512,384]{1,0:T(8,128)(2,1)}, bf16[512,384]{1,0:T(8,128)(2,1)S(1)}, u32[]{:S(2)}, u32[]{:S(2)}) collective-permute-start(bf16[512,384]{1,0:T(8,128)(2,1)} %hidden_grad.1.refs_4_), channel_id=1, source_target_pairs={{0,24},{8,16},{16,8},{24,0},{1,25},{9,17},{17,9},{25,1},{2,26},{10... | collective-permute-start | bytes 1179656 | tf_op jit(solution)/shard_map/ppermute | solution.py:465
  14.2 18.2 %collective-permute-start.4 = (bf16[512,384]{1,0:T(8,128)(2,1)}, bf16[512,384]{1,0:T(8,128)(2,1)S(1)}, u32[]{:S(2)}, u32[]{:S(2)}) collective-permute-start(bf16[512,384]{1,0:T(8,128)(2,1)} %hidden_grad.1.refs_4_), channel_id=1, source_target_pairs={{0,16},{8,24},{16,0},{24,8},{1,17},{9,25},{17,1},{25,9},{2,18},{10... | collective-permute-start | bytes 1179656 | tf_op jit(solution)/shard_map/ppermute | solution.py:465
  14.8 17.7 %collective-permute-start.3 = (bf16[512,384]{1,0:T(8,128)(2,1)}, bf16[512,384]{1,0:T(8,128)(2,1)S(1)}, u32[]{:S(2)}, u32[]{:S(2)}) collective-permute-start(bf16[512,384]{1,0:T(8,128)(2,1)} %hidden_grad.1.refs_4_), channel_id=1, source_target_pairs={{0,8},{8,0},{16,24},{24,16},{1,9},{9,1},{17,25},{25,17},{2,10},{10... | collective-permute-start | bytes 1179656 | tf_op jit(solution)/shard_map/ppermute | solution.py:465
  32.4 0.8 copy-start.23
  32.4 0.9 copy-start.24
  32.4 1.0 copy-start.25
  33.4 7.5 %collective-permute-start.6 = (bf16[384,2048]{1,0:T(8,128)(2,1)}, bf16[384,2048]{1,0:T(8,128)(2,1)S(1)}, u32[]{:S(2)}, u32[]{:S(2)}) collective-permute-start(bf16[384,2048]{1,0:T(8,128)(2,1)} %get-tuple-element.64), channel_id=1, source_target_pairs={{0,1},{1,0},{2,3},{3,2},{4,5},{5,4},{6,7},{7,6},{8,9},{9,8},{10,11... | collective-permute-start | bytes 4718600 | tf_op jit(solution)/shard_map/ppermute | solution.py:474
  35.5 5.5 %copy-start.1 = (bf16[384,512]{1,0:T(8,128)(2,1)S(1)}, bf16[384,512]{1,0:T(8,128)(2,1)}, u32[]{:S(2)}) copy-start(bf16[384,512]{1,0:T(8,128)(2,1)} %get-tuple-element.68.hidden_ref) | copy-start | bytes 1179652
  40.9 2.7 %copy-start = (f32[384,2048]{1,0:T(8,128)S(1)}, f32[384,2048]{1,0:T(8,128)}, u32[]{:S(2)}) copy-start(f32[384,2048]{1,0:T(8,128)} %own_part.1) | copy-start | bytes 9437188
  44.9 21.2 %collective-permute-start.7 = (bf16[96,2048]{1,0:T(8,128)(2,1)S(1)}, bf16[96,2048]{1,0:T(8,128)(2,1)S(1)}, u32[]{:S(2)}, u32[]{:S(2)}) collective-permute-start(bf16[96,2048]{1,0:T(8,128)(2,1)S(1)} %get-tuple-element.70), channel_id=1, source_target_pairs={{0,4},{1,5},{2,6},{3,7},{4,0},{5,1},{6,2},{7,3},{8,12},{9,13},{10,... | collective-permute-start | bytes 1179656 | tf_op jit(solution)/shard_map/ppermute | solution.py:474
  47.9 19.9 %collective-permute-start.8 = (bf16[384,1024]{1,0:T(8,128)(2,1)}, bf16[384,1024]{1,0:T(8,128)(2,1)S(1)}, u32[]{:S(2)}, u32[]{:S(2)}) collective-permute-start(bf16[384,1024]{1,0:T(8,128)(2,1)} %get-tuple-element.71), channel_id=1, source_target_pairs={{0,8},{8,0},{16,24},{24,16},{1,9},{9,1},{17,25},{25,17},{2,10},{10... | collective-permute-start | bytes 2359304 | tf_op jit(solution)/shard_map/ppermute | solution.py:465
  49.5 19.6 %collective-permute-start.9 = (bf16[384,1024]{1,0:T(8,128)(2,1)}, bf16[384,1024]{1,0:T(8,128)(2,1)S(1)}, u32[]{:S(2)}, u32[]{:S(2)}) collective-permute-start(bf16[384,1024]{1,0:T(8,128)(2,1)} %get-tuple-element.72), channel_id=1, source_target_pairs={{0,16},{8,24},{16,0},{24,8},{1,17},{9,25},{17,1},{25,9},{2,18},{10... | collective-permute-start | bytes 2359304 | tf_op jit(solution)/shard_map/ppermute | solution.py:465
  69.1 19.2 %collective-permute-start.10 = (bf16[96,2048]{1,0:T(8,128)(2,1)}, bf16[96,2048]{1,0:T(8,128)(2,1)S(1)}, u32[]{:S(2)}, u32[]{:S(2)}) collective-permute-start(bf16[96,2048]{1,0:T(8,128)(2,1)} %get-tuple-element.80), channel_id=1, source_target_pairs={{0,6},{1,7},{2,4},{3,5},{4,2},{5,3},{6,0},{7,1},{8,14},{9,15},{10,... | collective-permute-start | bytes 1179656 | tf_op jit(solution)/shard_map/ppermute | solution.py:474
  70.4 18.7 %collective-permute-start.11 = (bf16[96,2048]{1,0:T(8,128)(2,1)}, bf16[96,2048]{1,0:T(8,128)(2,1)S(1)}, u32[]{:S(2)}, u32[]{:S(2)}) collective-permute-start(bf16[96,2048]{1,0:T(8,128)(2,1)} %get-tuple-element.81), channel_id=1, source_target_pairs={{0,2},{1,3},{2,0},{3,1},{4,6},{5,7},{6,4},{7,5},{8,10},{9,11},{10,... | collective-permute-start | bytes 1179656 | tf_op jit(solution)/shard_map/ppermute | solution.py:474
  70.7 19.4 %collective-permute-start.12 = (bf16[384,1024]{1,0:T(8,128)(2,1)}, bf16[384,1024]{1,0:T(8,128)(2,1)S(1)}, u32[]{:S(2)}, u32[]{:S(2)}) collective-permute-start(bf16[384,1024]{1,0:T(8,128)(2,1)} %get-tuple-element.82), channel_id=1, source_target_pairs={{0,24},{8,16},{16,8},{24,0},{1,25},{9,17},{17,9},{25,1},{2,26},{10... | collective-permute-start | bytes 2359304 | tf_op jit(solution)/shard_map/ppermute | solution.py:465
  79.7 10.4 %collective-permute-start.13 = (bf16[192,2048]{1,0:T(8,128)(2,1)}, bf16[192,2048]{1,0:T(8,128)(2,1)S(1)}, u32[]{:S(2)}, u32[]{:S(2)}) collective-permute-start(bf16[192,2048]{1,0:T(8,128)(2,1)} %get-tuple-element.87), channel_id=1, source_target_pairs={{0,1},{1,0},{2,3},{3,2},{4,5},{5,4},{6,7},{7,6},{8,9},{9,8},{10,11... | collective-permute-start | bytes 2359304 | tf_op jit(solution)/shard_map/ppermute | solution.py:474
  87.2 2.8 %copy-start.22 = (bf16[192,2048]{1,0:T(8,128)(2,1)S(1)}, bf16[192,2048]{1,0:T(8,128)(2,1)}, u32[]{:S(2)}) copy-start(bf16[192,2048]{1,0:T(8,128)(2,1)} %get-tuple-element.98) | copy-start | bytes 2359300
  88.3 5.3 %copy-start.2 = (bf16[384,512]{1,0:T(8,128)(2,1)}, bf16[384,512]{1,0:T(8,128)(2,1)S(1)}, u32[]{:S(2)}) copy-start(bf16[384,512]{1,0:T(8,128)(2,1)S(1)} %get-tuple-element.117) | copy-start | bytes 1179652
  88.3 5.3 %copy-start.4 = (bf16[384,512]{1,0:T(8,128)(2,1)}, bf16[384,512]{1,0:T(8,128)(2,1)S(1)}, u32[]{:S(2)}) copy-start(bf16[384,512]{1,0:T(8,128)(2,1)S(1)} %get-tuple-element.127) | copy-start | bytes 1179652
  90.0 3.5 %copy-start.10 = (bf16[192,2048]{1,0:T(8,128)(2,1)}, bf16[192,2048]{1,0:T(8,128)(2,1)S(1)}, u32[]{:S(2)}) copy-start(bf16[192,2048]{1,0:T(8,128)(2,1)S(1)} %collective-permute-done.13) | copy-start | bytes 2359300
  90.0 3.5 %copy-start.8 = (f32[192,2048]{1,0:T(8,128)S(1)}, f32[192,2048]{1,0:T(8,128)}, u32[]{:S(2)}) copy-start(f32[192,2048]{1,0:T(8,128)} %get-tuple-element.92) | copy-start | bytes 4718596
  90.1 3.5 %copy-start.9 = (f32[192,2048]{1,0:T(8,128)S(1)}, f32[192,2048]{1,0:T(8,128)}, u32[]{:S(2)}) copy-start(f32[192,2048]{1,0:T(8,128)} %get-tuple-element.93) | copy-start | bytes 4718596
  90.1 3.5 %collective-permute-start.14 = (bf16[192,2048]{1,0:T(8,128)(2,1)S(1)}, bf16[192,2048]{1,0:T(8,128)(2,1)S(1)}, u32[]{:S(2)}, u32[]{:S(2)}) collective-permute-start(bf16[192,2048]{1,0:T(8,128)(2,1)S(1)} %copy-done.22), channel_id=1, source_target_pairs={{0,1},{1,0},{2,3},{3,2},{4,5},{5,4},{6,7},{7,6},{8,9},{9,8},{10,11... | collective-permute-start | bytes 2359304 | tf_op jit(solution)/shard_map/ppermute | solution.py:474
  91.0 4.2 %copy-start.6 = (bf16[384,512]{1,0:T(8,128)(2,1)}, bf16[384,512]{1,0:T(8,128)(2,1)S(1)}, u32[]{:S(2)}) copy-start(bf16[384,512]{1,0:T(8,128)(2,1)S(1)} %get-tuple-element.121) | copy-start | bytes 1179652
  92.1 40.0 %collective-permute-start.18 = (bf16[1152,512]{1,0:T(8,128)(2,1)}, bf16[1152,512]{1,0:T(8,128)(2,1)}, u32[]{:S(2)}, u32[]{:S(2)}) collective-permute-start(bf16[1152,512]{1,0:T(8,128)(2,1)} %pad_maximum_fusion), channel_id=1, source_target_pairs={{0,1},{1,0},{2,3},{3,2},{4,5},{5,4},{6,7},{7,6},{8,9},{9,8},{10,11... | collective-permute-start | bytes 3538952 | tf_op jit(solution)/shard_map/ppermute | solution.py:474
  96.1 36.6 %collective-permute-start.15 = (bf16[2,48,4096]{2,1,0:T(8,128)(2,1)}, bf16[2,48,4096]{2,1,0:T(8,128)(2,1)}, u32[]{:S(2)}, u32[]{:S(2)}) collective-permute-start(bf16[2,48,4096]{2,1,0:T(8,128)(2,1)} %fusion.30), channel_id=1, source_target_pairs={{0,2},{1,3},{2,0},{3,1},{4,6},{5,7},{6,4},{7,5},{8,10},{9,11},{10,... | collective-permute-start | bytes 2359304 | tf_op jit(solution)/shard_map/ppermute | solution.py:474
  97.8 29.4 %collective-permute-start.17 = (bf16[96,2048]{1,0:T(8,128)(2,1)}, bf16[96,2048]{1,0:T(8,128)(2,1)}, u32[]{:S(2)}, u32[]{:S(2)}) collective-permute-start(bf16[96,2048]{1,0:T(8,128)(2,1)} %add_convert_fusion.refs_0_), channel_id=1, source_target_pairs={{0,6},{1,7},{2,4},{3,5},{4,2},{5,3},{6,0},{7,1},{8,14},{9,15},{10,... | collective-permute-start | bytes 1179656 | tf_op jit(solution)/shard_map/ppermute | solution.py:474
  100.1 31.9 %collective-permute-start.16 = (bf16[96,2048]{1,0:T(8,128)(2,1)}, bf16[96,2048]{1,0:T(8,128)(2,1)}, u32[]{:S(2)}, u32[]{:S(2)}) collective-permute-start(bf16[96,2048]{1,0:T(8,128)(2,1)} %add_convert_fusion.refs_0_), channel_id=1, source_target_pairs={{0,4},{1,5},{2,6},{3,7},{4,0},{5,1},{6,2},{7,3},{8,12},{9,13},{10,... | collective-permute-start | bytes 1179656 | tf_op jit(solution)/shard_map/ppermute | solution.py:474
  110.4 28.7 %copy-start.3 = (bf16[384,512]{1,0:T(8,128)(2,1)S(1)}, bf16[384,512]{1,0:T(8,128)(2,1)}, u32[]{:S(2)}) copy-start(bf16[384,512]{1,0:T(8,128)(2,1)} %copy-done.2) | copy-start | bytes 1179652
  110.4 28.7 %copy-start.5 = (bf16[384,512]{1,0:T(8,128)(2,1)S(1)}, bf16[384,512]{1,0:T(8,128)(2,1)}, u32[]{:S(2)}) copy-start(bf16[384,512]{1,0:T(8,128)(2,1)} %copy-done.4) | copy-start | bytes 1179652
  110.4 28.7 %copy-start.7 = (bf16[384,512]{1,0:T(8,128)(2,1)S(1)}, bf16[384,512]{1,0:T(8,128)(2,1)}, u32[]{:S(2)}) copy-start(bf16[384,512]{1,0:T(8,128)(2,1)} %copy-done.6) | copy-start | bytes 1179652
  110.4 28.7 %copy-start.11 = (bf16[384,512]{1,0:T(8,128)(2,1)S(1)}, bf16[384,512]{1,0:T(8,128)(2,1)}, u32[]{:S(2)}) copy-start(bf16[384,512]{1,0:T(8,128)(2,1)} %get-tuple-element.116) | copy-start | bytes 1179652
  110.4 28.7 %copy-start.12 = (bf16[384,512]{1,0:T(8,128)(2,1)S(1)}, bf16[384,512]{1,0:T(8,128)(2,1)}, u32[]{:S(2)}) copy-start(bf16[384,512]{1,0:T(8,128)(2,1)} %get-tuple-element.128) | copy-start | bytes 1179652
  110.4 28.7 %copy-start.13 = (bf16[384,1,512]{2,0,1:T(8,128)(2,1)S(1)}, bf16[384,1,512]{2,0,1:T(8,128)(2,1)}, u32[]{:S(2)}) copy-start(bf16[384,1,512]{2,0,1:T(8,128)(2,1)} %copy.16) | copy-start | bytes 1179652
  110.4 28.7 %copy-start.14 = (bf16[384,1,512]{2,0,1:T(8,128)(2,1)S(1)}, bf16[384,1,512]{2,0,1:T(8,128)(2,1)}, u32[]{:S(2)}) copy-start(bf16[384,1,512]{2,0,1:T(8,128)(2,1)} %copy.17) | copy-start | bytes 1179652
  110.4 28.7 %copy-start.15 = (bf16[384,512]{1,0:T(8,128)(2,1)S(1)}, bf16[384,512]{1,0:T(8,128)(2,1)}, u32[]{:S(2)}) copy-start(bf16[384,512]{1,0:T(8,128)(2,1)} %get-tuple-element.120) | copy-start | bytes 1179652
  110.4 44.2 %collective-permute-start.20 = (bf16[96,2048]{1,0:T(8,128)(2,1)}, bf16[96,2048]{1,0:T(8,128)(2,1)S(1)}, u32[]{:S(2)}, u32[]{:S(2)}) collective-permute-start(bf16[96,2048]{1,0:T(8,128)(2,1)} %add_convert_fusion.refs_0_), channel_id=1, source_target_pairs={{0,1},{1,0},{2,3},{3,2},{4,5},{5,4},{6,7},{7,6},{8,9},{9,8},{10,11... | collective-permute-start | bytes 1179656 | tf_op jit(solution)/shard_map/ppermute | solution.py:474
  134.1 19.6 %collective-permute-start.24 = (bf16[1,48,4096]{2,1,0:T(8,128)(2,1)S(1)}, bf16[1,48,4096]{2,1,0:T(8,128)(2,1)S(1)}, u32[]{:S(2)}, u32[]{:S(2)}) collective-permute-start(bf16[1,48,4096]{2,1,0:T(8,128)(2,1)S(1)} %dynamic-slice_convert_fusion), channel_id=1, source_target_pairs={{0,4},{1,5},{2,6},{3,7},{4,0},{5,1},{6,2},{7,3},{8,12},{9,13},{10,... | collective-permute-start | bytes 1179656 | tf_op jit(solution)/shard_map/ppermute | solution.py:474
  136.9 16.2 %collective-permute-start.19 = (bf16[96,2048]{1,0:T(8,128)(2,1)}, bf16[96,2048]{1,0:T(8,128)(2,1)S(1)}, u32[]{:S(2)}, u32[]{:S(2)}) collective-permute-start(bf16[96,2048]{1,0:T(8,128)(2,1)} %add_convert_fusion.refs_0_), channel_id=1, source_target_pairs={{0,2},{1,3},{2,0},{3,1},{4,6},{5,7},{6,4},{7,5},{8,10},{9,11},{10,... | collective-permute-start | bytes 1179656 | tf_op jit(solution)/shard_map/ppermute | solution.py:474
  138.6 16.0 %collective-permute-start.22 = (bf16[96,2048]{1,0:T(8,128)(2,1)}, bf16[96,2048]{1,0:T(8,128)(2,1)S(1)}, u32[]{:S(2)}, u32[]{:S(2)}) collective-permute-start(bf16[96,2048]{1,0:T(8,128)(2,1)} %collective-permute-done.16.refs_2_), channel_id=1, source_target_pairs={{0,1},{1,0},{2,3},{3,2},{4,5},{5,4},{6,7},{7,6},{8,9},{9,8},{10,11... | collective-permute-start | bytes 1179656 | tf_op jit(solution)/shard_map/ppermute | solution.py:474
  138.6 16.0 %collective-permute-start.23 = (bf16[96,2048]{1,0:T(8,128)(2,1)}, bf16[96,2048]{1,0:T(8,128)(2,1)S(1)}, u32[]{:S(2)}, u32[]{:S(2)}) collective-permute-start(bf16[96,2048]{1,0:T(8,128)(2,1)} %collective-permute-done.17.refs_3_), channel_id=1, source_target_pairs={{0,1},{1,0},{2,3},{3,2},{4,5},{5,4},{6,7},{7,6},{8,9},{9,8},{10,11... | collective-permute-start | bytes 1179656 | tf_op jit(solution)/shard_map/ppermute | solution.py:474
  153.1 1.7 %copy-start.17 = (bf16[96,2048]{1,0:T(8,128)(2,1)}, bf16[96,2048]{1,0:T(8,128)(2,1)S(1)}, u32[]{:S(2)}) copy-start(bf16[96,2048]{1,0:T(8,128)(2,1)S(1)} %collective-permute-done.19.refs_1_) | copy-start | bytes 1179652
  153.1 1.7 %collective-permute-start.21 = (bf16[96,2048]{1,0:T(8,128)(2,1)S(1)}, bf16[96,2048]{1,0:T(8,128)(2,1)S(1)}, u32[]{:S(2)}, u32[]{:S(2)}) collective-permute-start(bf16[96,2048]{1,0:T(8,128)(2,1)S(1)} %collective-permute-done.19.refs_1_), channel_id=1, source_target_pairs={{0,1},{1,0},{2,3},{3,2},{4,5},{5,4},{6,7},{7,6},{8,9},{9,8},{10,11... | collective-permute-start | bytes 1179656 | tf_op jit(solution)/shard_map/ppermute | solution.py:474
  154.6 0.8 copy-start.16
  154.6 0.9 copy-start.18
  154.7 1.0 copy-start.19
  154.8 0.9 copy-start.20

commit v3 on v2

--- a/solution.py
+++ b/solution.py
@@ -89,27 +89,25 @@
     return copies
 
 
-def project(hidden, copies, weight, out_ref):
+def project(hidden, copies, weight, staged, out_ref, left):
     chunk = weight.shape[0] // len(copies)
+    leaving = []
     for index, copy in enumerate(copies):
         rows = slice(index * chunk, (index + 1) * chunk)
         copy.wait()
         value = lax.dot_general(hidden, weight[rows], CONTRACT_LAST, preferred_element_type=f32)
-        out_ref[:, rows] = value.astype(out_ref.dtype)
-
-
-def own_part_kernel(core_ref, hidden_ref, last_ref, out_ref, last, arrived):
-    copies = start_rows(last_ref, core_ref[0] * last.shape[0], last, arrived)
-    project(hidden_ref[...], copies, last, out_ref)
-
-
-def assemble_kernel(chip_ref, core_ref, *refs):
+        staged[:, rows] = value.astype(staged.dtype)
+        leaving.append(pltpu.make_async_copy(staged.at[:, rows], out_ref.at[:, rows], left.at[index]))
+        leaving[-1].start()
+    return leaving
+
+
+def assemble_kernel(steps, chip_ref, core_ref, *refs):
     out_ref = refs[-1]
-    chips = (len(refs) - 1) // 2
     rows, columns = refs[0].shape
-    for index in range(2 * chips):
-        place = jnp.bitwise_xor(chip_ref[0], index % chips)
-        side = core_ref[0] if index < chips else 1 - core_ref[0]
+    for index, step in enumerate(steps + steps):
+        place = jnp.bitwise_xor(chip_ref[0], step)
+        side = core_ref[0] if index < len(steps) else 1 - core_ref[0]
         at = (pl.ds(pl.multiple_of(place * rows, rows), rows), pl.ds(pl.multiple_of(side * columns, columns), columns))
         out_ref[at] = refs[index][...]
 
@@ -117,11 +115,12 @@
 def forward_kernel(shards, me_ref, core_ref, *refs):
     slots = refs[:shards]
     letters_ref, gain_ref, weight_ref, taps_ref, skip_ref, last_ref = refs[shards : shards + 6]
-    hidden_ref, mixed_ref, table_ref, theirs_ref = refs[shards + 6 : shards + 10]
-    normed, hot, filters, matrices, signal, exact, long_part, weight, arrived, last, last_arrived = refs[shards + 10 :]
+    hidden_ref, mixed_ref, table_ref, theirs_ref, mine_ref = refs[shards + 6 : shards + 11]
+    normed, hot, filters, matrices, signal, exact, long_part, weight, arrived, last, last_arrived = refs[shards + 11 : shards + 22]
+    own, own_arrived, table, staged, own_staged, left = refs[shards + 22 :]
     groups = filters.shape[0]
     local_rows = slots[0].shape[1]
-    channels = table_ref.shape[2]
+    channels = table.shape[2]
     width = channels // groups
     local_blocks = local_rows // LANES
     blocks = shards * local_blocks
@@ -139,6 +138,7 @@
         copies.append(pltpu.make_async_copy(weight_ref.at[:, rows], weight.at[:, rows], arrived.at[index]))
         copies[-1].start()
     last_copies = start_rows(last_ref, (1 - core_ref[0]) * last.shape[0], last, last_arrived)
+    own_copies = start_rows(last_ref, core_ref[0] * last.shape[0], own, own_arrived)
     for index, slot in enumerate(slots):
         place = lanes_at(jnp.bitwise_xor(me, index) * local_blocks, local_blocks)
         filters[:, place] = slot[:groups]
@@ -165,10 +165,12 @@
         copies[index].wait()
         for part in range(3):
             term = jnp.dot(normed[:, rows], weight[part, rows], preferred_element_type=f32)
-            table_ref[part] = term if index == 0 else table_ref[part] + term
-
-    key_weights = tap_weights(taps_ref, table_ref, 1)
-    value_weights = tap_weights(taps_ref, table_ref, 2)
+            table[part] = term if index == 0 else table[part] + term
+
+    table_copy = pltpu.make_async_copy(table, table_ref, left.at[0])
+    table_copy.start()
+    key_weights = tap_weights(taps_ref, table, 1)
+    value_weights = tap_weights(taps_ref, table, 2)
     for start in range(0, channels, LANES):
         rows = slice(start, start + LANES)
         mixture = expand(key_weights[:, rows], hot[:, :length]) * expand(value_weights[:, rows], hot[:, :length])
@@ -186,11 +188,16 @@
     lax.fori_loop(0, groups, one_group, 0, unroll=4)
     columns = channel_columns(taps_ref, skip_ref)
     mixed = columns[:, 3 * taps : 3 * taps + 1] * exact[:, lanes_at(first, window)] + long_part[...]
-    mixed_ref[...] = mixed
-    queries = expand(tap_weights(taps_ref, table_ref, 0), hot[:, lanes_at(first, local_blocks)])
+    long_part[...] = mixed
+    mixed_copy = pltpu.make_async_copy(long_part, mixed_ref, left.at[1])
+    mixed_copy.start()
+    queries = expand(tap_weights(taps_ref, table, 0), hot[:, lanes_at(first, local_blocks)])
     hidden = jnp.transpose(queries * mixed[:, :local_rows]).astype(bf16)
     hidden_ref[...] = hidden
-    project(hidden, last_copies, last, theirs_ref)
+    leaving = project(hidden, last_copies, last, staged, theirs_ref, left.at[2:6])
+    leaving += project(hidden, own_copies, own, own_staged, mine_ref, left.at[6:])
+    for copy in [table_copy, mixed_copy] + leaving:
+        copy.wait()
 
 
 def backward_kernel(shards, me_ref, *refs):
@@ -275,15 +282,13 @@
     out_ref[...] = jnp.transpose(total[...]).astype(bf16)
 
 
-def input_grad_kernel(chips, start, core_ref, *refs):
-    grad_ref, weight_ref, theirs_ref, mine_ref, weight, total, arrived = refs
+def input_grad_kernel(chips, core_ref, grad_ref, weight_ref, theirs_ref, mine_ref, weight, total, theirs, mine, arrived, left):
     chunks = arrived.shape[0]
     chunk = weight.shape[1] // chunks
     copies = []
     for index in range(chunks):
-        rows = slice(index * chunk, (index + 1) * chunk)
-        source = weight_ref.at[:, start + index * chunk : start + (index + 1) * chunk]
-        copies.append(pltpu.make_async_copy(source, weight.at[:, rows], arrived.at[index]))
+        columns = slice(index * chunk, (index + 1) * chunk)
+        copies.append(pltpu.make_async_copy(weight_ref.at[:, columns], weight.at[:, columns], arrived.at[index]))
         copies[-1].start()
     core = core_ref[0]
     rows = total.shape[0] // (2 * chips)
@@ -292,18 +297,42 @@
         starts = [pl.multiple_of((2 * chip + which) * rows, 8) for chip in range(chips)]
         return jnp.concatenate([total[pl.ds(start, rows), :] for start in starts], axis=0)
 
+    leaving = []
     for index in range(chunks):
-        part_rows = slice(index * chunk, (index + 1) * chunk)
+        columns = slice(index * chunk, (index + 1) * chunk)
         copies[index].wait()
         value = None
         for part in range(3):
             term = lax.dot_general(
-                grad_ref[part], weight[part, part_rows], CONTRACT_LAST, preferred_element_type=f32
+                grad_ref[part], weight[part, columns], CONTRACT_LAST, preferred_element_type=f32
             )
             value = term if value is None else value + term
         total[...] = value
-        mine_ref[:, part_rows] = half(core)
-        theirs_ref[:, part_rows] = half(1 - core).astype(bf16)
+        theirs[:, columns] = half(1 - core).astype(bf16)
+        mine[:, columns] = half(core).astype(bf16)
+        for slot, (source, target) in enumerate(((theirs, theirs_ref), (mine, mine_ref))):
+            copy = pltpu.make_async_copy(source.at[:, columns], target.at[:, columns], left.at[2 * index + slot])
+            copy.start()
+            leaving.append(copy)
+    for copy in leaving:
+        copy.wait()
+
+
+def weight_grad_kernel(shards, me_ref, grad_ref, hidden_ref, *refs):
+    slots = refs[: shards - 1]
+    out_ref, own, arrived = refs[shards - 1 :]
+    share = own.shape[1]
+    source = grad_ref.at[:, pl.ds(pl.multiple_of(me_ref[0] * share, share), share)]
+    copy = pltpu.make_async_copy(source, own, arrived)
+    copy.start()
+    chunk = share // 2
+    copy.wait()
+    for start in range(0, share, chunk):
+        columns = slice(start, start + chunk)
+        total = expand(own[:, columns], hidden_ref[...])
+        for slot in slots:
+            total = total + expand(slot[:, columns], slot[:, share:])
+        out_ref[columns, :] = total
 
 
 def in_vmem(count):
@@ -324,25 +353,37 @@
 SMALL_COST = pl.CostEstimate(flops=1000, bytes_accessed=1000, transcendentals=0)
 
 
-def run_own_part(core, hidden, output_weight):
-    half = output_weight.shape[0] // 2
+def insert_kernel(chip_ref, core_ref, own_ref, theirs_ref, base_ref, out_ref, moved):
+    rows, columns = own_ref.shape
+    place = pl.ds(pl.multiple_of(jnp.bitwise_xor(chip_ref[0], 1) * rows, rows), rows)
+    copies = []
+    for index, source in enumerate((own_ref, theirs_ref)):
+        side = core_ref[0] if index == 0 else 1 - core_ref[0]
+        target = out_ref.at[place, pl.ds(pl.multiple_of(side * columns, columns), columns)]
+        copies.append(pltpu.make_async_copy(source, target, moved.at[index]))
+        copies[-1].start()
+    for copy in copies:
+        copy.wait()
+
+
+def run_insert(chip, core, own, theirs, base):
     return pl.pallas_call(
-        own_part_kernel,
-        out_shape=jax.ShapeDtypeStruct((hidden.shape[0], half), f32),
-        in_specs=[SMEM_SPEC, VMEM_SPEC, ANY_SPEC],
-        out_specs=VMEM_SPEC,
-        scratch_shapes=[pltpu.VMEM((half, hidden.shape[1]), bf16), pltpu.SemaphoreType.DMA((4,))],
+        insert_kernel,
+        out_shape=jax.ShapeDtypeStruct(base.shape, base.dtype),
+        in_specs=[SMEM_SPEC, SMEM_SPEC, VMEM_SPEC, VMEM_SPEC, ANY_SPEC],
+        out_specs=ANY_SPEC,
+        scratch_shapes=[pltpu.SemaphoreType.DMA((2,))],
+        input_output_aliases={4: 0},
         compiler_params=params(),
         cost_estimate=SMALL_COST,
-        name="own_part",
-    )(core, hidden, output_weight)
-
-
-def run_assemble(chip, core, own, theirs):
-    chips = len(own)
+        name="insert",
+    )(chip, core, own, theirs, base)
+
+
+def run_assemble(chips, steps, chip, core, own, theirs):
     rows, columns = own[0].shape
     return pl.pallas_call(
-        assemble_kernel,
+        functools.partial(assemble_kernel, steps),
         out_shape=jax.ShapeDtypeStruct((chips * rows, 2 * columns), bf16),
         in_specs=[SMEM_SPEC, SMEM_SPEC] + in_vmem(2 * len(own)),
         out_specs=VMEM_SPEC,
@@ -367,12 +408,13 @@
             jax.ShapeDtypeStruct((channels, span), f32),
             jax.ShapeDtypeStruct((3, IDS, channels), f32),
             jax.ShapeDtypeStruct((local_rows, width // 2), bf16),
+            jax.ShapeDtypeStruct((local_rows, width // 2), bf16),
         ),
         in_specs=[SMEM_SPEC, SMEM_SPEC]
         + in_vmem(shards)
         + [pl.BlockSpec((IDS, width), lambda step: (FIRST_ID // IDS, 0)), VMEM_SPEC, ANY_SPEC, VMEM_SPEC, VMEM_SPEC]
         + [ANY_SPEC],
-        out_specs=tuple(in_vmem(4)),
+        out_specs=(VMEM_SPEC, ANY_SPEC, ANY_SPEC, ANY_SPEC, ANY_SPEC),
         scratch_shapes=[
             pltpu.VMEM((IDS, width), bf16),
             pltpu.VMEM((2 * taps.shape[0] * IDS, length + LANES), bf16),
@@ -385,6 +427,12 @@
             pltpu.SemaphoreType.DMA((CHUNKS,)),
             pltpu.VMEM((width // 2, channels), bf16),
             pltpu.SemaphoreType.DMA((4,)),
+            pltpu.VMEM((width // 2, channels), bf16),
+            pltpu.SemaphoreType.DMA((4,)),
+            pltpu.VMEM((3, IDS, channels), f32),
+            pltpu.VMEM((local_rows, width // 2), bf16),
+            pltpu.VMEM((local_rows, width // 2), bf16),
+            pltpu.SemaphoreType.DMA((10,)),
         ],
         compiler_params=params(),
         cost_estimate=LARGE_COST,
@@ -418,6 +466,22 @@
     )(me, *slots, *grads, table, taps, skip_gain, mixed)
 
 
+def run_weight_grad(me, output_grad, hidden, slots):
+    shards = len(slots) + 1
+    rows, width = output_grad.shape
+    share, channels = width // shards, hidden.shape[1]
+    return pl.pallas_call(
+        functools.partial(weight_grad_kernel, shards),
+        out_shape=jax.ShapeDtypeStruct((share, channels), f32),
+        in_specs=[SMEM_SPEC, ANY_SPEC] + in_vmem(shards),
+        out_specs=VMEM_SPEC,
+        scratch_shapes=[pltpu.VMEM((rows, share), bf16), pltpu.SemaphoreType.DMA],
+        compiler_params=params(),
+        cost_estimate=SMALL_COST,
+        name="weight_grad",
+    )(me, output_grad, hidden, *slots)
+
+
 def run_hidden_grad(output_grad, output_weight):
     rows, width = output_grad.shape
     channels = output_weight.shape[1]
@@ -438,24 +502,27 @@
     )(output_grad, output_weight)
 
 
-def run_input_grad(side, core, chips, projection_grad, weight):
+def run_input_grad(core, chips, projection_grad, weight):
     _, rows, channels = projection_grad.shape
-    width = weight.shape[1] // 2
+    width = weight.shape[1]
     return pl.pallas_call(
-        functools.partial(input_grad_kernel, chips, side * width),
+        functools.partial(input_grad_kernel, chips),
         out_shape=(
             jax.ShapeDtypeStruct((rows // 2, width), bf16),
-            jax.ShapeDtypeStruct((rows // 2, width), f32),
+            jax.ShapeDtypeStruct((rows // 2, width), bf16),
         ),
         in_specs=[SMEM_SPEC, VMEM_SPEC, ANY_SPEC],
-        out_specs=(VMEM_SPEC, VMEM_SPEC),
+        out_specs=(ANY_SPEC, ANY_SPEC),
         scratch_shapes=[
-            pltpu.VMEM((3, width, channels), bf16),
-            pltpu.VMEM((rows, width // 4), f32),
-            pltpu.SemaphoreType.DMA((4,)),
+            pltpu.VMEM(weight.shape, bf16),
+            pltpu.VMEM((rows, width // CHUNKS), f32),
+            pltpu.VMEM((rows // 2, width), bf16),
+            pltpu.VMEM((rows // 2, width), bf16),
+            pltpu.SemaphoreType.DMA((CHUNKS,)),
+            pltpu.SemaphoreType.DMA((2 * CHUNKS,)),
         ],
         compiler_params=params(),
-        cost_estimate=LARGE_COST,
+        cost_estimate=SMALL_COST,
         name="input_grad",
     )(core, projection_grad, weight)
 
@@ -510,128 +577,97 @@
 
     groups = filters.shape[0]
     row_number = lax.broadcasted_iota(jnp.int32, (groups + 8, local_rows), 0)
-    packed = jnp.where(
-        row_number < groups, jnp.pad(filters, ((0, 8), (0, 0))), token_ids.astype(f32)[None, :]
-    )
+    id_row = jnp.broadcast_to(token_ids[None, :], (groups + 8, local_rows)).astype(f32)
+    packed = jnp.where(row_number < groups, jnp.pad(filters, ((0, 8), (0, 0))), id_row)
     slots = gather_ctx(packed)
     hidden_grad = run_hidden_grad(output_grad, output_weight)
     arrived, hidden_grad, me_tie = together(slots[1:], hidden_grad, me_tie)
     slots = [packed] + arrived
     grad_slots = gather_ctx(hidden_grad)
 
-    hidden, mixed, table, for_sibling = run_forward(
+    hidden, mixed, table, for_sibling, mine = run_forward(
         me_tie, core_tie, slots, embed_table, norm_gain, weight, short_weight, skip_gain, output_weight
     )
-    for_sibling, hidden, grad_slots = together(for_sibling, hidden, grad_slots)
+    for_sibling, mine, hidden, grad_slots = together(for_sibling, mine, hidden, grad_slots)
     half = width // 2
     block_rows = local_rows // chips
     received = tp_exchange(for_sibling, 1)
-    mine = run_own_part(core_tie, hidden, output_weight)
-    received, mine, me_tie, late_hidden = together(received, mine, me_tie, hidden)
     mine = mine.reshape(chips, block_rows, half)
     received = received.reshape(chips, block_rows, half)
 
-    def out_block(index):
-        return pick(mine, index) + pick(received, index).astype(f32)
-
     order = list(range(2, chips)) + [1]
-    first, second = order[: (chips - 1) // 2], order[(chips - 1) // 2 :]
     share = width // shards
-    part = share // 2
-
-    def out_sends(steps):
-        return [out_block(jnp.bitwise_xor(chip, step)).astype(bf16) for step in steps]
-
-    def ctx_pieces(steps):
-        starts = [jnp.bitwise_xor(me, step) * share + core * part for step in steps]
-        return [
-            jnp.concatenate([lax.dynamic_slice_in_dim(output_grad, start, part, axis=1), late_hidden], axis=1)
-            for start in starts
-        ]
-
-    ctx_first, ctx_second = range(1, shards // 2 + 1), range(shards // 2 + 1, shards)
-    sends, pieces, me_tie = together(out_sends(first), ctx_pieces(ctx_first), me_tie)
-    out_arrived = [tp_exchange(value, 2 * step) for step, value in zip(first, sends)]
-    ctx_arrived = [ctx_exchange(value, step) for step, value in zip(ctx_first, pieces)]
-    projection_grad = run_backward(
-        me_tie, slots, grad_slots, table, short_weight, skip_gain, mixed
-    )
-    sends, pieces = out_sends(second), ctx_pieces(ctx_second)
-    out_arrived, ctx_arrived, projection_grad, sends, pieces, core_tie = together(
-        out_arrived, ctx_arrived, projection_grad, sends, pieces, core_tie
-    )
-    out_more = [tp_exchange(value, 2 * step) for step, value in zip(second, sends)]
-    ctx_more = [ctx_exchange(value, step) for step, value in zip(ctx_second, pieces)]
-    theirs_low, mine_low = run_input_grad(0, core_tie, chips, projection_grad, weight)
-    theirs_low, mine_low, core_tie = together(theirs_low, mine_low, core_tie)
-    received_low = tp_exchange(theirs_low, 1)
-    theirs_high, mine_high = run_input_grad(1, core_tie, chips, projection_grad, weight)
-    out_more, ctx_more, received_low, theirs_high, mine_high, core_tie = together(
-        out_more, ctx_more, received_low, theirs_high, mine_high, core_tie
-    )
-    ctx_arrived = ctx_arrived + ctx_more
-
-    received_high = tp_exchange(theirs_high, 1)
+
+    def out_send(step):
+        index = jnp.bitwise_xor(chip, step)
+        return (pick(mine, index).astype(f32) + pick(received, index).astype(f32)).astype(bf16)
+
+    def ctx_piece(step):
+        start = jnp.bitwise_xor(me, step) * share
+        return jnp.concatenate([lax.dynamic_slice_in_dim(output_grad, start, share, axis=1), hidden], axis=1)
+
+    near = range(1, shards // 2 + 1)
+    ctx_arrived = [ctx_exchange(ctx_piece(step), step) for step in near]
+    sends = [out_send(step) for step in order]
+    sends, me_tie = together(sends, me_tie)
+    out_arrived = [tp_exchange(value, 2 * step) for step, value in zip(order, sends)]
+    projection_grad = run_backward(me_tie, slots, grad_slots, table, short_weight, skip_gain, mixed)
+    ctx_sends = [ctx_piece(step) for step in range(shards // 2 + 1, shards)]
+    projection_grad, core_tie, ctx_sends = together(projection_grad, core_tie, ctx_sends)
+    theirs, mine_grad = run_input_grad(core_tie, chips, projection_grad, weight)
     own_ids = lax.dynamic_slice_in_dim(token_ids, chip * block_rows, block_rows, axis=0)
     own_hot = (own_ids[:, None] == jnp.arange(FIRST_ID, FIRST_ID + IDS)[None, :]).astype(bf16)
     own_letters = lax.dynamic_slice(embed_table, (FIRST_ID, core * half), (IDS, half))
-    block = jnp.dot(own_hot, own_letters, preferred_element_type=f32) + out_block(chip)
-    for value in out_arrived + out_more:
+    own_block = jnp.dot(own_hot, own_letters, preferred_element_type=f32)
+    own_block = own_block + pick(mine, chip).astype(f32) + pick(received, chip).astype(f32)
+    out_arrived, theirs, mine_grad, own_block, ctx_arrived, ctx_sends = together(
+        out_arrived, theirs, mine_grad, own_block, ctx_arrived, ctx_sends
+    )
+
+    received_grad = tp_exchange(theirs, 1)
+    block = own_block
+    for value in out_arrived:
         block = block + value.astype(f32)
     block = block.astype(bf16)
-    block, received_high = together(block, received_high)
-    line = {step: tp_exchange(block, 2 * step) for step in order[:-1]}
-    other_line = {0: tp_exchange(block, 1)}
-    line[0] = block
+    block, received_grad = together(block, received_grad)
     split = (chips, local_rows // (2 * chips), width)
-    total = jnp.concatenate([mine_low, mine_high], axis=1).reshape(split)
-    total = total + jnp.concatenate([received_low, received_high], axis=1).reshape(split).astype(f32)
-
-    def halve(value, bit):
-        pairs = value.reshape((value.shape[0] // 2, 2) + value.shape[1:])
+    terms = [mine_grad.reshape(split), received_grad.reshape(split)]
+
+    def pairs(value, which):
+        return pick(value.reshape((value.shape[0] // 2, 2) + value.shape[1:]), which, 1)
+
+    def leaving(bit):
+        which = 1 - (chip >> bit & 1)
+        return sum(pairs(term, which).astype(f32) for term in terms).astype(bf16)
+
+    def keep(bit, arriving):
         which = chip >> bit & 1
-        return pick(pairs, which, 1), pick(pairs, 1 - which, 1).astype(bf16)
-
+        return [pairs(term, which) for term in terms] + [arriving]
+
+    line = [tp_exchange(block, 2 * step) for step in order[:-1]]
+    arriving = tp_exchange(leaving(0), 2)
+    ctx_more = [
+        ctx_exchange(value, step) for step, value in zip(range(shards // 2 + 1, shards), ctx_sends)
+    ]
+    line, arriving, ctx_more, block = together(line, arriving, ctx_more, block)
+    terms = keep(0, arriving)
     levels = chips.bit_length() - 1
-    ctx_parts = jnp.concatenate([value[:, :part] for value in ctx_arrived], axis=0)
-    for bit in range(levels):
-        kept, leaving = halve(total, bit)
+    for bit in range(1, levels):
+        outgoing = leaving(bit)
         if bit == levels - 1:
-            line[1] = tp_exchange(block, 2)
-        arriving = tp_exchange(leaving, 2 << bit)
-        if bit == 0:
-            other_parts = tp_exchange(ctx_parts, 1)
-            steps = order[:-1]
-            values = [line[step] for step in steps]
-            arriving, values, other_parts, line[0], block = together(
-                arriving, values, other_parts, line[0], block
-            )
-            line.update(zip(steps, values))
-            for step in steps:
-                other_line[step] = tp_exchange(line[step], 1)
-        total = kept + arriving.astype(f32)
-    other_line[1] = tp_exchange(line[1], 1)
-
-    own_piece = lax.dynamic_slice_in_dim(output_grad, me * share, share, axis=1)
-    own_parts = own_piece.reshape(local_rows, 2, part)
-    my_columns = jnp.concatenate([pick(own_parts, core, 1), ctx_parts], axis=0)
-    other_columns = jnp.concatenate([pick(own_parts, 1 - core, 1), other_parts], axis=0)
-    columns = jnp.where(
-        core == 0,
-        jnp.concatenate([my_columns, other_columns], axis=1),
-        jnp.concatenate([other_columns, my_columns], axis=1),
+            outgoing, block, line, ctx_more = together(outgoing, block, line, ctx_more)
+            neighbour = tp_exchange(block, 2)
+        terms = keep(bit, tp_exchange(outgoing, 2 << bit))
+
+    line = [block] + line
+    base = run_assemble(
+        chips, [0] + order[:-1], chip_tie, core_tie, line, [tp_exchange(value, 1) for value in line]
     )
-    all_hidden = jnp.concatenate([late_hidden] + [value[:, part:] for value in ctx_arrived], axis=0)
-    output_weight_grad = lax.dot_general(
-        columns, all_hidden, (((0,), (0,)), ((), ())), preferred_element_type=f32
-    )
-    block_output = run_assemble(
-        chip_tie,
-        core_tie,
-        [line[step] for step in range(chips)],
-        [other_line[step] for step in range(chips)],
-    )
-    normed_grad = total.reshape(local_rows // (2 * chips), width)
+    output_weight_grad = run_weight_grad(me_tie, output_grad, hidden, ctx_arrived + ctx_more)
+    kept = sum(term.astype(f32) for term in terms[:-1])
+    base, output_weight_grad, neighbour, kept = together(base, output_weight_grad, neighbour, kept)
+    block_output = run_insert(chip_tie, core_tie, neighbour, tp_exchange(neighbour, 1), base)
+    normed_grad = (kept + terms[-1].astype(f32)).reshape(local_rows // (2 * chips), width)
     return (block_output, output_weight_grad, jnp.transpose(projection_grad, (1, 0, 2)), normed_grad)
 
 

time: 160 us -> 153 us (0.956)
  local copies, waits for them, and re-layouts: 18.3 us -> 4.21 us
  starting transfers between devices: 27.1 us -> 33.8 us
  matrix products: 6.07 us -> 1.38 us
  waiting for transfers between devices: 37.7 us -> 41.4 us
    ppermute x9, waiting for transfers between devices: 3.93 us -> 13.1 us  [ctx_exchange(): return lax.ppermute(value, 'ctx', [(i, i ^ step) for i in range(count)])]
    dynamic_slice x5 -> x1, local copies, waits for them, and re-layouts: 9.27 us -> 0.26 us  [ctx_piece(): lax.dynamic_slice_in_dim(output_grad, start, share, axis=1)]
    ppermute x16 -> x14, starting transfers between devices: 14.4 us -> 21.7 us  [tp_exchange(): return lax.ppermute(value, 'tp', [(i, i ^ mask) for i in range(count)])]
    ppermute x16 -> x14, waiting for transfers between devices: 33.8 us -> 28.2 us  [tp_exchange(): return lax.ppermute(value, 'tp', [(i, i ^ mask) for i in range(count)])]
    dot_general x2 -> x1, matrix products: 6.07 us -> 1.38 us  [body(): own_block = jnp.dot(own_hot, own_letters, preferred_element_type=f32)]
    convert_element_type x2 -> x3, other arithmetic: 1.9 us -> 4.52 us  [the longest x1 2.51 us: out_send(): (pick(mine, index).astype(f32) + pick(received, index).astype(f32)).astyp...]
    unnamed x59 -> x32, local copies, waits for them, and re-layouts: 5.41 us -> 3.19 us
    pallas_call x1, Pallas kernels: 17.5 us -> 19.6 us  [run_forward(): pl.pallas_call(functools.partial(forward_kernel, shards), grid=(1,), out_...]
  transfers between devices with their start and end apart: 25 -> 23, of which waited for: 11 -> 8; matrix products, arithmetic and copies ran while one was open for 17% -> 6% of each run, Pallas kernels for 35% -> 38%
where the time goes in v3:
time: 153 us; the launch traced here: 152 us
  Pallas kernels  59.7 us (39%)
  waiting for transfers between devices  41.4 us (27%)
  starting transfers between devices  33.8 us (22%)
  other arithmetic  10.3 us (7%)
  local copies, waits for them, and re-layouts  4.21 us (3%)
    ppermute x14, waiting for transfers between devices, tp_exchange(): return lax.ppermute(value, 'tp', [(i, i ^ mask) for i in range(count)])  28.2 us
    ppermute x14, starting transfers between devices, tp_exchange(): return lax.ppermute(value, 'tp', [(i, i ^ mask) for i in range(count)])  21.7 us
    pallas_call x1, Pallas kernels, run_forward(): pl.pallas_call(functools.partial(forward_kernel, shards), grid=(1,), out_...  19.6 us
    ppermute x9, waiting for transfers between devices, ctx_exchange(): return lax.ppermute(value, 'ctx', [(i, i ^ step) for i in range(count)])  13.1 us
    pallas_call x1, Pallas kernels, run_backward(): pl.pallas_call(functools.partial(backward_kernel, shards), out_shape=jax....  13 us
    ppermute x9, starting transfers between devices, ctx_exchange(): return lax.ppermute(value, 'ctx', [(i, i ^ step) for i in range(count)])  12.1 us
    pallas_call x1, Pallas kernels, run_input_grad(): pl.pallas_call(functools.partial(input_grad_kernel, chips), out_shape=(ja...  10.4 us
    pallas_call x1, Pallas kernels, run_weight_grad(): pl.pallas_call(functools.partial(weight_grad_kernel, shards), out_shape=j...  6.91 us
  transfers between devices with their start and end apart: 23, of which 8 were waited for; matrix products, arithmetic and copies ran while one was open for 6% of the time, Pallas kernels for 38%

profile of v3, /device:TPU:0, one launch (start us, length us, event | category | flops | bytes accessed | tf_op | source)
XLA Modules:
  0.0 151.9 jit_solution(17810160128260748216)
XLA Ops:
  0.6 0.7 convert_element_type.153
  1.3 0.9 pad_select_fusion.refs_0_
  2.2 4.0 %collective-permute-start.2 = (f32[40,384]{1,0:T(8,128)S(1)}, f32[40,384]{1,0:T(8,128)S(1)}, u32[]{:S(2)}, u32[]{:S(2)}) collective-permute-start(f32[40,384]{1,0:T(8,128)S(1)} %pad_select_fusion.refs_0_), channel_id=1, source_target_pairs={{0,24},{8,16},{16,8},{24,0},{1,25},{9,17},{17,9},{25,1},{2,26},{10... | collective-permute-start | bytes 184328 | tf_op jit(solution)/shard_map/ppermute | solution.py:532
  6.2 0.5 collective-permute-start.1
  6.7 0.1 collective-permute-start
  6.8 4.4 %hidden_grad.1.refs_4_ = bf16[512,384]{1,0:T(8,128)(2,1)} custom-call(bf16[384,4096]{1,0:T(8,128)(2,1)} %grad_ref.3, bf16[4096,512]{1,0:T(8,128)(2,1)} %refs_9_.2), custom_call_target="tpu_custom_call" | custom-call | flops 1000 | bytes 1000 | tf_op jit(solution)/shard_map/hidden_grad/pallas_call | solution.py:488
  11.3 0.0 collective-permute-done.2.refs_3_
  11.3 0.0 collective-permute-done.refs_1_
  11.3 2.9 %collective-permute-start.5 = (bf16[512,384]{1,0:T(8,128)(2,1)}, bf16[512,384]{1,0:T(8,128)(2,1)S(1)}, u32[]{:S(2)}, u32[]{:S(2)}) collective-permute-start(bf16[512,384]{1,0:T(8,128)(2,1)} %hidden_grad.1.refs_4_), channel_id=1, source_target_pairs={{0,24},{8,16},{16,8},{24,0},{1,25},{9,17},{17,9},{25,1},{2,26},{10... | collective-permute-start | bytes 1179656 | tf_op jit(solution)/shard_map/ppermute | solution.py:532
  14.2 0.5 collective-permute-start.4
  14.8 0.1 collective-permute-start.3
  14.9 19.6 %forward_conv.1 = (bf16[384,512]{1,0:T(8,128)(2,1)}, f32[512,512]{1,0:T(8,128)}, f32[3,32,512]{2,1,0:T(8,128)}, bf16[384,2048]{1,0:T(8,128)(2,1)}, bf16[384,2048]{1,0:T(8,128)(2,1)}) custom-call(s32[1]{0:T(128)} %bitcast.1.me_ref, s32[1]{0:T(128)} %bitcast.2.core_ref, f32[40,384]{1,0:T(8,128)} %copy-done.11, f32[40,384]{1,0:T(8,128)} %copy-done.15, ...), custom_call_target="tpu_custom_call" | custom-call | flops 20000000000 | bytes 10000000 | tf_op jit(solution)/shard_map/forward_conv/pallas_call | solution.py:403
  34.5 0.0 collective-permute-done.5.refs_7_
  34.5 0.0 collective-permute-done.3.refs_5_
  34.5 0.1 collective-permute-start.6
  34.7 0.8 dynamic_slice.71
  35.4 0.3 constant_dynamic-slice_fusion
  35.7 0.7 copy-done.1
  36.4 1.3 pad_maximum_fusion
  37.8 1.9 %collective-permute-start.11 = (bf16[384,1536]{1,0:T(8,128)(2,1)S(1)}, bf16[384,1536]{1,0:T(8,128)(2,1)}, u32[]{:S(2)}, u32[]{:S(2)}) collective-permute-start(bf16[384,1536]{1,0:T(8,128)(2,1)S(1)} %get-tuple-element.114), channel_id=1, source_target_pairs={{0,16},{8,24},{16,0},{24,8},{1,17},{9,25},{17,1},{25,9},{2,18},{10... | collective-permute-start | bytes 3538952 | tf_op jit(solution)/shard_map/ppermute | solution.py:532
  39.7 1.6 %collective-permute-start.10 = (bf16[384,1536]{1,0:T(8,128)(2,1)S(1)}, bf16[384,1536]{1,0:T(8,128)(2,1)}, u32[]{:S(2)}, u32[]{:S(2)}) collective-permute-start(bf16[384,1536]{1,0:T(8,128)(2,1)S(1)} %get-tuple-element.115), channel_id=1, source_target_pairs={{0,8},{8,0},{16,24},{24,16},{1,9},{9,1},{17,25},{25,17},{2,10},{10... | collective-permute-start | bytes 3538952 | tf_op jit(solution)/shard_map/ppermute | solution.py:532
  41.3 0.0 collective-permute-done.6
  41.3 2.5 %fusion.4 = (bf16[96,2048]{1,0:T(8,128)(2,1)S(1)}, bf16[96,2048]{1,0:T(8,128)(2,1)S(1)}, bf16[96,2048]{1,0:T(8,128)(2,1)}) fusion(bf16[4,96,2048]{2,1,0:T(8,128)(2,1)} %bitcast.5, s32[]{:T(128)S(6)} %select_n.78, bf16[4,96,2048]{2,1,0:T(8,128)(2,1)S(1)} %bitcast.37, s32[]{:T(128)S(6)} %select_n.77, s32[]{:T(128)S(6)} %select_n.76), kind=kLoop, calls=%fused_computation.17 | loop fusion | flops 2359296 | bytes 3538956 | tf_op jit(solution)/shard_map/convert_element_type | solution.py:603
  43.8 2.6 %collective-permute-start.7 = (bf16[96,2048]{1,0:T(8,128)(2,1)}, bf16[96,2048]{1,0:T(8,128)(2,1)S(1)}, u32[]{:S(2)}, u32[]{:S(2)}) collective-permute-start(bf16[96,2048]{1,0:T(8,128)(2,1)} %get-tuple-element.74), channel_id=1, source_target_pairs={{0,4},{1,5},{2,6},{3,7},{4,0},{5,1},{6,2},{7,3},{8,12},{9,13},{10,... | collective-permute-start | bytes 1179656 | tf_op jit(solution)/shard_map/ppermute | solution.py:541
  46.4 1.3 collective-permute-start.8
  47.7 0.2 collective-permute-start.9
  48.0 13.0 %backward_conv.1.grad_ref = bf16[3,384,512]{2,1,0:T(8,128)(2,1)} custom-call(s32[1]{0:T(128)} %bitcast.1.me_ref, f32[40,384]{1,0:T(8,128)} %copy-done.11, f32[40,384]{1,0:T(8,128)} %copy-done.15, f32[40,384]{1,0:T(8,128)} %copy-done.14, f32[40,384]{1,0:T(8,128)} %copy-done.13, bf16[512,384]{1,0:T(8,128)(2,1)} %hidden_grad.1.refs_4_, ...), custom_call_target="tpu_custom_call" | custom-call | flops 20000000000 | bytes 10000000 | tf_op jit(solution)/shard_map/backward_conv/pallas_call | solution.py:450
  61.0 10.4 %input_grad.1 = (bf16[192,4096]{1,0:T(8,128)(2,1)}, bf16[192,4096]{1,0:T(8,128)(2,1)}) custom-call(s32[1]{0:T(128)} %bitcast.2.core_ref, bf16[3,384,512]{2,1,0:T(8,128)(2,1)} %backward_conv.1.grad_ref, bf16[3,4096,512]{2,1,0:T(8,128)(2,1)} %bitcast.34), custom_call_target="tpu_custom_call" | custom-call | flops 1000 | bytes 1000 | tf_op jit(solution)/shard_map/input_grad/pallas_call | solution.py:508
  71.4 1.4 convert_add_fusion
  72.8 0.0 copy-start.2
  72.8 0.0 collective-permute-done.10.refs_0_
  72.8 1.0 collective-permute-done.7
  73.8 0.0 collective-permute-done.8
  73.8 0.0 collective-permute-done.9
  73.8 0.1 collective-permute-start.12
  73.9 0.7 copy-done.5
  74.6 0.5 collective-permute-start.16
  75.0 1.2 add_convert_fusion.1.refs_0_
  76.2 1.4 collective-permute-done.12
  77.6 1.3 fusion
  78.9 8.0 %collective-permute-start.15 = (bf16[2,48,4096]{2,1,0:T(8,128)(2,1)S(1)}, bf16[2,48,4096]{2,1,0:T(8,128)(2,1)S(1)}, u32[]{:S(2)}, u32[]{:S(2)}) collective-permute-start(bf16[2,48,4096]{2,1,0:T(8,128)(2,1)S(1)} %fusion), channel_id=1, source_target_pairs={{0,2},{1,3},{2,0},{3,1},{4,6},{5,7},{6,4},{7,5},{8,10},{9,11},{10,... | collective-permute-start | bytes 2359304 | tf_op jit(solution)/shard_map/ppermute | solution.py:541
  87.0 3.4 %collective-permute-start.14 = (bf16[96,2048]{1,0:T(8,128)(2,1)S(1)}, bf16[96,2048]{1,0:T(8,128)(2,1)}, u32[]{:S(2)}, u32[]{:S(2)}) collective-permute-start(bf16[96,2048]{1,0:T(8,128)(2,1)S(1)} %add_convert_fusion.1.refs_0_), channel_id=1, source_target_pairs={{0,6},{1,7},{2,4},{3,5},{4,2},{5,3},{6,0},{7,1},{8,14},{9,15},{10,... | collective-permute-start | bytes 1179656 | tf_op jit(solution)/shard_map/ppermute | solution.py:541
  90.3 0.0 collective-permute-start.13
  90.3 13.1 %collective-permute-done.16.refs_2_ = bf16[384,1536]{1,0:T(8,128)(2,1)} collective-permute-done((bf16[384,1536]{1,0:T(8,128)(2,1)}, bf16[384,1536]{1,0:T(8,128)(2,1)}, u32[]{:S(2)}, u32[]{:S(2)}) %collective-permute-start.16) | collective-permute-done | bytes 1179680 | tf_op jit(solution)/shard_map/ppermute | solution.py:532
  103.5 13.8 %collective-permute-done.14.refs_2_ = bf16[96,2048]{1,0:T(8,128)(2,1)} collective-permute-done((bf16[96,2048]{1,0:T(8,128)(2,1)S(1)}, bf16[96,2048]{1,0:T(8,128)(2,1)}, u32[]{:S(2)}, u32[]{:S(2)}) %collective-permute-start.14) | collective-permute-done | bytes 393248 | tf_op jit(solution)/shard_map/ppermute | solution.py:541
  117.2 3.7 %collective-permute-done.13.refs_1_ = bf16[96,2048]{1,0:T(8,128)(2,1)} collective-permute-done((bf16[96,2048]{1,0:T(8,128)(2,1)S(1)}, bf16[96,2048]{1,0:T(8,128)(2,1)}, u32[]{:S(2)}, u32[]{:S(2)}) %collective-permute-start.13) | collective-permute-done | bytes 393248 | tf_op jit(solution)/shard_map/ppermute | solution.py:541
  121.0 0.7 collective-permute-done.15
  121.7 1.4 bitcast_add_fusion
  123.0 0.1 collective-permute-start.18
  123.1 0.5 collective-permute-start.19
  123.6 0.1 collective-permute-start.17
  123.7 3.8 %collective-permute-start.20 = (bf16[96,2048]{1,0:T(8,128)(2,1)S(1)}, bf16[96,2048]{1,0:T(8,128)(2,1)S(1)}, u32[]{:S(2)}, u32[]{:S(2)}) collective-permute-start(bf16[96,2048]{1,0:T(8,128)(2,1)S(1)} %add_convert_fusion.1.refs_0_), channel_id=1, source_target_pairs={{0,2},{1,3},{2,0},{3,1},{4,6},{5,7},{6,4},{7,5},{8,10},{9,11},{10,... | collective-permute-start | bytes 1179656 | tf_op jit(solution)/shard_map/ppermute | solution.py:541
  127.5 1.6 %collective-permute-start.22 = (bf16[1,48,4096]{2,1,0:T(8,128)(2,1)S(1)}, bf16[1,48,4096]{2,1,0:T(8,128)(2,1)S(1)}, u32[]{:S(2)}, u32[]{:S(2)}) collective-permute-start(bf16[1,48,4096]{2,1,0:T(8,128)(2,1)S(1)} %get-tuple-element.105), channel_id=1, source_target_pairs={{0,4},{1,5},{2,6},{3,7},{4,0},{5,1},{6,2},{7,3},{8,12},{9,13},{10,... | collective-permute-start | bytes 1179656 | tf_op jit(solution)/shard_map/ppermute | solution.py:541
  129.1 6.9 %weight_grad.1 = f32[1024,512]{1,0:T(8,128)} custom-call(s32[1]{0:T(128)} %bitcast.1.me_ref, bf16[384,4096]{1,0:T(8,128)(2,1)} %grad_ref.3, bf16[384,512]{1,0:T(8,128)(2,1)} %get-tuple-element.72.hidden_ref, bf16[384,1536]{1,0:T(8,128)(2,1)} %collective-permute-done.10.refs_0_, bf16[384,1536]{1,0:T(8,128)(2,1)} %collective-permute-done.11.refs_1_, ...), custom_call_target="tpu_custom_call" | custom-call | flops 1000 | bytes 1000 | tf_op jit(solution)/shard_map/weight_grad/pallas_call | solution.py:473
  136.0 0.0 copy-start.8
  136.0 0.7 copy-done.6
  136.7 0.2 copy-done.7
  136.9 0.1 copy-done.8
  137.0 3.4 %assemble.1.base_ref = bf16[384,4096]{1,0:T(8,128)(2,1)} custom-call(s32[1]{0:T(128)} %bitcast.chip_ref, s32[1]{0:T(128)} %bitcast.2.core_ref, bf16[96,2048]{1,0:T(8,128)(2,1)} %copy-done.3, bf16[96,2048]{1,0:T(8,128)(2,1)} %collective-permute-done.13.refs_1_, bf16[96,2048]{1,0:T(8,128)(2,1)} %collective-permute-done.14.refs_2_, bf16[96,2048]{1,0:T(8,128)(2,1)} %copy-done.8, ...), custom_call_target="tpu_custom_call" | custom-call | flops 1000 | bytes 1000 | tf_op jit(solution)/shard_map/assemble/pallas_call | solution.py:385
  140.4 3.9 %collective-permute-done.20.own_ref = bf16[96,2048]{1,0:T(8,128)(2,1)S(1)} collective-permute-done((bf16[96,2048]{1,0:T(8,128)(2,1)S(1)}, bf16[96,2048]{1,0:T(8,128)(2,1)S(1)}, u32[]{:S(2)}, u32[]{:S(2)}) %collective-permute-start.20) | collective-permute-done | bytes 393248 | tf_op jit(solution)/shard_map/ppermute | solution.py:541
  144.3 3.7 %collective-permute-done.22 = bf16[1,48,4096]{2,1,0:T(8,128)(2,1)S(1)} collective-permute-done((bf16[1,48,4096]{2,1,0:T(8,128)(2,1)S(1)}, bf16[1,48,4096]{2,1,0:T(8,128)(2,1)S(1)}, u32[]{:S(2)}, u32[]{:S(2)}) %collective-permute-start.22) | collective-permute-done | bytes 393248 | tf_op jit(solution)/shard_map/ppermute | solution.py:541
  148.0 0.9 add_bitcast_fusion
  149.0 0.8 copy-done.10
  149.8 2.0 %insert.1 = bf16[384,4096]{1,0:T(8,128)(2,1)} custom-call(s32[1]{0:T(128)} %bitcast.chip_ref, s32[1]{0:T(128)} %bitcast.2.core_ref, bf16[96,2048]{1,0:T(8,128)(2,1)} %copy-done.9, bf16[96,2048]{1,0:T(8,128)(2,1)} %copy-done.10, bf16[384,4096]{1,0:T(8,128)(2,1)} %assemble.1.base_ref), custom_call_target="tpu_custom_call", output_to_operand_aliasing={{}: (4, {})} | custom-call | flops 1000 | bytes 1000 | tf_op jit(solution)/shard_map/insert/pallas_call | solution.py:370
  (34 shorter events, 0.1 us)
Async XLA Ops:
  2.2 9.0 %copy-start.11 = (f32[40,384]{1,0:T(8,128)}, f32[40,384]{1,0:T(8,128)S(1)}, u32[]{:S(2)}) copy-start(f32[40,384]{1,0:T(8,128)S(1)} %pad_select_fusion.refs_0_) | copy-start | bytes 184324
  2.2 9.1 %collective-permute-start.2 = (f32[40,384]{1,0:T(8,128)S(1)}, f32[40,384]{1,0:T(8,128)S(1)}, u32[]{:S(2)}, u32[]{:S(2)}) collective-permute-start(f32[40,384]{1,0:T(8,128)S(1)} %pad_select_fusion.refs_0_), channel_id=1, source_target_pairs={{0,24},{8,16},{16,8},{24,0},{1,25},{9,17},{17,9},{25,1},{2,26},{10... | collective-permute-start | bytes 184328 | tf_op jit(solution)/shard_map/ppermute | solution.py:532
  6.2 5.1 %collective-permute-start.1 = (f32[40,384]{1,0:T(8,128)S(1)}, f32[40,384]{1,0:T(8,128)S(1)}, u32[]{:S(2)}, u32[]{:S(2)}) collective-permute-start(f32[40,384]{1,0:T(8,128)S(1)} %pad_select_fusion.refs_0_), channel_id=1, source_target_pairs={{0,16},{8,24},{16,0},{24,8},{1,17},{9,25},{17,1},{25,9},{2,18},{10... | collective-permute-start | bytes 184328 | tf_op jit(solution)/shard_map/ppermute | solution.py:532
  6.7 4.7 %collective-permute-start = (f32[40,384]{1,0:T(8,128)S(1)}, f32[40,384]{1,0:T(8,128)S(1)}, u32[]{:S(2)}, u32[]{:S(2)}) collective-permute-start(f32[40,384]{1,0:T(8,128)S(1)} %pad_select_fusion.refs_0_), channel_id=1, source_target_pairs={{0,8},{8,0},{16,24},{24,16},{1,9},{9,1},{17,25},{25,17},{2,10},{10... | collective-permute-start | bytes 184328 | tf_op jit(solution)/shard_map/ppermute | solution.py:532
  11.3 3.6 %copy-start.13 = (f32[40,384]{1,0:T(8,128)}, f32[40,384]{1,0:T(8,128)S(1)}, u32[]{:S(2)}) copy-start(f32[40,384]{1,0:T(8,128)S(1)} %collective-permute-done.2.refs_3_) | copy-start | bytes 184324
  11.3 3.6 %copy-start.14 = (f32[40,384]{1,0:T(8,128)}, f32[40,384]{1,0:T(8,128)S(1)}, u32[]{:S(2)}) copy-start(f32[40,384]{1,0:T(8,128)S(1)} %collective-permute-done.1.refs_2_) | copy-start | bytes 184324
  11.3 3.6 %copy-start.15 = (f32[40,384]{1,0:T(8,128)}, f32[40,384]{1,0:T(8,128)S(1)}, u32[]{:S(2)}) copy-start(f32[40,384]{1,0:T(8,128)S(1)} %collective-permute-done.refs_1_) | copy-start | bytes 184324
  11.3 23.2 %collective-permute-start.5 = (bf16[512,384]{1,0:T(8,128)(2,1)}, bf16[512,384]{1,0:T(8,128)(2,1)S(1)}, u32[]{:S(2)}, u32[]{:S(2)}) collective-permute-start(bf16[512,384]{1,0:T(8,128)(2,1)} %hidden_grad.1.refs_4_), channel_id=1, source_target_pairs={{0,24},{8,16},{16,8},{24,0},{1,25},{9,17},{17,9},{25,1},{2,26},{10... | collective-permute-start | bytes 1179656 | tf_op jit(solution)/shard_map/ppermute | solution.py:532
  14.2 20.3 %collective-permute-start.4 = (bf16[512,384]{1,0:T(8,128)(2,1)}, bf16[512,384]{1,0:T(8,128)(2,1)}, u32[]{:S(2)}, u32[]{:S(2)}) collective-permute-start(bf16[512,384]{1,0:T(8,128)(2,1)} %hidden_grad.1.refs_4_), channel_id=1, source_target_pairs={{0,16},{8,24},{16,0},{24,8},{1,17},{9,25},{17,1},{25,9},{2,18},{10... | collective-permute-start | bytes 1179656 | tf_op jit(solution)/shard_map/ppermute | solution.py:532
  14.8 19.8 %collective-permute-start.3 = (bf16[512,384]{1,0:T(8,128)(2,1)}, bf16[512,384]{1,0:T(8,128)(2,1)}, u32[]{:S(2)}, u32[]{:S(2)}) collective-permute-start(bf16[512,384]{1,0:T(8,128)(2,1)} %hidden_grad.1.refs_4_), channel_id=1, source_target_pairs={{0,8},{8,0},{16,24},{24,16},{1,9},{9,1},{17,25},{25,17},{2,10},{10... | collective-permute-start | bytes 1179656 | tf_op jit(solution)/shard_map/ppermute | solution.py:532
  14.9 20.5 %copy-start = (bf16[384,4096]{1,0:T(8,128)(2,1)S(1)}, bf16[384,4096]{1,0:T(8,128)(2,1)}, u32[]{:S(2)}) copy-start(bf16[384,4096]{1,0:T(8,128)(2,1)} %grad_ref.3) | copy-start | bytes 9437188
  34.5 1.2 copy-start.12
  34.5 6.7 %collective-permute-start.6 = (bf16[384,2048]{1,0:T(8,128)(2,1)}, bf16[384,2048]{1,0:T(8,128)(2,1)}, u32[]{:S(2)}, u32[]{:S(2)}) collective-permute-start(bf16[384,2048]{1,0:T(8,128)(2,1)} %get-tuple-element.64), channel_id=1, source_target_pairs={{0,1},{1,0},{2,3},{3,2},{4,5},{5,4},{6,7},{7,6},{8,9},{9,8},{10,11... | collective-permute-start | bytes 4718600 | tf_op jit(solution)/shard_map/ppermute | solution.py:541
  35.4 1.0 copy-start.1
  36.4 4.8 %copy-start.4 = (bf16[384,2048]{1,0:T(8,128)(2,1)S(1)}, bf16[384,2048]{1,0:T(8,128)(2,1)}, u32[]{:S(2)}) copy-start(bf16[384,2048]{1,0:T(8,128)(2,1)} %get-tuple-element.63) | copy-start | bytes 4718596
  37.8 35.0 %collective-permute-start.11 = (bf16[384,1536]{1,0:T(8,128)(2,1)S(1)}, bf16[384,1536]{1,0:T(8,128)(2,1)}, u32[]{:S(2)}, u32[]{:S(2)}) collective-permute-start(bf16[384,1536]{1,0:T(8,128)(2,1)S(1)} %get-tuple-element.114), channel_id=1, source_target_pairs={{0,16},{8,24},{16,0},{24,8},{1,17},{9,25},{17,1},{25,9},{2,18},{10... | collective-permute-start | bytes 3538952 | tf_op jit(solution)/shard_map/ppermute | solution.py:532
  39.7 33.1 %collective-permute-start.10 = (bf16[384,1536]{1,0:T(8,128)(2,1)S(1)}, bf16[384,1536]{1,0:T(8,128)(2,1)}, u32[]{:S(2)}, u32[]{:S(2)}) collective-permute-start(bf16[384,1536]{1,0:T(8,128)(2,1)S(1)} %get-tuple-element.115), channel_id=1, source_target_pairs={{0,8},{8,0},{16,24},{24,16},{1,9},{9,1},{17,25},{25,17},{2,10},{10... | collective-permute-start | bytes 3538952 | tf_op jit(solution)/shard_map/ppermute | solution.py:532
  43.8 30.0 %collective-permute-start.7 = (bf16[96,2048]{1,0:T(8,128)(2,1)}, bf16[96,2048]{1,0:T(8,128)(2,1)S(1)}, u32[]{:S(2)}, u32[]{:S(2)}) collective-permute-start(bf16[96,2048]{1,0:T(8,128)(2,1)} %get-tuple-element.74), channel_id=1, source_target_pairs={{0,4},{1,5},{2,6},{3,7},{4,0},{5,1},{6,2},{7,3},{8,12},{9,13},{10,... | collective-permute-start | bytes 1179656 | tf_op jit(solution)/shard_map/ppermute | solution.py:541
  46.4 27.4 %collective-permute-start.8 = (bf16[96,2048]{1,0:T(8,128)(2,1)S(1)}, bf16[96,2048]{1,0:T(8,128)(2,1)S(1)}, u32[]{:S(2)}, u32[]{:S(2)}) collective-permute-start(bf16[96,2048]{1,0:T(8,128)(2,1)S(1)} %get-tuple-element.75), channel_id=1, source_target_pairs={{0,6},{1,7},{2,4},{3,5},{4,2},{5,3},{6,0},{7,1},{8,14},{9,15},{10,... | collective-permute-start | bytes 1179656 | tf_op jit(solution)/shard_map/ppermute | solution.py:541
  47.7 26.1 %collective-permute-start.9 = (bf16[96,2048]{1,0:T(8,128)(2,1)S(1)}, bf16[96,2048]{1,0:T(8,128)(2,1)S(1)}, u32[]{:S(2)}, u32[]{:S(2)}) collective-permute-start(bf16[96,2048]{1,0:T(8,128)(2,1)S(1)} %get-tuple-element.76), channel_id=1, source_target_pairs={{0,2},{1,3},{2,0},{3,1},{4,6},{5,7},{6,4},{7,5},{8,10},{9,11},{10,... | collective-permute-start | bytes 1179656 | tf_op jit(solution)/shard_map/ppermute | solution.py:541
  72.8 4.9 %copy-start.2 = (bf16[192,4096]{1,0:T(8,128)(2,1)S(1)}, bf16[192,4096]{1,0:T(8,128)(2,1)}, u32[]{:S(2)}) copy-start(bf16[192,4096]{1,0:T(8,128)(2,1)} %get-tuple-element.81) | copy-start | bytes 4718596
  73.8 0.8 copy-start.5
  73.8 3.8 %collective-permute-start.12 = (bf16[192,4096]{1,0:T(8,128)(2,1)}, bf16[192,4096]{1,0:T(8,128)(2,1)}, u32[]{:S(2)}, u32[]{:S(2)}) collective-permute-start(bf16[192,4096]{1,0:T(8,128)(2,1)} %get-tuple-element.86), channel_id=1, source_target_pairs={{0,1},{1,0},{2,3},{3,2},{4,5},{5,4},{6,7},{7,6},{8,9},{9,8},{10,11... | collective-permute-start | bytes 4718600 | tf_op jit(solution)/shard_map/ppermute | solution.py:541
  74.6 28.9 %collective-permute-start.16 = (bf16[384,1536]{1,0:T(8,128)(2,1)}, bf16[384,1536]{1,0:T(8,128)(2,1)}, u32[]{:S(2)}, u32[]{:S(2)}) collective-permute-start(bf16[384,1536]{1,0:T(8,128)(2,1)} %get-tuple-element.89), channel_id=1, source_target_pairs={{0,24},{8,16},{16,8},{24,0},{1,25},{9,17},{17,9},{25,1},{2,26},{10... | collective-permute-start | bytes 3538952 | tf_op jit(solution)/shard_map/ppermute | solution.py:532
  76.2 47.5 %copy-start.3 = (bf16[96,2048]{1,0:T(8,128)(2,1)}, bf16[96,2048]{1,0:T(8,128)(2,1)S(1)}, u32[]{:S(2)}) copy-start(bf16[96,2048]{1,0:T(8,128)(2,1)S(1)} %add_convert_fusion.1.refs_0_) | copy-start | bytes 1179652
  78.9 42.7 %collective-permute-start.15 = (bf16[2,48,4096]{2,1,0:T(8,128)(2,1)S(1)}, bf16[2,48,4096]{2,1,0:T(8,128)(2,1)S(1)}, u32[]{:S(2)}, u32[]{:S(2)}) collective-permute-start(bf16[2,48,4096]{2,1,0:T(8,128)(2,1)S(1)} %fusion), channel_id=1, source_target_pairs={{0,2},{1,3},{2,0},{3,1},{4,6},{5,7},{6,4},{7,5},{8,10},{9,11},{10,... | collective-permute-start | bytes 2359304 | tf_op jit(solution)/shard_map/ppermute | solution.py:541
  87.0 30.3 %collective-permute-start.14 = (bf16[96,2048]{1,0:T(8,128)(2,1)S(1)}, bf16[96,2048]{1,0:T(8,128)(2,1)}, u32[]{:S(2)}, u32[]{:S(2)}) collective-permute-start(bf16[96,2048]{1,0:T(8,128)(2,1)S(1)} %add_convert_fusion.1.refs_0_), channel_id=1, source_target_pairs={{0,6},{1,7},{2,4},{3,5},{4,2},{5,3},{6,0},{7,1},{8,14},{9,15},{10,... | collective-permute-start | bytes 1179656 | tf_op jit(solution)/shard_map/ppermute | solution.py:541
  90.3 30.6 %collective-permute-start.13 = (bf16[96,2048]{1,0:T(8,128)(2,1)S(1)}, bf16[96,2048]{1,0:T(8,128)(2,1)}, u32[]{:S(2)}, u32[]{:S(2)}) collective-permute-start(bf16[96,2048]{1,0:T(8,128)(2,1)S(1)} %add_convert_fusion.1.refs_0_), channel_id=1, source_target_pairs={{0,4},{1,5},{2,6},{3,7},{4,0},{5,1},{6,2},{7,3},{8,12},{9,13},{10,... | collective-permute-start | bytes 1179656 | tf_op jit(solution)/shard_map/ppermute | solution.py:541
  123.0 12.9 %collective-permute-start.18 = (bf16[96,2048]{1,0:T(8,128)(2,1)}, bf16[96,2048]{1,0:T(8,128)(2,1)S(1)}, u32[]{:S(2)}, u32[]{:S(2)}) collective-permute-start(bf16[96,2048]{1,0:T(8,128)(2,1)} %collective-permute-done.13.refs_1_), channel_id=1, source_target_pairs={{0,1},{1,0},{2,3},{3,2},{4,5},{5,4},{6,7},{7,6},{8,9},{9,8},{10,11... | collective-permute-start | bytes 1179656 | tf_op jit(solution)/shard_map/ppermute | solution.py:541
  123.1 12.9 %collective-permute-start.19 = (bf16[96,2048]{1,0:T(8,128)(2,1)}, bf16[96,2048]{1,0:T(8,128)(2,1)S(1)}, u32[]{:S(2)}, u32[]{:S(2)}) collective-permute-start(bf16[96,2048]{1,0:T(8,128)(2,1)} %collective-permute-done.14.refs_2_), channel_id=1, source_target_pairs={{0,1},{1,0},{2,3},{3,2},{4,5},{5,4},{6,7},{7,6},{8,9},{9,8},{10,11... | collective-permute-start | bytes 1179656 | tf_op jit(solution)/shard_map/ppermute | solution.py:541
  123.6 12.4 %collective-permute-start.17 = (bf16[96,2048]{1,0:T(8,128)(2,1)S(1)}, bf16[96,2048]{1,0:T(8,128)(2,1)S(1)}, u32[]{:S(2)}, u32[]{:S(2)}) collective-permute-start(bf16[96,2048]{1,0:T(8,128)(2,1)S(1)} %add_convert_fusion.1.refs_0_), channel_id=1, source_target_pairs={{0,1},{1,0},{2,3},{3,2},{4,5},{5,4},{6,7},{7,6},{8,9},{9,8},{10,11... | collective-permute-start | bytes 1179656 | tf_op jit(solution)/shard_map/ppermute | solution.py:541
  123.7 20.6 %collective-permute-start.20 = (bf16[96,2048]{1,0:T(8,128)(2,1)S(1)}, bf16[96,2048]{1,0:T(8,128)(2,1)S(1)}, u32[]{:S(2)}, u32[]{:S(2)}) collective-permute-start(bf16[96,2048]{1,0:T(8,128)(2,1)S(1)} %add_convert_fusion.1.refs_0_), channel_id=1, source_target_pairs={{0,2},{1,3},{2,0},{3,1},{4,6},{5,7},{6,4},{7,5},{8,10},{9,11},{10,... | collective-permute-start | bytes 1179656 | tf_op jit(solution)/shard_map/ppermute | solution.py:541
  127.5 20.6 %collective-permute-start.22 = (bf16[1,48,4096]{2,1,0:T(8,128)(2,1)S(1)}, bf16[1,48,4096]{2,1,0:T(8,128)(2,1)S(1)}, u32[]{:S(2)}, u32[]{:S(2)}) collective-permute-start(bf16[1,48,4096]{2,1,0:T(8,128)(2,1)S(1)} %get-tuple-element.105), channel_id=1, source_target_pairs={{0,4},{1,5},{2,6},{3,7},{4,0},{5,1},{6,2},{7,3},{8,12},{9,13},{10,... | collective-permute-start | bytes 1179656 | tf_op jit(solution)/shard_map/ppermute | solution.py:541
  136.0 0.7 copy-start.6
  136.0 0.9 copy-start.7
  136.0 1.0 copy-start.8
  144.3 4.7 %copy-start.9 = (bf16[96,2048]{1,0:T(8,128)(2,1)}, bf16[96,2048]{1,0:T(8,128)(2,1)S(1)}, u32[]{:S(2)}) copy-start(bf16[96,2048]{1,0:T(8,128)(2,1)S(1)} %collective-permute-done.20.own_ref) | copy-start | bytes 1179652
  144.3 4.7 %collective-permute-start.21 = (bf16[96,2048]{1,0:T(8,128)(2,1)S(1)}, bf16[96,2048]{1,0:T(8,128)(2,1)S(1)}, u32[]{:S(2)}, u32[]{:S(2)}) collective-permute-start(bf16[96,2048]{1,0:T(8,128)(2,1)S(1)} %collective-permute-done.20.own_ref), channel_id=1, source_target_pairs={{0,1},{1,0},{2,3},{3,2},{4,5},{5,4},{6,7},{7,6},{8,9},{9,8},{10,11... | collective-permute-start | bytes 1179656 | tf_op jit(solution)/shard_map/ppermute | solution.py:541
  149.0 0.8 copy-start.10

commit v4 on v3

--- a/solution.py
+++ b/solution.py
@@ -89,35 +89,73 @@
     return copies
 
 
-def project(hidden, copies, weight, staged, out_ref, left):
-    chunk = weight.shape[0] // len(copies)
+def split_blocks(total, chip, rows, send, kept, columns):
+    for index in range(total.shape[0] // (2 * rows)):
+        place = slice(index * rows, (index + 1) * rows)
+        for target, bit in ((send, 1 - chip % 2), (kept, chip % 2)):
+            source = pl.ds(pl.multiple_of((2 * index + bit) * rows, 8), rows)
+            target[place, columns] = total[source].astype(target.dtype)
+
+
+def write_out(pairs, columns, left, first):
+    copies = []
+    for index, (source, target) in enumerate(pairs):
+        copies.append(pltpu.make_async_copy(source.at[:, columns], target.at[:, columns], left.at[first + index]))
+        copies[-1].start()
+    return copies
+
+
+def project_kernel(
+    chips, core_ref, chip_ref, hidden_ref, other_ref, weight_ref, other_weight_ref, ids_ref, letters_ref,
+    send_ref, kept_ref, weight, arrived, other_weight, other_arrived, total, send, kept, left, letters, letters_arrived,
+):
+    half = weight.shape[0]
+    start = core_ref[0] * half
+    copies = start_rows(weight_ref, start, weight, arrived)
+    other_copies = start_rows(other_weight_ref, start, other_weight, other_arrived)
+    own_columns = pl.ds(pl.multiple_of(start, half), half)
+    letters_copy = pltpu.make_async_copy(letters_ref.at[FIRST_ID : FIRST_ID + IDS, own_columns], letters, letters_arrived)
+    letters_copy.start()
+    rows = total.shape[0] // chips
+    lane = lax.broadcasted_iota(jnp.int32, (IDS, total.shape[0]), 1)
+    first = chip_ref[0] * rows
+    marks = one_hot(ids_ref[ids_ref.shape[0] - 8 : ids_ref.shape[0] - 7].astype(jnp.int32), 1)
+    marks = jnp.where(jnp.logical_and(lane >= first, lane < first + rows), marks, 0.0).astype(bf16)
+    letters_copy.wait()
+    chunk = half // len(copies)
+    hidden, other = hidden_ref[...], other_ref[...]
     leaving = []
-    for index, copy in enumerate(copies):
-        rows = slice(index * chunk, (index + 1) * chunk)
+    for index in range(len(copies)):
+        columns = slice(index * chunk, (index + 1) * chunk)
+        copies[index].wait()
+        other_copies[index].wait()
+        total[...] = (
+            lax.dot_general(hidden, weight[columns], CONTRACT_LAST, preferred_element_type=f32)
+            + lax.dot_general(other, other_weight[columns], CONTRACT_LAST, preferred_element_type=f32)
+            + expand(marks, letters[:, columns])
+        )
+        split_blocks(total, chip_ref[0], rows, send, kept, columns)
+        leaving += write_out(((send, send_ref), (kept, kept_ref)), columns, left, 2 * index)
+    for copy in leaving:
         copy.wait()
-        value = lax.dot_general(hidden, weight[rows], CONTRACT_LAST, preferred_element_type=f32)
-        staged[:, rows] = value.astype(staged.dtype)
-        leaving.append(pltpu.make_async_copy(staged.at[:, rows], out_ref.at[:, rows], left.at[index]))
-        leaving[-1].start()
-    return leaving
-
-
-def assemble_kernel(steps, chip_ref, core_ref, *refs):
+
+
+def assemble_kernel(rows, steps, chip_ref, core_ref, *refs):
     out_ref = refs[-1]
-    rows, columns = refs[0].shape
-    for index, step in enumerate(steps + steps):
-        place = jnp.bitwise_xor(chip_ref[0], step)
+    columns = refs[0].shape[1]
+    for index, held in enumerate(steps + steps):
         side = core_ref[0] if index < len(steps) else 1 - core_ref[0]
-        at = (pl.ds(pl.multiple_of(place * rows, rows), rows), pl.ds(pl.multiple_of(side * columns, columns), columns))
-        out_ref[at] = refs[index][...]
-
-
-def forward_kernel(shards, me_ref, core_ref, *refs):
+        for slot, step in enumerate(held):
+            place = pl.ds(pl.multiple_of(jnp.bitwise_xor(chip_ref[0], step) * rows, rows), rows)
+            at = (place, pl.ds(pl.multiple_of(side * columns, columns), columns))
+            out_ref[at] = refs[index][slot * rows : (slot + 1) * rows]
+
+
+def forward_kernel(shards, me_ref, *refs):
     slots = refs[:shards]
-    letters_ref, gain_ref, weight_ref, taps_ref, skip_ref, last_ref = refs[shards : shards + 6]
-    hidden_ref, mixed_ref, table_ref, theirs_ref, mine_ref = refs[shards + 6 : shards + 11]
-    normed, hot, filters, matrices, signal, exact, long_part, weight, arrived, last, last_arrived = refs[shards + 11 : shards + 22]
-    own, own_arrived, table, staged, own_staged, left = refs[shards + 22 :]
+    letters_ref, gain_ref, weight_ref, taps_ref, skip_ref = refs[shards : shards + 5]
+    hidden_ref, mixed_ref, table_ref = refs[shards + 5 : shards + 8]
+    normed, hot, filters, matrices, signal, exact, long_part, weight, arrived, table, left = refs[shards + 8 :]
     groups = filters.shape[0]
     local_rows = slots[0].shape[1]
     channels = table.shape[2]
@@ -137,8 +175,6 @@
         rows = slice(index * chunk, (index + 1) * chunk)
         copies.append(pltpu.make_async_copy(weight_ref.at[:, rows], weight.at[:, rows], arrived.at[index]))
         copies[-1].start()
-    last_copies = start_rows(last_ref, (1 - core_ref[0]) * last.shape[0], last, last_arrived)
-    own_copies = start_rows(last_ref, core_ref[0] * last.shape[0], own, own_arrived)
     for index, slot in enumerate(slots):
         place = lanes_at(jnp.bitwise_xor(me, index) * local_blocks, local_blocks)
         filters[:, place] = slot[:groups]
@@ -192,12 +228,9 @@
     mixed_copy = pltpu.make_async_copy(long_part, mixed_ref, left.at[1])
     mixed_copy.start()
     queries = expand(tap_weights(taps_ref, table, 0), hot[:, lanes_at(first, local_blocks)])
-    hidden = jnp.transpose(queries * mixed[:, :local_rows]).astype(bf16)
-    hidden_ref[...] = hidden
-    leaving = project(hidden, last_copies, last, staged, theirs_ref, left.at[2:6])
-    leaving += project(hidden, own_copies, own, own_staged, mine_ref, left.at[6:])
-    for copy in [table_copy, mixed_copy] + leaving:
-        copy.wait()
+    hidden_ref[...] = jnp.transpose(queries * mixed[:, :local_rows]).astype(bf16)
+    table_copy.wait()
+    mixed_copy.wait()
 
 
 def backward_kernel(shards, me_ref, *refs):
@@ -282,57 +315,58 @@
     out_ref[...] = jnp.transpose(total[...]).astype(bf16)
 
 
-def input_grad_kernel(chips, core_ref, grad_ref, weight_ref, theirs_ref, mine_ref, weight, total, theirs, mine, arrived, left):
-    chunks = arrived.shape[0]
-    chunk = weight.shape[1] // chunks
+def input_grad_kernel(
+    chips, core_ref, chip_ref, grad_ref, other_grad_ref, weight_ref, other_weight_ref,
+    send_ref, kept_ref, weight, other_weight, arrived, total, send, kept, left,
+):
+    half = weight.shape[1]
+    chunks = arrived.shape[0] // 2
+    chunk = half // chunks
     copies = []
     for index in range(chunks):
         columns = slice(index * chunk, (index + 1) * chunk)
-        copies.append(pltpu.make_async_copy(weight_ref.at[:, columns], weight.at[:, columns], arrived.at[index]))
-        copies[-1].start()
-    core = core_ref[0]
-    rows = total.shape[0] // (2 * chips)
-
-    def half(which):
-        starts = [pl.multiple_of((2 * chip + which) * rows, 8) for chip in range(chips)]
-        return jnp.concatenate([total[pl.ds(start, rows), :] for start in starts], axis=0)
-
+        source = pl.ds(pl.multiple_of(core_ref[0] * half + index * chunk, chunk), chunk)
+        pair = (
+            pltpu.make_async_copy(weight_ref.at[:, source], weight.at[:, columns], arrived.at[2 * index]),
+            pltpu.make_async_copy(other_weight_ref.at[:, source], other_weight.at[:, columns], arrived.at[2 * index + 1]),
+        )
+        for copy in pair:
+            copy.start()
+        copies.append(pair)
+    rows = total.shape[0] // chips
     leaving = []
     for index in range(chunks):
         columns = slice(index * chunk, (index + 1) * chunk)
-        copies[index].wait()
         value = None
-        for part in range(3):
-            term = lax.dot_general(
-                grad_ref[part], weight[part, columns], CONTRACT_LAST, preferred_element_type=f32
-            )
-            value = term if value is None else value + term
+        for copy, grad, held in zip(copies[index], (grad_ref, other_grad_ref), (weight, other_weight)):
+            copy.wait()
+            for part in range(3):
+                term = lax.dot_general(grad[part], held[part, columns], CONTRACT_LAST, preferred_element_type=f32)
+                value = term if value is None else value + term
         total[...] = value
-        theirs[:, columns] = half(1 - core).astype(bf16)
-        mine[:, columns] = half(core).astype(bf16)
-        for slot, (source, target) in enumerate(((theirs, theirs_ref), (mine, mine_ref))):
-            copy = pltpu.make_async_copy(source.at[:, columns], target.at[:, columns], left.at[2 * index + slot])
-            copy.start()
-            leaving.append(copy)
+        split_blocks(total, chip_ref[0], rows, send, kept, columns)
+        leaving += write_out(((send, send_ref), (kept, kept_ref)), columns, left, 2 * index)
     for copy in leaving:
         copy.wait()
 
 
-def weight_grad_kernel(shards, me_ref, grad_ref, hidden_ref, *refs):
-    slots = refs[: shards - 1]
-    out_ref, own, arrived = refs[shards - 1 :]
+def weight_grad_kernel(shards, me_ref, core_ref, grad_ref, *refs):
+    hidden, mine, theirs = refs[:shards], refs[shards : 2 * shards - 1], refs[2 * shards - 1 : 3 * shards - 2]
+    out_ref, own, arrived = refs[3 * shards - 2 :]
     share = own.shape[1]
+    part = share // 2
     source = grad_ref.at[:, pl.ds(pl.multiple_of(me_ref[0] * share, share), share)]
     copy = pltpu.make_async_copy(source, own, arrived)
     copy.start()
-    chunk = share // 2
-    copy.wait()
-    for start in range(0, share, chunk):
-        columns = slice(start, start + chunk)
-        total = expand(own[:, columns], hidden_ref[...])
-        for slot in slots:
-            total = total + expand(slot[:, columns], slot[:, share:])
-        out_ref[columns, :] = total
+    for slots, side in ((mine, core_ref[0]), (theirs, 1 - core_ref[0])):
+        total = None
+        for slot, shard_hidden in zip(slots, hidden[1:]):
+            term = expand(slot[...], shard_hidden[...])
+            total = term if total is None else total + term
+        if slots is mine:
+            copy.wait()
+        place = pl.ds(pl.multiple_of(side * part, part), part)
+        out_ref[place, :] = total + expand(own[:, place], hidden[0][...])
 
 
 def in_vmem(count):
@@ -353,26 +387,28 @@
 SMALL_COST = pl.CostEstimate(flops=1000, bytes_accessed=1000, transcendentals=0)
 
 
-def insert_kernel(chip_ref, core_ref, own_ref, theirs_ref, base_ref, out_ref, moved):
-    rows, columns = own_ref.shape
-    place = pl.ds(pl.multiple_of(jnp.bitwise_xor(chip_ref[0], 1) * rows, rows), rows)
+def insert_kernel(rows, steps, chip_ref, core_ref, own_ref, theirs_ref, base_ref, out_ref, moved):
+    columns = own_ref.shape[1]
     copies = []
-    for index, source in enumerate((own_ref, theirs_ref)):
-        side = core_ref[0] if index == 0 else 1 - core_ref[0]
-        target = out_ref.at[place, pl.ds(pl.multiple_of(side * columns, columns), columns)]
-        copies.append(pltpu.make_async_copy(source, target, moved.at[index]))
-        copies[-1].start()
+    for index, step in enumerate(steps):
+        place = pl.ds(pl.multiple_of(jnp.bitwise_xor(chip_ref[0], step) * rows, rows), rows)
+        for which, source in enumerate((own_ref, theirs_ref)):
+            side = core_ref[0] if which == 0 else 1 - core_ref[0]
+            target = out_ref.at[place, pl.ds(pl.multiple_of(side * columns, columns), columns)]
+            part = source.at[index * rows : (index + 1) * rows]
+            copies.append(pltpu.make_async_copy(part, target, moved.at[2 * index + which]))
+            copies[-1].start()
     for copy in copies:
         copy.wait()
 
 
-def run_insert(chip, core, own, theirs, base):
+def run_insert(steps, chip, core, own, theirs, base):
     return pl.pallas_call(
-        insert_kernel,
+        functools.partial(insert_kernel, own.shape[0] // len(steps), steps),
         out_shape=jax.ShapeDtypeStruct(base.shape, base.dtype),
         in_specs=[SMEM_SPEC, SMEM_SPEC, VMEM_SPEC, VMEM_SPEC, ANY_SPEC],
         out_specs=ANY_SPEC,
-        scratch_shapes=[pltpu.SemaphoreType.DMA((2,))],
+        scratch_shapes=[pltpu.SemaphoreType.DMA((2 * len(steps),))],
         input_output_aliases={4: 0},
         compiler_params=params(),
         cost_estimate=SMALL_COST,
@@ -383,7 +419,7 @@
 def run_assemble(chips, steps, chip, core, own, theirs):
     rows, columns = own[0].shape
     return pl.pallas_call(
-        functools.partial(assemble_kernel, steps),
+        functools.partial(assemble_kernel, rows, steps),
         out_shape=jax.ShapeDtypeStruct((chips * rows, 2 * columns), bf16),
         in_specs=[SMEM_SPEC, SMEM_SPEC] + in_vmem(2 * len(own)),
         out_specs=VMEM_SPEC,
@@ -393,7 +429,7 @@
     )(chip, core, *own, *theirs)
 
 
-def run_forward(me, core, slots, embed_table, norm_gain, weight, taps, skip_gain, output_weight):
+def run_forward(me, slots, embed_table, norm_gain, weight, taps, skip_gain):
     shards = len(slots)
     local_rows = slots[0].shape[1]
     _, width, channels = weight.shape
@@ -407,14 +443,11 @@
             jax.ShapeDtypeStruct((local_rows, channels), bf16),
             jax.ShapeDtypeStruct((channels, span), f32),
             jax.ShapeDtypeStruct((3, IDS, channels), f32),
-            jax.ShapeDtypeStruct((local_rows, width // 2), bf16),
-            jax.ShapeDtypeStruct((local_rows, width // 2), bf16),
         ),
-        in_specs=[SMEM_SPEC, SMEM_SPEC]
+        in_specs=[SMEM_SPEC]
         + in_vmem(shards)
-        + [pl.BlockSpec((IDS, width), lambda step: (FIRST_ID // IDS, 0)), VMEM_SPEC, ANY_SPEC, VMEM_SPEC, VMEM_SPEC]
-        + [ANY_SPEC],
-        out_specs=(VMEM_SPEC, ANY_SPEC, ANY_SPEC, ANY_SPEC, ANY_SPEC),
+        + [pl.BlockSpec((IDS, width), lambda step: (FIRST_ID // IDS, 0)), VMEM_SPEC, ANY_SPEC, VMEM_SPEC, VMEM_SPEC],
+        out_specs=(VMEM_SPEC, ANY_SPEC, ANY_SPEC),
         scratch_shapes=[
             pltpu.VMEM((IDS, width), bf16),
             pltpu.VMEM((2 * taps.shape[0] * IDS, length + LANES), bf16),
@@ -425,19 +458,39 @@
             pltpu.VMEM((channels, span), f32),
             pltpu.VMEM(weight.shape, bf16),
             pltpu.SemaphoreType.DMA((CHUNKS,)),
-            pltpu.VMEM((width // 2, channels), bf16),
-            pltpu.SemaphoreType.DMA((4,)),
-            pltpu.VMEM((width // 2, channels), bf16),
-            pltpu.SemaphoreType.DMA((4,)),
             pltpu.VMEM((3, IDS, channels), f32),
-            pltpu.VMEM((local_rows, width // 2), bf16),
-            pltpu.VMEM((local_rows, width // 2), bf16),
-            pltpu.SemaphoreType.DMA((10,)),
+            pltpu.SemaphoreType.DMA((2,)),
         ],
         compiler_params=params(),
         cost_estimate=LARGE_COST,
         name="forward_conv",
-    )(me, core, *slots, embed_table, norm_gain, weight, taps, skip_gain, output_weight)
+    )(me, *slots, embed_table, norm_gain, weight, taps, skip_gain)
+
+
+def run_project(core, chip, chips, hidden, other_hidden, weight, other_weight, packed, embed_table):
+    rows, channels = hidden.shape
+    half = weight.shape[0] // 2
+    return pl.pallas_call(
+        functools.partial(project_kernel, chips),
+        out_shape=(jax.ShapeDtypeStruct((rows // 2, half), bf16), jax.ShapeDtypeStruct((rows // 2, half), f32)),
+        in_specs=[SMEM_SPEC, SMEM_SPEC, VMEM_SPEC, VMEM_SPEC, ANY_SPEC, ANY_SPEC, VMEM_SPEC, ANY_SPEC],
+        out_specs=(ANY_SPEC, ANY_SPEC),
+        scratch_shapes=[
+            pltpu.VMEM((half, channels), bf16),
+            pltpu.SemaphoreType.DMA((4,)),
+            pltpu.VMEM((half, channels), bf16),
+            pltpu.SemaphoreType.DMA((4,)),
+            pltpu.VMEM((rows, half // 4), f32),
+            pltpu.VMEM((rows // 2, half), bf16),
+            pltpu.VMEM((rows // 2, half), f32),
+            pltpu.SemaphoreType.DMA((8,)),
+            pltpu.VMEM((IDS, half), bf16),
+            pltpu.SemaphoreType.DMA,
+        ],
+        compiler_params=params(),
+        cost_estimate=SMALL_COST,
+        name="project",
+    )(core, chip, hidden, other_hidden, weight, other_weight, packed, embed_table)
 
 
 def run_backward(me, slots, grads, table, taps, skip_gain, mixed):
@@ -466,20 +519,20 @@
     )(me, *slots, *grads, table, taps, skip_gain, mixed)
 
 
-def run_weight_grad(me, output_grad, hidden, slots):
-    shards = len(slots) + 1
+def run_weight_grad(me, core, output_grad, hidden, mine, theirs):
+    shards = len(hidden)
     rows, width = output_grad.shape
-    share, channels = width // shards, hidden.shape[1]
+    share, channels = width // shards, hidden[0].shape[1]
     return pl.pallas_call(
         functools.partial(weight_grad_kernel, shards),
         out_shape=jax.ShapeDtypeStruct((share, channels), f32),
-        in_specs=[SMEM_SPEC, ANY_SPEC] + in_vmem(shards),
+        in_specs=[SMEM_SPEC, SMEM_SPEC, ANY_SPEC] + in_vmem(3 * shards - 2),
         out_specs=VMEM_SPEC,
         scratch_shapes=[pltpu.VMEM((rows, share), bf16), pltpu.SemaphoreType.DMA],
         compiler_params=params(),
         cost_estimate=SMALL_COST,
         name="weight_grad",
-    )(me, output_grad, hidden, *slots)
+    )(me, core, output_grad, *hidden, *mine, *theirs)
 
 
 def run_hidden_grad(output_grad, output_weight):
@@ -502,29 +555,27 @@
     )(output_grad, output_weight)
 
 
-def run_input_grad(core, chips, projection_grad, weight):
-    _, rows, channels = projection_grad.shape
-    width = weight.shape[1]
+def run_input_grad(core, chip, chips, grad, other_grad, weight, other_weight):
+    _, rows, channels = grad.shape
+    half = weight.shape[1] // 2
     return pl.pallas_call(
         functools.partial(input_grad_kernel, chips),
-        out_shape=(
-            jax.ShapeDtypeStruct((rows // 2, width), bf16),
-            jax.ShapeDtypeStruct((rows // 2, width), bf16),
-        ),
-        in_specs=[SMEM_SPEC, VMEM_SPEC, ANY_SPEC],
+        out_shape=(jax.ShapeDtypeStruct((rows // 2, half), bf16), jax.ShapeDtypeStruct((rows // 2, half), f32)),
+        in_specs=[SMEM_SPEC, SMEM_SPEC, VMEM_SPEC, VMEM_SPEC, ANY_SPEC, ANY_SPEC],
         out_specs=(ANY_SPEC, ANY_SPEC),
         scratch_shapes=[
-            pltpu.VMEM(weight.shape, bf16),
-            pltpu.VMEM((rows, width // CHUNKS), f32),
-            pltpu.VMEM((rows // 2, width), bf16),
-            pltpu.VMEM((rows // 2, width), bf16),
-            pltpu.SemaphoreType.DMA((CHUNKS,)),
-            pltpu.SemaphoreType.DMA((2 * CHUNKS,)),
+            pltpu.VMEM((3, half, channels), bf16),
+            pltpu.VMEM((3, half, channels), bf16),
+            pltpu.SemaphoreType.DMA((8,)),
+            pltpu.VMEM((rows, half // 4), f32),
+            pltpu.VMEM((rows // 2, half), bf16),
+            pltpu.VMEM((rows // 2, half), f32),
+            pltpu.SemaphoreType.DMA((8,)),
         ],
         compiler_params=params(),
         cost_estimate=SMALL_COST,
         name="input_grad",
-    )(core, projection_grad, weight)
+    )(core, chip, grad, other_grad, weight, other_weight)
 
 
 def ctx_exchange(value, step):
@@ -580,94 +631,99 @@
     id_row = jnp.broadcast_to(token_ids[None, :], (groups + 8, local_rows)).astype(f32)
     packed = jnp.where(row_number < groups, jnp.pad(filters, ((0, 8), (0, 0))), id_row)
     slots = gather_ctx(packed)
+    half = width // 2
+    levels = chips.bit_length() - 1
+    block_rows = local_rows // chips
+    other_weight, other_input = tp_exchange(output_weight, 1), tp_exchange(weight, 1)
     hidden_grad = run_hidden_grad(output_grad, output_weight)
     arrived, hidden_grad, me_tie = together(slots[1:], hidden_grad, me_tie)
     slots = [packed] + arrived
     grad_slots = gather_ctx(hidden_grad)
 
-    hidden, mixed, table, for_sibling, mine = run_forward(
-        me_tie, core_tie, slots, embed_table, norm_gain, weight, short_weight, skip_gain, output_weight
+    hidden, mixed, table = run_forward(
+        me_tie, slots, embed_table, norm_gain, weight, short_weight, skip_gain
     )
-    for_sibling, mine, hidden, grad_slots = together(for_sibling, mine, hidden, grad_slots)
-    half = width // 2
-    block_rows = local_rows // chips
-    received = tp_exchange(for_sibling, 1)
-    mine = mine.reshape(chips, block_rows, half)
-    received = received.reshape(chips, block_rows, half)
-
-    order = list(range(2, chips)) + [1]
-    share = width // shards
-
-    def out_send(step):
-        index = jnp.bitwise_xor(chip, step)
-        return (pick(mine, index).astype(f32) + pick(received, index).astype(f32)).astype(bf16)
-
-    def ctx_piece(step):
-        start = jnp.bitwise_xor(me, step) * share
-        return jnp.concatenate([lax.dynamic_slice_in_dim(output_grad, start, share, axis=1), hidden], axis=1)
-
-    near = range(1, shards // 2 + 1)
-    ctx_arrived = [ctx_exchange(ctx_piece(step), step) for step in near]
-    sends = [out_send(step) for step in order]
-    sends, me_tie = together(sends, me_tie)
-    out_arrived = [tp_exchange(value, 2 * step) for step, value in zip(order, sends)]
-    projection_grad = run_backward(me_tie, slots, grad_slots, table, short_weight, skip_gain, mixed)
-    ctx_sends = [ctx_piece(step) for step in range(shards // 2 + 1, shards)]
-    projection_grad, core_tie, ctx_sends = together(projection_grad, core_tie, ctx_sends)
-    theirs, mine_grad = run_input_grad(core_tie, chips, projection_grad, weight)
-    own_ids = lax.dynamic_slice_in_dim(token_ids, chip * block_rows, block_rows, axis=0)
-    own_hot = (own_ids[:, None] == jnp.arange(FIRST_ID, FIRST_ID + IDS)[None, :]).astype(bf16)
-    own_letters = lax.dynamic_slice(embed_table, (FIRST_ID, core * half), (IDS, half))
-    own_block = jnp.dot(own_hot, own_letters, preferred_element_type=f32)
-    own_block = own_block + pick(mine, chip).astype(f32) + pick(received, chip).astype(f32)
-    out_arrived, theirs, mine_grad, own_block, ctx_arrived, ctx_sends = together(
-        out_arrived, theirs, mine_grad, own_block, ctx_arrived, ctx_sends
+    hidden, grad_slots, other_weight = together(hidden, grad_slots, other_weight)
+    send, kept = run_project(
+        core_tie, chip_tie, chips, hidden, tp_exchange(hidden, 1), output_weight, other_weight, packed, embed_table
     )
-
-    received_grad = tp_exchange(theirs, 1)
-    block = own_block
-    for value in out_arrived:
-        block = block + value.astype(f32)
-    block = block.astype(bf16)
-    block, received_grad = together(block, received_grad)
-    split = (chips, local_rows // (2 * chips), width)
-    terms = [mine_grad.reshape(split), received_grad.reshape(split)]
 
     def pairs(value, which):
         return pick(value.reshape((value.shape[0] // 2, 2) + value.shape[1:]), which, 1)
 
-    def leaving(bit):
+    def leaving(terms, bit):
         which = 1 - (chip >> bit & 1)
         return sum(pairs(term, which).astype(f32) for term in terms).astype(bf16)
 
-    def keep(bit, arriving):
+    def keep(terms, bit):
         which = chip >> bit & 1
-        return [pairs(term, which) for term in terms] + [arriving]
-
-    line = [tp_exchange(block, 2 * step) for step in order[:-1]]
-    arriving = tp_exchange(leaving(0), 2)
-    ctx_more = [
-        ctx_exchange(value, step) for step, value in zip(range(shards // 2 + 1, shards), ctx_sends)
-    ]
-    line, arriving, ctx_more, block = together(line, arriving, ctx_more, block)
-    terms = keep(0, arriving)
-    levels = chips.bit_length() - 1
+        return [pairs(term, which) for term in terms]
+
+    blocks = (chips // 2, block_rows, half)
+    send, kept, me_tie, late_hidden = together(send, kept, me_tie, hidden)
+    out_arrived = tp_exchange(send, 2)
+
+    share = width // shards
+    part = share // 2
+
+    def ctx_piece(step):
+        start = jnp.bitwise_xor(me, step) * share + core * part
+        return lax.dynamic_slice_in_dim(output_grad, start, part, axis=1)
+
+    near, others = range(1, shards // 2 + 1), range(shards // 2 + 1, shards)
+    pieces = [ctx_piece(step) for step in range(1, shards)]
+    pieces, me_tie = together(pieces, me_tie)
+    near_grad = [ctx_exchange(pieces[step - 1], step) for step in near]
+    projection_grad = run_backward(me_tie, slots, grad_slots, table, short_weight, skip_gain, mixed)
+    projection_grad, near_grad, late_hidden = together(projection_grad, near_grad, late_hidden)
+    other_grad = tp_exchange(projection_grad, 1)
+    near_hidden = [ctx_exchange(late_hidden, step) for step in near]
+    grad_send, grad_kept = run_input_grad(
+        core_tie, chip_tie, chips, projection_grad, other_grad, weight, other_input
+    )
+    out_terms = [kept.reshape(blocks), out_arrived.reshape(blocks)]
     for bit in range(1, levels):
-        outgoing = leaving(bit)
-        if bit == levels - 1:
-            outgoing, block, line, ctx_more = together(outgoing, block, line, ctx_more)
-            neighbour = tp_exchange(block, 2)
-        terms = keep(bit, tp_exchange(outgoing, 2 << bit))
-
-    line = [block] + line
-    base = run_assemble(
-        chips, [0] + order[:-1], chip_tie, core_tie, line, [tp_exchange(value, 1) for value in line]
+        out_terms = keep(out_terms, bit) + [tp_exchange(leaving(out_terms, bit), 2 << bit)]
+    grad_send, grad_kept, near_hidden, late_hidden, pieces = together(
+        grad_send, grad_kept, near_hidden, late_hidden, pieces
     )
-    output_weight_grad = run_weight_grad(me_tie, output_grad, hidden, ctx_arrived + ctx_more)
-    kept = sum(term.astype(f32) for term in terms[:-1])
-    base, output_weight_grad, neighbour, kept = together(base, output_weight_grad, neighbour, kept)
-    block_output = run_insert(chip_tie, core_tie, neighbour, tp_exchange(neighbour, 1), base)
-    normed_grad = (kept + terms[-1].astype(f32)).reshape(local_rows // (2 * chips), width)
+    grad_arrived = tp_exchange(grad_send, 2)
+    far_grad = [ctx_exchange(pieces[step - 1], step) for step in others]
+    far_hidden = [ctx_exchange(late_hidden, step) for step in others]
+
+    block = sum(term.astype(f32) for term in out_terms).reshape(block_rows, half).astype(bf16)
+    line, steps = [block], [[0]]
+    for level in range(levels - 1):
+        mask = chips >> level + 1
+        held = line[0] if level == 0 else jnp.concatenate(line, axis=0)
+        line.append(tp_exchange(held, 2 * mask))
+        steps.append([step ^ mask for group in steps for step in group])
+    grad_arrived, far_grad, far_hidden = together(grad_arrived, far_grad, far_hidden)
+    grad_terms = [grad_kept.reshape(blocks), grad_arrived.reshape(blocks)]
+    for bit in range(1, levels):
+        grad_terms = keep(grad_terms, bit) + [tp_exchange(leaving(grad_terms, bit), 2 << bit)]
+    came = tp_exchange(jnp.concatenate(line, axis=0), 2)
+    came_steps = [step ^ 1 for group in steps for step in group]
+
+    base = run_assemble(chips, steps, chip_tie, core_tie, line, [tp_exchange(value, 1) for value in line])
+    mine = near_grad + far_grad
+    output_weight_grad = run_weight_grad(
+        me_tie, core_tie, output_grad, [late_hidden] + near_hidden + far_hidden, mine,
+        [tp_exchange(value, 1) for value in mine],
+    )
+    kept_sum = sum(term.astype(f32) for term in grad_terms[:-1])
+    base, output_weight_grad, came, kept_sum, last = together(
+        base, output_weight_grad, came, kept_sum, grad_terms[-1]
+    )
+    total = (kept_sum + last.astype(f32)).reshape(2, block_rows // 2, half)
+    my_rows, their_rows = pick(total, core), pick(total, 1 - core)
+    other_columns = tp_exchange(their_rows, 1)
+    block_output = run_insert(came_steps, chip_tie, core_tie, came, tp_exchange(came, 1), base)
+    normed_grad = jnp.where(
+        core == 0,
+        jnp.concatenate([my_rows, other_columns], axis=1),
+        jnp.concatenate([other_columns, my_rows], axis=1),
+    )
     return (block_output, output_weight_grad, jnp.transpose(projection_grad, (1, 0, 2)), normed_grad)
 
 

time: 153 us -> 145 us (0.948)
  starting transfers between devices: 33.8 us -> 26.9 us
  other arithmetic: 10.3 us -> 6.63 us
  Pallas kernels: 59.7 us -> 63 us
  local copies, waits for them, and re-layouts: 4.21 us -> 7.41 us
  waiting for transfers between devices: 41.4 us -> 39.6 us
    ppermute x9 -> x12, waiting for transfers between devices: 13.1 us -> 1.08 us  [ctx_exchange(): return lax.ppermute(value, 'ctx', [(i, i ^ step) for i in range(count)])]
    ppermute x14 -> x17, waiting for transfers between devices: 28.2 us -> 38.5 us  [tp_exchange(): return lax.ppermute(value, 'tp', [(i, i ^ mask) for i in range(count)])]
    ppermute x14 -> x17, starting transfers between devices: 21.7 us -> 11.7 us  [tp_exchange(): return lax.ppermute(value, 'tp', [(i, i ^ mask) for i in range(count)])]
    pallas_call x2 -> x3, Pallas kernels: 5.41 us -> 13 us  [the longest x1 7.37 us: run_project(): pl.pallas_call(functools.partial(project_kernel, chips), out_shape=(jax.S...]
    pallas_call x1, Pallas kernels: 19.6 us -> 16.1 us  [run_forward(): pl.pallas_call(functools.partial(forward_kernel, shards), grid=(1,), out_...]
    ppermute x9 -> x12, starting transfers between devices: 12.1 us -> 15.2 us  [ctx_exchange(): return lax.ppermute(value, 'ctx', [(i, i ^ step) for i in range(count)])]
    convert_element_type x2 -> x1, other arithmetic: 3.69 us -> 1.24 us  [body(): sum((term.astype(f32) for term in out_terms)).reshape(block_rows, half)]
    unnamed x32 -> x44, local copies, waits for them, and re-layouts: 3.19 us -> 5.27 us
  transfers between devices with their start and end apart: 23 -> 29, of which waited for: 8 -> 9; matrix products, arithmetic and copies ran while one was open for 6% -> 6% of each run, Pallas kernels for 38% -> 42%
where the time goes in v4:
time: 145 us
  Pallas kernels  63 us (43%)
  waiting for transfers between devices  39.6 us (27%)
  starting transfers between devices  26.9 us (19%)
  local copies, waits for them, and re-layouts  7.41 us (5%)
  other arithmetic  6.63 us (5%)
    ppermute x17, waiting for transfers between devices, tp_exchange(): return lax.ppermute(value, 'tp', [(i, i ^ mask) for i in range(count)])  38.5 us
    pallas_call x1, Pallas kernels, run_forward(): pl.pallas_call(functools.partial(forward_kernel, shards), grid=(1,), out_...  16.1 us
    ppermute x12, starting transfers between devices, ctx_exchange(): return lax.ppermute(value, 'ctx', [(i, i ^ step) for i in range(count)])  15.2 us
    pallas_call x1, Pallas kernels, run_backward(): pl.pallas_call(functools.partial(backward_kernel, shards), out_shape=jax....  13.2 us
    ppermute x17, starting transfers between devices, tp_exchange(): return lax.ppermute(value, 'tp', [(i, i ^ mask) for i in range(count)])  11.7 us
    pallas_call x1, Pallas kernels, run_input_grad(): pl.pallas_call(functools.partial(input_grad_kernel, chips), out_shape=(ja...  10.2 us
    pallas_call x1, Pallas kernels, run_project(): pl.pallas_call(functools.partial(project_kernel, chips), out_shape=(jax.S...  7.37 us
    pallas_call x1, Pallas kernels, run_weight_grad(): pl.pallas_call(functools.partial(weight_grad_kernel, shards), out_shape=j...  6.09 us
  transfers between devices with their start and end apart: 29, of which 9 were waited for; matrix products, arithmetic and copies ran while one was open for 6% of the time, Pallas kernels for 42%

profile of v4, /device:TPU:0, one launch (start us, length us, event | category | flops | bytes accessed | tf_op | source)
XLA Modules:
  0.0 144.6 jit_solution(7928912980751291947)
XLA Ops:
  0.6 0.5 collective-permute-start.16
  1.1 0.1 collective-permute-start.6
  1.2 0.7 convert_element_type.93
  1.9 0.9 pad_select_fusion.refs_0_.ids_ref
  2.8 3.0 %collective-permute-start = (f32[40,384]{1,0:T(8,128)S(1)}, f32[40,384]{1,0:T(8,128)S(1)}, u32[]{:S(2)}, u32[]{:S(2)}) collective-permute-start(f32[40,384]{1,0:T(8,128)S(1)} %pad_select_fusion.refs_0_.ids_ref), channel_id=1, source_target_pairs={{0,8},{8,0},{16,24},{24,16},{1,9},{9,1},{17,25},{25,17},{2,10},{10... | collective-permute-start | bytes 184328 | tf_op jit(solution)/shard_map/ppermute | solution.py:583
  5.8 1.5 %collective-permute-start.1 = (f32[40,384]{1,0:T(8,128)S(1)}, f32[40,384]{1,0:T(8,128)S(1)}, u32[]{:S(2)}, u32[]{:S(2)}) collective-permute-start(f32[40,384]{1,0:T(8,128)S(1)} %pad_select_fusion.refs_0_.ids_ref), channel_id=1, source_target_pairs={{0,16},{8,24},{16,0},{24,8},{1,17},{9,25},{17,1},{25,9},{2,18},{10... | collective-permute-start | bytes 184328 | tf_op jit(solution)/shard_map/ppermute | solution.py:583
  7.3 0.0 collective-permute-start.2
  7.3 4.4 %hidden_grad.1.refs_4_ = bf16[512,384]{1,0:T(8,128)(2,1)} custom-call(bf16[384,4096]{1,0:T(8,128)(2,1)} %grad_ref.3, bf16[4096,512]{1,0:T(8,128)(2,1)} %weight_ref.3), custom_call_target="tpu_custom_call" | custom-call | flops 1000 | bytes 1000 | tf_op jit(solution)/shard_map/hidden_grad/pallas_call | solution.py:541
  11.8 0.0 collective-permute-done.refs_1_
  11.8 0.6 collective-permute-done.2.refs_3_
  12.4 1.4 collective-permute-start.3
  13.8 1.5 %collective-permute-start.4 = (bf16[512,384]{1,0:T(8,128)(2,1)}, bf16[512,384]{1,0:T(8,128)(2,1)S(1)}, u32[]{:S(2)}, u32[]{:S(2)}) collective-permute-start(bf16[512,384]{1,0:T(8,128)(2,1)} %hidden_grad.1.refs_4_), channel_id=1, source_target_pairs={{0,16},{8,24},{16,0},{24,8},{1,17},{9,25},{17,1},{25,9},{2,18},{10... | collective-permute-start | bytes 1179656 | tf_op jit(solution)/shard_map/ppermute | solution.py:583
  15.4 0.5 collective-permute-start.5
  15.9 16.1 %forward_conv.1 = (bf16[384,512]{1,0:T(8,128)(2,1)}, f32[512,512]{1,0:T(8,128)}, f32[3,32,512]{2,1,0:T(8,128)}) custom-call(s32[1]{0:T(128)} %bitcast.2.me_ref, f32[40,384]{1,0:T(8,128)} %copy-done.15, f32[40,384]{1,0:T(8,128)} %copy-done.19, f32[40,384]{1,0:T(8,128)} %copy-done.20, f32[40,384]{1,0:T(8,128)} %copy-done.21, bf16[512,4096]{1,0:T(8,128)(2,1)} %letters_ref.1, ...), custom_call_target="tpu_custom_call" | custom-call | flops 20000000000 | bytes 10000000 | tf_op jit(solution)/shard_map/forward_conv/pallas_call | solution.py:439
  32.0 0.0 collective-permute-done.3.refs_5_
  32.0 0.4 collective-permute-done.4.refs_6_
  32.5 0.7 copy-done.17
  33.2 0.1 copy-done.18
  33.3 2.1 %constant_dynamic-slice_fusion = (bf16[384,512]{1,0:T(8,128)(2,1)}, bf16[384,512]{1,0:T(8,128)(2,1)S(1)}, bf16[384,512]{1,0:T(8,128)(2,1)S(1)}) fusion(bf16[384,4096]{1,0:T(8,128)(2,1)} %grad_ref.3, s32[]{:T(128)S(6)} %select_n.60, s32[]{:T(128)S(6)} %select_n.59, s32[]{:T(128)S(6)} %select_n.58), kind=kLoop, calls=%fused_computation.14 | loop fusion | bytes 2359308 | tf_op jit(solution)/shard_map/dynamic_slice | solution.py:671
  35.4 0.7 copy-done.9
  36.2 7.4 %project.1 = (bf16[192,2048]{1,0:T(8,128)(2,1)}, f32[192,2048]{1,0:T(8,128)}) custom-call(s32[1]{0:T(128)} %bitcast.1.core_ref, s32[1]{0:T(128)} %bitcast.chip_ref, bf16[384,512]{1,0:T(8,128)(2,1)} %get-tuple-element.76.hidden_ref.refs_0_, bf16[384,512]{1,0:T(8,128)(2,1)} %copy-done.9, bf16[4096,512]{1,0:T(8,128)(2,1)} %weight_ref.3, ...), custom_call_target="tpu_custom_call" | custom-call | flops 1000 | bytes 1000 | tf_op jit(solution)/shard_map/project/pallas_call | solution.py:473
  43.6 1.3 collective-permute-start.13
  44.9 1.4 collective-permute-start.14
  46.3 1.6 %collective-permute-start.8 = (bf16[192,2048]{1,0:T(8,128)(2,1)}, bf16[192,2048]{1,0:T(8,128)(2,1)}, u32[]{:S(2)}, u32[]{:S(2)}) collective-permute-start(bf16[192,2048]{1,0:T(8,128)(2,1)} %get-tuple-element.59), channel_id=1, source_target_pairs={{0,2},{1,3},{2,0},{3,1},{4,6},{5,7},{6,4},{7,5},{8,10},{9,11},{10,... | collective-permute-start | bytes 2359304 | tf_op jit(solution)/shard_map/ppermute | solution.py:592
  47.8 13.2 %backward_conv.1.grad_ref = bf16[3,384,512]{2,1,0:T(8,128)(2,1)} custom-call(s32[1]{0:T(128)} %bitcast.2.me_ref, f32[40,384]{1,0:T(8,128)} %copy-done.15, f32[40,384]{1,0:T(8,128)} %copy-done.19, f32[40,384]{1,0:T(8,128)} %copy-done.20, f32[40,384]{1,0:T(8,128)} %copy-done.21, bf16[512,384]{1,0:T(8,128)(2,1)} %hidden_grad.1.refs_4_, ...), custom_call_target="tpu_custom_call" | custom-call | flops 20000000000 | bytes 10000000 | tf_op jit(solution)/shard_map/backward_conv/pallas_call | solution.py:503
  61.0 0.1 collective-permute-start.15
  61.1 1.0 collective-permute-start.17
  62.2 0.5 collective-permute-start.18
  62.7 3.3 %collective-permute-done.8 = bf16[192,2048]{1,0:T(8,128)(2,1)} collective-permute-done((bf16[192,2048]{1,0:T(8,128)(2,1)}, bf16[192,2048]{1,0:T(8,128)(2,1)}, u32[]{:S(2)}, u32[]{:S(2)}) %collective-permute-start.8) | collective-permute-done | bytes 786464 | tf_op jit(solution)/shard_map/ppermute | solution.py:592
  66.0 1.8 %fusion.1 = bf16[1,96,2048]{2,1,0:T(8,128)(2,1)} fusion(f32[1,2,96,2048]{3,2,1,0:T(8,128)S(1)} %bitcast.32, s32[]{:T(128)S(6)} %select_n.57, bf16[1,2,96,2048]{3,2,1,0:T(8,128)(2,1)} %bitcast.5), kind=kLoop, calls=%fused_computation.8 | loop fusion | flops 589824 | bytes 1572868 | tf_op jit(solution)/shard_map/convert_element_type | solution.py:656
  67.8 2.6 %collective-permute-start.9 = (bf16[1,96,2048]{2,1,0:T(8,128)(2,1)}, bf16[1,96,2048]{2,1,0:T(8,128)(2,1)}, u32[]{:S(2)}, u32[]{:S(2)}) collective-permute-start(bf16[1,96,2048]{2,1,0:T(8,128)(2,1)} %fusion.1), channel_id=1, source_target_pairs={{0,4},{1,5},{2,6},{3,7},{4,0},{5,1},{6,2},{7,3},{8,12},{9,13},{10,... | collective-permute-start | bytes 1179656 | tf_op jit(solution)/shard_map/ppermute | solution.py:592
  70.4 1.0 copy-done.5
  71.4 10.2 %input_grad.1 = (bf16[192,2048]{1,0:T(8,128)(2,1)}, f32[192,2048]{1,0:T(8,128)}) custom-call(s32[1]{0:T(128)} %bitcast.1.core_ref, s32[1]{0:T(128)} %bitcast.chip_ref, bf16[3,384,512]{2,1,0:T(8,128)(2,1)} %backward_conv.1.grad_ref, bf16[3,384,512]{2,1,0:T(8,128)(2,1)} %copy-done.5, bf16[3,4096,512]{2,1,0:T(8,128)(2,1)} %bitcast.30, ...), custom_call_target="tpu_custom_call" | custom-call | flops 1000 | bytes 1000 | tf_op jit(solution)/shard_map/input_grad/pallas_call | solution.py:561
  81.7 0.0 copy-start.4
  81.7 1.6 %collective-permute-start.19 = (bf16[192,2048]{1,0:T(8,128)(2,1)}, bf16[192,2048]{1,0:T(8,128)(2,1)S(1)}, u32[]{:S(2)}, u32[]{:S(2)}) collective-permute-start(bf16[192,2048]{1,0:T(8,128)(2,1)} %get-tuple-element.79), channel_id=1, source_target_pairs={{0,2},{1,3},{2,0},{3,1},{4,6},{5,7},{6,4},{7,5},{8,10},{9,11},{10,... | collective-permute-start | bytes 2359304 | tf_op jit(solution)/shard_map/ppermute | solution.py:592
  83.3 4.3 %collective-permute-done.9 = bf16[1,96,2048]{2,1,0:T(8,128)(2,1)} collective-permute-done((bf16[1,96,2048]{2,1,0:T(8,128)(2,1)}, bf16[1,96,2048]{2,1,0:T(8,128)(2,1)}, u32[]{:S(2)}, u32[]{:S(2)}) %collective-permute-start.9) | collective-permute-done | bytes 393248 | tf_op jit(solution)/shard_map/ppermute | solution.py:592
  87.7 1.2 fusion.3.refs_0_
  88.9 0.1 collective-permute-start.10
  89.0 0.9 collective-permute-start.20
  89.9 2.1 %collective-permute-start.21 = (bf16[384,512]{1,0:T(8,128)(2,1)S(1)}, bf16[384,512]{1,0:T(8,128)(2,1)S(1)}, u32[]{:S(2)}, u32[]{:S(2)}) collective-permute-start(bf16[384,512]{1,0:T(8,128)(2,1)S(1)} %copy-done.1), channel_id=1, source_target_pairs={{0,24},{8,16},{16,8},{24,0},{1,25},{9,17},{17,9},{25,1},{2,26},{10... | collective-permute-start | bytes 1179656 | tf_op jit(solution)/shard_map/ppermute | solution.py:583
  92.0 15.8 %collective-permute-done.10.refs_1_ = bf16[96,2048]{1,0:T(8,128)(2,1)S(1)} collective-permute-done((bf16[96,2048]{1,0:T(8,128)(2,1)S(1)}, bf16[96,2048]{1,0:T(8,128)(2,1)S(1)}, u32[]{:S(2)}, u32[]{:S(2)}) %collective-permute-start.10) | collective-permute-done | bytes 393248 | tf_op jit(solution)/shard_map/ppermute | solution.py:592
  107.8 0.1 pad_maximum_fusion
  107.9 2.2 %collective-permute-start.25 = (bf16[192,2048]{1,0:T(8,128)(2,1)S(1)}, bf16[192,2048]{1,0:T(8,128)(2,1)S(1)}, u32[]{:S(2)}, u32[]{:S(2)}) collective-permute-start(bf16[192,2048]{1,0:T(8,128)(2,1)S(1)} %pad_maximum_fusion), channel_id=1, source_target_pairs={{0,2},{1,3},{2,0},{3,1},{4,6},{5,7},{6,4},{7,5},{8,10},{9,11},{10,... | collective-permute-start | bytes 2359304 | tf_op jit(solution)/shard_map/ppermute | solution.py:592
  110.1 0.2 collective-permute-start.22
  110.4 2.4 %collective-permute-done.19 = bf16[192,2048]{1,0:T(8,128)(2,1)S(1)} collective-permute-done((bf16[192,2048]{1,0:T(8,128)(2,1)}, bf16[192,2048]{1,0:T(8,128)(2,1)S(1)}, u32[]{:S(2)}, u32[]{:S(2)}) %collective-permute-start.19) | collective-permute-done | bytes 786464 | tf_op jit(solution)/shard_map/ppermute | solution.py:592
  112.8 0.5 collective-permute-start.24
  113.3 0.2 copy-done.13
  113.6 0.9 fusion.2
  114.5 0.0 copy-start.14
  114.5 0.7 copy-done.14
  115.3 1.6 %collective-permute-start.26 = (bf16[1,96,2048]{2,1,0:T(8,128)(2,1)}, bf16[1,96,2048]{2,1,0:T(8,128)(2,1)S(1)}, u32[]{:S(2)}, u32[]{:S(2)}) collective-permute-start(bf16[1,96,2048]{2,1,0:T(8,128)(2,1)} %get-tuple-element.95), channel_id=1, source_target_pairs={{0,4},{1,5},{2,6},{3,7},{4,0},{5,1},{6,2},{7,3},{8,12},{9,13},{10,... | collective-permute-start | bytes 1179656 | tf_op jit(solution)/shard_map/ppermute | solution.py:592
  116.8 3.1 %assemble.1.base_ref = bf16[384,4096]{1,0:T(8,128)(2,1)} custom-call(s32[1]{0:T(128)} %bitcast.chip_ref, s32[1]{0:T(128)} %bitcast.1.core_ref, bf16[96,2048]{1,0:T(8,128)(2,1)} %copy-done, bf16[96,2048]{1,0:T(8,128)(2,1)} %copy-done.3, bf16[96,2048]{1,0:T(8,128)(2,1)} %copy-done.13, bf16[96,2048]{1,0:T(8,128)(2,1)} %copy-done.14), custom_call_target="tpu_custom_call" | custom-call | flops 1000 | bytes 1000 | tf_op jit(solution)/shard_map/assemble/pallas_call | solution.py:421
  120.0 0.7 copy-done.11
  120.7 6.1 %weight_grad.1 = f32[1024,512]{1,0:T(8,128)} custom-call(s32[1]{0:T(128)} %bitcast.2.me_ref, s32[1]{0:T(128)} %bitcast.1.core_ref, bf16[384,4096]{1,0:T(8,128)(2,1)} %grad_ref.3, bf16[384,512]{1,0:T(8,128)(2,1)} %get-tuple-element.76.hidden_ref.refs_0_, bf16[384,512]{1,0:T(8,128)(2,1)} %copy-done.8, bf16[384,512]{1,0:T(8,128)(2,1)} %collective-permute-done.18.refs_2_, ...), custom_call_target="tpu_custom_call" | custom-call | flops 1000 | bytes 1000 | tf_op jit(solution)/shard_map/weight_grad/pallas_call | solution.py:526
  126.8 11.2 %collective-permute-done.25.own_ref = bf16[192,2048]{1,0:T(8,128)(2,1)S(1)} collective-permute-done((bf16[192,2048]{1,0:T(8,128)(2,1)S(1)}, bf16[192,2048]{1,0:T(8,128)(2,1)S(1)}, u32[]{:S(2)}, u32[]{:S(2)}) %collective-permute-start.25) | collective-permute-done | bytes 786464 | tf_op jit(solution)/shard_map/ppermute | solution.py:592
  138.0 0.1 convert_add_fusion
  138.1 0.1 dynamic-slice_bitcast_fusion.1
  138.2 0.1 collective-permute-start.28
  138.2 0.5 collective-permute-start.27
  138.7 1.2 collective-permute-done.28
  139.9 1.0 maximum_select_fusion
  140.9 0.2 collective-permute-done.27.theirs_ref
  141.1 0.9 copy-done.7
  142.0 2.5 %insert.1 = bf16[384,4096]{1,0:T(8,128)(2,1)} custom-call(s32[1]{0:T(128)} %bitcast.chip_ref, s32[1]{0:T(128)} %bitcast.1.core_ref, bf16[192,2048]{1,0:T(8,128)(2,1)} %copy-done.6, bf16[192,2048]{1,0:T(8,128)(2,1)} %copy-done.7, bf16[384,4096]{1,0:T(8,128)(2,1)} %assemble.1.base_ref), custom_call_target="tpu_custom_call", output_to_operand_aliasing={{}: (4, {})} | custom-call | flops 1000 | bytes 1000 | tf_op jit(solution)/shard_map/insert/pallas_call | solution.py:406
  (57 shorter events, 0.1 us)
Async XLA Ops:
  0.6 69.8 %collective-permute-start.16 = (bf16[3,4096,512]{2,1,0:T(8,128)(2,1)}, bf16[3,4096,512]{2,1,0:T(8,128)(2,1)}, u32[]{:S(2)}, u32[]{:S(2)}) collective-permute-start(bf16[3,4096,512]{2,1,0:T(8,128)(2,1)} %bitcast.28), channel_id=1, source_target_pairs={{0,1},{1,0},{2,3},{3,2},{4,5},{5,4},{6,7},{7,6},{8,9},{9,8},{10,11... | collective-permute-start | bytes 37748744 | tf_op jit(solution)/shard_map/ppermute | solution.py:592
  1.1 31.3 %collective-permute-start.6 = (bf16[4096,512]{1,0:T(8,128)(2,1)}, bf16[4096,512]{1,0:T(8,128)(2,1)}, u32[]{:S(2)}, u32[]{:S(2)}) collective-permute-start(bf16[4096,512]{1,0:T(8,128)(2,1)} %weight_ref.3), channel_id=1, source_target_pairs={{0,1},{1,0},{2,3},{3,2},{4,5},{5,4},{6,7},{7,6},{8,9},{9,8},{10,11... | collective-permute-start | bytes 12582920 | tf_op jit(solution)/shard_map/ppermute | solution.py:592
  2.8 9.0 %copy-start.15 = (f32[40,384]{1,0:T(8,128)}, f32[40,384]{1,0:T(8,128)S(1)}, u32[]{:S(2)}) copy-start(f32[40,384]{1,0:T(8,128)S(1)} %pad_select_fusion.refs_0_.ids_ref) | copy-start | bytes 184324
  2.8 9.0 %collective-permute-start = (f32[40,384]{1,0:T(8,128)S(1)}, f32[40,384]{1,0:T(8,128)S(1)}, u32[]{:S(2)}, u32[]{:S(2)}) collective-permute-start(f32[40,384]{1,0:T(8,128)S(1)} %pad_select_fusion.refs_0_.ids_ref), channel_id=1, source_target_pairs={{0,8},{8,0},{16,24},{24,16},{1,9},{9,1},{17,25},{25,17},{2,10},{10... | collective-permute-start | bytes 184328 | tf_op jit(solution)/shard_map/ppermute | solution.py:583
  5.8 6.0 %collective-permute-start.1 = (f32[40,384]{1,0:T(8,128)S(1)}, f32[40,384]{1,0:T(8,128)S(1)}, u32[]{:S(2)}, u32[]{:S(2)}) collective-permute-start(f32[40,384]{1,0:T(8,128)S(1)} %pad_select_fusion.refs_0_.ids_ref), channel_id=1, source_target_pairs={{0,16},{8,24},{16,0},{24,8},{1,17},{9,25},{17,1},{25,9},{2,18},{10... | collective-permute-start | bytes 184328 | tf_op jit(solution)/shard_map/ppermute | solution.py:583
  7.3 5.1 %collective-permute-start.2 = (f32[40,384]{1,0:T(8,128)S(1)}, f32[40,384]{1,0:T(8,128)S(1)}, u32[]{:S(2)}, u32[]{:S(2)}) collective-permute-start(f32[40,384]{1,0:T(8,128)S(1)} %pad_select_fusion.refs_0_.ids_ref), channel_id=1, source_target_pairs={{0,24},{8,16},{16,8},{24,0},{1,25},{9,17},{17,9},{25,1},{2,26},{10... | collective-permute-start | bytes 184328 | tf_op jit(solution)/shard_map/ppermute | solution.py:583
  11.8 4.1 %copy-start.19 = (f32[40,384]{1,0:T(8,128)}, f32[40,384]{1,0:T(8,128)S(1)}, u32[]{:S(2)}) copy-start(f32[40,384]{1,0:T(8,128)S(1)} %collective-permute-done.refs_1_) | copy-start | bytes 184324
  11.8 4.1 %copy-start.20 = (f32[40,384]{1,0:T(8,128)}, f32[40,384]{1,0:T(8,128)S(1)}, u32[]{:S(2)}) copy-start(f32[40,384]{1,0:T(8,128)S(1)} %collective-permute-done.1.refs_2_) | copy-start | bytes 184324
  12.4 3.5 %copy-start.21 = (f32[40,384]{1,0:T(8,128)}, f32[40,384]{1,0:T(8,128)S(1)}, u32[]{:S(2)}) copy-start(f32[40,384]{1,0:T(8,128)S(1)} %collective-permute-done.2.refs_3_) | copy-start | bytes 184324
  12.4 19.6 %collective-permute-start.3 = (bf16[512,384]{1,0:T(8,128)(2,1)}, bf16[512,384]{1,0:T(8,128)(2,1)S(1)}, u32[]{:S(2)}, u32[]{:S(2)}) collective-permute-start(bf16[512,384]{1,0:T(8,128)(2,1)} %hidden_grad.1.refs_4_), channel_id=1, source_target_pairs={{0,8},{8,0},{16,24},{24,16},{1,9},{9,1},{17,25},{25,17},{2,10},{10... | collective-permute-start | bytes 1179656 | tf_op jit(solution)/shard_map/ppermute | solution.py:583
  13.8 18.6 %collective-permute-start.4 = (bf16[512,384]{1,0:T(8,128)(2,1)}, bf16[512,384]{1,0:T(8,128)(2,1)S(1)}, u32[]{:S(2)}, u32[]{:S(2)}) collective-permute-start(bf16[512,384]{1,0:T(8,128)(2,1)} %hidden_grad.1.refs_4_), channel_id=1, source_target_pairs={{0,16},{8,24},{16,0},{24,8},{1,17},{9,25},{17,1},{25,9},{2,18},{10... | collective-permute-start | bytes 1179656 | tf_op jit(solution)/shard_map/ppermute | solution.py:583
  15.4 17.1 %collective-permute-start.5 = (bf16[512,384]{1,0:T(8,128)(2,1)}, bf16[512,384]{1,0:T(8,128)(2,1)S(1)}, u32[]{:S(2)}, u32[]{:S(2)}) collective-permute-start(bf16[512,384]{1,0:T(8,128)(2,1)} %hidden_grad.1.refs_4_), channel_id=1, source_target_pairs={{0,24},{8,16},{16,8},{24,0},{1,25},{9,17},{17,9},{25,1},{2,26},{10... | collective-permute-start | bytes 1179656 | tf_op jit(solution)/shard_map/ppermute | solution.py:583
  32.0 11.6 %copy-start.16 = (bf16[512,384]{1,0:T(8,128)(2,1)}, bf16[512,384]{1,0:T(8,128)(2,1)S(1)}, u32[]{:S(2)}) copy-start(bf16[512,384]{1,0:T(8,128)(2,1)S(1)} %collective-permute-done.3.refs_5_) | copy-start | bytes 1179652
  32.5 0.8 copy-start.17
  32.5 0.9 copy-start.18
  33.3 2.1 %collective-permute-start.7 = (bf16[384,512]{1,0:T(8,128)(2,1)}, bf16[384,512]{1,0:T(8,128)(2,1)S(1)}, u32[]{:S(2)}, u32[]{:S(2)}) collective-permute-start(bf16[384,512]{1,0:T(8,128)(2,1)} %get-tuple-element.76.hidden_ref.refs_0_), channel_id=1, source_target_pairs={{0,1},{1,0},{2,3},{3,2},{4,5},{5,4},{6,7},{7,6},{8,9},{9,8},{10,11... | collective-permute-start | bytes 1179656 | tf_op jit(solution)/shard_map/ppermute | solution.py:592
  35.4 0.7 copy-start.9
  43.6 17.4 %collective-permute-start.13 = (bf16[384,512]{1,0:T(8,128)(2,1)S(1)}, bf16[384,512]{1,0:T(8,128)(2,1)}, u32[]{:S(2)}, u32[]{:S(2)}) collective-permute-start(bf16[384,512]{1,0:T(8,128)(2,1)S(1)} %get-tuple-element.68), channel_id=1, source_target_pairs={{0,8},{8,0},{16,24},{24,16},{1,9},{9,1},{17,25},{25,17},{2,10},{10... | collective-permute-start | bytes 1179656 | tf_op jit(solution)/shard_map/ppermute | solution.py:583
  44.9 16.1 %collective-permute-start.14 = (bf16[384,512]{1,0:T(8,128)(2,1)S(1)}, bf16[384,512]{1,0:T(8,128)(2,1)}, u32[]{:S(2)}, u32[]{:S(2)}) collective-permute-start(bf16[384,512]{1,0:T(8,128)(2,1)S(1)} %get-tuple-element.69), channel_id=1, source_target_pairs={{0,16},{8,24},{16,0},{24,8},{1,17},{9,25},{17,1},{25,9},{2,18},{10... | collective-permute-start | bytes 1179656 | tf_op jit(solution)/shard_map/ppermute | solution.py:583
  46.3 19.7 %collective-permute-start.8 = (bf16[192,2048]{1,0:T(8,128)(2,1)}, bf16[192,2048]{1,0:T(8,128)(2,1)}, u32[]{:S(2)}, u32[]{:S(2)}) collective-permute-start(bf16[192,2048]{1,0:T(8,128)(2,1)} %get-tuple-element.59), channel_id=1, source_target_pairs={{0,2},{1,3},{2,0},{3,1},{4,6},{5,7},{6,4},{7,5},{8,10},{9,11},{10,... | collective-permute-start | bytes 2359304 | tf_op jit(solution)/shard_map/ppermute | solution.py:592
  47.8 13.3 %copy-start.1 = (bf16[384,512]{1,0:T(8,128)(2,1)S(1)}, bf16[384,512]{1,0:T(8,128)(2,1)}, u32[]{:S(2)}) copy-start(bf16[384,512]{1,0:T(8,128)(2,1)} %get-tuple-element.76.hidden_ref.refs_0_) | copy-start | bytes 1179652
  47.8 18.1 %copy-start.2 = (f32[192,2048]{1,0:T(8,128)S(1)}, f32[192,2048]{1,0:T(8,128)}, u32[]{:S(2)}) copy-start(f32[192,2048]{1,0:T(8,128)} %get-tuple-element.58) | copy-start | bytes 4718596
  61.0 9.4 %collective-permute-start.15 = (bf16[3,384,512]{2,1,0:T(8,128)(2,1)}, bf16[3,384,512]{2,1,0:T(8,128)(2,1)S(1)}, u32[]{:S(2)}, u32[]{:S(2)}) collective-permute-start(bf16[3,384,512]{2,1,0:T(8,128)(2,1)} %backward_conv.1.grad_ref), channel_id=1, source_target_pairs={{0,1},{1,0},{2,3},{3,2},{4,5},{5,4},{6,7},{7,6},{8,9},{9,8},{10,11... | collective-permute-start | bytes 3538952 | tf_op jit(solution)/shard_map/ppermute | solution.py:592
  61.1 20.6 %collective-permute-start.17 = (bf16[384,512]{1,0:T(8,128)(2,1)S(1)}, bf16[384,512]{1,0:T(8,128)(2,1)S(1)}, u32[]{:S(2)}, u32[]{:S(2)}) collective-permute-start(bf16[384,512]{1,0:T(8,128)(2,1)S(1)} %copy-done.1), channel_id=1, source_target_pairs={{0,8},{8,0},{16,24},{24,16},{1,9},{9,1},{17,25},{25,17},{2,10},{10... | collective-permute-start | bytes 1179656 | tf_op jit(solution)/shard_map/ppermute | solution.py:583
  62.2 19.5 %collective-permute-start.18 = (bf16[384,512]{1,0:T(8,128)(2,1)S(1)}, bf16[384,512]{1,0:T(8,128)(2,1)}, u32[]{:S(2)}, u32[]{:S(2)}) collective-permute-start(bf16[384,512]{1,0:T(8,128)(2,1)S(1)} %copy-done.1), channel_id=1, source_target_pairs={{0,16},{8,24},{16,0},{24,8},{1,17},{9,25},{17,1},{25,9},{2,18},{10... | collective-permute-start | bytes 1179656 | tf_op jit(solution)/shard_map/ppermute | solution.py:583
  67.8 19.9 %collective-permute-start.9 = (bf16[1,96,2048]{2,1,0:T(8,128)(2,1)}, bf16[1,96,2048]{2,1,0:T(8,128)(2,1)}, u32[]{:S(2)}, u32[]{:S(2)}) collective-permute-start(bf16[1,96,2048]{2,1,0:T(8,128)(2,1)} %fusion.1), channel_id=1, source_target_pairs={{0,4},{1,5},{2,6},{3,7},{4,0},{5,1},{6,2},{7,3},{8,12},{9,13},{10,... | collective-permute-start | bytes 1179656 | tf_op jit(solution)/shard_map/ppermute | solution.py:592
  70.4 18.6 %copy-start.12 = (bf16[384,512]{1,0:T(8,128)(2,1)S(1)}, bf16[384,512]{1,0:T(8,128)(2,1)}, u32[]{:S(2)}) copy-start(bf16[384,512]{1,0:T(8,128)(2,1)} %get-tuple-element.80) | copy-start | bytes 1179652
  70.4 1.0 copy-start.5
  81.7 31.9 %copy-start.4 = (f32[192,2048]{1,0:T(8,128)S(1)}, f32[192,2048]{1,0:T(8,128)}, u32[]{:S(2)}) copy-start(f32[192,2048]{1,0:T(8,128)} %get-tuple-element.85) | copy-start | bytes 4718596
  81.7 26.1 %copy-start.8 = (bf16[384,512]{1,0:T(8,128)(2,1)}, bf16[384,512]{1,0:T(8,128)(2,1)S(1)}, u32[]{:S(2)}) copy-start(bf16[384,512]{1,0:T(8,128)(2,1)S(1)} %collective-permute-done.17.refs_1_) | copy-start | bytes 1179652
  81.7 31.1 %collective-permute-start.19 = (bf16[192,2048]{1,0:T(8,128)(2,1)}, bf16[192,2048]{1,0:T(8,128)(2,1)S(1)}, u32[]{:S(2)}, u32[]{:S(2)}) collective-permute-start(bf16[192,2048]{1,0:T(8,128)(2,1)} %get-tuple-element.79), channel_id=1, source_target_pairs={{0,2},{1,3},{2,0},{3,1},{4,6},{5,7},{6,4},{7,5},{8,10},{9,11},{10,... | collective-permute-start | bytes 2359304 | tf_op jit(solution)/shard_map/ppermute | solution.py:592
  88.9 25.6 %copy-start = (bf16[96,2048]{1,0:T(8,128)(2,1)}, bf16[96,2048]{1,0:T(8,128)(2,1)S(1)}, u32[]{:S(2)}) copy-start(bf16[96,2048]{1,0:T(8,128)(2,1)S(1)} %fusion.3.refs_0_) | copy-start | bytes 1179652
  88.9 18.9 %collective-permute-start.10 = (bf16[96,2048]{1,0:T(8,128)(2,1)S(1)}, bf16[96,2048]{1,0:T(8,128)(2,1)S(1)}, u32[]{:S(2)}, u32[]{:S(2)}) collective-permute-start(bf16[96,2048]{1,0:T(8,128)(2,1)S(1)} %fusion.3.refs_0_), channel_id=1, source_target_pairs={{0,4},{1,5},{2,6},{3,7},{4,0},{5,1},{6,2},{7,3},{8,12},{9,13},{10,... | collective-permute-start | bytes 1179656 | tf_op jit(solution)/shard_map/ppermute | solution.py:592
  89.0 18.9 %collective-permute-start.20 = (bf16[384,512]{1,0:T(8,128)(2,1)S(1)}, bf16[384,512]{1,0:T(8,128)(2,1)}, u32[]{:S(2)}, u32[]{:S(2)}) collective-permute-start(bf16[384,512]{1,0:T(8,128)(2,1)S(1)} %copy-done.12), channel_id=1, source_target_pairs={{0,24},{8,16},{16,8},{24,0},{1,25},{9,17},{17,9},{25,1},{2,26},{10... | collective-permute-start | bytes 1179656 | tf_op jit(solution)/shard_map/ppermute | solution.py:583
  89.9 20.2 %collective-permute-start.21 = (bf16[384,512]{1,0:T(8,128)(2,1)S(1)}, bf16[384,512]{1,0:T(8,128)(2,1)S(1)}, u32[]{:S(2)}, u32[]{:S(2)}) collective-permute-start(bf16[384,512]{1,0:T(8,128)(2,1)S(1)} %copy-done.1), channel_id=1, source_target_pairs={{0,24},{8,16},{16,8},{24,0},{1,25},{9,17},{17,9},{25,1},{2,26},{10... | collective-permute-start | bytes 1179656 | tf_op jit(solution)/shard_map/ppermute | solution.py:583
  92.0 20.8 %collective-permute-start.11 = (bf16[96,2048]{1,0:T(8,128)(2,1)S(1)}, bf16[96,2048]{1,0:T(8,128)(2,1)S(1)}, u32[]{:S(2)}, u32[]{:S(2)}) collective-permute-start(bf16[96,2048]{1,0:T(8,128)(2,1)S(1)} %fusion.3.refs_0_), channel_id=1, source_target_pairs={{0,1},{1,0},{2,3},{3,2},{4,5},{5,4},{6,7},{7,6},{8,9},{9,8},{10,11... | collective-permute-start | bytes 1179656 | tf_op jit(solution)/shard_map/ppermute | solution.py:592
  107.8 6.7 %copy-start.3 = (bf16[96,2048]{1,0:T(8,128)(2,1)}, bf16[96,2048]{1,0:T(8,128)(2,1)S(1)}, u32[]{:S(2)}) copy-start(bf16[96,2048]{1,0:T(8,128)(2,1)S(1)} %collective-permute-done.10.refs_1_) | copy-start | bytes 1179652
  107.8 6.7 %collective-permute-start.12 = (bf16[96,2048]{1,0:T(8,128)(2,1)S(1)}, bf16[96,2048]{1,0:T(8,128)(2,1)S(1)}, u32[]{:S(2)}, u32[]{:S(2)}) collective-permute-start(bf16[96,2048]{1,0:T(8,128)(2,1)S(1)} %collective-permute-done.10.refs_1_), channel_id=1, source_target_pairs={{0,1},{1,0},{2,3},{3,2},{4,5},{5,4},{6,7},{7,6},{8,9},{9,8},{10,11... | collective-permute-start | bytes 1179656 | tf_op jit(solution)/shard_map/ppermute | solution.py:592
  107.9 30.1 %collective-permute-start.25 = (bf16[192,2048]{1,0:T(8,128)(2,1)S(1)}, bf16[192,2048]{1,0:T(8,128)(2,1)S(1)}, u32[]{:S(2)}, u32[]{:S(2)}) collective-permute-start(bf16[192,2048]{1,0:T(8,128)(2,1)S(1)} %pad_maximum_fusion), channel_id=1, source_target_pairs={{0,2},{1,3},{2,0},{3,1},{4,6},{5,7},{6,4},{7,5},{8,10},{9,11},{10,... | collective-permute-start | bytes 2359304 | tf_op jit(solution)/shard_map/ppermute | solution.py:592
  110.1 3.2 %copy-start.10 = (bf16[384,512]{1,0:T(8,128)(2,1)}, bf16[384,512]{1,0:T(8,128)(2,1)S(1)}, u32[]{:S(2)}) copy-start(bf16[384,512]{1,0:T(8,128)(2,1)S(1)} %collective-permute-done.21.refs_3_) | copy-start | bytes 1179652
  110.1 9.8 %collective-permute-start.22 = (bf16[384,512]{1,0:T(8,128)(2,1)}, bf16[384,512]{1,0:T(8,128)(2,1)S(1)}, u32[]{:S(2)}, u32[]{:S(2)}) collective-permute-start(bf16[384,512]{1,0:T(8,128)(2,1)} %collective-permute-done.13.refs_4_), channel_id=1, source_target_pairs={{0,1},{1,0},{2,3},{3,2},{4,5},{5,4},{6,7},{7,6},{8,9},{9,8},{10,11... | collective-permute-start | bytes 1179656 | tf_op jit(solution)/shard_map/ppermute | solution.py:592
  112.8 7.2 %collective-permute-start.23 = (bf16[384,512]{1,0:T(8,128)(2,1)}, bf16[384,512]{1,0:T(8,128)(2,1)}, u32[]{:S(2)}, u32[]{:S(2)}) collective-permute-start(bf16[384,512]{1,0:T(8,128)(2,1)} %collective-permute-done.14.refs_5_), channel_id=1, source_target_pairs={{0,1},{1,0},{2,3},{3,2},{4,5},{5,4},{6,7},{7,6},{8,9},{9,8},{10,11... | collective-permute-start | bytes 1179656 | tf_op jit(solution)/shard_map/ppermute | solution.py:592
  112.8 0.7 copy-start.13
  112.8 7.1 %collective-permute-start.24 = (bf16[384,512]{1,0:T(8,128)(2,1)}, bf16[384,512]{1,0:T(8,128)(2,1)}, u32[]{:S(2)}, u32[]{:S(2)}) collective-permute-start(bf16[384,512]{1,0:T(8,128)(2,1)} %collective-permute-done.20.refs_6_), channel_id=1, source_target_pairs={{0,1},{1,0},{2,3},{3,2},{4,5},{5,4},{6,7},{7,6},{8,9},{9,8},{10,11... | collective-permute-start | bytes 1179656 | tf_op jit(solution)/shard_map/ppermute | solution.py:592
  114.5 0.7 copy-start.14
  115.3 22.8 %collective-permute-start.26 = (bf16[1,96,2048]{2,1,0:T(8,128)(2,1)}, bf16[1,96,2048]{2,1,0:T(8,128)(2,1)S(1)}, u32[]{:S(2)}, u32[]{:S(2)}) collective-permute-start(bf16[1,96,2048]{2,1,0:T(8,128)(2,1)} %get-tuple-element.95), channel_id=1, source_target_pairs={{0,4},{1,5},{2,6},{3,7},{4,0},{5,1},{6,2},{7,3},{8,12},{9,13},{10,... | collective-permute-start | bytes 1179656 | tf_op jit(solution)/shard_map/ppermute | solution.py:592
  120.0 0.7 copy-start.11
  138.0 2.9 %copy-start.6 = (bf16[192,2048]{1,0:T(8,128)(2,1)}, bf16[192,2048]{1,0:T(8,128)(2,1)S(1)}, u32[]{:S(2)}) copy-start(bf16[192,2048]{1,0:T(8,128)(2,1)S(1)} %collective-permute-done.25.own_ref) | copy-start | bytes 2359300
  138.2 1.8 %collective-permute-start.28 = (f32[48,2048]{1,0:T(8,128)S(1)}, f32[48,2048]{1,0:T(8,128)S(1)}, u32[]{:S(2)}, u32[]{:S(2)}) collective-permute-start(f32[48,2048]{1,0:T(8,128)S(1)} %get-tuple-element.98), channel_id=1, source_target_pairs={{0,1},{1,0},{2,3},{3,2},{4,5},{5,4},{6,7},{7,6},{8,9},{9,8},{10,11... | collective-permute-start | bytes 1179656 | tf_op jit(solution)/shard_map/ppermute | solution.py:592
  138.2 2.8 %collective-permute-start.27 = (bf16[192,2048]{1,0:T(8,128)(2,1)S(1)}, bf16[192,2048]{1,0:T(8,128)(2,1)S(1)}, u32[]{:S(2)}, u32[]{:S(2)}) collective-permute-start(bf16[192,2048]{1,0:T(8,128)(2,1)S(1)} %collective-permute-done.25.own_ref), channel_id=1, source_target_pairs={{0,1},{1,0},{2,3},{3,2},{4,5},{5,4},{6,7},{7,6},{8,9},{9,8},{10,11... | collective-permute-start | bytes 2359304 | tf_op jit(solution)/shard_map/ppermute | solution.py:592
  141.1 0.9 copy-start.7

commit v5 on v4

--- a/solution.py
+++ b/solution.py
@@ -106,34 +106,31 @@
 
 
 def project_kernel(
-    chips, core_ref, chip_ref, hidden_ref, other_ref, weight_ref, other_weight_ref, ids_ref, letters_ref,
-    send_ref, kept_ref, weight, arrived, other_weight, other_arrived, total, send, kept, left, letters, letters_arrived,
+    chips, core_ref, chip_ref, hidden_ref, other_ref, weight_ref, other_weight_ref,
+    send_ref, kept_ref, weight, arrived, other_weight, other_arrived, total, send, kept, left, hidden, other, came,
 ):
+    operands = [
+        pltpu.make_async_copy(hidden_ref, hidden, came.at[0]),
+        pltpu.make_async_copy(other_ref, other, came.at[1]),
+    ]
+    for copy in operands:
+        copy.start()
     half = weight.shape[0]
     start = core_ref[0] * half
     copies = start_rows(weight_ref, start, weight, arrived)
     other_copies = start_rows(other_weight_ref, start, other_weight, other_arrived)
-    own_columns = pl.ds(pl.multiple_of(start, half), half)
-    letters_copy = pltpu.make_async_copy(letters_ref.at[FIRST_ID : FIRST_ID + IDS, own_columns], letters, letters_arrived)
-    letters_copy.start()
     rows = total.shape[0] // chips
-    lane = lax.broadcasted_iota(jnp.int32, (IDS, total.shape[0]), 1)
-    first = chip_ref[0] * rows
-    marks = one_hot(ids_ref[ids_ref.shape[0] - 8 : ids_ref.shape[0] - 7].astype(jnp.int32), 1)
-    marks = jnp.where(jnp.logical_and(lane >= first, lane < first + rows), marks, 0.0).astype(bf16)
-    letters_copy.wait()
     chunk = half // len(copies)
-    hidden, other = hidden_ref[...], other_ref[...]
+    for copy in operands:
+        copy.wait()
     leaving = []
     for index in range(len(copies)):
         columns = slice(index * chunk, (index + 1) * chunk)
         copies[index].wait()
         other_copies[index].wait()
-        total[...] = (
-            lax.dot_general(hidden, weight[columns], CONTRACT_LAST, preferred_element_type=f32)
-            + lax.dot_general(other, other_weight[columns], CONTRACT_LAST, preferred_element_type=f32)
-            + expand(marks, letters[:, columns])
-        )
+        total[...] = lax.dot_general(
+            hidden[...], weight[columns], CONTRACT_LAST, preferred_element_type=f32
+        ) + lax.dot_general(other[...], other_weight[columns], CONTRACT_LAST, preferred_element_type=f32)
         split_blocks(total, chip_ref[0], rows, send, kept, columns)
         leaving += write_out(((send, send_ref), (kept, kept_ref)), columns, left, 2 * index)
     for copy in leaving:
@@ -189,20 +186,22 @@
     inverse = lax.rsqrt(jnp.mean(values * values, axis=-1, keepdims=True) + 1e-06)
     normed[...] = (values * inverse * gain_ref[...][None, :]).astype(bf16)
 
-    def one_matrix(group, carry):
-        tiles = toeplitz_tiles(filters[pl.ds(group, 1), :], blocks, False)
-        for q in range(blocks):
-            matrices[group, (blocks - 1 - q) * LANES : (blocks - q) * LANES] = tiles[q]
+    table[...] = jnp.zeros(table.shape, f32)
+    share = groups // chunks
+
+    def one_chunk(index, carry):
+        rows = pl.ds(pl.multiple_of(index * chunk, chunk), chunk)
+        pltpu.make_async_copy(weight_ref.at[:, rows], weight.at[:, rows], arrived.at[index]).wait()
+        for offset in range(share):
+            group = index * share + offset
+            tiles = toeplitz_tiles(filters[pl.ds(group, 1), :], blocks, False)
+            for q in range(blocks):
+                matrices[group, (blocks - 1 - q) * LANES : (blocks - q) * LANES] = tiles[q]
+        for part in range(3):
+            table[part] += jnp.dot(normed[:, rows], weight[part, rows], preferred_element_type=f32)
         return carry
 
-    for index in range(chunks):
-        lax.fori_loop(index * groups // chunks, (index + 1) * groups // chunks, one_matrix, 0)
-        rows = slice(index * chunk, (index + 1) * chunk)
-        copies[index].wait()
-        for part in range(3):
-            term = jnp.dot(normed[:, rows], weight[part, rows], preferred_element_type=f32)
-            table[part] = term if index == 0 else table[part] + term
-
+    lax.fori_loop(0, chunks, one_chunk, 0)
     table_copy = pltpu.make_async_copy(table, table_ref, left.at[0])
     table_copy.start()
     key_weights = tap_weights(taps_ref, table, 1)
@@ -233,11 +232,23 @@
     mixed_copy.wait()
 
 
-def backward_kernel(shards, me_ref, *refs):
+def backward_kernel(shards, me_ref, core_ref, *refs):
     slots, grad_slots = refs[:shards], refs[shards : 2 * shards]
-    table_ref, taps_ref, skip_ref, mixed_ref, out_ref = refs[2 * shards : 2 * shards + 5]
-    hot, filters, grads, signal, exact, long_part = refs[2 * shards + 5 :]
+    table_ref, taps_ref, skip_ref, mixed_ref, output_grad_ref, hidden_ref, out_ref = refs[2 * shards : 2 * shards + 7]
+    piece_refs = refs[2 * shards + 7 : 3 * shards + 6]
+    hot, filters, grads, signal, exact, long_part, pieces, came, left = refs[3 * shards + 6 :]
     me = me_ref[0]
+    share = output_grad_ref.shape[1] // shards
+    part = share // 2
+    incoming = []
+    for step in range(1, shards):
+        start = jnp.bitwise_xor(me, step) * share + core_ref[0] * part
+        source = output_grad_ref.at[:, pl.ds(pl.multiple_of(start, part), part)]
+        slot = pieces.at[step - 1]
+        incoming.append(pltpu.make_async_copy(source, slot.at[:, :part], came.at[2 * step - 2]))
+        incoming.append(pltpu.make_async_copy(hidden_ref, slot.at[:, part:], came.at[2 * step - 1]))
+    for copy in incoming:
+        copy.start()
     groups = filters.shape[0]
     local_rows = slots[0].shape[1]
     channels = table_ref.shape[2]
@@ -267,6 +278,12 @@
         exact[rows, :length] = mixed_grad
         signal[rows, :length] = mixed_grad.astype(bf16)
 
+    for copy in incoming:
+        copy.wait()
+    outgoing = []
+    for step in range(1, shards):
+        outgoing.append(pltpu.make_async_copy(pieces.at[step - 1], piece_refs[step - 1], left.at[step - 1]))
+        outgoing[-1].start()
     first = me * local_blocks
 
     def one_group(group, carry):
@@ -294,6 +311,8 @@
             column = 3 * tap + part
             total = total + columns[:, column : column + 1] * pltpu.roll(feature_grad, span - tap, axis=1)
         out_ref[part] = jnp.transpose(total[:, :local_rows]).astype(bf16)
+    for copy in outgoing:
+        copy.wait()
 
 
 def hidden_grad_kernel(grad_ref, weight_ref, out_ref, grad, weight, total, arrived):
@@ -350,23 +369,29 @@
         copy.wait()
 
 
-def weight_grad_kernel(shards, me_ref, core_ref, grad_ref, *refs):
-    hidden, mine, theirs = refs[:shards], refs[shards : 2 * shards - 1], refs[2 * shards - 1 : 3 * shards - 2]
-    out_ref, own, arrived = refs[3 * shards - 2 :]
+def weight_grad_kernel(shards, me_ref, core_ref, grad_ref, hidden_ref, *refs):
+    mine, theirs = refs[: shards - 1], refs[shards - 1 : 2 * shards - 2]
+    out_ref, own, arrived = refs[2 * shards - 2 :]
     share = own.shape[1]
     part = share // 2
     source = grad_ref.at[:, pl.ds(pl.multiple_of(me_ref[0] * share, share), share)]
     copy = pltpu.make_async_copy(source, own, arrived)
     copy.start()
-    for slots, side in ((mine, core_ref[0]), (theirs, 1 - core_ref[0])):
+    for pieces, side in ((mine, core_ref[0]), (theirs, 1 - core_ref[0])):
         total = None
-        for slot, shard_hidden in zip(slots, hidden[1:]):
-            term = expand(slot[...], shard_hidden[...])
+        for piece, with_hidden in zip(pieces, mine):
+            term = expand(piece[:, :part], with_hidden[:, part:])
             total = term if total is None else total + term
-        if slots is mine:
+        if pieces is mine:
             copy.wait()
         place = pl.ds(pl.multiple_of(side * part, part), part)
-        out_ref[place, :] = total + expand(own[:, place], hidden[0][...])
+        out_ref[place, :] = total + expand(own[:, place], hidden_ref[...])
+
+
+def pack_kernel(filters_ref, ids_ref, out_ref):
+    groups = filters_ref.shape[0]
+    out_ref[:groups] = filters_ref[...]
+    out_ref[groups:] = jnp.broadcast_to(ids_ref[...].astype(f32)[None, :], (8, ids_ref.shape[0]))
 
 
 def in_vmem(count):
@@ -467,13 +492,13 @@
     )(me, *slots, embed_table, norm_gain, weight, taps, skip_gain)
 
 
-def run_project(core, chip, chips, hidden, other_hidden, weight, other_weight, packed, embed_table):
+def run_project(core, chip, chips, hidden, other_hidden, weight, other_weight):
     rows, channels = hidden.shape
     half = weight.shape[0] // 2
     return pl.pallas_call(
         functools.partial(project_kernel, chips),
         out_shape=(jax.ShapeDtypeStruct((rows // 2, half), bf16), jax.ShapeDtypeStruct((rows // 2, half), f32)),
-        in_specs=[SMEM_SPEC, SMEM_SPEC, VMEM_SPEC, VMEM_SPEC, ANY_SPEC, ANY_SPEC, VMEM_SPEC, ANY_SPEC],
+        in_specs=[SMEM_SPEC, SMEM_SPEC] + [ANY_SPEC] * 4,
         out_specs=(ANY_SPEC, ANY_SPEC),
         scratch_shapes=[
             pltpu.VMEM((half, channels), bf16),
@@ -484,27 +509,30 @@
             pltpu.VMEM((rows // 2, half), bf16),
             pltpu.VMEM((rows // 2, half), f32),
             pltpu.SemaphoreType.DMA((8,)),
-            pltpu.VMEM((IDS, half), bf16),
-            pltpu.SemaphoreType.DMA,
+            pltpu.VMEM((rows, channels), bf16),
+            pltpu.VMEM((rows, channels), bf16),
+            pltpu.SemaphoreType.DMA((2,)),
         ],
         compiler_params=params(),
         cost_estimate=SMALL_COST,
         name="project",
-    )(core, chip, hidden, other_hidden, weight, other_weight, packed, embed_table)
-
-
-def run_backward(me, slots, grads, table, taps, skip_gain, mixed):
+    )(core, chip, hidden, other_hidden, weight, other_weight)
+
+
+def run_backward(me, core, slots, grads, table, taps, skip_gain, mixed, output_grad, hidden):
     shards = len(slots)
     local_rows = slots[0].shape[1]
     channels = table.shape[2]
     groups = slots[0].shape[0] - 8
     length = shards * local_rows
     span = local_rows + LANES
+    part = output_grad.shape[1] // (2 * shards)
     return pl.pallas_call(
         functools.partial(backward_kernel, shards),
-        out_shape=jax.ShapeDtypeStruct((3, local_rows, channels), bf16),
-        in_specs=[SMEM_SPEC] + in_vmem(2 * shards + 4),
-        out_specs=VMEM_SPEC,
+        out_shape=[jax.ShapeDtypeStruct((3, local_rows, channels), bf16)]
+        + [jax.ShapeDtypeStruct((local_rows, part + channels), bf16)] * (shards - 1),
+        in_specs=[SMEM_SPEC, SMEM_SPEC] + in_vmem(2 * shards + 4) + [ANY_SPEC, ANY_SPEC],
+        out_specs=[VMEM_SPEC] + [ANY_SPEC] * (shards - 1),
         scratch_shapes=[
             pltpu.VMEM((2 * taps.shape[0] * IDS, length + LANES), bf16),
             pltpu.VMEM((groups, length), f32),
@@ -512,27 +540,30 @@
             pltpu.VMEM((channels, 2 * length + LANES), bf16),
             pltpu.VMEM((channels, length + LANES), f32),
             pltpu.VMEM((channels, span), f32),
+            pltpu.VMEM((shards - 1, local_rows, part + channels), bf16),
+            pltpu.SemaphoreType.DMA((2 * shards - 2,)),
+            pltpu.SemaphoreType.DMA((shards - 1,)),
         ],
         compiler_params=params(),
         cost_estimate=LARGE_COST,
         name="backward_conv",
-    )(me, *slots, *grads, table, taps, skip_gain, mixed)
+    )(me, core, *slots, *grads, table, taps, skip_gain, mixed, output_grad, hidden)
 
 
 def run_weight_grad(me, core, output_grad, hidden, mine, theirs):
-    shards = len(hidden)
+    shards = len(mine) + 1
     rows, width = output_grad.shape
-    share, channels = width // shards, hidden[0].shape[1]
+    share, channels = width // shards, hidden.shape[1]
     return pl.pallas_call(
         functools.partial(weight_grad_kernel, shards),
         out_shape=jax.ShapeDtypeStruct((share, channels), f32),
-        in_specs=[SMEM_SPEC, SMEM_SPEC, ANY_SPEC] + in_vmem(3 * shards - 2),
+        in_specs=[SMEM_SPEC, SMEM_SPEC, ANY_SPEC] + in_vmem(2 * shards - 1),
         out_specs=VMEM_SPEC,
         scratch_shapes=[pltpu.VMEM((rows, share), bf16), pltpu.SemaphoreType.DMA],
         compiler_params=params(),
         cost_estimate=SMALL_COST,
         name="weight_grad",
-    )(me, core, output_grad, *hidden, *mine, *theirs)
+    )(me, core, output_grad, hidden, *mine, *theirs)
 
 
 def run_hidden_grad(output_grad, output_weight):
@@ -576,6 +607,18 @@
         cost_estimate=SMALL_COST,
         name="input_grad",
     )(core, chip, grad, other_grad, weight, other_weight)
+
+
+def run_pack(filters, ids):
+    return pl.pallas_call(
+        pack_kernel,
+        out_shape=jax.ShapeDtypeStruct((filters.shape[0] + 8, filters.shape[1]), f32),
+        in_specs=[VMEM_SPEC, VMEM_SPEC],
+        out_specs=VMEM_SPEC,
+        compiler_params=params(),
+        cost_estimate=SMALL_COST,
+        name="pack",
+    )(filters, ids)
 
 
 def ctx_exchange(value, step):
@@ -626,14 +669,11 @@
     me_tie, core_tie, chip_tie = scalar_array(me), scalar_array(core), scalar_array(chip)
     weight = jnp.transpose(input_weight, (1, 0, 2))
 
-    groups = filters.shape[0]
-    row_number = lax.broadcasted_iota(jnp.int32, (groups + 8, local_rows), 0)
-    id_row = jnp.broadcast_to(token_ids[None, :], (groups + 8, local_rows)).astype(f32)
-    packed = jnp.where(row_number < groups, jnp.pad(filters, ((0, 8), (0, 0))), id_row)
-    slots = gather_ctx(packed)
     half = width // 2
     levels = chips.bit_length() - 1
     block_rows = local_rows // chips
+    packed = run_pack(filters, token_ids)
+    slots = gather_ctx(packed)
     other_weight, other_input = tp_exchange(output_weight, 1), tp_exchange(weight, 1)
     hidden_grad = run_hidden_grad(output_grad, output_weight)
     arrived, hidden_grad, me_tie = together(slots[1:], hidden_grad, me_tie)
@@ -645,7 +685,7 @@
     )
     hidden, grad_slots, other_weight = together(hidden, grad_slots, other_weight)
     send, kept = run_project(
-        core_tie, chip_tie, chips, hidden, tp_exchange(hidden, 1), output_weight, other_weight, packed, embed_table
+        core_tie, chip_tie, chips, hidden, tp_exchange(hidden, 1), output_weight, other_weight
     )
 
     def pairs(value, which):
@@ -660,61 +700,56 @@
         return [pairs(term, which) for term in terms]
 
     blocks = (chips // 2, block_rows, half)
-    send, kept, me_tie, late_hidden = together(send, kept, me_tie, hidden)
+    near, others = range(1, shards // 2 + 1), range(shards // 2 + 1, shards)
+    send, kept, me_tie = together(send, kept, me_tie)
     out_arrived = tp_exchange(send, 2)
-
-    share = width // shards
-    part = share // 2
-
-    def ctx_piece(step):
-        start = jnp.bitwise_xor(me, step) * share + core * part
-        return lax.dynamic_slice_in_dim(output_grad, start, part, axis=1)
-
-    near, others = range(1, shards // 2 + 1), range(shards // 2 + 1, shards)
-    pieces = [ctx_piece(step) for step in range(1, shards)]
-    pieces, me_tie = together(pieces, me_tie)
-    near_grad = [ctx_exchange(pieces[step - 1], step) for step in near]
-    projection_grad = run_backward(me_tie, slots, grad_slots, table, short_weight, skip_gain, mixed)
-    projection_grad, near_grad, late_hidden = together(projection_grad, near_grad, late_hidden)
+    projection_grad, *pieces = run_backward(
+        me_tie, core_tie, slots, grad_slots, table, short_weight, skip_gain, mixed, output_grad, hidden
+    )
+    projection_grad, pieces = together(projection_grad, pieces)
     other_grad = tp_exchange(projection_grad, 1)
-    near_hidden = [ctx_exchange(late_hidden, step) for step in near]
+    near_pieces = [ctx_exchange(pieces[step - 1], step) for step in near]
     grad_send, grad_kept = run_input_grad(
         core_tie, chip_tie, chips, projection_grad, other_grad, weight, other_input
     )
     out_terms = [kept.reshape(blocks), out_arrived.reshape(blocks)]
     for bit in range(1, levels):
         out_terms = keep(out_terms, bit) + [tp_exchange(leaving(out_terms, bit), 2 << bit)]
-    grad_send, grad_kept, near_hidden, late_hidden, pieces = together(
-        grad_send, grad_kept, near_hidden, late_hidden, pieces
+    grad_send, grad_kept, pieces, near_pieces, late_ids = together(
+        grad_send, grad_kept, pieces, near_pieces, token_ids
     )
     grad_arrived = tp_exchange(grad_send, 2)
-    far_grad = [ctx_exchange(pieces[step - 1], step) for step in others]
-    far_hidden = [ctx_exchange(late_hidden, step) for step in others]
-
-    block = sum(term.astype(f32) for term in out_terms).reshape(block_rows, half).astype(bf16)
+    far_pieces = [ctx_exchange(pieces[step - 1], step) for step in others]
+
+    own_ids = lax.dynamic_slice_in_dim(late_ids, chip * block_rows, block_rows, axis=0)
+    own_hot = (own_ids[:, None] == jnp.arange(FIRST_ID, FIRST_ID + IDS)[None, :]).astype(bf16)
+    own_letters = lax.dynamic_slice(embed_table, (FIRST_ID, core * half), (IDS, half))
+    own_tokens = jnp.dot(own_hot, own_letters, preferred_element_type=f32)
+    block = sum(term.astype(f32) for term in out_terms).reshape(block_rows, half)
+    block = (own_tokens + block).astype(bf16)
     line, steps = [block], [[0]]
     for level in range(levels - 1):
         mask = chips >> level + 1
         held = line[0] if level == 0 else jnp.concatenate(line, axis=0)
-        line.append(tp_exchange(held, 2 * mask))
+        came = tp_exchange(held, 2 * mask)
+        line.append(came)
         steps.append([step ^ mask for group in steps for step in group])
-    grad_arrived, far_grad, far_hidden = together(grad_arrived, far_grad, far_hidden)
+    grad_arrived, far_pieces = together(grad_arrived, far_pieces)
     grad_terms = [grad_kept.reshape(blocks), grad_arrived.reshape(blocks)]
+    held = jnp.concatenate(line, axis=0)
     for bit in range(1, levels):
         grad_terms = keep(grad_terms, bit) + [tp_exchange(leaving(grad_terms, bit), 2 << bit)]
-    came = tp_exchange(jnp.concatenate(line, axis=0), 2)
+    came = tp_exchange(held, 2)
     came_steps = [step ^ 1 for group in steps for step in group]
 
     base = run_assemble(chips, steps, chip_tie, core_tie, line, [tp_exchange(value, 1) for value in line])
-    mine = near_grad + far_grad
+    mine = near_pieces + far_pieces
     output_weight_grad = run_weight_grad(
-        me_tie, core_tie, output_grad, [late_hidden] + near_hidden + far_hidden, mine,
-        [tp_exchange(value, 1) for value in mine],
+        me_tie, core_tie, output_grad, hidden, mine, [tp_exchange(value, 1) for value in mine]
     )
     kept_sum = sum(term.astype(f32) for term in grad_terms[:-1])
-    base, output_weight_grad, came, kept_sum, last = together(
-        base, output_weight_grad, came, kept_sum, grad_terms[-1]
-    )
+    base, output_weight_grad, came = together(base, output_weight_grad, came)
+    output_weight_grad, kept_sum, last = together(output_weight_grad, kept_sum, grad_terms[-1])
     total = (kept_sum + last.astype(f32)).reshape(2, block_rows // 2, half)
     my_rows, their_rows = pick(total, core), pick(total, 1 - core)
     other_columns = tp_exchange(their_rows, 1)

time: 145 us -> 142 us (0.979)
  waiting for transfers between devices: 39.6 us -> 45.6 us
  other arithmetic: 6.63 us -> 3.12 us
  local copies, waits for them, and re-layouts: 7.41 us -> 4.26 us
  starting transfers between devices: 26.9 us -> 24.9 us
    ppermute x12 -> x9, waiting for transfers between devices: 1.08 us -> 6.31 us  [ctx_exchange(): return lax.ppermute(value, 'ctx', [(i, i ^ step) for i in range(count)])]
    ppermute x12 -> x9, starting transfers between devices: 15.2 us -> 12 us  [ctx_exchange(): return lax.ppermute(value, 'ctx', [(i, i ^ step) for i in range(count)])]
    pallas_call x1, Pallas kernels: 16.1 us -> 13.3 us  [run_forward(): pl.pallas_call(functools.partial(forward_kernel, shards), grid=(1,), out_...]
    pallas_call x1 -> x2, Pallas kernels: 13.2 us -> 15.9 us  [the longest x1 14.4 us: run_backward(): pl.pallas_call(functools.partial(backward_kernel, shards), out_shape=[jax...]
    convert_element_type x2 -> x0, other arithmetic: 1.92 us -> none  [the longest x1 1.24 us: body(): sum((term.astype(f32) for term in out_terms)).reshape(block_rows, half)]
    unnamed x44 -> x34, local copies, waits for them, and re-layouts: 5.27 us -> 3.44 us
    pallas_call x1, Pallas kernels: 7.37 us -> 5.72 us  [run_project(): pl.pallas_call(functools.partial(project_kernel, chips), out_shape=(jax.S...]
  transfers between devices with their start and end apart: 29 -> 26, of which waited for: 9 -> 13; matrix products, arithmetic and copies ran while one was open for 6% -> 4% of each run, Pallas kernels for 42% -> 42%
where the time goes in v5:
time: 142 us
  Pallas kernels  61.6 us (43%)
  waiting for transfers between devices  45.6 us (32%)
  starting transfers between devices  24.9 us (18%)
  local copies, waits for them, and re-layouts  4.26 us (3%)
  other arithmetic  3.12 us (2%)
    ppermute x17, waiting for transfers between devices, tp_exchange(): return lax.ppermute(value, 'tp', [(i, i ^ mask) for i in range(count)])  39.3 us
    pallas_call x1, Pallas kernels, run_backward(): pl.pallas_call(functools.partial(backward_kernel, shards), out_shape=[jax...  14.4 us
    pallas_call x1, Pallas kernels, run_forward(): pl.pallas_call(functools.partial(forward_kernel, shards), grid=(1,), out_...  13.3 us
    ppermute x17, starting transfers between devices, tp_exchange(): return lax.ppermute(value, 'tp', [(i, i ^ mask) for i in range(count)])  12.9 us
    ppermute x9, starting transfers between devices, ctx_exchange(): return lax.ppermute(value, 'ctx', [(i, i ^ step) for i in range(count)])  12 us
    pallas_call x1, Pallas kernels, run_input_grad(): pl.pallas_call(functools.partial(input_grad_kernel, chips), out_shape=(ja...  10.2 us
    pallas_call x1, Pallas kernels, run_weight_grad(): pl.pallas_call(functools.partial(weight_grad_kernel, shards), out_shape=j...  6.45 us
    ppermute x9, waiting for transfers between devices, ctx_exchange(): return lax.ppermute(value, 'ctx', [(i, i ^ step) for i in range(count)])  6.31 us
  transfers between devices with their start and end apart: 26, of which 13 were waited for; matrix products, arithmetic and copies ran while one was open for 4% of the time, Pallas kernels for 42%

profile of v5, /device:TPU:0, one launch (start us, length us, event | category | flops | bytes accessed | tf_op | source)
XLA Modules:
  0.0 141.8 jit_solution(10759775059082253961)
XLA Ops:
  0.6 0.5 collective-permute-start.9
  1.1 0.1 collective-permute-start.6
  1.2 1.4 %pack.1.refs_0_ = f32[40,384]{1,0:T(8,128)} custom-call(f32[32,384]{1,0:T(8,128)} %filters_ref.1, s32[384]{0:T(512)} %ids_ref.1), custom_call_target="tpu_custom_call" | custom-call | flops 1000 | bytes 1000 | tf_op jit(solution)/shard_map/pack/pallas_call | solution.py:613
  2.7 2.9 %collective-permute-start = (f32[40,384]{1,0:T(8,128)}, f32[40,384]{1,0:T(8,128)S(1)}, u32[]{:S(2)}, u32[]{:S(2)}) collective-permute-start(f32[40,384]{1,0:T(8,128)} %pack.1.refs_0_), channel_id=1, source_target_pairs={{0,8},{8,0},{16,24},{24,16},{1,9},{9,1},{17,25},{25,17},{2,10},{10... | collective-permute-start | bytes 184328 | tf_op jit(solution)/shard_map/ppermute | solution.py:626
  5.6 1.5 %collective-permute-start.1 = (f32[40,384]{1,0:T(8,128)}, f32[40,384]{1,0:T(8,128)S(1)}, u32[]{:S(2)}, u32[]{:S(2)}) collective-permute-start(f32[40,384]{1,0:T(8,128)} %pack.1.refs_0_), channel_id=1, source_target_pairs={{0,16},{8,24},{16,0},{24,8},{1,17},{9,25},{17,1},{25,9},{2,18},{10... | collective-permute-start | bytes 184328 | tf_op jit(solution)/shard_map/ppermute | solution.py:626
  7.1 4.4 %hidden_grad.1.refs_4_ = bf16[512,384]{1,0:T(8,128)(2,1)} custom-call(bf16[384,4096]{1,0:T(8,128)(2,1)} %grad_ref.3, bf16[4096,512]{1,0:T(8,128)(2,1)} %weight_ref.3), custom_call_target="tpu_custom_call" | custom-call | flops 1000 | bytes 1000 | tf_op jit(solution)/shard_map/hidden_grad/pallas_call | solution.py:572
  11.5 0.0 collective-permute-done.refs_1_
  11.6 0.8 collective-permute-done.2.refs_3_
  12.4 1.2 collective-permute-start.3
  13.6 1.5 %collective-permute-start.4 = (bf16[512,384]{1,0:T(8,128)(2,1)}, bf16[512,384]{1,0:T(8,128)(2,1)S(1)}, u32[]{:S(2)}, u32[]{:S(2)}) collective-permute-start(bf16[512,384]{1,0:T(8,128)(2,1)} %hidden_grad.1.refs_4_), channel_id=1, source_target_pairs={{0,16},{8,24},{16,0},{24,8},{1,17},{9,25},{17,1},{25,9},{2,18},{10... | collective-permute-start | bytes 1179656 | tf_op jit(solution)/shard_map/ppermute | solution.py:626
  15.1 0.8 collective-permute-start.5
  15.9 13.3 %forward_conv.1 = (bf16[384,512]{1,0:T(8,128)(2,1)}, f32[512,512]{1,0:T(8,128)}, f32[3,32,512]{2,1,0:T(8,128)}) custom-call(s32[1]{0:T(128)} %bitcast.2.me_ref, f32[40,384]{1,0:T(8,128)} %pack.1.refs_0_, f32[40,384]{1,0:T(8,128)} %copy-done.14, f32[40,384]{1,0:T(8,128)} %copy-done.15, f32[40,384]{1,0:T(8,128)} %copy-done.16, bf16[512,4096]{1,0:T(8,128)(2,1)} %refs_4_.1, ...), custom_call_target="tpu_custom_call" | custom-call | flops 20000000000 | bytes 10000000 | tf_op jit(solution)/shard_map/forward_conv/pallas_call | solution.py:464
  29.2 0.0 collective-permute-done.3.refs_5_
  29.2 3.0 %collective-permute-done.4.refs_6_ = bf16[512,384]{1,0:T(8,128)(2,1)S(1)} collective-permute-done((bf16[512,384]{1,0:T(8,128)(2,1)}, bf16[512,384]{1,0:T(8,128)(2,1)S(1)}, u32[]{:S(2)}, u32[]{:S(2)}) %collective-permute-start.4) | collective-permute-done | bytes 393248 | tf_op jit(solution)/shard_map/ppermute | solution.py:626
  32.3 0.1 collective-permute-start.7
  32.4 1.9 %collective-permute-done.7.other_ref = bf16[384,512]{1,0:T(8,128)(2,1)S(1)} collective-permute-done((bf16[384,512]{1,0:T(8,128)(2,1)}, bf16[384,512]{1,0:T(8,128)(2,1)S(1)}, u32[]{:S(2)}, u32[]{:S(2)}) %collective-permute-start.7) | collective-permute-done | bytes 393248 | tf_op jit(solution)/shard_map/ppermute | solution.py:635
  34.3 0.7 copy-done.7
  35.0 5.7 %project.1 = (bf16[192,2048]{1,0:T(8,128)(2,1)}, f32[192,2048]{1,0:T(8,128)}) custom-call(s32[1]{0:T(128)} %bitcast.1.core_ref, s32[1]{0:T(128)} %bitcast.chip_ref, bf16[384,512]{1,0:T(8,128)(2,1)} %get-tuple-element.49.hidden_ref.refs_13_, bf16[384,512]{1,0:T(8,128)(2,1)} %copy-done.7, bf16[4096,512]{1,0:T(8,128)(2,1)} %weight_ref.3, ...), custom_call_target="tpu_custom_call" | custom-call | flops 1000 | bytes 1000 | tf_op jit(solution)/shard_map/project/pallas_call | solution.py:498
  40.7 1.6 %collective-permute-start.12 = (bf16[192,2048]{1,0:T(8,128)(2,1)}, bf16[192,2048]{1,0:T(8,128)(2,1)}, u32[]{:S(2)}, u32[]{:S(2)}) collective-permute-start(bf16[192,2048]{1,0:T(8,128)(2,1)} %get-tuple-element.68), channel_id=1, source_target_pairs={{0,2},{1,3},{2,0},{3,1},{4,6},{5,7},{6,4},{7,5},{8,10},{9,11},{10,... | collective-permute-start | bytes 2359304 | tf_op jit(solution)/shard_map/ppermute | solution.py:635
  42.4 14.4 %backward_conv.1 = (bf16[3,384,512]{2,1,0:T(8,128)(2,1)}, bf16[384,1024]{1,0:T(8,128)(2,1)}, bf16[384,1024]{1,0:T(8,128)(2,1)}, bf16[384,1024]{1,0:T(8,128)(2,1)}) custom-call(s32[1]{0:T(128)} %bitcast.2.me_ref, s32[1]{0:T(128)} %bitcast.1.core_ref, f32[40,384]{1,0:T(8,128)} %pack.1.refs_0_, f32[40,384]{1,0:T(8,128)} %copy-done.14, f32[40,384]{1,0:T(8,128)} %copy-done.15, ...), custom_call_target="tpu_custom_call" | custom-call | flops 20000000000 | bytes 10000000 | tf_op jit(solution)/shard_map/backward_conv/pallas_call | solution.py:530
  56.8 0.1 collective-permute-start.8
  56.9 1.3 collective-permute-start.10
  58.2 0.9 collective-permute-start.11
  59.1 1.6 %collective-permute-done.12 = bf16[192,2048]{1,0:T(8,128)(2,1)} collective-permute-done((bf16[192,2048]{1,0:T(8,128)(2,1)}, bf16[192,2048]{1,0:T(8,128)(2,1)}, u32[]{:S(2)}, u32[]{:S(2)}) %collective-permute-start.12) | collective-permute-done | bytes 786464 | tf_op jit(solution)/shard_map/ppermute | solution.py:635
  60.7 1.1 fusion.1
  61.8 2.6 %collective-permute-start.13 = (bf16[1,96,2048]{2,1,0:T(8,128)(2,1)S(1)}, bf16[1,96,2048]{2,1,0:T(8,128)(2,1)S(1)}, u32[]{:S(2)}, u32[]{:S(2)}) collective-permute-start(bf16[1,96,2048]{2,1,0:T(8,128)(2,1)S(1)} %fusion.1), channel_id=1, source_target_pairs={{0,4},{1,5},{2,6},{3,7},{4,0},{5,1},{6,2},{7,3},{8,12},{9,13},{10,... | collective-permute-start | bytes 1179656 | tf_op jit(solution)/shard_map/ppermute | solution.py:635
  64.4 0.0 collective-permute-done.9.other_weight_ref
  64.5 1.0 copy-done.4
  65.5 10.2 %input_grad.1 = (bf16[192,2048]{1,0:T(8,128)(2,1)}, f32[192,2048]{1,0:T(8,128)}) custom-call(s32[1]{0:T(128)} %bitcast.1.core_ref, s32[1]{0:T(128)} %bitcast.chip_ref, bf16[3,384,512]{2,1,0:T(8,128)(2,1)} %get-tuple-element.60.grad_ref, bf16[3,384,512]{2,1,0:T(8,128)(2,1)} %copy-done.4, bf16[3,4096,512]{2,1,0:T(8,128)(2,1)} %bitcast.30, ...), custom_call_target="tpu_custom_call" | custom-call | flops 1000 | bytes 1000 | tf_op jit(solution)/shard_map/input_grad/pallas_call | solution.py:592
  75.7 0.0 copy-start.3
  75.7 1.5 %collective-permute-done.10.refs_0_ = bf16[384,1024]{1,0:T(8,128)(2,1)} collective-permute-done((bf16[384,1024]{1,0:T(8,128)(2,1)}, bf16[384,1024]{1,0:T(8,128)(2,1)}, u32[]{:S(2)}, u32[]{:S(2)}) %collective-permute-start.10) | collective-permute-done | bytes 786464 | tf_op jit(solution)/shard_map/ppermute | solution.py:626
  77.2 0.9 collective-permute-done.11.refs_1_
  78.1 0.4 collective-permute-start.17
  78.6 1.8 %collective-permute-start.18 = (bf16[384,1024]{1,0:T(8,128)(2,1)S(1)}, bf16[384,1024]{1,0:T(8,128)(2,1)}, u32[]{:S(2)}, u32[]{:S(2)}) collective-permute-start(bf16[384,1024]{1,0:T(8,128)(2,1)S(1)} %copy-done.10), channel_id=1, source_target_pairs={{0,24},{8,16},{16,8},{24,0},{1,25},{9,17},{17,9},{25,1},{2,26},{10... | collective-permute-start | bytes 2359304 | tf_op jit(solution)/shard_map/ppermute | solution.py:626
  80.4 0.8 dynamic_slice.39
  81.2 0.4 collective-permute-done.13
  81.6 1.4 fusion.refs_0_
  83.0 2.2 %collective-permute-start.14 = (bf16[96,2048]{1,0:T(8,128)(2,1)S(1)}, bf16[96,2048]{1,0:T(8,128)(2,1)S(1)}, u32[]{:S(2)}, u32[]{:S(2)}) collective-permute-start(bf16[96,2048]{1,0:T(8,128)(2,1)S(1)} %fusion.refs_0_), channel_id=1, source_target_pairs={{0,4},{1,5},{2,6},{3,7},{4,0},{5,1},{6,2},{7,3},{8,12},{9,13},{10,... | collective-permute-start | bytes 1179656 | tf_op jit(solution)/shard_map/ppermute | solution.py:635
  85.2 0.5 collective-permute-start.19
  85.7 17.8 %collective-permute-done.14.refs_1_ = bf16[96,2048]{1,0:T(8,128)(2,1)S(1)} collective-permute-done((bf16[96,2048]{1,0:T(8,128)(2,1)S(1)}, bf16[96,2048]{1,0:T(8,128)(2,1)S(1)}, u32[]{:S(2)}, u32[]{:S(2)}) %collective-permute-start.14) | collective-permute-done | bytes 393248 | tf_op jit(solution)/shard_map/ppermute | solution.py:635
  103.5 0.1 pad_maximum_fusion
  103.6 3.2 %collective-permute-done.17 = bf16[192,2048]{1,0:T(8,128)(2,1)S(1)} collective-permute-done((bf16[192,2048]{1,0:T(8,128)(2,1)}, bf16[192,2048]{1,0:T(8,128)(2,1)S(1)}, u32[]{:S(2)}, u32[]{:S(2)}) %collective-permute-start.17) | collective-permute-done | bytes 786464 | tf_op jit(solution)/shard_map/ppermute | solution.py:635
  106.8 0.0 collective-permute-done.18.refs_2_
  106.8 0.0 collective-permute-start.21
  106.8 2.0 %collective-permute-start.22 = (bf16[192,2048]{1,0:T(8,128)(2,1)S(1)}, bf16[192,2048]{1,0:T(8,128)(2,1)S(1)}, u32[]{:S(2)}, u32[]{:S(2)}) collective-permute-start(bf16[192,2048]{1,0:T(8,128)(2,1)S(1)} %pad_maximum_fusion), channel_id=1, source_target_pairs={{0,2},{1,3},{2,0},{3,1},{4,6},{5,7},{6,4},{7,5},{8,10},{9,11},{10,... | collective-permute-start | bytes 2359304 | tf_op jit(solution)/shard_map/ppermute | solution.py:635
  108.8 1.0 fusion.2
  109.8 0.7 collective-permute-done.16.refs_3_
  110.5 0.7 copy-done.9
  111.3 2.0 %collective-permute-start.24 = (bf16[1,96,2048]{2,1,0:T(8,128)(2,1)}, bf16[1,96,2048]{2,1,0:T(8,128)(2,1)S(1)}, u32[]{:S(2)}, u32[]{:S(2)}) collective-permute-start(bf16[1,96,2048]{2,1,0:T(8,128)(2,1)} %get-tuple-element.82), channel_id=1, source_target_pairs={{0,4},{1,5},{2,6},{3,7},{4,0},{5,1},{6,2},{7,3},{8,12},{9,13},{10,... | collective-permute-start | bytes 1179656 | tf_op jit(solution)/shard_map/ppermute | solution.py:635
  113.3 3.1 %assemble.1.base_ref = bf16[384,4096]{1,0:T(8,128)(2,1)} custom-call(s32[1]{0:T(128)} %bitcast.chip_ref, s32[1]{0:T(128)} %bitcast.1.core_ref, bf16[96,2048]{1,0:T(8,128)(2,1)} %copy-done, bf16[96,2048]{1,0:T(8,128)(2,1)} %copy-done.2, bf16[96,2048]{1,0:T(8,128)(2,1)} %copy-done.8, bf16[96,2048]{1,0:T(8,128)(2,1)} %copy-done.9), custom_call_target="tpu_custom_call" | custom-call | flops 1000 | bytes 1000 | tf_op jit(solution)/shard_map/assemble/pallas_call | solution.py:446
  116.4 0.0 collective-permute-done.19.refs_3_
  116.4 0.0 collective-permute-done.20.refs_4_
  116.5 0.0 collective-permute-done.21.refs_5_
  116.5 6.4 %weight_grad.1 = f32[1024,512]{1,0:T(8,128)} custom-call(s32[1]{0:T(128)} %bitcast.2.me_ref, s32[1]{0:T(128)} %bitcast.1.core_ref, bf16[384,4096]{1,0:T(8,128)(2,1)} %grad_ref.3, bf16[384,512]{1,0:T(8,128)(2,1)} %get-tuple-element.49.hidden_ref.refs_13_, bf16[384,1024]{1,0:T(8,128)(2,1)} %collective-permute-done.10.refs_0_, ...), custom_call_target="tpu_custom_call" | custom-call | flops 1000 | bytes 1000 | tf_op jit(solution)/shard_map/weight_grad/pallas_call | solution.py:557
  122.9 12.3 %collective-permute-done.22.own_ref = bf16[192,2048]{1,0:T(8,128)(2,1)S(1)} collective-permute-done((bf16[192,2048]{1,0:T(8,128)(2,1)S(1)}, bf16[192,2048]{1,0:T(8,128)(2,1)S(1)}, u32[]{:S(2)}, u32[]{:S(2)}) %collective-permute-start.22) | collective-permute-done | bytes 786464 | tf_op jit(solution)/shard_map/ppermute | solution.py:635
  135.2 0.1 convert_add_fusion
  135.3 0.1 dynamic-slice_bitcast_fusion.1
  135.3 0.1 collective-permute-start.25
  135.4 0.5 collective-permute-start.23
  135.9 1.2 collective-permute-done.25
  137.1 1.0 maximum_select_fusion
  138.1 0.2 collective-permute-done.23.theirs_ref
  138.2 0.9 copy-done.6
  139.1 2.5 %insert.1 = bf16[384,4096]{1,0:T(8,128)(2,1)} custom-call(s32[1]{0:T(128)} %bitcast.chip_ref, s32[1]{0:T(128)} %bitcast.1.core_ref, bf16[192,2048]{1,0:T(8,128)(2,1)} %copy-done.5, bf16[192,2048]{1,0:T(8,128)(2,1)} %copy-done.6, bf16[384,4096]{1,0:T(8,128)(2,1)} %assemble.1.base_ref), custom_call_target="tpu_custom_call", output_to_operand_aliasing={{}: (4, {})} | custom-call | flops 1000 | bytes 1000 | tf_op jit(solution)/shard_map/insert/pallas_call | solution.py:431
  (40 shorter events, 0.1 us)
Async XLA Ops:
  0.6 63.8 %collective-permute-start.9 = (bf16[3,4096,512]{2,1,0:T(8,128)(2,1)}, bf16[3,4096,512]{2,1,0:T(8,128)(2,1)}, u32[]{:S(2)}, u32[]{:S(2)}) collective-permute-start(bf16[3,4096,512]{2,1,0:T(8,128)(2,1)} %bitcast.28), channel_id=1, source_target_pairs={{0,1},{1,0},{2,3},{3,2},{4,5},{5,4},{6,7},{7,6},{8,9},{9,8},{10,11... | collective-permute-start | bytes 37748744 | tf_op jit(solution)/shard_map/ppermute | solution.py:635
  1.1 31.1 %collective-permute-start.6 = (bf16[4096,512]{1,0:T(8,128)(2,1)}, bf16[4096,512]{1,0:T(8,128)(2,1)}, u32[]{:S(2)}, u32[]{:S(2)}) collective-permute-start(bf16[4096,512]{1,0:T(8,128)(2,1)} %weight_ref.3), channel_id=1, source_target_pairs={{0,1},{1,0},{2,3},{3,2},{4,5},{5,4},{6,7},{7,6},{8,9},{9,8},{10,11... | collective-permute-start | bytes 12582920 | tf_op jit(solution)/shard_map/ppermute | solution.py:635
  2.7 8.9 %collective-permute-start = (f32[40,384]{1,0:T(8,128)}, f32[40,384]{1,0:T(8,128)S(1)}, u32[]{:S(2)}, u32[]{:S(2)}) collective-permute-start(f32[40,384]{1,0:T(8,128)} %pack.1.refs_0_), channel_id=1, source_target_pairs={{0,8},{8,0},{16,24},{24,16},{1,9},{9,1},{17,25},{25,17},{2,10},{10... | collective-permute-start | bytes 184328 | tf_op jit(solution)/shard_map/ppermute | solution.py:626
  5.6 6.0 %collective-permute-start.1 = (f32[40,384]{1,0:T(8,128)}, f32[40,384]{1,0:T(8,128)S(1)}, u32[]{:S(2)}, u32[]{:S(2)}) collective-permute-start(f32[40,384]{1,0:T(8,128)} %pack.1.refs_0_), channel_id=1, source_target_pairs={{0,16},{8,24},{16,0},{24,8},{1,17},{9,25},{17,1},{25,9},{2,18},{10... | collective-permute-start | bytes 184328 | tf_op jit(solution)/shard_map/ppermute | solution.py:626
  7.1 5.3 %collective-permute-start.2 = (f32[40,384]{1,0:T(8,128)}, f32[40,384]{1,0:T(8,128)S(1)}, u32[]{:S(2)}, u32[]{:S(2)}) collective-permute-start(f32[40,384]{1,0:T(8,128)} %pack.1.refs_0_), channel_id=1, source_target_pairs={{0,24},{8,16},{16,8},{24,0},{1,25},{9,17},{17,9},{25,1},{2,26},{10... | collective-permute-start | bytes 184328 | tf_op jit(solution)/shard_map/ppermute | solution.py:626
  11.5 4.4 %copy-start.14 = (f32[40,384]{1,0:T(8,128)}, f32[40,384]{1,0:T(8,128)S(1)}, u32[]{:S(2)}) copy-start(f32[40,384]{1,0:T(8,128)S(1)} %collective-permute-done.refs_1_) | copy-start | bytes 184324
  11.6 4.4 %copy-start.15 = (f32[40,384]{1,0:T(8,128)}, f32[40,384]{1,0:T(8,128)S(1)}, u32[]{:S(2)}) copy-start(f32[40,384]{1,0:T(8,128)S(1)} %collective-permute-done.1.refs_2_) | copy-start | bytes 184324
  12.4 3.5 %copy-start.16 = (f32[40,384]{1,0:T(8,128)}, f32[40,384]{1,0:T(8,128)S(1)}, u32[]{:S(2)}) copy-start(f32[40,384]{1,0:T(8,128)S(1)} %collective-permute-done.2.refs_3_) | copy-start | bytes 184324
  12.4 16.8 %collective-permute-start.3 = (bf16[512,384]{1,0:T(8,128)(2,1)}, bf16[512,384]{1,0:T(8,128)(2,1)S(1)}, u32[]{:S(2)}, u32[]{:S(2)}) collective-permute-start(bf16[512,384]{1,0:T(8,128)(2,1)} %hidden_grad.1.refs_4_), channel_id=1, source_target_pairs={{0,8},{8,0},{16,24},{24,16},{1,9},{9,1},{17,25},{25,17},{2,10},{10... | collective-permute-start | bytes 1179656 | tf_op jit(solution)/shard_map/ppermute | solution.py:626
  13.6 18.6 %collective-permute-start.4 = (bf16[512,384]{1,0:T(8,128)(2,1)}, bf16[512,384]{1,0:T(8,128)(2,1)S(1)}, u32[]{:S(2)}, u32[]{:S(2)}) collective-permute-start(bf16[512,384]{1,0:T(8,128)(2,1)} %hidden_grad.1.refs_4_), channel_id=1, source_target_pairs={{0,16},{8,24},{16,0},{24,8},{1,17},{9,25},{17,1},{25,9},{2,18},{10... | collective-permute-start | bytes 1179656 | tf_op jit(solution)/shard_map/ppermute | solution.py:626
  15.1 17.1 %collective-permute-start.5 = (bf16[512,384]{1,0:T(8,128)(2,1)}, bf16[512,384]{1,0:T(8,128)(2,1)S(1)}, u32[]{:S(2)}, u32[]{:S(2)}) collective-permute-start(bf16[512,384]{1,0:T(8,128)(2,1)} %hidden_grad.1.refs_4_), channel_id=1, source_target_pairs={{0,24},{8,16},{16,8},{24,0},{1,25},{9,17},{17,9},{25,1},{2,26},{10... | collective-permute-start | bytes 1179656 | tf_op jit(solution)/shard_map/ppermute | solution.py:626
  29.2 13.2 %copy-start.11 = (bf16[512,384]{1,0:T(8,128)(2,1)}, bf16[512,384]{1,0:T(8,128)(2,1)S(1)}, u32[]{:S(2)}) copy-start(bf16[512,384]{1,0:T(8,128)(2,1)S(1)} %collective-permute-done.3.refs_5_) | copy-start | bytes 1179652
  32.2 10.1 %copy-start.12 = (bf16[512,384]{1,0:T(8,128)(2,1)}, bf16[512,384]{1,0:T(8,128)(2,1)S(1)}, u32[]{:S(2)}) copy-start(bf16[512,384]{1,0:T(8,128)(2,1)S(1)} %collective-permute-done.4.refs_6_) | copy-start | bytes 1179652
  32.3 10.1 %copy-start.13 = (bf16[512,384]{1,0:T(8,128)(2,1)}, bf16[512,384]{1,0:T(8,128)(2,1)S(1)}, u32[]{:S(2)}) copy-start(bf16[512,384]{1,0:T(8,128)(2,1)S(1)} %collective-permute-done.5.refs_7_) | copy-start | bytes 1179652
  32.3 2.0 %collective-permute-start.7 = (bf16[384,512]{1,0:T(8,128)(2,1)}, bf16[384,512]{1,0:T(8,128)(2,1)S(1)}, u32[]{:S(2)}, u32[]{:S(2)}) collective-permute-start(bf16[384,512]{1,0:T(8,128)(2,1)} %get-tuple-element.49.hidden_ref.refs_13_), channel_id=1, source_target_pairs={{0,1},{1,0},{2,3},{3,2},{4,5},{5,4},{6,7},{7,6},{8,9},{9,8},{10,11... | collective-permute-start | bytes 1179656 | tf_op jit(solution)/shard_map/ppermute | solution.py:635
  34.3 0.7 copy-start.7
  40.7 20.0 %collective-permute-start.12 = (bf16[192,2048]{1,0:T(8,128)(2,1)}, bf16[192,2048]{1,0:T(8,128)(2,1)}, u32[]{:S(2)}, u32[]{:S(2)}) collective-permute-start(bf16[192,2048]{1,0:T(8,128)(2,1)} %get-tuple-element.68), channel_id=1, source_target_pairs={{0,2},{1,3},{2,0},{3,1},{4,6},{5,7},{6,4},{7,5},{8,10},{9,11},{10,... | collective-permute-start | bytes 2359304 | tf_op jit(solution)/shard_map/ppermute | solution.py:635
  42.4 18.3 %copy-start.1 = (f32[192,2048]{1,0:T(8,128)S(1)}, f32[192,2048]{1,0:T(8,128)}, u32[]{:S(2)}) copy-start(f32[192,2048]{1,0:T(8,128)} %get-tuple-element.67) | copy-start | bytes 4718596
  56.8 7.6 %collective-permute-start.8 = (bf16[3,384,512]{2,1,0:T(8,128)(2,1)}, bf16[3,384,512]{2,1,0:T(8,128)(2,1)S(1)}, u32[]{:S(2)}, u32[]{:S(2)}) collective-permute-start(bf16[3,384,512]{2,1,0:T(8,128)(2,1)} %get-tuple-element.60.grad_ref), channel_id=1, source_target_pairs={{0,1},{1,0},{2,3},{3,2},{4,5},{5,4},{6,7},{7,6},{8,9},{9,8},{10,11... | collective-permute-start | bytes 3538952 | tf_op jit(solution)/shard_map/ppermute | solution.py:635
  56.9 20.3 %collective-permute-start.10 = (bf16[384,1024]{1,0:T(8,128)(2,1)}, bf16[384,1024]{1,0:T(8,128)(2,1)}, u32[]{:S(2)}, u32[]{:S(2)}) collective-permute-start(bf16[384,1024]{1,0:T(8,128)(2,1)} %get-tuple-element.63), channel_id=1, source_target_pairs={{0,8},{8,0},{16,24},{24,16},{1,9},{9,1},{17,25},{25,17},{2,10},{10... | collective-permute-start | bytes 2359304 | tf_op jit(solution)/shard_map/ppermute | solution.py:626
  58.2 19.9 %collective-permute-start.11 = (bf16[384,1024]{1,0:T(8,128)(2,1)}, bf16[384,1024]{1,0:T(8,128)(2,1)}, u32[]{:S(2)}, u32[]{:S(2)}) collective-permute-start(bf16[384,1024]{1,0:T(8,128)(2,1)} %get-tuple-element.64), channel_id=1, source_target_pairs={{0,16},{8,24},{16,0},{24,8},{1,17},{9,25},{17,1},{25,9},{2,18},{10... | collective-permute-start | bytes 2359304 | tf_op jit(solution)/shard_map/ppermute | solution.py:626
  61.8 19.8 %collective-permute-start.13 = (bf16[1,96,2048]{2,1,0:T(8,128)(2,1)S(1)}, bf16[1,96,2048]{2,1,0:T(8,128)(2,1)S(1)}, u32[]{:S(2)}, u32[]{:S(2)}) collective-permute-start(bf16[1,96,2048]{2,1,0:T(8,128)(2,1)S(1)} %fusion.1), channel_id=1, source_target_pairs={{0,4},{1,5},{2,6},{3,7},{4,0},{5,1},{6,2},{7,3},{8,12},{9,13},{10,... | collective-permute-start | bytes 1179656 | tf_op jit(solution)/shard_map/ppermute | solution.py:635
  64.4 14.1 %copy-start.10 = (bf16[384,1024]{1,0:T(8,128)(2,1)S(1)}, bf16[384,1024]{1,0:T(8,128)(2,1)}, u32[]{:S(2)}) copy-start(bf16[384,1024]{1,0:T(8,128)(2,1)} %get-tuple-element.72) | copy-start | bytes 2359300
  64.4 1.0 copy-start.4
  75.7 33.1 %copy-start.3 = (f32[192,2048]{1,0:T(8,128)S(1)}, f32[192,2048]{1,0:T(8,128)}, u32[]{:S(2)}) copy-start(f32[192,2048]{1,0:T(8,128)} %get-tuple-element.77) | copy-start | bytes 4718596
  78.1 28.7 %collective-permute-start.17 = (bf16[192,2048]{1,0:T(8,128)(2,1)}, bf16[192,2048]{1,0:T(8,128)(2,1)S(1)}, u32[]{:S(2)}, u32[]{:S(2)}) collective-permute-start(bf16[192,2048]{1,0:T(8,128)(2,1)} %get-tuple-element.71), channel_id=1, source_target_pairs={{0,2},{1,3},{2,0},{3,1},{4,6},{5,7},{6,4},{7,5},{8,10},{9,11},{10,... | collective-permute-start | bytes 2359304 | tf_op jit(solution)/shard_map/ppermute | solution.py:635
  78.6 28.2 %collective-permute-start.18 = (bf16[384,1024]{1,0:T(8,128)(2,1)S(1)}, bf16[384,1024]{1,0:T(8,128)(2,1)}, u32[]{:S(2)}, u32[]{:S(2)}) collective-permute-start(bf16[384,1024]{1,0:T(8,128)(2,1)S(1)} %copy-done.10), channel_id=1, source_target_pairs={{0,24},{8,16},{16,8},{24,0},{1,25},{9,17},{17,9},{25,1},{2,26},{10... | collective-permute-start | bytes 2359304 | tf_op jit(solution)/shard_map/ppermute | solution.py:626
  83.0 26.8 %copy-start = (bf16[96,2048]{1,0:T(8,128)(2,1)}, bf16[96,2048]{1,0:T(8,128)(2,1)S(1)}, u32[]{:S(2)}) copy-start(bf16[96,2048]{1,0:T(8,128)(2,1)S(1)} %fusion.refs_0_) | copy-start | bytes 1179652
  83.0 20.5 %collective-permute-start.14 = (bf16[96,2048]{1,0:T(8,128)(2,1)S(1)}, bf16[96,2048]{1,0:T(8,128)(2,1)S(1)}, u32[]{:S(2)}, u32[]{:S(2)}) collective-permute-start(bf16[96,2048]{1,0:T(8,128)(2,1)S(1)} %fusion.refs_0_), channel_id=1, source_target_pairs={{0,4},{1,5},{2,6},{3,7},{4,0},{5,1},{6,2},{7,3},{8,12},{9,13},{10,... | collective-permute-start | bytes 1179656 | tf_op jit(solution)/shard_map/ppermute | solution.py:635
  85.2 23.6 %collective-permute-start.15 = (bf16[96,2048]{1,0:T(8,128)(2,1)S(1)}, bf16[96,2048]{1,0:T(8,128)(2,1)S(1)}, u32[]{:S(2)}, u32[]{:S(2)}) collective-permute-start(bf16[96,2048]{1,0:T(8,128)(2,1)S(1)} %fusion.refs_0_), channel_id=1, source_target_pairs={{0,1},{1,0},{2,3},{3,2},{4,5},{5,4},{6,7},{7,6},{8,9},{9,8},{10,11... | collective-permute-start | bytes 1179656 | tf_op jit(solution)/shard_map/ppermute | solution.py:635
  85.2 31.2 %collective-permute-start.19 = (bf16[384,1024]{1,0:T(8,128)(2,1)}, bf16[384,1024]{1,0:T(8,128)(2,1)}, u32[]{:S(2)}, u32[]{:S(2)}) collective-permute-start(bf16[384,1024]{1,0:T(8,128)(2,1)} %collective-permute-done.10.refs_0_), channel_id=1, source_target_pairs={{0,1},{1,0},{2,3},{3,2},{4,5},{5,4},{6,7},{7,6},{8,9},{9,8},{10,11... | collective-permute-start | bytes 2359304 | tf_op jit(solution)/shard_map/ppermute | solution.py:635
  103.5 6.3 %copy-start.2 = (bf16[96,2048]{1,0:T(8,128)(2,1)}, bf16[96,2048]{1,0:T(8,128)(2,1)S(1)}, u32[]{:S(2)}) copy-start(bf16[96,2048]{1,0:T(8,128)(2,1)S(1)} %collective-permute-done.14.refs_1_) | copy-start | bytes 1179652
  103.5 12.9 %collective-permute-start.20 = (bf16[384,1024]{1,0:T(8,128)(2,1)}, bf16[384,1024]{1,0:T(8,128)(2,1)}, u32[]{:S(2)}, u32[]{:S(2)}) collective-permute-start(bf16[384,1024]{1,0:T(8,128)(2,1)} %collective-permute-done.11.refs_1_), channel_id=1, source_target_pairs={{0,1},{1,0},{2,3},{3,2},{4,5},{5,4},{6,7},{7,6},{8,9},{9,8},{10,11... | collective-permute-start | bytes 2359304 | tf_op jit(solution)/shard_map/ppermute | solution.py:635
  106.8 9.7 %collective-permute-start.21 = (bf16[384,1024]{1,0:T(8,128)(2,1)}, bf16[384,1024]{1,0:T(8,128)(2,1)}, u32[]{:S(2)}, u32[]{:S(2)}) collective-permute-start(bf16[384,1024]{1,0:T(8,128)(2,1)} %collective-permute-done.18.refs_2_), channel_id=1, source_target_pairs={{0,1},{1,0},{2,3},{3,2},{4,5},{5,4},{6,7},{7,6},{8,9},{9,8},{10,11... | collective-permute-start | bytes 2359304 | tf_op jit(solution)/shard_map/ppermute | solution.py:635
  106.8 28.4 %collective-permute-start.22 = (bf16[192,2048]{1,0:T(8,128)(2,1)S(1)}, bf16[192,2048]{1,0:T(8,128)(2,1)S(1)}, u32[]{:S(2)}, u32[]{:S(2)}) collective-permute-start(bf16[192,2048]{1,0:T(8,128)(2,1)S(1)} %pad_maximum_fusion), channel_id=1, source_target_pairs={{0,2},{1,3},{2,0},{3,1},{4,6},{5,7},{6,4},{7,5},{8,10},{9,11},{10,... | collective-permute-start | bytes 2359304 | tf_op jit(solution)/shard_map/ppermute | solution.py:635
  108.8 4.5 %copy-start.8 = (bf16[96,2048]{1,0:T(8,128)(2,1)}, bf16[96,2048]{1,0:T(8,128)(2,1)S(1)}, u32[]{:S(2)}) copy-start(bf16[96,2048]{1,0:T(8,128)(2,1)S(1)} %collective-permute-done.15.refs_2_) | copy-start | bytes 1179652
  108.8 1.7 %collective-permute-start.16 = (bf16[96,2048]{1,0:T(8,128)(2,1)S(1)}, bf16[96,2048]{1,0:T(8,128)(2,1)S(1)}, u32[]{:S(2)}, u32[]{:S(2)}) collective-permute-start(bf16[96,2048]{1,0:T(8,128)(2,1)S(1)} %collective-permute-done.14.refs_1_), channel_id=1, source_target_pairs={{0,1},{1,0},{2,3},{3,2},{4,5},{5,4},{6,7},{7,6},{8,9},{9,8},{10,11... | collective-permute-start | bytes 1179656 | tf_op jit(solution)/shard_map/ppermute | solution.py:635
  110.5 0.7 copy-start.9
  111.3 23.9 %collective-permute-start.24 = (bf16[1,96,2048]{2,1,0:T(8,128)(2,1)}, bf16[1,96,2048]{2,1,0:T(8,128)(2,1)S(1)}, u32[]{:S(2)}, u32[]{:S(2)}) collective-permute-start(bf16[1,96,2048]{2,1,0:T(8,128)(2,1)} %get-tuple-element.82), channel_id=1, source_target_pairs={{0,4},{1,5},{2,6},{3,7},{4,0},{5,1},{6,2},{7,3},{8,12},{9,13},{10,... | collective-permute-start | bytes 1179656 | tf_op jit(solution)/shard_map/ppermute | solution.py:635
  135.2 2.9 %copy-start.5 = (bf16[192,2048]{1,0:T(8,128)(2,1)}, bf16[192,2048]{1,0:T(8,128)(2,1)S(1)}, u32[]{:S(2)}) copy-start(bf16[192,2048]{1,0:T(8,128)(2,1)S(1)} %collective-permute-done.22.own_ref) | copy-start | bytes 2359300
  135.3 1.8 %collective-permute-start.25 = (f32[48,2048]{1,0:T(8,128)S(1)}, f32[48,2048]{1,0:T(8,128)S(1)}, u32[]{:S(2)}, u32[]{:S(2)}) collective-permute-start(f32[48,2048]{1,0:T(8,128)S(1)} %get-tuple-element.85), channel_id=1, source_target_pairs={{0,1},{1,0},{2,3},{3,2},{4,5},{5,4},{6,7},{7,6},{8,9},{9,8},{10,11... | collective-permute-start | bytes 1179656 | tf_op jit(solution)/shard_map/ppermute | solution.py:635
  135.4 2.8 %collective-permute-start.23 = (bf16[192,2048]{1,0:T(8,128)(2,1)S(1)}, bf16[192,2048]{1,0:T(8,128)(2,1)S(1)}, u32[]{:S(2)}, u32[]{:S(2)}) collective-permute-start(bf16[192,2048]{1,0:T(8,128)(2,1)S(1)} %collective-permute-done.22.own_ref), channel_id=1, source_target_pairs={{0,1},{1,0},{2,3},{3,2},{4,5},{5,4},{6,7},{7,6},{8,9},{9,8},{10,11... | collective-permute-start | bytes 2359304 | tf_op jit(solution)/shard_map/ppermute | solution.py:635
  138.2 0.9 copy-start.6

commit v6 on v5

--- a/solution.py
+++ b/solution.py
@@ -89,26 +89,39 @@
     return copies
 
 
-def split_blocks(total, chip, rows, send, kept, columns):
-    for index in range(total.shape[0] // (2 * rows)):
+def split_blocks(total, chip, rows, parts, columns):
+    low, high = chip % 2, chip // 2 % 2
+    for index in range(total.shape[0] // (4 * rows)):
         place = slice(index * rows, (index + 1) * rows)
-        for target, bit in ((send, 1 - chip % 2), (kept, chip % 2)):
-            source = pl.ds(pl.multiple_of((2 * index + bit) * rows, 8), rows)
+        for target, first, second in zip(parts, (1 - low, 1 - low, low, low), (1 - high, high, 1 - high, high)):
+            source = pl.ds(pl.multiple_of((4 * index + 2 * second + first) * rows, 8), rows)
             target[place, columns] = total[source].astype(target.dtype)
 
 
-def write_out(pairs, columns, left, first):
+def write_out(sources, targets, columns, left, first):
     copies = []
-    for index, (source, target) in enumerate(pairs):
+    for index, (source, target) in enumerate(zip(sources, targets)):
         copies.append(pltpu.make_async_copy(source.at[:, columns], target.at[:, columns], left.at[first + index]))
         copies[-1].start()
     return copies
 
 
+PARTS = 4
+
+
+def part_shapes(rows, half):
+    return [jax.ShapeDtypeStruct((rows // PARTS, half), kind) for kind in (bf16, bf16, f32, f32)]
+
+
+def part_buffers(rows, half):
+    return [pltpu.VMEM((rows // PARTS, half), kind) for kind in (bf16, bf16, f32, f32)]
+
+
 def project_kernel(
-    chips, core_ref, chip_ref, hidden_ref, other_ref, weight_ref, other_weight_ref,
-    send_ref, kept_ref, weight, arrived, other_weight, other_arrived, total, send, kept, left, hidden, other, came,
+    chips, core_ref, chip_ref, hidden_ref, other_ref, weight_ref, other_weight_ref, *refs
 ):
+    out_refs, parts = refs[:PARTS], refs[PARTS : 2 * PARTS]
+    weight, arrived, other_weight, other_arrived, total, left, hidden, other, came = refs[2 * PARTS :]
     operands = [
         pltpu.make_async_copy(hidden_ref, hidden, came.at[0]),
         pltpu.make_async_copy(other_ref, other, came.at[1]),
@@ -131,8 +144,8 @@
         total[...] = lax.dot_general(
             hidden[...], weight[columns], CONTRACT_LAST, preferred_element_type=f32
         ) + lax.dot_general(other[...], other_weight[columns], CONTRACT_LAST, preferred_element_type=f32)
-        split_blocks(total, chip_ref[0], rows, send, kept, columns)
-        leaving += write_out(((send, send_ref), (kept, kept_ref)), columns, left, 2 * index)
+        split_blocks(total, chip_ref[0], rows, parts, columns)
+        leaving += write_out(parts, out_refs, columns, left, PARTS * index)
     for copy in leaving:
         copy.wait()
 
@@ -148,11 +161,14 @@
             out_ref[at] = refs[index][slot * rows : (slot + 1) * rows]
 
 
-def forward_kernel(shards, me_ref, *refs):
+def forward_kernel(shards, me_ref, core_ref, *refs):
     slots = refs[:shards]
-    letters_ref, gain_ref, weight_ref, taps_ref, skip_ref = refs[shards : shards + 5]
-    hidden_ref, mixed_ref, table_ref = refs[shards + 5 : shards + 8]
-    normed, hot, filters, matrices, signal, exact, long_part, weight, arrived, table, left = refs[shards + 8 :]
+    letters_ref, gain_ref, weight_ref, taps_ref, skip_ref, output_grad_ref = refs[shards : shards + 6]
+    hidden_ref, mixed_ref, table_ref = refs[shards + 6 : shards + 9]
+    piece_refs = refs[shards + 9 : 2 * shards + 8]
+    normed, hot, filters, matrices, signal, exact, long_part, weight, arrived, table, left, pieces, came, pieces_left = refs[
+        2 * shards + 8 :
+    ]
     groups = filters.shape[0]
     local_rows = slots[0].shape[1]
     channels = table.shape[2]
@@ -172,6 +188,14 @@
         rows = slice(index * chunk, (index + 1) * chunk)
         copies.append(pltpu.make_async_copy(weight_ref.at[:, rows], weight.at[:, rows], arrived.at[index]))
         copies[-1].start()
+    share = output_grad_ref.shape[1] // shards
+    part = share // 2
+    incoming = []
+    for step in range(1, shards):
+        start = jnp.bitwise_xor(me, step) * share + core_ref[0] * part
+        source = output_grad_ref.at[:, pl.ds(pl.multiple_of(start, part), part)]
+        incoming.append(pltpu.make_async_copy(source, pieces.at[step - 1, :, :part], came.at[step - 1]))
+        incoming[-1].start()
     for index, slot in enumerate(slots):
         place = lanes_at(jnp.bitwise_xor(me, index) * local_blocks, local_blocks)
         filters[:, place] = slot[:groups]
@@ -187,13 +211,13 @@
     normed[...] = (values * inverse * gain_ref[...][None, :]).astype(bf16)
 
     table[...] = jnp.zeros(table.shape, f32)
-    share = groups // chunks
+    per_chunk = groups // chunks
 
     def one_chunk(index, carry):
         rows = pl.ds(pl.multiple_of(index * chunk, chunk), chunk)
         pltpu.make_async_copy(weight_ref.at[:, rows], weight.at[:, rows], arrived.at[index]).wait()
-        for offset in range(share):
-            group = index * share + offset
+        for offset in range(per_chunk):
+            group = index * per_chunk + offset
             tiles = toeplitz_tiles(filters[pl.ds(group, 1), :], blocks, False)
             for q in range(blocks):
                 matrices[group, (blocks - 1 - q) * LANES : (blocks - q) * LANES] = tiles[q]
@@ -220,35 +244,32 @@
             long_part[rows, i * LANES : (i + 1) * LANES] = result[i * width : (i + 1) * width]
         return carry
 
-    lax.fori_loop(0, groups, one_group, 0, unroll=4)
+    lax.fori_loop(0, groups, one_group, 0, unroll=8)
     columns = channel_columns(taps_ref, skip_ref)
     mixed = columns[:, 3 * taps : 3 * taps + 1] * exact[:, lanes_at(first, window)] + long_part[...]
     long_part[...] = mixed
     mixed_copy = pltpu.make_async_copy(long_part, mixed_ref, left.at[1])
     mixed_copy.start()
     queries = expand(tap_weights(taps_ref, table, 0), hot[:, lanes_at(first, local_blocks)])
-    hidden_ref[...] = jnp.transpose(queries * mixed[:, :local_rows]).astype(bf16)
+    hidden = jnp.transpose(queries * mixed[:, :local_rows]).astype(bf16)
+    hidden_ref[...] = hidden
+    outgoing = []
+    for step in range(1, shards):
+        incoming[step - 1].wait()
+        pieces[step - 1, :, part:] = hidden
+        outgoing.append(pltpu.make_async_copy(pieces.at[step - 1], piece_refs[step - 1], pieces_left.at[step - 1]))
+        outgoing[-1].start()
+    for copy in outgoing:
+        copy.wait()
     table_copy.wait()
     mixed_copy.wait()
 
 
-def backward_kernel(shards, me_ref, core_ref, *refs):
+def backward_kernel(shards, me_ref, *refs):
     slots, grad_slots = refs[:shards], refs[shards : 2 * shards]
-    table_ref, taps_ref, skip_ref, mixed_ref, output_grad_ref, hidden_ref, out_ref = refs[2 * shards : 2 * shards + 7]
-    piece_refs = refs[2 * shards + 7 : 3 * shards + 6]
-    hot, filters, grads, signal, exact, long_part, pieces, came, left = refs[3 * shards + 6 :]
+    table_ref, taps_ref, skip_ref, mixed_ref, out_ref = refs[2 * shards : 2 * shards + 5]
+    hot, filters, grads, signal, exact, long_part = refs[2 * shards + 5 :]
     me = me_ref[0]
-    share = output_grad_ref.shape[1] // shards
-    part = share // 2
-    incoming = []
-    for step in range(1, shards):
-        start = jnp.bitwise_xor(me, step) * share + core_ref[0] * part
-        source = output_grad_ref.at[:, pl.ds(pl.multiple_of(start, part), part)]
-        slot = pieces.at[step - 1]
-        incoming.append(pltpu.make_async_copy(source, slot.at[:, :part], came.at[2 * step - 2]))
-        incoming.append(pltpu.make_async_copy(hidden_ref, slot.at[:, part:], came.at[2 * step - 1]))
-    for copy in incoming:
-        copy.start()
     groups = filters.shape[0]
     local_rows = slots[0].shape[1]
     channels = table_ref.shape[2]
@@ -278,12 +299,6 @@
         exact[rows, :length] = mixed_grad
         signal[rows, :length] = mixed_grad.astype(bf16)
 
-    for copy in incoming:
-        copy.wait()
-    outgoing = []
-    for step in range(1, shards):
-        outgoing.append(pltpu.make_async_copy(pieces.at[step - 1], piece_refs[step - 1], left.at[step - 1]))
-        outgoing[-1].start()
     first = me * local_blocks
 
     def one_group(group, carry):
@@ -295,7 +310,7 @@
             long_part[rows, i * LANES : (i + 1) * LANES] = result[i * width : (i + 1) * width]
         return carry
 
-    lax.fori_loop(0, groups, one_group, 0, unroll=4)
+    lax.fori_loop(0, groups, one_group, 0, unroll=8)
     own = lanes_at(first, window)
     columns = channel_columns(taps_ref, skip_ref)
     mixture_grad = columns[:, 3 * taps : 3 * taps + 1] * exact[:, own] + long_part[...]
@@ -311,8 +326,6 @@
             column = 3 * tap + part
             total = total + columns[:, column : column + 1] * pltpu.roll(feature_grad, span - tap, axis=1)
         out_ref[part] = jnp.transpose(total[:, :local_rows]).astype(bf16)
-    for copy in outgoing:
-        copy.wait()
 
 
 def hidden_grad_kernel(grad_ref, weight_ref, out_ref, grad, weight, total, arrived):
@@ -335,9 +348,10 @@
 
 
 def input_grad_kernel(
-    chips, core_ref, chip_ref, grad_ref, other_grad_ref, weight_ref, other_weight_ref,
-    send_ref, kept_ref, weight, other_weight, arrived, total, send, kept, left,
+    chips, core_ref, chip_ref, grad_ref, other_grad_ref, weight_ref, other_weight_ref, *refs
 ):
+    out_refs, parts = refs[:PARTS], refs[PARTS : 2 * PARTS]
+    weight, other_weight, arrived, total, left = refs[2 * PARTS :]
     half = weight.shape[1]
     chunks = arrived.shape[0] // 2
     chunk = half // chunks
@@ -363,8 +377,8 @@
                 term = lax.dot_general(grad[part], held[part, columns], CONTRACT_LAST, preferred_element_type=f32)
                 value = term if value is None else value + term
         total[...] = value
-        split_blocks(total, chip_ref[0], rows, send, kept, columns)
-        leaving += write_out(((send, send_ref), (kept, kept_ref)), columns, left, 2 * index)
+        split_blocks(total, chip_ref[0], rows, parts, columns)
+        leaving += write_out(parts, out_refs, columns, left, PARTS * index)
     for copy in leaving:
         copy.wait()
 
@@ -454,13 +468,14 @@
     )(chip, core, *own, *theirs)
 
 
-def run_forward(me, slots, embed_table, norm_gain, weight, taps, skip_gain):
+def run_forward(me, core, slots, embed_table, norm_gain, weight, taps, skip_gain, output_grad):
     shards = len(slots)
     local_rows = slots[0].shape[1]
     _, width, channels = weight.shape
     groups = slots[0].shape[0] - 8
     length = shards * local_rows
     span = local_rows + LANES
+    part = width // (2 * shards)
     return pl.pallas_call(
         functools.partial(forward_kernel, shards),
         grid=(1,),
@@ -468,11 +483,13 @@
             jax.ShapeDtypeStruct((local_rows, channels), bf16),
             jax.ShapeDtypeStruct((channels, span), f32),
             jax.ShapeDtypeStruct((3, IDS, channels), f32),
-        ),
-        in_specs=[SMEM_SPEC]
+        )
+        + (jax.ShapeDtypeStruct((local_rows, part + channels), bf16),) * (shards - 1),
+        in_specs=[SMEM_SPEC, SMEM_SPEC]
         + in_vmem(shards)
-        + [pl.BlockSpec((IDS, width), lambda step: (FIRST_ID // IDS, 0)), VMEM_SPEC, ANY_SPEC, VMEM_SPEC, VMEM_SPEC],
-        out_specs=(VMEM_SPEC, ANY_SPEC, ANY_SPEC),
+        + [pl.BlockSpec((IDS, width), lambda step: (FIRST_ID // IDS, 0)), VMEM_SPEC, ANY_SPEC, VMEM_SPEC, VMEM_SPEC]
+        + [ANY_SPEC],
+        out_specs=(VMEM_SPEC,) + (ANY_SPEC,) * (shards + 1),
         scratch_shapes=[
             pltpu.VMEM((IDS, width), bf16),
             pltpu.VMEM((2 * taps.shape[0] * IDS, length + LANES), bf16),
@@ -485,11 +502,14 @@
             pltpu.SemaphoreType.DMA((CHUNKS,)),
             pltpu.VMEM((3, IDS, channels), f32),
             pltpu.SemaphoreType.DMA((2,)),
+            pltpu.VMEM((shards - 1, local_rows, part + channels), bf16),
+            pltpu.SemaphoreType.DMA((shards - 1,)),
+            pltpu.SemaphoreType.DMA((shards - 1,)),
         ],
         compiler_params=params(),
         cost_estimate=LARGE_COST,
         name="forward_conv",
-    )(me, *slots, embed_table, norm_gain, weight, taps, skip_gain)
+    )(me, core, *slots, embed_table, norm_gain, weight, taps, skip_gain, output_grad)
 
 
 def run_project(core, chip, chips, hidden, other_hidden, weight, other_weight):
@@ -497,18 +517,17 @@
     half = weight.shape[0] // 2
     return pl.pallas_call(
         functools.partial(project_kernel, chips),
-        out_shape=(jax.ShapeDtypeStruct((rows // 2, half), bf16), jax.ShapeDtypeStruct((rows // 2, half), f32)),
+        out_shape=part_shapes(rows, half),
         in_specs=[SMEM_SPEC, SMEM_SPEC] + [ANY_SPEC] * 4,
-        out_specs=(ANY_SPEC, ANY_SPEC),
-        scratch_shapes=[
+        out_specs=[ANY_SPEC] * PARTS,
+        scratch_shapes=part_buffers(rows, half)
+        + [
             pltpu.VMEM((half, channels), bf16),
             pltpu.SemaphoreType.DMA((4,)),
             pltpu.VMEM((half, channels), bf16),
             pltpu.SemaphoreType.DMA((4,)),
             pltpu.VMEM((rows, half // 4), f32),
-            pltpu.VMEM((rows // 2, half), bf16),
-            pltpu.VMEM((rows // 2, half), f32),
-            pltpu.SemaphoreType.DMA((8,)),
+            pltpu.SemaphoreType.DMA((4 * PARTS,)),
             pltpu.VMEM((rows, channels), bf16),
             pltpu.VMEM((rows, channels), bf16),
             pltpu.SemaphoreType.DMA((2,)),
@@ -519,20 +538,18 @@
     )(core, chip, hidden, other_hidden, weight, other_weight)
 
 
-def run_backward(me, core, slots, grads, table, taps, skip_gain, mixed, output_grad, hidden):
+def run_backward(me, slots, grads, table, taps, skip_gain, mixed):
     shards = len(slots)
     local_rows = slots[0].shape[1]
     channels = table.shape[2]
     groups = slots[0].shape[0] - 8
     length = shards * local_rows
     span = local_rows + LANES
-    part = output_grad.shape[1] // (2 * shards)
     return pl.pallas_call(
         functools.partial(backward_kernel, shards),
-        out_shape=[jax.ShapeDtypeStruct((3, local_rows, channels), bf16)]
-        + [jax.ShapeDtypeStruct((local_rows, part + channels), bf16)] * (shards - 1),
-        in_specs=[SMEM_SPEC, SMEM_SPEC] + in_vmem(2 * shards + 4) + [ANY_SPEC, ANY_SPEC],
-        out_specs=[VMEM_SPEC] + [ANY_SPEC] * (shards - 1),
+        out_shape=jax.ShapeDtypeStruct((3, local_rows, channels), bf16),
+        in_specs=[SMEM_SPEC] + in_vmem(2 * shards + 4),
+        out_specs=VMEM_SPEC,
         scratch_shapes=[
             pltpu.VMEM((2 * taps.shape[0] * IDS, length + LANES), bf16),
             pltpu.VMEM((groups, length), f32),
@@ -540,14 +557,11 @@
             pltpu.VMEM((channels, 2 * length + LANES), bf16),
             pltpu.VMEM((channels, length + LANES), f32),
             pltpu.VMEM((channels, span), f32),
-            pltpu.VMEM((shards - 1, local_rows, part + channels), bf16),
-            pltpu.SemaphoreType.DMA((2 * shards - 2,)),
-            pltpu.SemaphoreType.DMA((shards - 1,)),
         ],
         compiler_params=params(),
         cost_estimate=LARGE_COST,
         name="backward_conv",
-    )(me, core, *slots, *grads, table, taps, skip_gain, mixed, output_grad, hidden)
+    )(me, *slots, *grads, table, taps, skip_gain, mixed)
 
 
 def run_weight_grad(me, core, output_grad, hidden, mine, theirs):
@@ -591,17 +605,16 @@
     half = weight.shape[1] // 2
     return pl.pallas_call(
         functools.partial(input_grad_kernel, chips),
-        out_shape=(jax.ShapeDtypeStruct((rows // 2, half), bf16), jax.ShapeDtypeStruct((rows // 2, half), f32)),
+        out_shape=part_shapes(rows, half),
         in_specs=[SMEM_SPEC, SMEM_SPEC, VMEM_SPEC, VMEM_SPEC, ANY_SPEC, ANY_SPEC],
-        out_specs=(ANY_SPEC, ANY_SPEC),
-        scratch_shapes=[
+        out_specs=[ANY_SPEC] * PARTS,
+        scratch_shapes=part_buffers(rows, half)
+        + [
             pltpu.VMEM((3, half, channels), bf16),
             pltpu.VMEM((3, half, channels), bf16),
             pltpu.SemaphoreType.DMA((8,)),
             pltpu.VMEM((rows, half // 4), f32),
-            pltpu.VMEM((rows // 2, half), bf16),
-            pltpu.VMEM((rows // 2, half), f32),
-            pltpu.SemaphoreType.DMA((8,)),
+            pltpu.SemaphoreType.DMA((4 * PARTS,)),
         ],
         compiler_params=params(),
         cost_estimate=SMALL_COST,
@@ -680,11 +693,11 @@
     slots = [packed] + arrived
     grad_slots = gather_ctx(hidden_grad)
 
-    hidden, mixed, table = run_forward(
-        me_tie, slots, embed_table, norm_gain, weight, short_weight, skip_gain
+    hidden, mixed, table, *pieces = run_forward(
+        me_tie, core_tie, slots, embed_table, norm_gain, weight, short_weight, skip_gain, output_grad
     )
     hidden, grad_slots, other_weight = together(hidden, grad_slots, other_weight)
-    send, kept = run_project(
+    project_parts = run_project(
         core_tie, chip_tie, chips, hidden, tp_exchange(hidden, 1), output_weight, other_weight
     )
 
@@ -699,27 +712,37 @@
         which = chip >> bit & 1
         return [pairs(term, which) for term in terms]
 
-    blocks = (chips // 2, block_rows, half)
+    def halving(parts):
+        leave, stay, kept_leave, kept_stay = parts
+        arrived_leave = tp_exchange(leave, 2)
+        arrived_stay = tp_exchange(stay, 2)
+        return arrived_leave, arrived_stay, kept_leave, kept_stay
+
+    def second_exchange(arrived_leave, kept_leave):
+        return tp_exchange((kept_leave + arrived_leave.astype(f32)).astype(bf16), 4)
+
+    def remaining(terms):
+        terms = [term.reshape(chips // PARTS, block_rows, half) for term in terms]
+        for bit in range(2, levels):
+            terms = keep(terms, bit) + [tp_exchange(leaving(terms, bit), 2 << bit)]
+        return terms
+
     near, others = range(1, shards // 2 + 1), range(shards // 2 + 1, shards)
-    send, kept, me_tie = together(send, kept, me_tie)
-    out_arrived = tp_exchange(send, 2)
-    projection_grad, *pieces = run_backward(
-        me_tie, core_tie, slots, grad_slots, table, short_weight, skip_gain, mixed, output_grad, hidden
-    )
+    project_parts, me_tie, other_input = together(project_parts, me_tie, other_input)
+    out_leave, out_stay, out_kept_leave, out_kept_stay = halving(project_parts)
+    projection_grad = run_backward(me_tie, slots, grad_slots, table, short_weight, skip_gain, mixed)
     projection_grad, pieces = together(projection_grad, pieces)
     other_grad = tp_exchange(projection_grad, 1)
     near_pieces = [ctx_exchange(pieces[step - 1], step) for step in near]
-    grad_send, grad_kept = run_input_grad(
+    grad_parts = run_input_grad(
         core_tie, chip_tie, chips, projection_grad, other_grad, weight, other_input
     )
-    out_terms = [kept.reshape(blocks), out_arrived.reshape(blocks)]
-    for bit in range(1, levels):
-        out_terms = keep(out_terms, bit) + [tp_exchange(leaving(out_terms, bit), 2 << bit)]
-    grad_send, grad_kept, pieces, near_pieces, late_ids = together(
-        grad_send, grad_kept, pieces, near_pieces, token_ids
-    )
-    grad_arrived = tp_exchange(grad_send, 2)
+    out_far = second_exchange(out_leave, out_kept_leave)
+    grad_parts, pieces, near_pieces, late_ids = together(grad_parts, pieces, near_pieces, token_ids)
+    grad_leave, grad_stay, grad_kept_leave, grad_kept_stay = grad_parts
+    grad_leave = tp_exchange(grad_leave, 2)
     far_pieces = [ctx_exchange(pieces[step - 1], step) for step in others]
+    out_terms = remaining([out_kept_stay, out_stay, out_far])
 
     own_ids = lax.dynamic_slice_in_dim(late_ids, chip * block_rows, block_rows, axis=0)
     own_hot = (own_ids[:, None] == jnp.arange(FIRST_ID, FIRST_ID + IDS)[None, :]).astype(bf16)
@@ -734,26 +757,28 @@
         came = tp_exchange(held, 2 * mask)
         line.append(came)
         steps.append([step ^ mask for group in steps for step in group])
-    grad_arrived, far_pieces = together(grad_arrived, far_pieces)
-    grad_terms = [grad_kept.reshape(blocks), grad_arrived.reshape(blocks)]
-    held = jnp.concatenate(line, axis=0)
-    for bit in range(1, levels):
-        grad_terms = keep(grad_terms, bit) + [tp_exchange(leaving(grad_terms, bit), 2 << bit)]
-    came = tp_exchange(held, 2)
-    came_steps = [step ^ 1 for group in steps for step in group]
-
-    base = run_assemble(chips, steps, chip_tie, core_tie, line, [tp_exchange(value, 1) for value in line])
+    outgoing = (grad_kept_leave + grad_leave.astype(f32)).astype(bf16)
+    outgoing, grad_stay = together(outgoing, grad_stay)
+    grad_far, grad_stay = tp_exchange(outgoing, 4), tp_exchange(grad_stay, 2)
+    grad_terms = remaining([grad_kept_stay, grad_stay, grad_far])
+    from_neighbour = [tp_exchange(value, 2) for value in line]
+    neighbour_steps = [[step ^ 1 for step in group] for group in steps]
+
+    came = from_neighbour[-1]
+    line, early_steps = line + from_neighbour[:-1], steps + neighbour_steps[:-1]
+    base = run_assemble(chips, early_steps, chip_tie, core_tie, line, [tp_exchange(value, 1) for value in line])
     mine = near_pieces + far_pieces
     output_weight_grad = run_weight_grad(
         me_tie, core_tie, output_grad, hidden, mine, [tp_exchange(value, 1) for value in mine]
     )
     kept_sum = sum(term.astype(f32) for term in grad_terms[:-1])
-    base, output_weight_grad, came = together(base, output_weight_grad, came)
-    output_weight_grad, kept_sum, last = together(output_weight_grad, kept_sum, grad_terms[-1])
+    base, output_weight_grad, came, kept_sum, last = together(
+        base, output_weight_grad, came, kept_sum, grad_terms[-1]
+    )
     total = (kept_sum + last.astype(f32)).reshape(2, block_rows // 2, half)
     my_rows, their_rows = pick(total, core), pick(total, 1 - core)
     other_columns = tp_exchange(their_rows, 1)
-    block_output = run_insert(came_steps, chip_tie, core_tie, came, tp_exchange(came, 1), base)
+    block_output = run_insert(neighbour_steps[-1], chip_tie, core_tie, came, tp_exchange(came, 1), base)
     normed_grad = jnp.where(
         core == 0,
         jnp.concatenate([my_rows, other_columns], axis=1),

time: 142 us -> 142 us (level)
  Pallas kernels: 61.6 us -> 59.6 us
  other arithmetic: 3.12 us -> 4.91 us
    pallas_call x3, Pallas kernels: 30.4 us -> 28.2 us  [the longest x1 12.2 us: run_backward(): pl.pallas_call(functools.partial(backward_kernel, shards), out_shape=jax....]
    ppermute x17 -> x21, waiting for transfers between devices: 39.3 us -> 37.6 us  [tp_exchange(): return lax.ppermute(value, 'tp', [(i, i ^ mask) for i in range(count)])]
    ppermute x17 -> x21, starting transfers between devices: 12.9 us -> 14.2 us  [tp_exchange(): return lax.ppermute(value, 'tp', [(i, i ^ mask) for i in range(count)])]
    unnamed x34 -> x42, local copies, waits for them, and re-layouts: 3.44 us -> 2.96 us
  transfers between devices with their start and end apart: 26 -> 30, of which waited for: 13 -> 12; matrix products, arithmetic and copies ran while one was open for 4% -> 3% of each run, Pallas kernels for 42% -> 42%
where the time goes in v6:
time: 142 us; the launch traced here: 141 us
  Pallas kernels  59.6 us (42%)
  waiting for transfers between devices  45 us (32%)
  starting transfers between devices  25.6 us (18%)
  other arithmetic  4.91 us (3%)
  local copies, waits for them, and re-layouts  3.77 us (3%)
    ppermute x21, waiting for transfers between devices, tp_exchange(): return lax.ppermute(value, 'tp', [(i, i ^ mask) for i in range(count)])  37.6 us
    ppermute x21, starting transfers between devices, tp_exchange(): return lax.ppermute(value, 'tp', [(i, i ^ mask) for i in range(count)])  14.2 us
    pallas_call x1, Pallas kernels, run_forward(): pl.pallas_call(functools.partial(forward_kernel, shards), grid=(1,), out_...  13.7 us
    pallas_call x1, Pallas kernels, run_backward(): pl.pallas_call(functools.partial(backward_kernel, shards), out_shape=jax....  12.2 us
    ppermute x9, starting transfers between devices, ctx_exchange(): return lax.ppermute(value, 'ctx', [(i, i ^ step) for i in range(count)])  11.4 us
    pallas_call x1, Pallas kernels, run_input_grad(): pl.pallas_call(functools.partial(input_grad_kernel, chips), out_shape=par...  10.2 us
    ppermute x9, waiting for transfers between devices, ctx_exchange(): return lax.ppermute(value, 'ctx', [(i, i ^ step) for i in range(count)])  7.45 us
    pallas_call x1, Pallas kernels, run_weight_grad(): pl.pallas_call(functools.partial(weight_grad_kernel, shards), out_shape=j...  6.45 us
  transfers between devices with their start and end apart: 30, of which 12 were waited for; matrix products, arithmetic and copies ran while one was open for 3% of the time, Pallas kernels for 42%

profile of v6, /device:TPU:0, one launch (start us, length us, event | category | flops | bytes accessed | tf_op | source)
XLA Modules:
  0.0 141.1 jit_solution(13662298046729131302)
XLA Ops:
  0.6 0.5 collective-permute-start.8
  1.1 0.1 collective-permute-start.6
  1.2 1.4 %pack.1.refs_0_ = f32[40,384]{1,0:T(8,128)} custom-call(f32[32,384]{1,0:T(8,128)} %filters_ref.1, s32[384]{0:T(512)} %ids_ref.1), custom_call_target="tpu_custom_call" | custom-call | flops 1000 | bytes 1000 | tf_op jit(solution)/shard_map/pack/pallas_call | solution.py:626
  2.7 2.9 %collective-permute-start = (f32[40,384]{1,0:T(8,128)}, f32[40,384]{1,0:T(8,128)S(1)}, u32[]{:S(2)}, u32[]{:S(2)}) collective-permute-start(f32[40,384]{1,0:T(8,128)} %pack.1.refs_0_), channel_id=1, source_target_pairs={{0,8},{8,0},{16,24},{24,16},{1,9},{9,1},{17,25},{25,17},{2,10},{10... | collective-permute-start | bytes 184328 | tf_op jit(solution)/shard_map/ppermute | solution.py:639
  5.6 1.5 %collective-permute-start.1 = (f32[40,384]{1,0:T(8,128)}, f32[40,384]{1,0:T(8,128)S(1)}, u32[]{:S(2)}, u32[]{:S(2)}) collective-permute-start(f32[40,384]{1,0:T(8,128)} %pack.1.refs_0_), channel_id=1, source_target_pairs={{0,16},{8,24},{16,0},{24,8},{1,17},{9,25},{17,1},{25,9},{2,18},{10... | collective-permute-start | bytes 184328 | tf_op jit(solution)/shard_map/ppermute | solution.py:639
  7.1 0.0 collective-permute-start.2
  7.1 4.4 %hidden_grad.1.refs_4_ = bf16[512,384]{1,0:T(8,128)(2,1)} custom-call(bf16[384,4096]{1,0:T(8,128)(2,1)} %grad_ref.3, bf16[4096,512]{1,0:T(8,128)(2,1)} %weight_ref.3), custom_call_target="tpu_custom_call" | custom-call | flops 1000 | bytes 1000 | tf_op jit(solution)/shard_map/hidden_grad/pallas_call | solution.py:586
  11.5 0.0 collective-permute-done.refs_1_
  11.6 0.8 collective-permute-done.2.refs_3_
  12.4 1.2 collective-permute-start.3
  13.6 1.5 %collective-permute-start.4 = (bf16[512,384]{1,0:T(8,128)(2,1)}, bf16[512,384]{1,0:T(8,128)(2,1)S(1)}, u32[]{:S(2)}, u32[]{:S(2)}) collective-permute-start(bf16[512,384]{1,0:T(8,128)(2,1)} %hidden_grad.1.refs_4_), channel_id=1, source_target_pairs={{0,16},{8,24},{16,0},{24,8},{1,17},{9,25},{17,1},{25,9},{2,18},{10... | collective-permute-start | bytes 1179656 | tf_op jit(solution)/shard_map/ppermute | solution.py:639
  15.2 0.8 collective-permute-start.5
  15.9 13.7 %forward_conv.1 = (bf16[384,512]{1,0:T(8,128)(2,1)}, f32[512,512]{1,0:T(8,128)}, f32[3,32,512]{2,1,0:T(8,128)}, bf16[384,1024]{1,0:T(8,128)(2,1)}, bf16[384,1024]{1,0:T(8,128)(2,1)}, /*index=5*/bf16[384,1024]{1,0:T(8,128)(2,1)}) custom-call(s32[1]{0:T(128)} %bitcast.2.me_ref, s32[1]{0:T(128)} %bitcast.1.core_ref, f32[40,384]{1,0:T(8,128)} %pack.1.refs_0_, ...), custom_call_target="tpu_custom_call" | custom-call | flops 20000000000 | bytes 10000000 | tf_op jit(solution)/shard_map/forward_conv/pallas_call | solution.py:479
  29.6 0.0 collective-permute-done.3.refs_5_
  29.7 2.6 %collective-permute-done.4.refs_6_ = bf16[512,384]{1,0:T(8,128)(2,1)S(1)} collective-permute-done((bf16[512,384]{1,0:T(8,128)(2,1)}, bf16[512,384]{1,0:T(8,128)(2,1)S(1)}, u32[]{:S(2)}, u32[]{:S(2)}) %collective-permute-start.4) | collective-permute-done | bytes 393248 | tf_op jit(solution)/shard_map/ppermute | solution.py:639
  32.3 0.1 collective-permute-start.7
  32.4 1.9 %collective-permute-done.7.other_ref = bf16[384,512]{1,0:T(8,128)(2,1)S(1)} collective-permute-done((bf16[384,512]{1,0:T(8,128)(2,1)}, bf16[384,512]{1,0:T(8,128)(2,1)S(1)}, u32[]{:S(2)}, u32[]{:S(2)}) %collective-permute-start.7) | collective-permute-done | bytes 393248 | tf_op jit(solution)/shard_map/ppermute | solution.py:648
  34.3 0.7 copy-done.8
  35.0 5.7 %project.1 = (bf16[96,2048]{1,0:T(8,128)(2,1)}, bf16[96,2048]{1,0:T(8,128)(2,1)}, f32[96,2048]{1,0:T(8,128)}, f32[96,2048]{1,0:T(8,128)}) custom-call(s32[1]{0:T(128)} %bitcast.1.core_ref, s32[1]{0:T(128)} %bitcast.chip_ref, bf16[384,512]{1,0:T(8,128)(2,1)} %get-tuple-element.60.hidden_ref, bf16[384,512]{1,0:T(8,128)(2,1)} %copy-done.8, ...), custom_call_target="tpu_custom_call" | custom-call | flops 1000 | bytes 1000 | tf_op jit(solution)/shard_map/project/pallas_call | solution.py:518
  40.8 0.0 collective-permute-done.8.other_weight_ref
  40.8 1.6 %collective-permute-start.13 = (bf16[96,2048]{1,0:T(8,128)(2,1)}, bf16[96,2048]{1,0:T(8,128)(2,1)S(1)}, u32[]{:S(2)}, u32[]{:S(2)}) collective-permute-start(bf16[96,2048]{1,0:T(8,128)(2,1)} %get-tuple-element.89), channel_id=1, source_target_pairs={{0,2},{1,3},{2,0},{3,1},{4,6},{5,7},{6,4},{7,5},{8,10},{9,11},{10,... | collective-permute-start | bytes 1179656 | tf_op jit(solution)/shard_map/ppermute | solution.py:648
  42.4 12.2 %backward_conv.1.grad_ref = bf16[3,384,512]{2,1,0:T(8,128)(2,1)} custom-call(s32[1]{0:T(128)} %bitcast.2.me_ref, f32[40,384]{1,0:T(8,128)} %pack.1.refs_0_, f32[40,384]{1,0:T(8,128)} %copy-done.18, f32[40,384]{1,0:T(8,128)} %copy-done.19, f32[40,384]{1,0:T(8,128)} %copy-done.20, bf16[512,384]{1,0:T(8,128)(2,1)} %hidden_grad.1.refs_4_, ...), custom_call_target="tpu_custom_call" | custom-call | flops 20000000000 | bytes 10000000 | tf_op jit(solution)/shard_map/backward_conv/pallas_call | solution.py:548
  54.6 0.4 collective-permute-start.12
  55.1 1.2 collective-permute-start.10
  56.3 0.9 collective-permute-start.11
  57.2 0.8 add_convert_fusion.2
  58.0 2.6 %collective-permute-start.14 = (bf16[96,2048]{1,0:T(8,128)(2,1)}, bf16[96,2048]{1,0:T(8,128)(2,1)S(1)}, u32[]{:S(2)}, u32[]{:S(2)}) collective-permute-start(bf16[96,2048]{1,0:T(8,128)(2,1)} %add_convert_fusion.2), channel_id=1, source_target_pairs={{0,4},{1,5},{2,6},{3,7},{4,0},{5,1},{6,2},{7,3},{8,12},{9,13},{10,... | collective-permute-start | bytes 1179656 | tf_op jit(solution)/shard_map/ppermute | solution.py:648
  60.6 0.0 copy-start.1
  60.6 1.0 copy-done.1
  61.6 10.2 %input_grad.1 = (bf16[96,2048]{1,0:T(8,128)(2,1)}, bf16[96,2048]{1,0:T(8,128)(2,1)}, f32[96,2048]{1,0:T(8,128)}, f32[96,2048]{1,0:T(8,128)}) custom-call(s32[1]{0:T(128)} %bitcast.1.core_ref, s32[1]{0:T(128)} %bitcast.chip_ref, bf16[3,384,512]{2,1,0:T(8,128)(2,1)} %backward_conv.1.grad_ref, bf16[3,384,512]{2,1,0:T(8,128)(2,1)} %copy-done.1, ...), custom_call_target="tpu_custom_call" | custom-call | flops 1000 | bytes 1000 | tf_op jit(solution)/shard_map/input_grad/pallas_call | solution.py:606
  71.9 3.1 %collective-permute-done.10.refs_0_ = bf16[384,1024]{1,0:T(8,128)(2,1)S(1)} collective-permute-done((bf16[384,1024]{1,0:T(8,128)(2,1)}, bf16[384,1024]{1,0:T(8,128)(2,1)S(1)}, u32[]{:S(2)}, u32[]{:S(2)}) %collective-permute-start.10) | collective-permute-done | bytes 786464 | tf_op jit(solution)/shard_map/ppermute | solution.py:639
  75.0 0.9 collective-permute-done.11.refs_1_
  75.9 0.8 dynamic_slice.13
  76.7 0.0 collective-permute-done.12
  76.7 1.6 %collective-permute-done.14 = bf16[96,2048]{1,0:T(8,128)(2,1)S(1)} collective-permute-done((bf16[96,2048]{1,0:T(8,128)(2,1)}, bf16[96,2048]{1,0:T(8,128)(2,1)S(1)}, u32[]{:S(2)}, u32[]{:S(2)}) %collective-permute-start.14) | collective-permute-done | bytes 393248 | tf_op jit(solution)/shard_map/ppermute | solution.py:648
  78.3 1.2 add_convert_fusion.1.refs_0_
  79.5 1.1 collective-permute-start.15
  80.6 3.1 %collective-permute-start.16 = (bf16[96,2048]{1,0:T(8,128)(2,1)S(1)}, bf16[96,2048]{1,0:T(8,128)(2,1)}, u32[]{:S(2)}, u32[]{:S(2)}) collective-permute-start(bf16[96,2048]{1,0:T(8,128)(2,1)S(1)} %add_convert_fusion.1.refs_0_), channel_id=1, source_target_pairs={{0,2},{1,3},{2,0},{3,1},{4,6},{5,7},{6,4},{7,5},{8,10},{9,11},{10,... | collective-permute-start | bytes 1179656 | tf_op jit(solution)/shard_map/ppermute | solution.py:648
  83.8 0.0 collective-permute-start.25
  83.8 1.4 collective-permute-start.20
  85.2 0.0 collective-permute-start.17
  85.2 13.7 %collective-permute-done.15.refs_1_ = bf16[96,2048]{1,0:T(8,128)(2,1)S(1)} collective-permute-done((bf16[96,2048]{1,0:T(8,128)(2,1)S(1)}, bf16[96,2048]{1,0:T(8,128)(2,1)S(1)}, u32[]{:S(2)}, u32[]{:S(2)}) %collective-permute-start.15) | collective-permute-done | bytes 393248 | tf_op jit(solution)/shard_map/ppermute | solution.py:648
  98.9 2.4 %collective-permute-done.16.refs_2_ = bf16[96,2048]{1,0:T(8,128)(2,1)} collective-permute-done((bf16[96,2048]{1,0:T(8,128)(2,1)S(1)}, bf16[96,2048]{1,0:T(8,128)(2,1)}, u32[]{:S(2)}, u32[]{:S(2)}) %collective-permute-start.16) | collective-permute-done | bytes 393248 | tf_op jit(solution)/shard_map/ppermute | solution.py:648
  101.3 0.0 collective-permute-start.19
  101.3 6.1 %collective-permute-done.25 = bf16[96,2048]{1,0:T(8,128)(2,1)S(1)} collective-permute-done((bf16[96,2048]{1,0:T(8,128)(2,1)}, bf16[96,2048]{1,0:T(8,128)(2,1)S(1)}, u32[]{:S(2)}, u32[]{:S(2)}) %collective-permute-start.25) | collective-permute-done | bytes 393248 | tf_op jit(solution)/shard_map/ppermute | solution.py:648
  107.4 2.0 %add_convert_fusion = bf16[96,2048]{1,0:T(8,128)(2,1)} fusion(f32[96,2048]{1,0:T(8,128)} %get-tuple-element.94, bf16[96,2048]{1,0:T(8,128)(2,1)S(1)} %collective-permute-done.25), kind=kLoop, calls=%fused_computation.3 | loop fusion | flops 589824 | bytes 1572864 | tf_op jit(solution)/shard_map/convert_element_type | solution.py:760
  109.3 0.3 collective-permute-start.26
  109.6 0.5 collective-permute-start.22
  110.1 0.2 copy-done.11
  110.4 0.2 copy-done.12
  110.5 0.4 collective-permute-start.23
  110.9 2.9 %collective-permute-start.27 = (bf16[96,2048]{1,0:T(8,128)(2,1)}, bf16[96,2048]{1,0:T(8,128)(2,1)S(1)}, u32[]{:S(2)}, u32[]{:S(2)}) collective-permute-start(bf16[96,2048]{1,0:T(8,128)(2,1)} %add_convert_fusion), channel_id=1, source_target_pairs={{0,4},{1,5},{2,6},{3,7},{4,0},{5,1},{6,2},{7,3},{8,12},{9,13},{10,... | collective-permute-start | bytes 1179656 | tf_op jit(solution)/shard_map/ppermute | solution.py:648
  113.8 3.4 %assemble.1.base_ref = bf16[384,4096]{1,0:T(8,128)(2,1)} custom-call(s32[1]{0:T(128)} %bitcast.chip_ref, s32[1]{0:T(128)} %bitcast.1.core_ref, bf16[96,2048]{1,0:T(8,128)(2,1)} %copy-done, bf16[96,2048]{1,0:T(8,128)(2,1)} %copy-done.9, bf16[96,2048]{1,0:T(8,128)(2,1)} %collective-permute-done.16.refs_2_, bf16[96,2048]{1,0:T(8,128)(2,1)} %copy-done.11, ...), custom_call_target="tpu_custom_call" | custom-call | flops 1000 | bytes 1000 | tf_op jit(solution)/shard_map/assemble/pallas_call | solution.py:460
  117.2 7.7 %collective-permute-done.26 = bf16[96,2048]{1,0:T(8,128)(2,1)} collective-permute-done((bf16[96,2048]{1,0:T(8,128)(2,1)}, bf16[96,2048]{1,0:T(8,128)(2,1)}, u32[]{:S(2)}, u32[]{:S(2)}) %collective-permute-start.26) | collective-permute-done | bytes 393248 | tf_op jit(solution)/shard_map/ppermute | solution.py:648
  124.9 1.1 add_bitcast_fusion
  126.0 6.4 %weight_grad.1 = f32[1024,512]{1,0:T(8,128)} custom-call(s32[1]{0:T(128)} %bitcast.2.me_ref, s32[1]{0:T(128)} %bitcast.1.core_ref, bf16[384,4096]{1,0:T(8,128)(2,1)} %grad_ref.3, bf16[384,512]{1,0:T(8,128)(2,1)} %get-tuple-element.60.hidden_ref, bf16[384,1024]{1,0:T(8,128)(2,1)} %copy-done.5, bf16[384,1024]{1,0:T(8,128)(2,1)} %copy-done.6, ...), custom_call_target="tpu_custom_call" | custom-call | flops 1000 | bytes 1000 | tf_op jit(solution)/shard_map/weight_grad/pallas_call | solution.py:571
  132.5 2.9 %collective-permute-done.24.own_ref = bf16[96,2048]{1,0:T(8,128)(2,1)} collective-permute-done((bf16[96,2048]{1,0:T(8,128)(2,1)S(1)}, bf16[96,2048]{1,0:T(8,128)(2,1)}, u32[]{:S(2)}, u32[]{:S(2)}) %collective-permute-start.24) | collective-permute-done | bytes 393248 | tf_op jit(solution)/shard_map/ppermute | solution.py:648
  135.4 0.1 convert_add_fusion
  135.5 0.1 dynamic-slice_bitcast_fusion.1
  135.6 0.6 collective-permute-start.29
  136.1 1.2 collective-permute-done.28.theirs_ref
  137.4 0.7 copy-done.13
  138.1 2.0 %insert.1 = bf16[384,4096]{1,0:T(8,128)(2,1)} custom-call(s32[1]{0:T(128)} %bitcast.chip_ref, s32[1]{0:T(128)} %bitcast.1.core_ref, bf16[96,2048]{1,0:T(8,128)(2,1)} %collective-permute-done.24.own_ref, bf16[96,2048]{1,0:T(8,128)(2,1)} %copy-done.13, bf16[384,4096]{1,0:T(8,128)(2,1)} %assemble.1.base_ref), custom_call_target="tpu_custom_call", output_to_operand_aliasing={{}: (4, {})} | custom-call | flops 1000 | bytes 1000 | tf_op jit(solution)/shard_map/insert/pallas_call | solution.py:445
  140.1 1.0 maximum_select_fusion
  (56 shorter events, 0.1 us)
Async XLA Ops:
  0.6 40.1 %collective-permute-start.8 = (bf16[3,4096,512]{2,1,0:T(8,128)(2,1)}, bf16[3,4096,512]{2,1,0:T(8,128)(2,1)}, u32[]{:S(2)}, u32[]{:S(2)}) collective-permute-start(bf16[3,4096,512]{2,1,0:T(8,128)(2,1)} %bitcast.13), channel_id=1, source_target_pairs={{0,1},{1,0},{2,3},{3,2},{4,5},{5,4},{6,7},{7,6},{8,9},{9,8},{10,11... | collective-permute-start | bytes 37748744 | tf_op jit(solution)/shard_map/ppermute | solution.py:648
  1.1 31.1 %collective-permute-start.6 = (bf16[4096,512]{1,0:T(8,128)(2,1)}, bf16[4096,512]{1,0:T(8,128)(2,1)}, u32[]{:S(2)}, u32[]{:S(2)}) collective-permute-start(bf16[4096,512]{1,0:T(8,128)(2,1)} %weight_ref.3), channel_id=1, source_target_pairs={{0,1},{1,0},{2,3},{3,2},{4,5},{5,4},{6,7},{7,6},{8,9},{9,8},{10,11... | collective-permute-start | bytes 12582920 | tf_op jit(solution)/shard_map/ppermute | solution.py:648
  2.7 8.9 %collective-permute-start = (f32[40,384]{1,0:T(8,128)}, f32[40,384]{1,0:T(8,128)S(1)}, u32[]{:S(2)}, u32[]{:S(2)}) collective-permute-start(f32[40,384]{1,0:T(8,128)} %pack.1.refs_0_), channel_id=1, source_target_pairs={{0,8},{8,0},{16,24},{24,16},{1,9},{9,1},{17,25},{25,17},{2,10},{10... | collective-permute-start | bytes 184328 | tf_op jit(solution)/shard_map/ppermute | solution.py:639
  5.6 6.0 %collective-permute-start.1 = (f32[40,384]{1,0:T(8,128)}, f32[40,384]{1,0:T(8,128)S(1)}, u32[]{:S(2)}, u32[]{:S(2)}) collective-permute-start(f32[40,384]{1,0:T(8,128)} %pack.1.refs_0_), channel_id=1, source_target_pairs={{0,16},{8,24},{16,0},{24,8},{1,17},{9,25},{17,1},{25,9},{2,18},{10... | collective-permute-start | bytes 184328 | tf_op jit(solution)/shard_map/ppermute | solution.py:639
  7.1 5.3 %collective-permute-start.2 = (f32[40,384]{1,0:T(8,128)}, f32[40,384]{1,0:T(8,128)S(1)}, u32[]{:S(2)}, u32[]{:S(2)}) collective-permute-start(f32[40,384]{1,0:T(8,128)} %pack.1.refs_0_), channel_id=1, source_target_pairs={{0,24},{8,16},{16,8},{24,0},{1,25},{9,17},{17,9},{25,1},{2,26},{10... | collective-permute-start | bytes 184328 | tf_op jit(solution)/shard_map/ppermute | solution.py:639
  11.6 4.4 %copy-start.18 = (f32[40,384]{1,0:T(8,128)}, f32[40,384]{1,0:T(8,128)S(1)}, u32[]{:S(2)}) copy-start(f32[40,384]{1,0:T(8,128)S(1)} %collective-permute-done.refs_1_) | copy-start | bytes 184324
  11.6 4.4 %copy-start.19 = (f32[40,384]{1,0:T(8,128)}, f32[40,384]{1,0:T(8,128)S(1)}, u32[]{:S(2)}) copy-start(f32[40,384]{1,0:T(8,128)S(1)} %collective-permute-done.1.refs_2_) | copy-start | bytes 184324
  12.4 3.5 %copy-start.20 = (f32[40,384]{1,0:T(8,128)}, f32[40,384]{1,0:T(8,128)S(1)}, u32[]{:S(2)}) copy-start(f32[40,384]{1,0:T(8,128)S(1)} %collective-permute-done.2.refs_3_) | copy-start | bytes 184324
  12.4 17.2 %collective-permute-start.3 = (bf16[512,384]{1,0:T(8,128)(2,1)}, bf16[512,384]{1,0:T(8,128)(2,1)S(1)}, u32[]{:S(2)}, u32[]{:S(2)}) collective-permute-start(bf16[512,384]{1,0:T(8,128)(2,1)} %hidden_grad.1.refs_4_), channel_id=1, source_target_pairs={{0,8},{8,0},{16,24},{24,16},{1,9},{9,1},{17,25},{25,17},{2,10},{10... | collective-permute-start | bytes 1179656 | tf_op jit(solution)/shard_map/ppermute | solution.py:639
  13.6 18.6 %collective-permute-start.4 = (bf16[512,384]{1,0:T(8,128)(2,1)}, bf16[512,384]{1,0:T(8,128)(2,1)S(1)}, u32[]{:S(2)}, u32[]{:S(2)}) collective-permute-start(bf16[512,384]{1,0:T(8,128)(2,1)} %hidden_grad.1.refs_4_), channel_id=1, source_target_pairs={{0,16},{8,24},{16,0},{24,8},{1,17},{9,25},{17,1},{25,9},{2,18},{10... | collective-permute-start | bytes 1179656 | tf_op jit(solution)/shard_map/ppermute | solution.py:639
  15.2 17.1 %collective-permute-start.5 = (bf16[512,384]{1,0:T(8,128)(2,1)}, bf16[512,384]{1,0:T(8,128)(2,1)S(1)}, u32[]{:S(2)}, u32[]{:S(2)}) collective-permute-start(bf16[512,384]{1,0:T(8,128)(2,1)} %hidden_grad.1.refs_4_), channel_id=1, source_target_pairs={{0,24},{8,16},{16,8},{24,0},{1,25},{9,17},{17,9},{25,1},{2,26},{10... | collective-permute-start | bytes 1179656 | tf_op jit(solution)/shard_map/ppermute | solution.py:639
  29.7 12.7 %copy-start.15 = (bf16[512,384]{1,0:T(8,128)(2,1)}, bf16[512,384]{1,0:T(8,128)(2,1)S(1)}, u32[]{:S(2)}) copy-start(bf16[512,384]{1,0:T(8,128)(2,1)S(1)} %collective-permute-done.3.refs_5_) | copy-start | bytes 1179652
  32.3 10.2 %copy-start.16 = (bf16[512,384]{1,0:T(8,128)(2,1)}, bf16[512,384]{1,0:T(8,128)(2,1)S(1)}, u32[]{:S(2)}) copy-start(bf16[512,384]{1,0:T(8,128)(2,1)S(1)} %collective-permute-done.4.refs_6_) | copy-start | bytes 1179652
  32.3 10.2 %copy-start.17 = (bf16[512,384]{1,0:T(8,128)(2,1)}, bf16[512,384]{1,0:T(8,128)(2,1)S(1)}, u32[]{:S(2)}) copy-start(bf16[512,384]{1,0:T(8,128)(2,1)S(1)} %collective-permute-done.5.refs_7_) | copy-start | bytes 1179652
  32.3 2.0 %collective-permute-start.7 = (bf16[384,512]{1,0:T(8,128)(2,1)}, bf16[384,512]{1,0:T(8,128)(2,1)S(1)}, u32[]{:S(2)}, u32[]{:S(2)}) collective-permute-start(bf16[384,512]{1,0:T(8,128)(2,1)} %get-tuple-element.60.hidden_ref), channel_id=1, source_target_pairs={{0,1},{1,0},{2,3},{3,2},{4,5},{5,4},{6,7},{7,6},{8,9},{9,8},{10,11... | collective-permute-start | bytes 1179656 | tf_op jit(solution)/shard_map/ppermute | solution.py:648
  34.3 0.7 copy-start.8
  40.8 16.4 %collective-permute-start.13 = (bf16[96,2048]{1,0:T(8,128)(2,1)}, bf16[96,2048]{1,0:T(8,128)(2,1)S(1)}, u32[]{:S(2)}, u32[]{:S(2)}) collective-permute-start(bf16[96,2048]{1,0:T(8,128)(2,1)} %get-tuple-element.89), channel_id=1, source_target_pairs={{0,2},{1,3},{2,0},{3,1},{4,6},{5,7},{6,4},{7,5},{8,10},{9,11},{10,... | collective-permute-start | bytes 1179656 | tf_op jit(solution)/shard_map/ppermute | solution.py:648
  42.4 14.8 %copy-start.3 = (f32[96,2048]{1,0:T(8,128)S(1)}, f32[96,2048]{1,0:T(8,128)}, u32[]{:S(2)}) copy-start(f32[96,2048]{1,0:T(8,128)} %get-tuple-element.88) | copy-start | bytes 2359300
  54.6 6.0 %collective-permute-start.9 = (bf16[3,384,512]{2,1,0:T(8,128)(2,1)}, bf16[3,384,512]{2,1,0:T(8,128)(2,1)S(1)}, u32[]{:S(2)}, u32[]{:S(2)}) collective-permute-start(bf16[3,384,512]{2,1,0:T(8,128)(2,1)} %backward_conv.1.grad_ref), channel_id=1, source_target_pairs={{0,1},{1,0},{2,3},{3,2},{4,5},{5,4},{6,7},{7,6},{8,9},{9,8},{10,11... | collective-permute-start | bytes 3538952 | tf_op jit(solution)/shard_map/ppermute | solution.py:648
  54.6 22.0 %collective-permute-start.12 = (bf16[96,2048]{1,0:T(8,128)(2,1)}, bf16[96,2048]{1,0:T(8,128)(2,1)S(1)}, u32[]{:S(2)}, u32[]{:S(2)}) collective-permute-start(bf16[96,2048]{1,0:T(8,128)(2,1)} %get-tuple-element.87), channel_id=1, source_target_pairs={{0,2},{1,3},{2,0},{3,1},{4,6},{5,7},{6,4},{7,5},{8,10},{9,11},{10,... | collective-permute-start | bytes 1179656 | tf_op jit(solution)/shard_map/ppermute | solution.py:648
  55.1 19.9 %collective-permute-start.10 = (bf16[384,1024]{1,0:T(8,128)(2,1)}, bf16[384,1024]{1,0:T(8,128)(2,1)S(1)}, u32[]{:S(2)}, u32[]{:S(2)}) collective-permute-start(bf16[384,1024]{1,0:T(8,128)(2,1)} %get-tuple-element.82), channel_id=1, source_target_pairs={{0,8},{8,0},{16,24},{24,16},{1,9},{9,1},{17,25},{25,17},{2,10},{10... | collective-permute-start | bytes 2359304 | tf_op jit(solution)/shard_map/ppermute | solution.py:639
  56.3 19.6 %collective-permute-start.11 = (bf16[384,1024]{1,0:T(8,128)(2,1)}, bf16[384,1024]{1,0:T(8,128)(2,1)S(1)}, u32[]{:S(2)}, u32[]{:S(2)}) collective-permute-start(bf16[384,1024]{1,0:T(8,128)(2,1)} %get-tuple-element.83), channel_id=1, source_target_pairs={{0,16},{8,24},{16,0},{24,8},{1,17},{9,25},{17,1},{25,9},{2,18},{10... | collective-permute-start | bytes 2359304 | tf_op jit(solution)/shard_map/ppermute | solution.py:639
  58.0 20.3 %collective-permute-start.14 = (bf16[96,2048]{1,0:T(8,128)(2,1)}, bf16[96,2048]{1,0:T(8,128)(2,1)S(1)}, u32[]{:S(2)}, u32[]{:S(2)}) collective-permute-start(bf16[96,2048]{1,0:T(8,128)(2,1)} %add_convert_fusion.2), channel_id=1, source_target_pairs={{0,4},{1,5},{2,6},{3,7},{4,0},{5,1},{6,2},{7,3},{8,12},{9,13},{10,... | collective-permute-start | bytes 1179656 | tf_op jit(solution)/shard_map/ppermute | solution.py:648
  60.6 17.7 %copy-start.2 = (f32[96,2048]{1,0:T(8,128)S(1)}, f32[96,2048]{1,0:T(8,128)}, u32[]{:S(2)}) copy-start(f32[96,2048]{1,0:T(8,128)} %get-tuple-element.86) | copy-start | bytes 2359300
  60.6 23.2 %copy-start.14 = (bf16[384,1024]{1,0:T(8,128)(2,1)S(1)}, bf16[384,1024]{1,0:T(8,128)(2,1)}, u32[]{:S(2)}) copy-start(bf16[384,1024]{1,0:T(8,128)(2,1)} %get-tuple-element.92) | copy-start | bytes 2359300
  60.6 1.0 copy-start.1
  75.0 42.2 %copy-start.5 = (bf16[384,1024]{1,0:T(8,128)(2,1)}, bf16[384,1024]{1,0:T(8,128)(2,1)S(1)}, u32[]{:S(2)}) copy-start(bf16[384,1024]{1,0:T(8,128)(2,1)S(1)} %collective-permute-done.10.refs_0_) | copy-start | bytes 2359300
  75.9 41.3 %copy-start.6 = (bf16[384,1024]{1,0:T(8,128)(2,1)}, bf16[384,1024]{1,0:T(8,128)(2,1)S(1)}, u32[]{:S(2)}) copy-start(bf16[384,1024]{1,0:T(8,128)(2,1)S(1)} %collective-permute-done.11.refs_1_) | copy-start | bytes 2359300
  76.7 48.3 %copy-start.4 = (f32[96,2048]{1,0:T(8,128)S(1)}, f32[96,2048]{1,0:T(8,128)}, u32[]{:S(2)}) copy-start(f32[96,2048]{1,0:T(8,128)} %get-tuple-element.93) | copy-start | bytes 2359300
  79.5 34.3 %copy-start = (bf16[96,2048]{1,0:T(8,128)(2,1)}, bf16[96,2048]{1,0:T(8,128)(2,1)S(1)}, u32[]{:S(2)}) copy-start(bf16[96,2048]{1,0:T(8,128)(2,1)S(1)} %add_convert_fusion.1.refs_0_) | copy-start | bytes 1179652
  79.5 19.3 %collective-permute-start.15 = (bf16[96,2048]{1,0:T(8,128)(2,1)S(1)}, bf16[96,2048]{1,0:T(8,128)(2,1)S(1)}, u32[]{:S(2)}, u32[]{:S(2)}) collective-permute-start(bf16[96,2048]{1,0:T(8,128)(2,1)S(1)} %add_convert_fusion.1.refs_0_), channel_id=1, source_target_pairs={{0,4},{1,5},{2,6},{3,7},{4,0},{5,1},{6,2},{7,3},{8,12},{9,13},{10,... | collective-permute-start | bytes 1179656 | tf_op jit(solution)/shard_map/ppermute | solution.py:648
  80.6 20.6 %collective-permute-start.16 = (bf16[96,2048]{1,0:T(8,128)(2,1)S(1)}, bf16[96,2048]{1,0:T(8,128)(2,1)}, u32[]{:S(2)}, u32[]{:S(2)}) collective-permute-start(bf16[96,2048]{1,0:T(8,128)(2,1)S(1)} %add_convert_fusion.1.refs_0_), channel_id=1, source_target_pairs={{0,2},{1,3},{2,0},{3,1},{4,6},{5,7},{6,4},{7,5},{8,10},{9,11},{10,... | collective-permute-start | bytes 1179656 | tf_op jit(solution)/shard_map/ppermute | solution.py:648
  83.8 23.6 %collective-permute-start.25 = (bf16[96,2048]{1,0:T(8,128)(2,1)}, bf16[96,2048]{1,0:T(8,128)(2,1)S(1)}, u32[]{:S(2)}, u32[]{:S(2)}) collective-permute-start(bf16[96,2048]{1,0:T(8,128)(2,1)} %get-tuple-element.95), channel_id=1, source_target_pairs={{0,2},{1,3},{2,0},{3,1},{4,6},{5,7},{6,4},{7,5},{8,10},{9,11},{10,... | collective-permute-start | bytes 1179656 | tf_op jit(solution)/shard_map/ppermute | solution.py:648
  83.8 26.3 %collective-permute-start.20 = (bf16[384,1024]{1,0:T(8,128)(2,1)S(1)}, bf16[384,1024]{1,0:T(8,128)(2,1)S(1)}, u32[]{:S(2)}, u32[]{:S(2)}) collective-permute-start(bf16[384,1024]{1,0:T(8,128)(2,1)S(1)} %copy-done.14), channel_id=1, source_target_pairs={{0,24},{8,16},{16,8},{24,0},{1,25},{9,17},{17,9},{25,1},{2,26},{10... | collective-permute-start | bytes 2359304 | tf_op jit(solution)/shard_map/ppermute | solution.py:639
  85.2 24.4 %collective-permute-start.17 = (bf16[96,2048]{1,0:T(8,128)(2,1)S(1)}, bf16[96,2048]{1,0:T(8,128)(2,1)S(1)}, u32[]{:S(2)}, u32[]{:S(2)}) collective-permute-start(bf16[96,2048]{1,0:T(8,128)(2,1)S(1)} %add_convert_fusion.1.refs_0_), channel_id=1, source_target_pairs={{0,1},{1,0},{2,3},{3,2},{4,5},{5,4},{6,7},{7,6},{8,9},{9,8},{10,11... | collective-permute-start | bytes 1179656 | tf_op jit(solution)/shard_map/ppermute | solution.py:648
  98.9 11.3 %copy-start.9 = (bf16[96,2048]{1,0:T(8,128)(2,1)}, bf16[96,2048]{1,0:T(8,128)(2,1)S(1)}, u32[]{:S(2)}) copy-start(bf16[96,2048]{1,0:T(8,128)(2,1)S(1)} %collective-permute-done.15.refs_1_) | copy-start | bytes 1179652
  98.9 10.8 %collective-permute-start.18 = (bf16[96,2048]{1,0:T(8,128)(2,1)S(1)}, bf16[96,2048]{1,0:T(8,128)(2,1)S(1)}, u32[]{:S(2)}, u32[]{:S(2)}) collective-permute-start(bf16[96,2048]{1,0:T(8,128)(2,1)S(1)} %collective-permute-done.15.refs_1_), channel_id=1, source_target_pairs={{0,1},{1,0},{2,3},{3,2},{4,5},{5,4},{6,7},{7,6},{8,9},{9,8},{10,11... | collective-permute-start | bytes 1179656 | tf_op jit(solution)/shard_map/ppermute | solution.py:648
  101.3 9.6 %collective-permute-start.19 = (bf16[96,2048]{1,0:T(8,128)(2,1)}, bf16[96,2048]{1,0:T(8,128)(2,1)}, u32[]{:S(2)}, u32[]{:S(2)}) collective-permute-start(bf16[96,2048]{1,0:T(8,128)(2,1)} %collective-permute-done.16.refs_2_), channel_id=1, source_target_pairs={{0,1},{1,0},{2,3},{3,2},{4,5},{5,4},{6,7},{7,6},{8,9},{9,8},{10,11... | collective-permute-start | bytes 1179656 | tf_op jit(solution)/shard_map/ppermute | solution.py:648
  109.3 15.6 %collective-permute-start.26 = (bf16[96,2048]{1,0:T(8,128)(2,1)}, bf16[96,2048]{1,0:T(8,128)(2,1)}, u32[]{:S(2)}, u32[]{:S(2)}) collective-permute-start(bf16[96,2048]{1,0:T(8,128)(2,1)} %get-tuple-element.97), channel_id=1, source_target_pairs={{0,2},{1,3},{2,0},{3,1},{4,6},{5,7},{6,4},{7,5},{8,10},{9,11},{10,... | collective-permute-start | bytes 1179656 | tf_op jit(solution)/shard_map/ppermute | solution.py:648
  109.6 0.8 copy-start.11
  109.6 16.4 %collective-permute-start.21 = (bf16[384,1024]{1,0:T(8,128)(2,1)S(1)}, bf16[384,1024]{1,0:T(8,128)(2,1)}, u32[]{:S(2)}, u32[]{:S(2)}) collective-permute-start(bf16[384,1024]{1,0:T(8,128)(2,1)S(1)} %collective-permute-done.10.refs_0_), channel_id=1, source_target_pairs={{0,1},{1,0},{2,3},{3,2},{4,5},{5,4},{6,7},{7,6},{8,9},{9,8},{10,11... | collective-permute-start | bytes 2359304 | tf_op jit(solution)/shard_map/ppermute | solution.py:648
  109.6 0.9 copy-start.12
  109.6 16.4 %collective-permute-start.22 = (bf16[384,1024]{1,0:T(8,128)(2,1)S(1)}, bf16[384,1024]{1,0:T(8,128)(2,1)}, u32[]{:S(2)}, u32[]{:S(2)}) collective-permute-start(bf16[384,1024]{1,0:T(8,128)(2,1)S(1)} %collective-permute-done.11.refs_1_), channel_id=1, source_target_pairs={{0,1},{1,0},{2,3},{3,2},{4,5},{5,4},{6,7},{7,6},{8,9},{9,8},{10,11... | collective-permute-start | bytes 2359304 | tf_op jit(solution)/shard_map/ppermute | solution.py:648
  110.5 15.5 %copy-start.7 = (bf16[384,1024]{1,0:T(8,128)(2,1)}, bf16[384,1024]{1,0:T(8,128)(2,1)S(1)}, u32[]{:S(2)}) copy-start(bf16[384,1024]{1,0:T(8,128)(2,1)S(1)} %collective-permute-done.20.refs_2_) | copy-start | bytes 2359300
  110.5 15.5 %collective-permute-start.23 = (bf16[384,1024]{1,0:T(8,128)(2,1)S(1)}, bf16[384,1024]{1,0:T(8,128)(2,1)}, u32[]{:S(2)}, u32[]{:S(2)}) collective-permute-start(bf16[384,1024]{1,0:T(8,128)(2,1)S(1)} %collective-permute-done.20.refs_2_), channel_id=1, source_target_pairs={{0,1},{1,0},{2,3},{3,2},{4,5},{5,4},{6,7},{7,6},{8,9},{9,8},{10,11... | collective-permute-start | bytes 2359304 | tf_op jit(solution)/shard_map/ppermute | solution.py:648
  110.9 14.0 %copy-start.10 = (bf16[96,2048]{1,0:T(8,128)(2,1)S(1)}, bf16[96,2048]{1,0:T(8,128)(2,1)}, u32[]{:S(2)}) copy-start(bf16[96,2048]{1,0:T(8,128)(2,1)} %copy-done.9) | copy-start | bytes 1179652
  110.9 24.5 %collective-permute-start.27 = (bf16[96,2048]{1,0:T(8,128)(2,1)}, bf16[96,2048]{1,0:T(8,128)(2,1)S(1)}, u32[]{:S(2)}, u32[]{:S(2)}) collective-permute-start(bf16[96,2048]{1,0:T(8,128)(2,1)} %add_convert_fusion), channel_id=1, source_target_pairs={{0,4},{1,5},{2,6},{3,7},{4,0},{5,1},{6,2},{7,3},{8,12},{9,13},{10,... | collective-permute-start | bytes 1179656 | tf_op jit(solution)/shard_map/ppermute | solution.py:648
  124.9 10.5 %collective-permute-start.24 = (bf16[96,2048]{1,0:T(8,128)(2,1)S(1)}, bf16[96,2048]{1,0:T(8,128)(2,1)}, u32[]{:S(2)}, u32[]{:S(2)}) collective-permute-start(bf16[96,2048]{1,0:T(8,128)(2,1)S(1)} %copy-done.10), channel_id=1, source_target_pairs={{0,2},{1,3},{2,0},{3,1},{4,6},{5,7},{6,4},{7,5},{8,10},{9,11},{10,... | collective-permute-start | bytes 1179656 | tf_op jit(solution)/shard_map/ppermute | solution.py:648
  135.4 1.9 %collective-permute-start.28 = (bf16[96,2048]{1,0:T(8,128)(2,1)}, bf16[96,2048]{1,0:T(8,128)(2,1)S(1)}, u32[]{:S(2)}, u32[]{:S(2)}) collective-permute-start(bf16[96,2048]{1,0:T(8,128)(2,1)} %collective-permute-done.24.own_ref), channel_id=1, source_target_pairs={{0,1},{1,0},{2,3},{3,2},{4,5},{5,4},{6,7},{7,6},{8,9},{9,8},{10,11... | collective-permute-start | bytes 1179656 | tf_op jit(solution)/shard_map/ppermute | solution.py:648
  135.6 4.5 %collective-permute-start.29 = (f32[48,2048]{1,0:T(8,128)S(1)}, f32[48,2048]{1,0:T(8,128)S(1)}, u32[]{:S(2)}, u32[]{:S(2)}) collective-permute-start(f32[48,2048]{1,0:T(8,128)S(1)} %get-tuple-element.105), channel_id=1, source_target_pairs={{0,1},{1,0},{2,3},{3,2},{4,5},{5,4},{6,7},{7,6},{8,9},{9,8},{10,11... | collective-permute-start | bytes 1179656 | tf_op jit(solution)/shard_map/ppermute | solution.py:648
  137.4 0.7 copy-start.13
